TPU v7x, 32 devices: a whole 2x2x4 slice. The times are simulated.
32 devices in a mesh: fsdp: 8 (over z, x), tensor: 4 (over y, core).
Axes of the slice: x: 2, y: 2, z: 4, core: 2. Of those that a mesh axis runs over, the one named last changes fastest.
Arguments:
- momentum: float32 [1920, 6144], P('fsdp', 'tensor'), may hold values from -100 to 100
- gradient: bfloat16 [1920, 6144], P('fsdp', 'tensor'), may hold values from -3 to 3
- right_basis: float32 [6144, 512], P('tensor'), may hold values from -0.078125 to 0.078125
Outputs:
- update: bfloat16 [1920, 6144], P('fsdp', 'tensor')
- new_momentum: float32 [1920, 6144], P('fsdp', 'tensor')
- left_scaled: float32 [1920, 512], P('fsdp')
- next_basis: float32 [6144, 512], P(('tensor', 'fsdp'))
All inputs are finite; a program needn't handle non-finite values.
Results may differ from a plain program's by a relative error of at most 0.001.
Values sent between devices are 32-bit elements; how exact they have to be, the bound alone decides.
No kernel may reach another device: no remote copies, remote signals or barrier semaphores. Data moves between devices by JAX's collectives and lax.ppermute only.
A program may use at most 64 MiB of HBM per device.

v0:
```python
import math

import jax
import jax.numpy as jnp
from jax import lax
from jax.sharding import PartitionSpec as P

epsilon = 1e-06


def share_norms(right_rows):
    squares = lax.psum(jnp.sum(right_rows * right_rows, axis=0), ("fsdp", "tensor"))
    return jnp.sqrt(squares + epsilon)


def planes_for(left, scaled_left, right_rows):
    highest = lax.Precision.HIGHEST
    product = jnp.dot(left, right_rows.T, precision=highest)
    update = jnp.dot(scaled_left, right_rows.T, precision=highest)
    return jnp.stack((product, update))


def on_device(momentum, gradient, right_basis):
    highest = lax.Precision.HIGHEST
    summed = momentum + gradient.astype(jnp.float32)
    left_part = jnp.dot(summed, right_basis, precision=highest)
    left_raw = lax.psum(left_part, "tensor")
    gram = lax.psum(jnp.dot(left_raw.T, left_raw, precision=highest), "fsdp")
    factor_lower = jnp.linalg.cholesky(gram)
    left = jax.scipy.linalg.solve_triangular(factor_lower, left_raw.T, lower=True).T
    groups = lax.axis_size("fsdp")
    total_rows = left.shape[0] * groups
    total_cols = summed.shape[1] * lax.axis_size("tensor")
    factor = math.sqrt(total_rows / total_cols)
    right_rows = lax.psum_scatter(
        jnp.dot(summed.T, left, precision=highest), "fsdp", scatter_dimension=0, tiled=True
    )
    column_norm = share_norms(right_rows)
    scaled_left = left * (factor / column_norm)[None, :]
    planes = planes_for(left, scaled_left, lax.all_gather(right_rows, "fsdp", axis=0, tiled=True))
    product = planes[0]
    update = planes[1].astype(jnp.bfloat16)
    new_momentum = summed - 0.5 * product
    next_basis = right_rows / column_norm[None, :]
    return (update, new_momentum, left * math.sqrt(total_rows), next_basis)


def solution(mesh):
    in_specs = (P("fsdp", "tensor"), P("fsdp", "tensor"), P("tensor", None))
    out_specs = (
        P("fsdp", "tensor"),
        P("fsdp", "tensor"),
        P("fsdp", None),
        P(("tensor", "fsdp"), None),
    )
    return jax.shard_map(
        on_device, mesh=mesh, in_specs=in_specs, out_specs=out_specs, check_vma=False
    )
```

profile of v0, /device:TPU:0, one launch (start us, length us, event | category | flops | bytes accessed | tf_op | source)
XLA Modules:
  0.0 454.8 jit_solution(7510781662236354324)
XLA Ops:
  9.1 5.1 %fusion.3 = f32[240,512]{1,0:T(8,128)} fusion(f32[1536,512]{1,0:T(8,128)S(1)} %copy-done, f32[240,1536]{1,0:T(8,128)} %param.3, bf16[240,1536]{1,0:T(8,128)(2,1)} %param.4), kind=kOutput, calls=%fused_computation.19 | convolution fusion | flops 2265661440 | bytes 5849088 | tf_op jit(solution)/shard_map/dot_general | solution.py:26
  14.2 35.7 %all-reduce.4.cloned.1.call-done = f32[240,512]{1,0:T(8,128)} async-done(((f32[240,512]{1,0:T(8,128)}), f32[240,512]{1,0:T(8,128)}) %all-reduce.4.cloned.1.call-update) | async-done | bytes 491536 | tf_op jit(solution)/shard_map/psum | solution.py:27
  49.9 3.2 fusion.36
  53.8 78.8 %all-reduce.6.cloned.1.call-done = f32[512,512]{0,1:T(8,128)} async-done(((f32[512,512]{0,1:T(8,128)}), f32[512,512]{0,1:T(8,128)}) %all-reduce.6.cloned.1.call-update) | async-done | bytes 1048592 | tf_op jit(solution)/shard_map/psum | solution.py:28
  137.8 11.7 %cholesky.104 = f32[128,128]{1,0:T(8,128)S(1)} custom-call(f32[128,128]{1,0:T(8,128)S(1)} %cholesky.266), custom_call_target="Cholesky" | custom-call | tf_op jit(solution)/shard_map/jit(cholesky)/cholesky | solution.py:29
  150.7 9.8 %custom-call.31 = f32[1,128,128]{1,2,0:T(8,128)S(1)} custom-call(f32[1,128,128]{2,1,0:T(8,128)S(1)} %get-tuple-element.31), custom_call_target="InvertDiagBlocksLowerTriangular" | custom-call | tf_op jit(solution)/shard_map/jit(cholesky)/cholesky | solution.py:29
  163.7 11.7 %cholesky.217 = f32[128,128]{1,0:T(8,128)S(1)} custom-call(f32[128,128]{1,0:T(8,128)S(1)} %cholesky.270), custom_call_target="Cholesky" | custom-call | tf_op jit(solution)/shard_map/jit(cholesky)/cholesky | solution.py:29
  176.0 9.9 %custom-call.32 = f32[1,128,128]{1,2,0:T(8,128)S(1)} custom-call(f32[1,128,128]{2,1,0:T(8,128)S(1)} %get-tuple-element.28), custom_call_target="InvertDiagBlocksLowerTriangular" | custom-call | tf_op jit(solution)/shard_map/jit(cholesky)/cholesky | solution.py:29
  188.4 11.7 %cholesky.238 = f32[128,128]{1,0:T(8,128)S(1)} custom-call(f32[128,128]{1,0:T(8,128)S(1)} %cholesky.275), custom_call_target="Cholesky" | custom-call | tf_op jit(solution)/shard_map/jit(cholesky)/cholesky | solution.py:29
  200.7 9.8 %custom-call.33 = f32[1,128,128]{1,2,0:T(8,128)S(1)} custom-call(f32[1,128,128]{2,1,0:T(8,128)S(1)} %get-tuple-element.25), custom_call_target="InvertDiagBlocksLowerTriangular" | custom-call | tf_op jit(solution)/shard_map/jit(cholesky)/cholesky | solution.py:29
  212.8 11.7 %cholesky.255 = f32[128,128]{1,0:T(8,128)S(1)} custom-call(f32[128,128]{1,0:T(8,128)S(1)} %convolution_subtract_fusion.5), custom_call_target="Cholesky" | custom-call | tf_op jit(solution)/shard_map/jit(cholesky)/cholesky | solution.py:29
  229.7 2.5 select_select_fusion
  232.2 14.5 %while.1 = (s32[]{:T(128)}, f32[512,512]{1,0:T(8,128)}, s32[4,2]{0,1:T(2,128)S(1)}, f32[4,128,128]{2,1,0:T(8,128)}, s32[]{:T(128)}) while((s32[]{:T(128)}, f32[512,512]{1,0:T(8,128)}, s32[4,2]{0,1:T(2,128)S(1)}, f32[4,128,128]{2,1,0:T(8,128)}, s32[]{:T(128)}) %tuple.32), condition=%wide.while_cond, body=%wide.while_body.sunk | while | flops 2 | bytes 132205 | solution.py:30
  232.9 3.0 bitcast_dynamic-update-slice_fusion.2
  236.5 3.0 bitcast_dynamic-update-slice_fusion.2
  240.2 3.0 bitcast_dynamic-update-slice_fusion.2
  243.8 2.9 bitcast_dynamic-update-slice_fusion.2
  246.7 40.1 %custom-call.34 = f32[4,128,128]{1,2,0:T(8,128)S(1)} custom-call(f32[4,128,128]{2,1,0:T(8,128)} %get-tuple-element.11), custom_call_target="InvertDiagBlocksLowerTriangular" | custom-call | tf_op jit(solution)/shard_map/jit(_solve_triangular)/triangular_solve | solution.py:30
  296.3 4.4 fusion.2
  300.8 74.2 %reduce-scatter.2.cloned.1.call-done = f32[192,512]{1,0:T(8,128)} async-done(((f32[1536,512]{1,0:T(8,128)}), f32[192,512]{1,0:T(8,128)}) %reduce-scatter.2.cloned.1.call-update) | async-done | bytes 393232 | tf_op jit(solution)/shard_map/reduce_scatter | solution.py:35
  377.8 40.4 %psum.23 = f32[512]{0:T(512)S(1)} all-reduce(f32[512]{0:T(512)S(1)} %multiply_reduce_fusion), channel_id=1, replica_groups=mesh['fsdp'=8,'tensor'=4] {'fsdp','tensor'}, use_global_device_ids=true, to_apply=%region_12.13 | all-reduce | flops 512 | bytes 4096 | tf_op jit(solution)/shard_map/psum | solution.py:12
  420.1 17.6 %all-gather.2.cloned.1.call-done = f32[1536,512]{1,0:T(8,128)} async-done(((f32[192,512]{1,0:T(8,128)}), f32[1536,512]{1,0:T(8,128)}) %all-gather.2.cloned.1.call-update) | async-done | bytes 3145744 | tf_op jit(solution)/shard_map/all_gather | solution.py:40
  437.7 6.6 %fusion = f32[240,1536]{1,0:T(8,128)} fusion(f32[1536,512]{1,0:T(8,128)} %all-gather.2.cloned.1.call-done, f32[240,1536]{1,0:T(8,128)} %param.3, bf16[240,1536]{1,0:T(8,128)(2,1)} %param.4, f32[128,240]{0,1:T(8,128)} %copy-done.4, f32[128,240]{0,1:T(8,128)S(1)} %fusion.25, f32[128,240]{0,1:T(8,128)S(1)} %fusion.27, f32[128,240]{0,1:T(8,128)S(1)} %fusion.22), kind=kOutput, calls=%fused_computation.3 | convolution fusion | flops 2266767360 | bytes 7323648 | tf_op jit(solution)/shard_map/dot_general | solution.py:18
  444.3 3.7 convolution_convert_fusion
  (65 shorter events, 37.4 us)
Async XLA Ops:
  7.2 1.9 copy-start
  7.2 42.8 %all-reduce.4.cloned.1.call-start = ((), (), s32[]{:S(2)}) async-start(), calls=%async_computation.1 | async-start | bytes 983040 | tf_op jit(solution)/shard_map/psum | solution.py:27
  14.1 118.4 %all-reduce.6.cloned.1.call-start = ((), (), s32[]{:S(2)}) async-start(), calls=%async_computation.2 | async-start | bytes 2097152 | tf_op jit(solution)/shard_map/psum | solution.py:28
  53.2 321.8 %reduce-scatter.2.cloned.1.call-start = ((), (), s32[]{:S(2)}) async-start(), calls=%async_computation.3 | async-start | bytes 3538944 | tf_op jit(solution)/shard_map/reduce_scatter | solution.py:35
  136.8 1.0 copy-start.6
  286.8 1.3 copy-start.7
  288.1 8.2 %copy-start.1 = (f32[240,1536]{1,0:T(8,128)S(1)}, f32[240,1536]{1,0:T(8,128)}, u32[]{:S(2)}) copy-start(f32[240,1536]{1,0:T(8,128)} %param.3) | copy-start | bytes 4423684
  288.1 8.2 %copy-start.3 = (bf16[240,1536]{1,0:T(8,128)(2,1)S(1)}, bf16[240,1536]{1,0:T(8,128)(2,1)}, u32[]{:S(2)}) copy-start(bf16[240,1536]{1,0:T(8,128)(2,1)} %param.4) | copy-start | bytes 2211844
  295.6 0.7 copy-start.4
  300.7 137.0 %all-gather.2.cloned.1.call-start = ((), (), s32[]{:S(2)}) async-start(), calls=%async_computation.4 | async-start | bytes 3538944 | tf_op jit(solution)/shard_map/all_gather | solution.py:40
  437.7 6.6 %copy-start.2 = (f32[1536,512]{1,0:T(8,128)S(1)}, f32[1536,512]{1,0:T(8,128)}, u32[]{:S(2)}) copy-start(f32[1536,512]{1,0:T(8,128)} %all-gather.2.cloned.1.call-done) | copy-start | bytes 9437188
  437.7 6.6 %copy-start.5 = (f32[128,240]{0,1:T(8,128)S(1)}, f32[128,240]{0,1:T(8,128)}, u32[]{:S(2)}) copy-start(f32[128,240]{0,1:T(8,128)} %copy-done.4) | copy-start | bytes 368644
Sparse Core Ops, SparseCore 0:
  14.3 35.6 all-reduce.3
  54.4 78.0 all-reduce.5
  300.9 74.0 reduce-scatter.1
  377.0 60.6 all-gather.1
where the time goes:
time: 459 us; the launch traced here: 455 us
  waiting for transfers between devices  206 us (45%)
  other arithmetic  129 us (28%)
  blocking collectives  40.4 us (9%)
  matrix products  39.5 us (9%)
  local copies, waits for them, and re-layouts  21.6 us (5%)
  between operations  16.8 us (4%)
    another operation x14, other arithmetic, on_device(): factor_lower = jnp.linalg.cholesky(gram)  80.4 us
    psum x1, waiting for transfers between devices, on_device(): gram = lax.psum(jnp.dot(left_raw.T, left_raw, precision=highest), 'fsdp')  78.8 us
    reduce_scatter x1, waiting for transfers between devices, on_device(): lax.psum_scatter(jnp.dot(summed.T, left, precision=highest), 'fsdp', scat...  74.2 us
    another operation x3, other arithmetic, on_device(): jax.scipy.linalg.solve_triangular(factor_lower, left_raw.T, lower=True)  42.7 us
    psum x1, blocking collectives, share_norms(): lax.psum(jnp.sum(right_rows * right_rows, axis=0), ('fsdp', 'tensor'))  40.4 us
    psum x1, waiting for transfers between devices, on_device(): left_raw = lax.psum(left_part, 'tensor')  35.7 us
    all_gather x1, waiting for transfers between devices, on_device(): lax.all_gather(right_rows, 'fsdp', axis=0, tiled=True)  17.6 us
    another operation x12, local copies, waits for them, and re-layouts  14.5 us
  transfers between devices with their start and end apart: 4, of which 4 were waited for; matrix products, arithmetic and copies ran while one was open for 1% of the time, Pallas kernels for 0%

commit v1 on v0

v1 whole, which is shorter than its diff:
```python
import functools
import math

import jax
import jax.numpy as jnp
from jax import lax
from jax.experimental import pallas as pl
from jax.experimental.pallas import tpu as pltpu
from jax.sharding import PartitionSpec as P

epsilon = 1e-06
highest = lax.Precision.HIGHEST
lanes = 128
panel = 8
square = 4


def dot(a, b, contract=((1,), (0,))):
    return lax.dot_general(
        a, b, (contract, ((), ())), precision=highest, preferred_element_type=jnp.float32
    )


def factor_block(block):
    size = block.shape[0]
    lane = lax.broadcasted_iota(jnp.int32, (panel, size), 1)
    row = lax.broadcasted_iota(jnp.int32, (panel, size), 0)
    for first in range(0, size, panel):
        count = size - first
        now = block[first:, :]
        columns = [
            jnp.broadcast_to(now[:, first + k : first + k + 1], (count, size)) for k in range(panel)
        ]
        inside = (lane >= first) & (lane < first + panel)
        head = jnp.where(inside, jnp.where(lane - first == row, 1.0, 0.0), now[:panel])
        tail = None
        if count > panel:
            lane_below = lax.broadcasted_iota(jnp.int32, (count - panel, size), 1)
            inside_below = (lane_below >= first) & (lane_below < first + panel)
            tail = jnp.where(inside_below, 0.0, now[panel:])
        for j in range(panel):
            inverse = lax.rsqrt(columns[j][j : j + 1, :])
            multiplier = columns[j] * inverse
            for k in range(j + 1, panel):
                columns[k] = columns[k] - multiplier * (columns[k][j : j + 1, :] * inverse)
            pivot = head[j : j + 1, :] * inverse
            below = jnp.where(row > j, head - multiplier[:panel] * pivot, head)
            head = jnp.where(row == j, pivot, below)
            if tail is not None:
                tail = tail - multiplier[panel:] * pivot
        block[first : first + panel, :] = head
        if tail is not None:
            block[first + panel :, :] = tail


def inverse_factor_kernel(gram_ref, out_ref, work, block):
    size = gram_ref.shape[0]
    count = size // lanes
    work[...] = gram_ref[...]
    row = lax.broadcasted_iota(jnp.int32, (lanes, lanes), 0)
    lower = row >= lax.broadcasted_iota(jnp.int32, (lanes, lanes), 1)
    column_block = lax.broadcasted_iota(jnp.int32, (lanes, size), 1) // lanes

    def step(b, carry):
        own_rows = pl.ds(pl.multiple_of(b * lanes, lanes), lanes)
        block[...] = work[own_rows, own_rows]
        factor_block(block)
        inverse = jnp.where(lower, block[...], 0.0)
        own = column_block == b
        work[own_rows, :] = dot(inverse, jnp.where(own, 0.0, work[own_rows, :]))
        work[own_rows, own_rows] = inverse
        out_ref[own_rows, :] = jnp.where(column_block <= b, work[own_rows, :], 0.0)

        def update(i, carry):
            rows = pl.ds(pl.multiple_of(i * lanes, lanes), lanes)
            change = dot(work[own_rows, rows], work[own_rows, :], ((0,), (0,)))
            work[rows, :] = jnp.where(own, 0.0, work[rows, :]) - change
            return carry

        return lax.fori_loop(b + 1, count, update, carry)

    lax.fori_loop(0, count, step, 0)


def inverse_factor(gram):
    size = gram.shape[0]
    return pl.pallas_call(
        inverse_factor_kernel,
        out_shape=jax.ShapeDtypeStruct((size, size), jnp.float32),
        scratch_shapes=[
            pltpu.VMEM((size, size), jnp.float32),
            pltpu.VMEM((lanes, lanes), jnp.float32),
        ],
        compiler_params=pltpu.CompilerParams(vmem_limit_bytes=32 * 2**20),
        cost_estimate=pl.CostEstimate(
            flops=12 * size**3, bytes_accessed=8 * size * size, transcendentals=size
        ),
        name="inverse_factor",
    )(gram)


def share_norms(right_rows):
    squares = lax.psum(jnp.sum(right_rows * right_rows, axis=0), ("fsdp", "tensor"))
    return jnp.sqrt(squares + epsilon)


def any_mesh(momentum, gradient, right_basis):
    summed = momentum + gradient.astype(jnp.float32)
    left_raw = lax.psum(dot(summed, right_basis), "tensor")
    gram = lax.psum(dot(left_raw, left_raw, ((0,), (0,))), "fsdp")
    inverse = inverse_factor(gram)
    left = dot(left_raw, inverse, ((1,), (1,)))
    total_rows = left.shape[0] * lax.axis_size("fsdp")
    total_cols = summed.shape[1] * lax.axis_size("tensor")
    raw_rows = lax.psum_scatter(
        dot(summed, left_raw, ((0,), (0,))), "fsdp", scatter_dimension=0, tiled=True
    )
    right_rows = dot(raw_rows, inverse, ((1,), (1,)))
    column_norm = share_norms(right_rows)
    scaled_left = left * (math.sqrt(total_rows / total_cols) / column_norm)[None, :]
    raw = lax.all_gather(raw_rows, "fsdp", axis=0, tiled=True)
    product = dot(dot(left, inverse), raw, ((1,), (1,)))
    update = dot(dot(scaled_left, inverse), raw, ((1,), (1,))).astype(jnp.bfloat16)
    new_momentum = summed - 0.5 * product
    return (update, new_momentum, left * math.sqrt(total_rows), right_rows / column_norm[None, :])


def swap(value, axis, flip):
    return lax.ppermute(value, axis, [(i, i ^ flip) for i in range(lax.axis_size(axis))])


def split_kernel(place, momentum, gradient, *pieces):
    width = pieces[0].shape[1]
    for k, piece in enumerate(pieces):
        at = pl.ds(pl.multiple_of((place[0] ^ k) * width, lanes), width)
        piece[...] = momentum[:, at] + gradient[:, at].astype(jnp.float32)


def split_sum(place, momentum, gradient):
    rows, cols = momentum.shape
    return pl.pallas_call(
        split_kernel,
        out_shape=[jax.ShapeDtypeStruct((rows, cols // square), jnp.float32)] * square,
        in_specs=[
            pl.BlockSpec(memory_space=pltpu.SMEM),
            pl.BlockSpec(memory_space=pltpu.VMEM),
            pl.BlockSpec(memory_space=pltpu.VMEM),
        ],
        compiler_params=pltpu.CompilerParams(vmem_limit_bytes=32 * 2**20),
        cost_estimate=pl.CostEstimate(
            flops=rows * cols, bytes_accessed=10 * rows * cols, transcendentals=0
        ),
        name="split_sum",
    )(place, momentum, gradient)


def ordered(bit, mine, other):
    first = jnp.where(bit == 0, mine, other)
    second = jnp.where(bit == 0, other, mine)
    return jnp.concatenate([first, second], axis=0)


def in_squares(momentum, gradient, right_basis):
    device = lax.axis_index("fsdp")
    place = device % square
    tensor = lax.axis_index("tensor")
    core, plane = tensor % 2, tensor // 2
    rows, cols = momentum.shape
    rank = right_basis.shape[1]
    half, width = rows // 2, cols // square
    total_rows = rows * lax.axis_size("fsdp")
    total_cols = cols * lax.axis_size("tensor")

    pieces = split_sum(place.reshape(1), momentum, gradient)
    columns = [pieces[0]] + [swap(pieces[k], "fsdp", k) for k in range(1, square)]

    summed = momentum + gradient.astype(jnp.float32)
    part = dot(summed, right_basis)
    sent = lax.dynamic_slice_in_dim(part, (1 - core) * half, half, 0)
    kept = lax.dynamic_slice_in_dim(part, core * half, half, 0)
    mine = kept + swap(sent, "tensor", 1)
    mine = mine + swap(mine, "tensor", 2)
    in_square = jnp.concatenate(
        [mine] + [swap(mine, "fsdp", k) for k in range(1, square)], axis=0
    )
    other = swap(in_square, "tensor", 1)

    part_gram = dot(in_square, in_square, ((0,), (0,)))
    count = rank // lanes
    blocks = [(i, j) for j in range(count) for i in range(j, count)]
    stack = jnp.concatenate(
        [part_gram[i * lanes : (i + 1) * lanes, j * lanes : (j + 1) * lanes] for i, j in blocks], axis=0
    )
    share = stack.shape[0] // 4
    sent = lax.dynamic_slice_in_dim(stack, (2 * plane + 1 - core) * share, share, 0)
    kept = lax.dynamic_slice_in_dim(stack, (2 * plane + core) * share, share, 0)
    quarter = kept + swap(sent, "tensor", 1)
    quarter = quarter + swap(quarter, "fsdp", square)
    over_cores = ordered(core, quarter, swap(quarter, "tensor", 1))
    stack = ordered(plane, over_cores, swap(over_cores, "tensor", 2))
    found = {}
    for at, (i, j) in enumerate(blocks):
        block = stack[at * lanes : (at + 1) * lanes]
        found[i, j] = block
        found[j, i] = block if i == j else block.T
    gram = jnp.concatenate(
        [jnp.concatenate([found[i, j] for j in range(count)], axis=1) for i in range(count)], axis=0
    )

    square_rows = jnp.concatenate(
        [ordered(core, in_square[k * half : (k + 1) * half], other[k * half : (k + 1) * half]) for k in range(square)],
        axis=0,
    )
    part_raw = dot(jnp.concatenate(columns, axis=0), square_rows, ((0,), (0,)))
    step = lanes
    raw = jnp.zeros((cols, rank), jnp.float32)
    own = []
    for at in range(0, width, step):
        share_raw = part_raw[at : at + step]
        share_raw = share_raw + swap(share_raw, "fsdp", square)
        own.append(share_raw)
        for k in range(square):
            block = share_raw if k == 0 else swap(share_raw, "fsdp", k)
            raw = lax.dynamic_update_slice_in_dim(raw, block, (place ^ k) * width + at, 0)
    own = jnp.concatenate(own, axis=0)

    inverse = inverse_factor(gram)
    left_raw = square_rows[:rows]
    left = dot(left_raw, inverse, ((1,), (1,)))
    norm_rows = lax.dynamic_slice_in_dim(own, (device // square) * (width // 2), width // 2, 0)
    norm_rows = dot(norm_rows, inverse, ((1,), (1,)))
    squares = jnp.sum(norm_rows * norm_rows, axis=0, keepdims=True)
    for axis in ("tensor", "fsdp"):
        flip = 1
        while flip < lax.axis_size(axis):
            squares = squares + swap(squares, axis, flip)
            flip *= 2
    column_norm = jnp.sqrt(squares + epsilon)
    scaled_left = left * (math.sqrt(total_rows / total_cols) / column_norm)
    planes = dot(jnp.concatenate([left, scaled_left], axis=0), inverse)

    both = dot(planes, raw, ((1,), (1,)))
    new_momentum = summed - 0.5 * both[:rows]
    update = both[rows:].astype(jnp.bfloat16)
    out_rows = cols // lax.axis_size("fsdp")
    right_rows = dot(
        lax.dynamic_slice_in_dim(raw, device * out_rows, out_rows, 0), inverse, ((1,), (1,))
    )
    return (update, new_momentum, left * math.sqrt(total_rows), right_rows / column_norm)


def on_device(momentum, gradient, right_basis):
    rows, cols = momentum.shape
    pairs = lax.axis_size("fsdp") == 2 * square and lax.axis_size("tensor") == 4
    aligned = rows % 16 == 0 and cols % (square * lanes) == 0 and right_basis.shape[1] % lanes == 0
    plan = in_squares if pairs and aligned else any_mesh
    return plan(momentum, gradient, right_basis)


def solution(mesh):
    in_specs = (P("fsdp", "tensor"), P("fsdp", "tensor"), P("tensor", None))
    out_specs = (
        P("fsdp", "tensor"),
        P("fsdp", "tensor"),
        P("fsdp", None),
        P(("tensor", "fsdp"), None),
    )
    return jax.shard_map(
        on_device, mesh=mesh, in_specs=in_specs, out_specs=out_specs, check_vma=False
    )
```

time: 459 us -> 215 us (0.47)
  waiting for transfers between devices: 206 us -> 67.2 us
  other arithmetic: 129 us -> 29 us
  blocking collectives: 40.4 us -> 0 us
  starting transfers between devices: 0.69 us -> 37.8 us
  Pallas kernels: 0 us -> 19.7 us
  between operations: 16.8 us -> 1 us
  matrix products: 39.5 us -> 28 us
  local copies, waits for them, and re-layouts: 21.6 us -> 31.3 us
    another operation x17 -> x0, other arithmetic: 123 us -> none  [the longest x14 80.4 us: on_device(): factor_lower = jnp.linalg.cholesky(gram)]
    psum x2 -> x0, waiting for transfers between devices: 115 us -> none  [the longest x1 78.8 us: on_device(): gram = lax.psum(jnp.dot(left_raw.T, left_raw, precision=highest), 'fsdp')]
    reduce_scatter x1 -> x0, waiting for transfers between devices: 74.2 us -> none  [on_device(): lax.psum_scatter(jnp.dot(summed.T, left, precision=highest), 'fsdp', scat...]
    ppermute x0 -> x30, waiting for transfers between devices: none -> 67.2 us  [swap(): lax.ppermute(value, axis, [(i, i ^ flip) for i in range(lax.axis_size(axi...]
    psum x1 -> x0, blocking collectives: 40.4 us -> none  [share_norms(): lax.psum(jnp.sum(right_rows * right_rows, axis=0), ('fsdp', 'tensor'))]
    ppermute x0 -> x30, starting transfers between devices: none -> 37.8 us  [swap(): lax.ppermute(value, axis, [(i, i ^ flip) for i in range(lax.axis_size(axi...]
    pallas_call x0 -> x2, Pallas kernels: none -> 19.7 us  [the longest x1 18.6 us: inverse_factor(): pl.pallas_call(inverse_factor_kernel, out_shape=jax.ShapeDtypeStruct((siz...]
    all_gather x1 -> x0, waiting for transfers between devices: 17.6 us -> none  [on_device(): lax.all_gather(right_rows, 'fsdp', axis=0, tiled=True)]
  transfers between devices with their start and end apart: 4 -> 30, of which waited for: 4 -> 16; matrix products, arithmetic and copies ran while one was open for 1% -> 23% of each run, Pallas kernels for 0% -> 9%
where the time goes in v1:
time: 215 us; the launch traced here: 214 us
  waiting for transfers between devices  67.2 us (31%)
  starting transfers between devices  37.8 us (18%)
  local copies, waits for them, and re-layouts  31.3 us (15%)
  other arithmetic  29 us (13%)
  matrix products  28 us (13%)
  Pallas kernels  19.7 us (9%)
    ppermute x30, waiting for transfers between devices, swap(): lax.ppermute(value, axis, [(i, i ^ flip) for i in range(lax.axis_size(axi...  67.2 us
    ppermute x30, starting transfers between devices, swap(): lax.ppermute(value, axis, [(i, i ^ flip) for i in range(lax.axis_size(axi...  37.8 us
    dot_general x8, matrix products, dot(): lax.dot_general(a, b, (contract, ((), ())), precision=highest, preferred_...  28 us
    pallas_call x1, Pallas kernels, inverse_factor(): pl.pallas_call(inverse_factor_kernel, out_shape=jax.ShapeDtypeStruct((siz...  18.6 us
    unnamed x38, local copies, waits for them, and re-layouts  12.4 us
    dynamic_update_slice x9, local copies, waits for them, and re-layouts, in_squares(): lax.dynamic_update_slice_in_dim(raw, block, (place ^ k) * width + at, 0)  9.29 us
    unnamed x7, other arithmetic  8.74 us
    dynamic_update_slice x3, other arithmetic, in_squares(): lax.dynamic_update_slice_in_dim(raw, block, (place ^ k) * width + at, 0)  5.21 us
  transfers between devices with their start and end apart: 30, of which 16 were waited for; matrix products, arithmetic and copies ran while one was open for 23% of the time, Pallas kernels for 9%

profile of v1, /device:TPU:0, one launch (start us, length us, event | category | flops | bytes accessed | tf_op | source)
XLA Modules:
  0.0 213.9 jit_solution(2567683276580381837)
XLA Ops:
  2.5 4.3 %fusion.10 = f32[240,512]{1,0:T(8,128)S(1)} fusion(f32[1536,512]{1,0:T(8,128)S(1)} %copy-done, f32[240,1536]{1,0:T(8,128)} %momentum.1, bf16[240,1536]{1,0:T(8,128)(2,1)} %gradient.1), kind=kOutput, calls=%fused_computation.16 | convolution fusion | flops 2265661440 | bytes 5849088 | tf_op jit(solution)/shard_map/dot_general | solution.py:19
  10.5 3.0 %collective-permute-start.1 = (f32[120,512]{1,0:T(8,128)S(1)}, f32[120,512]{1,0:T(8,128)S(1)}, u32[]{:S(2)}, u32[]{:S(2)}) collective-permute-start(f32[120,512]{1,0:T(8,128)S(1)} %dynamic-slice_add_fusion), channel_id=1, source_target_pairs={{0,2},{1,3},{2,0},{3,1},{4,6},{5,7},{6,4},{7,5},{8,10},{9,11},{10,... | collective-permute-start | bytes 737288 | tf_op jit(solution)/shard_map/ppermute | solution.py:129
  13.5 6.3 %collective-permute-done.1 = f32[120,512]{1,0:T(8,128)S(1)} collective-permute-done((f32[120,512]{1,0:T(8,128)S(1)}, f32[120,512]{1,0:T(8,128)S(1)}, u32[]{:S(2)}, u32[]{:S(2)}) %collective-permute-start.1) | collective-permute-done | bytes 245792 | tf_op jit(solution)/shard_map/ppermute | solution.py:129
  23.3 4.6 %collective-permute-done.2 = f32[120,512]{1,0:T(8,128)} collective-permute-done((f32[120,512]{1,0:T(8,128)S(1)}, f32[120,512]{1,0:T(8,128)}, u32[]{:S(2)}, u32[]{:S(2)}) %collective-permute-start.2) | collective-permute-done | bytes 245792 | tf_op jit(solution)/shard_map/ppermute | solution.py:129
  27.9 2.6 %collective-permute-done.3 = f32[120,512]{1,0:T(8,128)} collective-permute-done((f32[120,512]{1,0:T(8,128)S(1)}, f32[120,512]{1,0:T(8,128)}, u32[]{:S(2)}, u32[]{:S(2)}) %collective-permute-start.3) | collective-permute-done | bytes 245792 | tf_op jit(solution)/shard_map/ppermute | solution.py:129
  30.5 3.3 %collective-permute-done.4 = f32[120,512]{1,0:T(8,128)} collective-permute-done((f32[120,512]{1,0:T(8,128)S(1)}, f32[120,512]{1,0:T(8,128)}, u32[]{:S(2)}, u32[]{:S(2)}) %collective-permute-start.4) | collective-permute-done | bytes 245792 | tf_op jit(solution)/shard_map/ppermute | solution.py:129
  33.9 3.4 %fusion.29 = f32[512,512]{1,0:T(8,128)S(1)} fusion(f32[120,512]{1,0:T(8,128)} %collective-permute-done.4, f32[120,512]{1,0:T(8,128)} %collective-permute-done.3, f32[120,512]{1,0:T(8,128)} %collective-permute-done.2, f32[120,512]{1,0:T(8,128)S(1)} %add.159), kind=kOutput, calls=%fused_computation.83 | convolution fusion | flops 1510686720 | bytes 2031616 | tf_op jit(solution)/shard_map/dot_general | solution.py:19
  38.9 2.2 %pad_maximum_fusion = f32[480,512]{1,0:T(8,128)} fusion(f32[120,512]{1,0:T(8,128)} %collective-permute-done.4, f32[120,512]{1,0:T(8,128)} %collective-permute-done.3, f32[120,512]{1,0:T(8,128)} %collective-permute-done.2, f32[120,512]{1,0:T(8,128)S(1)} %add.159), kind=kLoop, calls=%fused_computation.17 | loop fusion | flops 737280 | bytes 1966080 | tf_op jit(solution)/shard_map/concatenate | solution.py:183
  42.6 2.6 %collective-permute-start.7 = (f32[320,128]{1,0:T(8,128)S(1)}, f32[320,128]{1,0:T(8,128)S(1)}, u32[]{:S(2)}, u32[]{:S(2)}) collective-permute-start(f32[320,128]{1,0:T(8,128)S(1)} %dynamic-slice_add_fusion.1), channel_id=1, source_target_pairs={{0,16},{4,20},{8,24},{12,28},{16,0},{20,4},{24,8},{28,12},{1,17},{... | collective-permute-start | bytes 491528 | tf_op jit(solution)/shard_map/ppermute | solution.py:129
  45.1 8.0 %collective-permute-done.7 = f32[320,128]{1,0:T(8,128)S(1)} collective-permute-done((f32[320,128]{1,0:T(8,128)S(1)}, f32[320,128]{1,0:T(8,128)S(1)}, u32[]{:S(2)}, u32[]{:S(2)}) %collective-permute-start.7) | collective-permute-done | bytes 163872 | tf_op jit(solution)/shard_map/ppermute | solution.py:129
  74.0 3.8 %collective-permute-done.12 = f32[240,384]{1,0:T(8,128)} collective-permute-done((f32[240,384]{1,0:T(8,128)}, f32[240,384]{1,0:T(8,128)}, u32[]{:S(2)}, u32[]{:S(2)}) %collective-permute-start.12) | collective-permute-done | bytes 368672 | tf_op jit(solution)/shard_map/ppermute | solution.py:129
  77.9 4.0 %fusion.1 = f32[384,512]{1,0:T(8,128)S(1)} fusion(f32[960,512]{1,0:T(8,128)S(1)} %select_dynamic-update-slice_fusion, f32[240,384]{1,0:T(8,128)} %collective-permute-done.12, f32[240,384]{1,0:T(8,128)} %collective-permute-done.11, f32[240,384]{1,0:T(8,128)} %collective-permute-done.10, f32[240,384]{1,0:T(8,128)S(1)} %get-tuple-element.8), kind=kOutput, calls=%fused_computation.3 | convolution fusion | flops 2266030080 | bytes 4227072 | tf_op jit(solution)/shard_map/dot_general | solution.py:19
  83.5 2.2 %collective-permute-start.13 = (f32[128,512]{1,0:T(8,128)}, f32[128,512]{1,0:T(8,128)S(1)}, u32[]{:S(2)}, u32[]{:S(2)}) collective-permute-start(f32[128,512]{1,0:T(8,128)} %slice.120), channel_id=1, source_target_pairs={{0,16},{4,20},{8,24},{12,28},{16,0},{20,4},{24,8},{28,12},{1,17},{... | collective-permute-start | bytes 786440 | tf_op jit(solution)/shard_map/ppermute | solution.py:129
  86.9 10.9 %collective-permute-done.13 = f32[128,512]{1,0:T(8,128)S(1)} collective-permute-done((f32[128,512]{1,0:T(8,128)}, f32[128,512]{1,0:T(8,128)S(1)}, u32[]{:S(2)}, u32[]{:S(2)}) %collective-permute-start.13) | collective-permute-done | bytes 262176 | tf_op jit(solution)/shard_map/ppermute | solution.py:129
  126.1 6.7 %collective-permute-done.14 = f32[128,512]{1,0:T(8,128)S(1)} collective-permute-done((f32[128,512]{1,0:T(8,128)}, f32[128,512]{1,0:T(8,128)S(1)}, u32[]{:S(2)}, u32[]{:S(2)}) %collective-permute-start.14) | collective-permute-done | bytes 262176 | tf_op jit(solution)/shard_map/ppermute | solution.py:129
  139.3 18.6 %inverse_factor.1 = f32[512,512]{1,0:T(8,128)S(1)} custom-call(f32[512,512]{1,0:T(8,128)S(1)} %maximum_maximum_fusion.gram_ref), custom_call_target="tpu_custom_call" | custom-call | flops 1610612736 | bytes 2097152 | tf_op jit(solution)/shard_map/inverse_factor/pallas_call | solution.py:87
  157.9 2.2 %collective-permute-start.15 = (f32[128,512]{1,0:T(8,128)S(1)}, f32[128,512]{1,0:T(8,128)S(1)}, u32[]{:S(2)}, u32[]{:S(2)}) collective-permute-start(f32[128,512]{1,0:T(8,128)S(1)} %copy-done.15), channel_id=1, source_target_pairs={{0,16},{4,20},{8,24},{12,28},{16,0},{20,4},{24,8},{28,12},{1,17},{... | collective-permute-start | bytes 786440 | tf_op jit(solution)/shard_map/ppermute | solution.py:129
  162.3 9.4 %collective-permute-done.15 = f32[128,512]{1,0:T(8,128)S(1)} collective-permute-done((f32[128,512]{1,0:T(8,128)S(1)}, f32[128,512]{1,0:T(8,128)S(1)}, u32[]{:S(2)}, u32[]{:S(2)}) %collective-permute-start.15) | collective-permute-done | bytes 262176 | tf_op jit(solution)/shard_map/ppermute | solution.py:129
  180.9 2.1 %collective-permute-done.18 = f32[1,512]{1,0:T(1,128)S(1)} collective-permute-done((f32[1,512]{1,0:T(1,128)S(1)}, f32[1,512]{1,0:T(1,128)S(1)}, u32[]{:S(2)}, u32[]{:S(2)}) %collective-permute-start.18) | collective-permute-done | bytes 2080 | tf_op jit(solution)/shard_map/ppermute | solution.py:129
  183.8 2.8 %collective-permute-done.19 = f32[1,512]{1,0:T(1,128)S(1)} collective-permute-done((f32[1,512]{1,0:T(1,128)S(1)}, f32[1,512]{1,0:T(1,128)S(1)}, u32[]{:S(2)}, u32[]{:S(2)}) %collective-permute-start.19) | collective-permute-done | bytes 2080 | tf_op jit(solution)/shard_map/ppermute | solution.py:129
  186.6 2.1 collective-permute-start.20
  192.3 3.3 %broadcast_multiply_fusion = (f32[240,512]{1,0:T(8,128)}, f32[240,512]{1,0:T(8,128)S(1)}, f32[240,512]{1,0:T(8,128)S(1)}) fusion(f32[512]{0:T(512)S(1)} %bitcast.27, f32[512,512]{1,0:T(8,128)} %copy-done.1, f32[120,512]{1,0:T(8,128)} %get-tuple-element.21, f32[120,512]{1,0:T(8,128)} %get-tuple-element.23), kind=kOutput, calls=%fused_computation.36 | convolution fusion | flops 755343360 | bytes 3016704 | tf_op jit(solution)/shard_map/dot_general | solution.py:19
  201.5 7.1 %fusion.32 = f32[480,1536]{1,0:T(8,128)S(1)} fusion(f32[480,512]{1,0:T(8,128)S(1)} %fusion.11, f32[1536,512]{1,0:T(8,128)} %constant_dynamic-update-slice_fusion.2), kind=kOutput, calls=%fused_computation.86 | convolution fusion | flops 4529848320 | bytes 7077888 | tf_op jit(solution)/shard_map/dot_general | solution.py:19
  211.0 2.9 %convolution_divide_fusion = f32[192,512]{1,0:T(8,128)} fusion(f32[512,512]{1,0:T(8,128)S(1)} %copy-done.2, f32[1536,512]{1,0:T(8,128)} %constant_dynamic-update-slice_fusion.2, s32[]{:T(128)S(6)} %select_n.168, f32[512]{0:T(512)S(1)} %bitcast.26), kind=kOutput, calls=%fused_computation.13 | convolution fusion | flops 604078080 | bytes 1837060 | tf_op jit(solution)/shard_map/dot_general | solution.py:19
  (135 shorter events, 94.4 us)
Async XLA Ops:
  10.5 9.2 %collective-permute-start.1 = (f32[120,512]{1,0:T(8,128)S(1)}, f32[120,512]{1,0:T(8,128)S(1)}, u32[]{:S(2)}, u32[]{:S(2)}) collective-permute-start(f32[120,512]{1,0:T(8,128)S(1)} %dynamic-slice_add_fusion), channel_id=1, source_target_pairs={{0,2},{1,3},{2,0},{3,1},{4,6},{5,7},{6,4},{7,5},{8,10},{9,11},{10,... | collective-permute-start | bytes 737288 | tf_op jit(solution)/shard_map/ppermute | solution.py:129
  19.8 8.2 %collective-permute-start.2 = (f32[120,512]{1,0:T(8,128)S(1)}, f32[120,512]{1,0:T(8,128)}, u32[]{:S(2)}, u32[]{:S(2)}) collective-permute-start(f32[120,512]{1,0:T(8,128)S(1)} %add.159), channel_id=1, source_target_pairs={{0,4},{4,0},{8,12},{12,8},{16,20},{20,16},{24,28},{28,24},{1,5},{5... | collective-permute-start | bytes 737288 | tf_op jit(solution)/shard_map/ppermute | solution.py:129
  21.5 9.0 %collective-permute-start.3 = (f32[120,512]{1,0:T(8,128)S(1)}, f32[120,512]{1,0:T(8,128)}, u32[]{:S(2)}, u32[]{:S(2)}) collective-permute-start(f32[120,512]{1,0:T(8,128)S(1)} %add.159), channel_id=1, source_target_pairs={{0,8},{4,12},{8,0},{12,4},{16,24},{20,28},{24,16},{28,20},{1,9},{5... | collective-permute-start | bytes 737288 | tf_op jit(solution)/shard_map/ppermute | solution.py:129
  23.1 10.8 %collective-permute-start.4 = (f32[120,512]{1,0:T(8,128)S(1)}, f32[120,512]{1,0:T(8,128)}, u32[]{:S(2)}, u32[]{:S(2)}) collective-permute-start(f32[120,512]{1,0:T(8,128)S(1)} %add.159), channel_id=1, source_target_pairs={{0,12},{4,8},{8,4},{12,0},{16,28},{20,24},{24,20},{28,16},{1,13},{... | collective-permute-start | bytes 737288 | tf_op jit(solution)/shard_map/ppermute | solution.py:129
  41.1 23.1 %collective-permute-start.5 = (f32[480,512]{1,0:T(8,128)}, f32[480,512]{1,0:T(8,128)}, u32[]{:S(2)}, u32[]{:S(2)}) collective-permute-start(f32[480,512]{1,0:T(8,128)} %pad_maximum_fusion), channel_id=1, source_target_pairs={{0,1},{1,0},{2,3},{3,2},{4,5},{5,4},{6,7},{7,6},{8,9},{9,8},{10,11... | collective-permute-start | bytes 2949128 | tf_op jit(solution)/shard_map/ppermute | solution.py:129
  42.6 10.6 %collective-permute-start.7 = (f32[320,128]{1,0:T(8,128)S(1)}, f32[320,128]{1,0:T(8,128)S(1)}, u32[]{:S(2)}, u32[]{:S(2)}) collective-permute-start(f32[320,128]{1,0:T(8,128)S(1)} %dynamic-slice_add_fusion.1), channel_id=1, source_target_pairs={{0,16},{4,20},{8,24},{12,28},{16,0},{20,4},{24,8},{28,12},{1,17},{... | collective-permute-start | bytes 491528 | tf_op jit(solution)/shard_map/ppermute | solution.py:129
  53.9 7.1 %collective-permute-start.8 = (f32[320,128]{1,0:T(8,128)}, f32[320,128]{1,0:T(8,128)}, u32[]{:S(2)}, u32[]{:S(2)}) collective-permute-start(f32[320,128]{1,0:T(8,128)} %add.165), channel_id=1, source_target_pairs={{0,1},{1,0},{2,3},{3,2},{4,5},{5,4},{6,7},{7,6},{8,9},{9,8},{10,11... | collective-permute-start | bytes 491528 | tf_op jit(solution)/shard_map/ppermute | solution.py:129
  57.5 16.5 %collective-permute-start.10 = (f32[240,384]{1,0:T(8,128)}, f32[240,384]{1,0:T(8,128)}, u32[]{:S(2)}, u32[]{:S(2)}) collective-permute-start(f32[240,384]{1,0:T(8,128)} %get-tuple-element.9), channel_id=1, source_target_pairs={{0,4},{4,0},{8,12},{12,8},{16,20},{20,16},{24,28},{28,24},{1,5},{5... | collective-permute-start | bytes 1105928 | tf_op jit(solution)/shard_map/ppermute | solution.py:129
  58.8 15.2 %collective-permute-start.11 = (f32[240,384]{1,0:T(8,128)}, f32[240,384]{1,0:T(8,128)}, u32[]{:S(2)}, u32[]{:S(2)}) collective-permute-start(f32[240,384]{1,0:T(8,128)} %get-tuple-element.10), channel_id=1, source_target_pairs={{0,8},{4,12},{8,0},{12,4},{16,24},{20,28},{24,16},{28,20},{1,9},{5... | collective-permute-start | bytes 1105928 | tf_op jit(solution)/shard_map/ppermute | solution.py:129
  59.5 18.3 %collective-permute-start.12 = (f32[240,384]{1,0:T(8,128)}, f32[240,384]{1,0:T(8,128)}, u32[]{:S(2)}, u32[]{:S(2)}) collective-permute-start(f32[240,384]{1,0:T(8,128)} %get-tuple-element.11), channel_id=1, source_target_pairs={{0,12},{4,8},{8,4},{12,0},{16,28},{20,24},{24,20},{28,16},{1,13},{... | collective-permute-start | bytes 1105928 | tf_op jit(solution)/shard_map/ppermute | solution.py:129
  62.8 22.9 %collective-permute-start.9 = (f32[640,128]{1,0:T(8,128)}, f32[640,128]{1,0:T(8,128)}, u32[]{:S(2)}, u32[]{:S(2)}) collective-permute-start(f32[640,128]{1,0:T(8,128)} %pad_maximum_fusion.2), channel_id=1, source_target_pairs={{0,2},{1,3},{2,0},{3,1},{4,6},{5,7},{6,4},{7,5},{8,10},{9,11},{10,... | collective-permute-start | bytes 983048 | tf_op jit(solution)/shard_map/ppermute | solution.py:129
  83.5 14.3 %collective-permute-start.13 = (f32[128,512]{1,0:T(8,128)}, f32[128,512]{1,0:T(8,128)S(1)}, u32[]{:S(2)}, u32[]{:S(2)}) collective-permute-start(f32[128,512]{1,0:T(8,128)} %slice.120), channel_id=1, source_target_pairs={{0,16},{4,20},{8,24},{12,28},{16,0},{20,4},{24,8},{28,12},{1,17},{... | collective-permute-start | bytes 786440 | tf_op jit(solution)/shard_map/ppermute | solution.py:129
  102.4 18.7 %collective-permute-start.21 = (f32[128,512]{1,0:T(8,128)S(1)}, f32[128,512]{1,0:T(8,128)}, u32[]{:S(2)}, u32[]{:S(2)}) collective-permute-start(f32[128,512]{1,0:T(8,128)S(1)} %get-tuple-element.17), channel_id=1, source_target_pairs={{0,4},{4,0},{8,12},{12,8},{16,20},{20,16},{24,28},{28,24},{1,5},{5... | collective-permute-start | bytes 786440 | tf_op jit(solution)/shard_map/ppermute | solution.py:129
  106.2 16.5 %collective-permute-start.22 = (f32[128,512]{1,0:T(8,128)S(1)}, f32[128,512]{1,0:T(8,128)}, u32[]{:S(2)}, u32[]{:S(2)}) collective-permute-start(f32[128,512]{1,0:T(8,128)S(1)} %get-tuple-element.17), channel_id=1, source_target_pairs={{0,8},{4,12},{8,0},{12,4},{16,24},{20,28},{24,16},{28,20},{1,9},{5... | collective-permute-start | bytes 786440 | tf_op jit(solution)/shard_map/ppermute | solution.py:129
  111.8 12.5 %collective-permute-start.23 = (f32[128,512]{1,0:T(8,128)S(1)}, f32[128,512]{1,0:T(8,128)}, u32[]{:S(2)}, u32[]{:S(2)}) collective-permute-start(f32[128,512]{1,0:T(8,128)S(1)} %get-tuple-element.17), channel_id=1, source_target_pairs={{0,12},{4,8},{8,4},{12,0},{16,28},{20,24},{24,20},{28,16},{1,13},{... | collective-permute-start | bytes 786440 | tf_op jit(solution)/shard_map/ppermute | solution.py:129
  119.1 13.7 %collective-permute-start.14 = (f32[128,512]{1,0:T(8,128)}, f32[128,512]{1,0:T(8,128)S(1)}, u32[]{:S(2)}, u32[]{:S(2)}) collective-permute-start(f32[128,512]{1,0:T(8,128)} %get-tuple-element.25), channel_id=1, source_target_pairs={{0,16},{4,20},{8,24},{12,28},{16,0},{20,4},{24,8},{28,12},{1,17},{... | collective-permute-start | bytes 786440 | tf_op jit(solution)/shard_map/ppermute | solution.py:129
  134.5 25.7 %collective-permute-start.24 = (f32[128,512]{1,0:T(8,128)S(1)}, f32[128,512]{1,0:T(8,128)S(1)}, u32[]{:S(2)}, u32[]{:S(2)}) collective-permute-start(f32[128,512]{1,0:T(8,128)S(1)} %get-tuple-element.15), channel_id=1, source_target_pairs={{0,4},{4,0},{8,12},{12,8},{16,20},{20,16},{24,28},{28,24},{1,5},{5... | collective-permute-start | bytes 786440 | tf_op jit(solution)/shard_map/ppermute | solution.py:129
  137.2 23.6 %collective-permute-start.25 = (f32[128,512]{1,0:T(8,128)S(1)}, f32[128,512]{1,0:T(8,128)S(1)}, u32[]{:S(2)}, u32[]{:S(2)}) collective-permute-start(f32[128,512]{1,0:T(8,128)S(1)} %get-tuple-element.15), channel_id=1, source_target_pairs={{0,8},{4,12},{8,0},{12,4},{16,24},{20,28},{24,16},{28,20},{1,9},{5... | collective-permute-start | bytes 786440 | tf_op jit(solution)/shard_map/ppermute | solution.py:129
  138.1 23.5 %collective-permute-start.26 = (f32[128,512]{1,0:T(8,128)S(1)}, f32[128,512]{1,0:T(8,128)S(1)}, u32[]{:S(2)}, u32[]{:S(2)}) collective-permute-start(f32[128,512]{1,0:T(8,128)S(1)} %get-tuple-element.15), channel_id=1, source_target_pairs={{0,12},{4,8},{8,4},{12,0},{16,28},{20,24},{24,20},{28,16},{1,13},{... | collective-permute-start | bytes 786440 | tf_op jit(solution)/shard_map/ppermute | solution.py:129
  157.9 13.8 %collective-permute-start.15 = (f32[128,512]{1,0:T(8,128)S(1)}, f32[128,512]{1,0:T(8,128)S(1)}, u32[]{:S(2)}, u32[]{:S(2)}) collective-permute-start(f32[128,512]{1,0:T(8,128)S(1)} %copy-done.15), channel_id=1, source_target_pairs={{0,16},{4,20},{8,24},{12,28},{16,0},{20,4},{24,8},{28,12},{1,17},{... | collective-permute-start | bytes 786440 | tf_op jit(solution)/shard_map/ppermute | solution.py:129
  186.6 5.6 %collective-permute-start.20 = (f32[1,512]{1,0:T(1,128)S(1)}, f32[1,512]{1,0:T(1,128)S(1)}, u32[]{:S(2)}, u32[]{:S(2)}) collective-permute-start(f32[1,512]{1,0:T(1,128)S(1)} %add.174), channel_id=1, source_target_pairs={{0,16},{4,20},{8,24},{12,28},{16,0},{20,4},{24,8},{28,12},{1,17},{... | collective-permute-start | bytes 6152 | tf_op jit(solution)/shard_map/ppermute | solution.py:129
  188.7 9.2 %collective-permute-start.27 = (f32[128,512]{1,0:T(8,128)}, f32[128,512]{1,0:T(8,128)S(1)}, u32[]{:S(2)}, u32[]{:S(2)}) collective-permute-start(f32[128,512]{1,0:T(8,128)} %copy-done.14), channel_id=1, source_target_pairs={{0,4},{4,0},{8,12},{12,8},{16,20},{20,16},{24,28},{28,24},{1,5},{5... | collective-permute-start | bytes 786440 | tf_op jit(solution)/shard_map/ppermute | solution.py:129
  190.2 8.5 %collective-permute-start.28 = (f32[128,512]{1,0:T(8,128)}, f32[128,512]{1,0:T(8,128)S(1)}, u32[]{:S(2)}, u32[]{:S(2)}) collective-permute-start(f32[128,512]{1,0:T(8,128)} %copy-done.14), channel_id=1, source_target_pairs={{0,8},{4,12},{8,0},{12,4},{16,24},{20,28},{24,16},{28,20},{1,9},{5... | collective-permute-start | bytes 786440 | tf_op jit(solution)/shard_map/ppermute | solution.py:129
  192.2 8.6 %collective-permute-start.29 = (f32[128,512]{1,0:T(8,128)}, f32[128,512]{1,0:T(8,128)S(1)}, u32[]{:S(2)}, u32[]{:S(2)}) collective-permute-start(f32[128,512]{1,0:T(8,128)} %copy-done.14), channel_id=1, source_target_pairs={{0,12},{4,8},{8,4},{12,0},{16,28},{20,24},{24,20},{28,16},{1,13},{... | collective-permute-start | bytes 786440 | tf_op jit(solution)/shard_map/ppermute | solution.py:129
  (23 other events, 141.0 us)

commit v2 on v1

v2 whole, which is shorter than its diff:
```python
import functools
import math

import jax
import jax.numpy as jnp
from jax import lax
from jax.experimental import pallas as pl
from jax.experimental.pallas import tpu as pltpu
from jax.sharding import PartitionSpec as P

epsilon = 1e-06
highest = lax.Precision.HIGHEST
lanes = 128
panel = 8
square = 4


def dot(a, b, contract=((1,), (0,))):
    return lax.dot_general(
        a, b, (contract, ((), ())), precision=highest, preferred_element_type=jnp.float32
    )


vmem = pl.BlockSpec(memory_space=pltpu.VMEM)
smem = pl.BlockSpec(memory_space=pltpu.SMEM)
anywhere = pl.BlockSpec(memory_space=pl.ANY)


def kernel(body, out_shape, in_specs, scratch, name):
    return pl.pallas_call(
        body,
        out_shape=out_shape,
        in_specs=in_specs,
        scratch_shapes=scratch,
        compiler_params=pltpu.CompilerParams(vmem_limit_bytes=32 * 2**20),
        cost_estimate=pl.CostEstimate(flops=0, bytes_accessed=0, transcendentals=0),
        name=name,
    )


def shape(*dims, dtype=jnp.float32):
    return jax.ShapeDtypeStruct(dims, dtype)


def factor_block(block):
    size = block.shape[0]
    lane = lax.broadcasted_iota(jnp.int32, (panel, size), 1)
    row = lax.broadcasted_iota(jnp.int32, (panel, size), 0)
    for first in range(0, size, panel):
        count = size - first
        now = block[first:, :]
        columns = [
            jnp.broadcast_to(now[:, first + k : first + k + 1], (count, size)) for k in range(panel)
        ]
        inside = (lane >= first) & (lane < first + panel)
        head = jnp.where(inside, jnp.where(lane - first == row, 1.0, 0.0), now[:panel])
        tail = None
        if count > panel:
            lane_below = lax.broadcasted_iota(jnp.int32, (count - panel, size), 1)
            inside_below = (lane_below >= first) & (lane_below < first + panel)
            tail = jnp.where(inside_below, 0.0, now[panel:])
        for j in range(panel):
            inverse = lax.rsqrt(columns[j][j : j + 1, :])
            multiplier = columns[j] * inverse
            for k in range(j + 1, panel):
                columns[k] = columns[k] - multiplier * (columns[k][j : j + 1, :] * inverse)
            pivot = head[j : j + 1, :] * inverse
            below = jnp.where(row > j, head - multiplier[:panel] * pivot, head)
            head = jnp.where(row == j, pivot, below)
            if tail is not None:
                tail = tail - multiplier[panel:] * pivot
        block[first : first + panel, :] = head
        if tail is not None:
            block[first + panel :, :] = tail


def place_gram(bits, shares, work):
    size = work.shape[0]
    count = size // lanes
    core, plane = bits[0], bits[1]
    stack = shares.pop()
    share = shares[0].shape[0]
    for flip_plane in range(2):
        for flip_core in range(2):
            at = pl.multiple_of(((plane ^ flip_plane) * 2 + (core ^ flip_core)) * share, 8)
            stack[pl.ds(at, share), :] = shares[flip_plane * 2 + flip_core][...]
    at = 0
    for j in range(count):
        for i in range(j, count):
            block = stack[at * lanes : (at + 1) * lanes, :]
            work[j * lanes : (j + 1) * lanes, i * lanes : (i + 1) * lanes] = block.T
            at += 1


def factor_step(b, work, out, block):
    size = work.shape[0]
    count = size // lanes
    row = lax.broadcasted_iota(jnp.int32, (lanes, lanes), 0)
    lower = row >= lax.broadcasted_iota(jnp.int32, (lanes, lanes), 1)
    rows = slice(b * lanes, (b + 1) * lanes)
    past = (b + 1) * lanes
    block[...] = work[rows, rows]
    factor_block(block)
    inverse = jnp.where(lower, block[...], 0.0)
    out[:, rows] = inverse
    if b:
        out[:, : b * lanes] = dot(inverse, work[rows, : b * lanes])
    if past < size:
        out[:, past:] = jnp.zeros((lanes, size - past), jnp.float32)
        upper = dot(inverse, work[rows, past:])
        own = out[:, :past]
        for i in range(b + 1, count):
            at = (i - b - 1) * lanes
            left = upper[:, at : at + lanes]
            below = slice(i * lanes, (i + 1) * lanes)
            work[below, i * lanes :] = work[below, i * lanes :] - dot(left, upper[:, at:], ((0,), (0,)))
            change = dot(left, own, ((0,), (0,)))
            if b:
                work[below, : b * lanes] = work[below, : b * lanes] - change[:, : b * lanes]
            work[below, b * lanes : past] = -change[:, b * lanes :]


def whole_kernel(gram, out, work, block):
    work[...] = gram[...]
    for b in range(work.shape[0] // lanes):
        factor_step(b, work, out.at[b * lanes : (b + 1) * lanes], block)


def inverse_factor(gram):
    size = gram.shape[0]
    return kernel(
        whole_kernel,
        jax.ShapeDtypeStruct((size, size), jnp.float32),
        [vmem],
        [pltpu.VMEM((size, size), jnp.float32), pltpu.VMEM((lanes, lanes), jnp.float32)],
        "inverse_factor",
    )(gram)


def first_kernel(bits, a, b, c, d, token, out, work, stack, block):
    place_gram(bits, [a, b, c, d, stack], work)
    factor_step(0, work, out, block)


def first_step(bits, shares, size, token):
    blocks = sum(x.shape[0] for x in shares)
    return kernel(
        first_kernel,
        [
            jax.ShapeDtypeStruct((lanes, size), jnp.float32),
            jax.ShapeDtypeStruct((size, size), jnp.float32),
        ],
        [smem] + [vmem] * 4 + [anywhere],
        [pltpu.VMEM((blocks, lanes), jnp.float32), pltpu.VMEM((lanes, lanes), jnp.float32)],
        "factor_first",
    )(bits, *shares, token)


def later_kernel(b, before, token, out, work, block):
    work[...] = before[...]
    factor_step(b, work, out, block)


def later_step(b, work, token):
    size = work.shape[0]
    return kernel(
        functools.partial(later_kernel, b),
        [
            jax.ShapeDtypeStruct((lanes, size), jnp.float32),
            jax.ShapeDtypeStruct((size, size), jnp.float32),
        ],
        [vmem, anywhere],
        [pltpu.VMEM((lanes, lanes), jnp.float32)],
        "factor_later",
    )(work, token)


def share_norms(right_rows):
    squares = lax.psum(jnp.sum(right_rows * right_rows, axis=0), ("fsdp", "tensor"))
    return jnp.sqrt(squares + epsilon)


def any_mesh(momentum, gradient, right_basis):
    summed = momentum + gradient.astype(jnp.float32)
    left_raw = lax.psum(dot(summed, right_basis), "tensor")
    gram = lax.psum(dot(left_raw, left_raw, ((0,), (0,))), "fsdp")
    inverse = inverse_factor(gram)
    left = dot(left_raw, inverse, ((1,), (1,)))
    total_rows = left.shape[0] * lax.axis_size("fsdp")
    total_cols = summed.shape[1] * lax.axis_size("tensor")
    raw_rows = lax.psum_scatter(
        dot(summed, left_raw, ((0,), (0,))), "fsdp", scatter_dimension=0, tiled=True
    )
    right_rows = dot(raw_rows, inverse, ((1,), (1,)))
    column_norm = share_norms(right_rows)
    scaled_left = left * (math.sqrt(total_rows / total_cols) / column_norm)[None, :]
    raw = lax.all_gather(raw_rows, "fsdp", axis=0, tiled=True)
    product = dot(dot(left, inverse), raw, ((1,), (1,)))
    update = dot(dot(scaled_left, inverse), raw, ((1,), (1,))).astype(jnp.bfloat16)
    new_momentum = summed - 0.5 * product
    return (update, new_momentum, left * math.sqrt(total_rows), right_rows / column_norm[None, :])


def swap(value, axis, flip):
    return lax.ppermute(value, axis, [(i, i ^ flip) for i in range(lax.axis_size(axis))])


def split_kernel(bits, momentum, gradient, *pieces):
    width = pieces[0].shape[1]
    for k, piece in enumerate(pieces):
        at = pl.ds(pl.multiple_of((bits[2] ^ k) * width, lanes), width)
        piece[...] = momentum[:, at] + gradient[:, at].astype(jnp.float32)


def part_left_kernel(bits, basis, *refs):
    pieces, (sent, kept, total) = refs[:square], refs[square:]
    width = pieces[0].shape[1]
    half = sent.shape[0]
    for k, piece in enumerate(pieces):
        rows = pl.ds(pl.multiple_of((bits[2] ^ k) * width, lanes), width)
        part = dot(piece[...], basis[rows, :])
        total[...] = part if k == 0 else total[...] + part
    sent[...] = total[pl.ds(pl.multiple_of((1 - bits[0]) * half, 8), half), :]
    kept[...] = total[pl.ds(pl.multiple_of(bits[0] * half, 8), half), :]


def gram_kernel(bits, *refs):
    rows, (in_square, sent, kept, stack) = refs[:square], refs[square:]
    half, rank = rows[0].shape
    share = sent.shape[0]
    for k, part in enumerate(rows):
        in_square[k * half : (k + 1) * half, :] = part[...]
    at = 0
    for first in range(0, rank, lanes):
        left, right = in_square[:, first:], in_square[:, first : first + lanes]
        stack[at : at + rank - first, :] = dot(left, right, ((0,), (0,)))
        at += rank - first
    sent[...] = stack[pl.ds(pl.multiple_of((2 * bits[1] + 1 - bits[0]) * share, 8), share), :]
    kept[...] = stack[pl.ds(pl.multiple_of((2 * bits[1] + bits[0]) * share, 8), share), :]


def raw_kernel(bits, in_square, other, *refs):
    columns, pieces, (left, right) = refs[:square], refs[square:-2], refs[-2:]
    rows = columns[0].shape[0]
    half = rows // 2
    for k in range(square):
        own = slice(k * half, (k + 1) * half)
        left[k * rows : (k + 1) * rows, :] = columns[k][...]
        right[pl.ds(pl.multiple_of(k * rows + bits[0] * half, 8), half), :] = in_square[own, :]
        right[pl.ds(pl.multiple_of(k * rows + (1 - bits[0]) * half, 8), half), :] = other[own, :]
    step = pieces[0].shape[0]
    raw = dot(left[...], right[...], ((0,), (0,)))
    for at, piece in enumerate(pieces):
        piece[...] = raw[at * step : (at + 1) * step]


def left_kernel(bits, in_square, other, *refs):
    count = refs[-2].shape[0] // lanes
    inverses, refs = refs[:count], refs[count:]
    own, (left, squares, inverse, rows) = refs[:-4], refs[-4:]
    half = left.shape[0] // 2
    for b, part in enumerate(inverses):
        inverse[b * lanes : (b + 1) * lanes, :] = part[...]
    rows[pl.ds(pl.multiple_of(bits[0] * half, 8), half), :] = in_square[:half, :]
    rows[pl.ds(pl.multiple_of((1 - bits[0]) * half, 8), half), :] = other[:half, :]
    total = None
    for part in own:
        right = dot(part[...], inverse[...], ((1,), (1,)))
        part_total = jnp.sum(right * right, axis=0, keepdims=True)
        total = part_total if total is None else total + part_total
    squares[...] = total
    left[...] = dot(rows[...], inverse[...], ((1,), (1,)))


def plane_kernel(scale, left, inverse, left_scaled, plane):
    left_scaled[...] = left[...] * scale
    plane[...] = dot(left[...], inverse[...])


def last_kernel(factor, steps, bits, squares, left, inverse, plane, *refs):
    pieces, refs = refs[:square], refs[square:]
    raws, (new_momentum, update, next_basis, raw, planes) = refs[: square * steps], refs[square * steps :]
    rows, width = pieces[0].shape
    step = raws[0].shape[0]
    column_norm = jnp.sqrt(squares[...] + epsilon)
    planes[:rows, :] = plane[...]
    planes[rows:, :] = dot(left[...] * (factor / column_norm), inverse[...])
    for k in range(square):
        first = (bits[2] ^ k) * width
        new_momentum[:, pl.ds(pl.multiple_of(first, lanes), width)] = pieces[k][...]
        for i in range(steps):
            raw[pl.ds(pl.multiple_of(first + i * step, lanes), step), :] = raws[i * square + k][...]
    cols, chunk = raw.shape[0], raw.shape[1]
    for first in range(0, cols, chunk):
        at = slice(first, min(first + chunk, cols))
        both = dot(planes[...], raw[at, :], ((1,), (1,)))
        new_momentum[:, at] = new_momentum[:, at] - 0.5 * both[:rows]
        update[:, at] = both[rows:].astype(jnp.bfloat16)
    count = next_basis.shape[0]
    own = raw[pl.ds(pl.multiple_of(bits[3] * count, 8), count), :]
    next_basis[...] = dot(own, inverse[...], ((1,), (1,))) / column_norm


def in_squares(momentum, gradient, right_basis):
    device = lax.axis_index("fsdp")
    tensor = lax.axis_index("tensor")
    bits = jnp.stack([tensor % 2, tensor // 2, device % square, device]).astype(jnp.int32)
    rows, cols = momentum.shape
    rank = right_basis.shape[1]
    half, width = rows // 2, cols // square
    total_rows = rows * lax.axis_size("fsdp")
    total_cols = cols * lax.axis_size("tensor")

    pieces = kernel(split_kernel, [shape(rows, width)] * square, [smem, vmem, vmem], [], "split_sum")(
        bits, momentum, gradient
    )
    columns = [pieces[0]] + [swap(pieces[k], "fsdp", k) for k in range(1, square)]

    sent, kept = kernel(
        part_left_kernel,
        [shape(half, rank)] * 2,
        [smem] + [vmem] * (1 + square),
        [pltpu.VMEM((rows, rank), jnp.float32)],
        "part_left",
    )(bits, right_basis, *pieces)
    mine = kept + swap(sent, "tensor", 1)
    mine = mine + swap(mine, "tensor", 2)
    gathered = [mine] + [swap(mine, "fsdp", k) for k in range(1, square)]

    count = rank // lanes
    stacked = count * (count + 1) // 2 * lanes
    share = stacked // 4
    in_square, sent, kept = kernel(
        gram_kernel,
        [shape(square * half, rank), shape(share, lanes), shape(share, lanes)],
        [smem] + [vmem] * square,
        [pltpu.VMEM((stacked, lanes), jnp.float32)],
        "part_gram",
    )(bits, *gathered)
    other = swap(in_square, "tensor", 1)
    quarter = kept + swap(sent, "tensor", 1)
    quarter = quarter + swap(quarter, "fsdp", square)
    over_planes = swap(quarter, "tensor", 2)
    shares = [quarter, swap(quarter, "tensor", 1), over_planes, swap(over_planes, "tensor", 1)]

    steps = width // lanes
    parts = kernel(
        raw_kernel,
        [shape(lanes, rank)] * steps,
        [smem] + [vmem] * (2 + square),
        [
            pltpu.VMEM((square * rows, width), jnp.float32),
            pltpu.VMEM((square * rows, rank), jnp.float32),
        ],
        "part_raw",
    )(bits, in_square, other, *columns)
    own, raws = [], []
    for part in parts:
        part = part + swap(part, "fsdp", square)
        own.append(part)
        raws += [part] + [swap(part, "fsdp", k) for k in range(1, square)]

    factors = []
    out, work = first_step(bits, shares, rank, parts[0])
    factors.append(out)
    for b in range(1, count):
        out, work = later_step(b, work, own[min(b // 2, len(own) - 1)])
        factors.append(out)

    left, squares, inverse = kernel(
        left_kernel,
        [shape(rows, rank), shape(1, rank), shape(rank, rank)],
        [smem] + [vmem] * (2 + count + steps),
        [pltpu.VMEM((rows, rank), jnp.float32)],
        "left",
    )(bits, in_square, other, *factors, *own)
    for axis, last in (("tensor", lax.axis_size("tensor")), ("fsdp", square)):
        flip = 1
        while flip < last:
            squares = squares + swap(squares, axis, flip)
            flip *= 2
    left_scaled, plane = kernel(
        functools.partial(plane_kernel, math.sqrt(total_rows)),
        [shape(rows, rank)] * 2,
        [vmem] * 2,
        [],
        "plane",
    )(left, inverse)

    new_momentum, update, next_basis = kernel(
        functools.partial(last_kernel, math.sqrt(total_rows / total_cols), steps),
        [
            shape(rows, cols),
            shape(rows, cols, dtype=jnp.bfloat16),
            shape(cols // lax.axis_size("fsdp"), rank),
        ],
        [smem] + [vmem] * (4 + square + square * steps),
        [pltpu.VMEM((cols, rank), jnp.float32), pltpu.VMEM((2 * rows, rank), jnp.float32)],
        "last",
    )(bits, squares, left, inverse, plane, *pieces, *raws)
    return (update, new_momentum, left_scaled, next_basis)


def on_device(momentum, gradient, right_basis):
    rows, cols = momentum.shape
    pairs = lax.axis_size("fsdp") == 2 * square and lax.axis_size("tensor") == 4
    aligned = rows % 16 == 0 and cols % (square * lanes) == 0 and right_basis.shape[1] % lanes == 0
    plan = in_squares if pairs and aligned else any_mesh
    return plan(momentum, gradient, right_basis)


def solution(mesh):
    in_specs = (P("fsdp", "tensor"), P("fsdp", "tensor"), P("tensor", None))
    out_specs = (
        P("fsdp", "tensor"),
        P("fsdp", "tensor"),
        P("fsdp", None),
        P(("tensor", "fsdp"), None),
    )
    return jax.shard_map(
        on_device, mesh=mesh, in_specs=in_specs, out_specs=out_specs, check_vma=False
    )
```

time: 215 us -> 163 us (0.76)
  other arithmetic: 29 us -> 0.33 us
  matrix products: 28 us -> 0 us
  local copies, waits for them, and re-layouts: 31.3 us -> 4.37 us
  Pallas kernels: 19.7 us -> 44.9 us
  waiting for transfers between devices: 67.2 us -> 81 us
  starting transfers between devices: 37.8 us -> 31.2 us
    dot_general x8 -> x0, matrix products: 28 us -> none  [dot(): lax.dot_general(a, b, (contract, ((), ())), precision=highest, preferred_...]
    pallas_call x2 -> x11, Pallas kernels: 19.7 us -> 44.9 us  [the longest x3 14 us: later_step(): kernel(functools.partial(later_kernel, b), [jax.ShapeDtypeStruct((lanes,...]
    ppermute x30, waiting for transfers between devices: 67.2 us -> 81 us  [swap(): lax.ppermute(value, axis, [(i, i ^ flip) for i in range(lax.axis_size(axi...]
    dynamic_update_slice x9 -> x0, local copies, waits for them, and re-layouts: 9.29 us -> none  [in_squares(): lax.dynamic_update_slice_in_dim(raw, block, (place ^ k) * width + at, 0)]
    unnamed x7 -> x0, other arithmetic: 8.74 us -> none
    concatenate x7 -> x0, other arithmetic: 8.6 us -> none  [the longest x2 3.28 us: in_squares(): jnp.concatenate([found[i, j] for j in range(count)], axis=1)]
    unnamed x38 -> x6, local copies, waits for them, and re-layouts: 12.4 us -> 4.37 us
    ppermute x30, starting transfers between devices: 37.8 us -> 31.2 us  [swap(): lax.ppermute(value, axis, [(i, i ^ flip) for i in range(lax.axis_size(axi...]
  transfers between devices with their start and end apart: 30 -> 30, of which waited for: 16 -> 15; matrix products, arithmetic and copies ran while one was open for 23% -> 0% of each run, Pallas kernels for 9% -> 18%
where the time goes in v2:
time: 163 us
  waiting for transfers between devices  81 us (50%)
  Pallas kernels  44.9 us (28%)
  starting transfers between devices  31.2 us (19%)
  local copies, waits for them, and re-layouts  4.37 us (3%)
    ppermute x30, waiting for transfers between devices, swap(): lax.ppermute(value, axis, [(i, i ^ flip) for i in range(lax.axis_size(axi...  81 us
    ppermute x30, starting transfers between devices, swap(): lax.ppermute(value, axis, [(i, i ^ flip) for i in range(lax.axis_size(axi...  31.2 us
    pallas_call x3, Pallas kernels, later_step(): kernel(functools.partial(later_kernel, b), [jax.ShapeDtypeStruct((lanes,...  14 us
    pallas_call x1, Pallas kernels, in_squares(): kernel(functools.partial(last_kernel, math.sqrt(total_rows / total_cols),...  8.13 us
    pallas_call x1, Pallas kernels, first_step(): kernel(first_kernel, [jax.ShapeDtypeStruct((lanes, size), jnp.float32), j...  5.24 us
    pallas_call x1, Pallas kernels, in_squares(): kernel(left_kernel, [shape(rows, rank), shape(1, rank), shape(rank, rank)...  4.75 us
    unnamed x6, local copies, waits for them, and re-layouts  4.37 us
    pallas_call x1, Pallas kernels, in_squares(): kernel(part_left_kernel, [shape(half, rank)] * 2, [smem] + [vmem] * (1 +...  3.94 us
  transfers between devices with their start and end apart: 30, of which 15 were waited for; matrix products, arithmetic and copies ran while one was open for 0% of the time, Pallas kernels for 18%

profile of v2, /device:TPU:0, one launch (start us, length us, event | category | flops | bytes accessed | tf_op | source)
XLA Modules:
  0.0 162.6 jit_solution(13556485521364852759)
XLA Ops:
  5.8 3.9 %part_left.1 = (f32[120,512]{1,0:T(8,128)S(1)}, f32[120,512]{1,0:T(8,128)S(1)}) custom-call(s32[4]{0:T(128)S(1)} %pad_add_fusion.bits, f32[1536,512]{1,0:T(8,128)S(1)} %copy-done, f32[240,384]{1,0:T(8,128)S(1)} %get-tuple-element.31.refs_0_, f32[240,384]{1,0:T(8,128)S(1)} %get-tuple-element.32.refs_1_, f32[240,384]{1,0:T(8,128)S(1)} %get-tuple-element.33.refs_2_, ...), custom_call_target="tpu_custom_call" | custom-call | tf_op jit(solution)/shard_map/part_left/pallas_call | solution.py:319
  11.5 3.0 %collective-permute-start.1 = (f32[120,512]{1,0:T(8,128)S(1)}, f32[120,512]{1,0:T(8,128)S(1)}, u32[]{:S(2)}, u32[]{:S(2)}) collective-permute-start(f32[120,512]{1,0:T(8,128)S(1)} %add.43), channel_id=1, source_target_pairs={{0,2},{1,3},{2,0},{3,1},{4,6},{5,7},{6,4},{7,5},{8,10},{9,11},{10,... | collective-permute-start | bytes 737288 | tf_op jit(solution)/shard_map/ppermute | solution.py:205
  14.4 6.3 %collective-permute-done.1 = f32[120,512]{1,0:T(8,128)S(1)} collective-permute-done((f32[120,512]{1,0:T(8,128)S(1)}, f32[120,512]{1,0:T(8,128)S(1)}, u32[]{:S(2)}, u32[]{:S(2)}) %collective-permute-start.1) | collective-permute-done | bytes 245792 | tf_op jit(solution)/shard_map/ppermute | solution.py:205
  24.3 6.3 %collective-permute-done.4.refs_3_ = f32[120,512]{1,0:T(8,128)S(1)} collective-permute-done((f32[120,512]{1,0:T(8,128)S(1)}, f32[120,512]{1,0:T(8,128)S(1)}, u32[]{:S(2)}, u32[]{:S(2)}) %collective-permute-start.4) | collective-permute-done | bytes 245792 | tf_op jit(solution)/shard_map/ppermute | solution.py:205
  30.6 3.8 %collective-permute-done.3.refs_2_ = f32[120,512]{1,0:T(8,128)S(1)} collective-permute-done((f32[120,512]{1,0:T(8,128)S(1)}, f32[120,512]{1,0:T(8,128)S(1)}, u32[]{:S(2)}, u32[]{:S(2)}) %collective-permute-start.3) | collective-permute-done | bytes 245792 | tf_op jit(solution)/shard_map/ppermute | solution.py:205
  34.4 3.0 %part_gram.1 = (f32[480,512]{1,0:T(8,128)S(1)}, f32[320,128]{1,0:T(8,128)S(1)}, f32[320,128]{1,0:T(8,128)S(1)}) custom-call(s32[4]{0:T(128)S(1)} %pad_add_fusion.bits, f32[120,512]{1,0:T(8,128)S(1)} %add.44.refs_0_, f32[120,512]{1,0:T(8,128)S(1)} %collective-permute-done.2.refs_1_, f32[120,512]{1,0:T(8,128)S(1)} %collective-permute-done.3.refs_2_, ...), custom_call_target="tpu_custom_call" | custom-call | tf_op jit(solution)/shard_map/part_gram/pallas_call | solution.py:333
  44.2 16.0 %collective-permute-done.7 = f32[320,128]{1,0:T(8,128)S(1)} collective-permute-done((f32[320,128]{1,0:T(8,128)S(1)}, f32[320,128]{1,0:T(8,128)S(1)}, u32[]{:S(2)}, u32[]{:S(2)}) %collective-permute-start.7) | collective-permute-done | bytes 163872 | tf_op jit(solution)/shard_map/ppermute | solution.py:205
  61.8 3.3 %part_raw.1 = (f32[128,512]{1,0:T(8,128)S(1)}, f32[128,512]{1,0:T(8,128)S(1)}, f32[128,512]{1,0:T(8,128)S(1)}) custom-call(s32[4]{0:T(128)S(1)} %pad_add_fusion.bits, f32[480,512]{1,0:T(8,128)S(1)} %get-tuple-element.37.in_square, f32[480,512]{1,0:T(8,128)S(1)} %collective-permute-done.5.other, f32[240,384]{1,0:T(8,128)S(1)} %get-tuple-element.31.refs_0_, ...), custom_call_target="tpu_custom_call" | custom-call | tf_op jit(solution)/shard_map/part_raw/pallas_call | solution.py:347
  65.2 3.4 %collective-permute-start.15 = (f32[128,512]{1,0:T(8,128)S(1)}, f32[128,512]{1,0:T(8,128)S(1)}, u32[]{:S(2)}, u32[]{:S(2)}) collective-permute-start(f32[128,512]{1,0:T(8,128)S(1)} %get-tuple-element.45), channel_id=1, source_target_pairs={{0,16},{4,20},{8,24},{12,28},{16,0},{20,4},{24,8},{28,12},{1,17},{... | collective-permute-start | bytes 786440 | tf_op jit(solution)/shard_map/ppermute | solution.py:205
  69.2 2.8 %collective-permute-start.14 = (f32[128,512]{1,0:T(8,128)S(1)}, f32[128,512]{1,0:T(8,128)S(1)}, u32[]{:S(2)}, u32[]{:S(2)}) collective-permute-start(f32[128,512]{1,0:T(8,128)S(1)} %get-tuple-element.40.token), channel_id=1, source_target_pairs={{0,16},{4,20},{8,24},{12,28},{16,0},{20,4},{24,8},{28,12},{1,17},{... | collective-permute-start | bytes 786440 | tf_op jit(solution)/shard_map/ppermute | solution.py:205
  72.1 20.7 %collective-permute-done.15 = f32[128,512]{1,0:T(8,128)S(1)} collective-permute-done((f32[128,512]{1,0:T(8,128)S(1)}, f32[128,512]{1,0:T(8,128)S(1)}, u32[]{:S(2)}, u32[]{:S(2)}) %collective-permute-start.15) | collective-permute-done | bytes 262176 | tf_op jit(solution)/shard_map/ppermute | solution.py:205
  92.9 5.5 %collective-permute-done.16 = f32[128,512]{1,0:T(8,128)S(1)} collective-permute-done((f32[128,512]{1,0:T(8,128)S(1)}, f32[128,512]{1,0:T(8,128)S(1)}, u32[]{:S(2)}, u32[]{:S(2)}) %collective-permute-start.16) | collective-permute-done | bytes 262176 | tf_op jit(solution)/shard_map/ppermute | solution.py:205
  99.2 2.9 %collective-permute-start.29 = (f32[128,512]{1,0:T(8,128)S(1)}, f32[128,512]{1,0:T(8,128)S(1)}, u32[]{:S(2)}, u32[]{:S(2)}) collective-permute-start(f32[128,512]{1,0:T(8,128)S(1)} %add.49.refs_6_.refs_12_), channel_id=1, source_target_pairs={{0,12},{4,8},{8,4},{12,0},{16,28},{20,24},{24,20},{28,16},{1,13},{... | collective-permute-start | bytes 786440 | tf_op jit(solution)/shard_map/ppermute | solution.py:205
  102.0 5.2 %factor_first.1 = (f32[128,512]{1,0:T(8,128)S(1)}, f32[512,512]{1,0:T(8,128)S(1)}) custom-call(s32[4]{0:T(128)S(1)} %pad_add_fusion.bits, f32[320,128]{1,0:T(8,128)S(1)} %add.46.a, f32[320,128]{1,0:T(8,128)S(1)} %collective-permute-done.8.b, f32[320,128]{1,0:T(8,128)S(1)} %collective-permute-done.9.c, f32[320,128]{1,0:T(8,128)S(1)} %collective-permute-done.10.d, ...), custom_call_target="tpu_custom_call" | custom-call | tf_op jit(solution)/shard_map/factor_first/pallas_call | solution.py:147
  107.3 4.6 %factor_later.3 = (f32[128,512]{1,0:T(8,128)S(1)}, f32[512,512]{1,0:T(8,128)S(1)}) custom-call(f32[512,512]{1,0:T(8,128)S(1)} %get-tuple-element.42.before, f32[128,512]{1,0:T(8,128)S(1)} %add.47.token.refs_4_), custom_call_target="tpu_custom_call" | custom-call | tf_op jit(solution)/shard_map/factor_later/pallas_call | solution.py:166
  111.9 4.3 %factor_later.4 = (f32[128,512]{1,0:T(8,128)S(1)}, f32[512,512]{1,0:T(8,128)S(1)}) custom-call(f32[512,512]{1,0:T(8,128)S(1)} %get-tuple-element.44.before, f32[128,512]{1,0:T(8,128)S(1)} %add.48.token.refs_5_.refs_8_), custom_call_target="tpu_custom_call" | custom-call | tf_op jit(solution)/shard_map/factor_later/pallas_call | solution.py:166
  116.2 5.2 %factor_later.5 = (f32[128,512]{1,0:T(8,128)S(1)}, f32[512,512]{1,0:T(8,128)}) custom-call(f32[512,512]{1,0:T(8,128)S(1)} %get-tuple-element.47.before, f32[128,512]{1,0:T(8,128)S(1)} %add.48.token.refs_5_.refs_8_), custom_call_target="tpu_custom_call" | custom-call | tf_op jit(solution)/shard_map/factor_later/pallas_call | solution.py:166
  121.4 4.8 %left.1 = (f32[240,512]{1,0:T(8,128)S(1)}, f32[1,512]{1,0:T(1,128)S(1)}, f32[512,512]{1,0:T(8,128)S(1)}) custom-call(s32[4]{0:T(128)S(1)} %pad_add_fusion.bits, f32[480,512]{1,0:T(8,128)S(1)} %get-tuple-element.37.in_square, f32[480,512]{1,0:T(8,128)S(1)} %collective-permute-done.5.other, f32[128,512]{1,0:T(8,128)S(1)} %get-tuple-element.41.refs_0_, ...), custom_call_target="tpu_custom_call" | custom-call | tf_op jit(solution)/shard_map/left/pallas_call | solution.py:370
  127.9 3.1 %collective-permute-done.18 = f32[1,512]{1,0:T(1,128)S(1)} collective-permute-done((f32[1,512]{1,0:T(1,128)S(1)}, f32[1,512]{1,0:T(1,128)S(1)}, u32[]{:S(2)}, u32[]{:S(2)}) %collective-permute-start.18) | collective-permute-done | bytes 2080 | tf_op jit(solution)/shard_map/ppermute | solution.py:205
  131.6 3.0 %collective-permute-done.19 = f32[1,512]{1,0:T(1,128)S(1)} collective-permute-done((f32[1,512]{1,0:T(1,128)S(1)}, f32[1,512]{1,0:T(1,128)S(1)}, u32[]{:S(2)}, u32[]{:S(2)}) %collective-permute-start.19) | collective-permute-done | bytes 2080 | tf_op jit(solution)/shard_map/ppermute | solution.py:205
  134.6 3.6 %collective-permute-done.20 = f32[1,512]{1,0:T(1,128)S(1)} collective-permute-done((f32[1,512]{1,0:T(1,128)S(1)}, f32[1,512]{1,0:T(1,128)S(1)}, u32[]{:S(2)}, u32[]{:S(2)}) %collective-permute-start.20) | collective-permute-done | bytes 2080 | tf_op jit(solution)/shard_map/ppermute | solution.py:205
  138.8 2.9 %collective-permute-start.23 = (f32[128,512]{1,0:T(8,128)S(1)}, f32[128,512]{1,0:T(8,128)S(1)}, u32[]{:S(2)}, u32[]{:S(2)}) collective-permute-start(f32[128,512]{1,0:T(8,128)S(1)} %add.47.token.refs_4_), channel_id=1, source_target_pairs={{0,12},{4,8},{8,4},{12,0},{16,28},{20,24},{24,20},{28,16},{1,13},{... | collective-permute-start | bytes 786440 | tf_op jit(solution)/shard_map/ppermute | solution.py:205
  144.1 3.3 %collective-permute-done.28.refs_14_ = f32[128,512]{1,0:T(8,128)S(1)} collective-permute-done((f32[128,512]{1,0:T(8,128)S(1)}, f32[128,512]{1,0:T(8,128)S(1)}, u32[]{:S(2)}, u32[]{:S(2)}) %collective-permute-start.28) | collective-permute-done | bytes 262176 | tf_op jit(solution)/shard_map/ppermute | solution.py:205
  154.4 8.1 %last.1 = (f32[240,1536]{1,0:T(8,128)}, bf16[240,1536]{1,0:T(8,128)(2,1)}, f32[192,512]{1,0:T(8,128)}) custom-call(s32[4]{0:T(128)S(1)} %pad_add_fusion.bits, f32[1,512]{1,0:T(1,128)S(1)} %add.53.squares, f32[240,512]{1,0:T(8,128)S(1)} %get-tuple-element.51.left, f32[512,512]{1,0:T(8,128)S(1)} %get-tuple-element.52.inverse, ...), custom_call_target="tpu_custom_call" | custom-call | tf_op jit(solution)/shard_map/last/pallas_call | solution.py:390
  (65 shorter events, 32.7 us)
Async XLA Ops:
  11.5 9.2 %collective-permute-start.1 = (f32[120,512]{1,0:T(8,128)S(1)}, f32[120,512]{1,0:T(8,128)S(1)}, u32[]{:S(2)}, u32[]{:S(2)}) collective-permute-start(f32[120,512]{1,0:T(8,128)S(1)} %add.43), channel_id=1, source_target_pairs={{0,2},{1,3},{2,0},{3,1},{4,6},{5,7},{6,4},{7,5},{8,10},{9,11},{10,... | collective-permute-start | bytes 737288 | tf_op jit(solution)/shard_map/ppermute | solution.py:205
  20.7 9.9 %collective-permute-start.4 = (f32[120,512]{1,0:T(8,128)S(1)}, f32[120,512]{1,0:T(8,128)S(1)}, u32[]{:S(2)}, u32[]{:S(2)}) collective-permute-start(f32[120,512]{1,0:T(8,128)S(1)} %add.44.refs_0_), channel_id=1, source_target_pairs={{0,12},{4,8},{8,4},{12,0},{16,28},{20,24},{24,20},{28,16},{1,13},{... | collective-permute-start | bytes 737288 | tf_op jit(solution)/shard_map/ppermute | solution.py:205
  23.5 10.9 %collective-permute-start.3 = (f32[120,512]{1,0:T(8,128)S(1)}, f32[120,512]{1,0:T(8,128)S(1)}, u32[]{:S(2)}, u32[]{:S(2)}) collective-permute-start(f32[120,512]{1,0:T(8,128)S(1)} %add.44.refs_0_), channel_id=1, source_target_pairs={{0,8},{4,12},{8,0},{12,4},{16,24},{20,28},{24,16},{28,20},{1,9},{5... | collective-permute-start | bytes 737288 | tf_op jit(solution)/shard_map/ppermute | solution.py:205
  24.0 10.5 %collective-permute-start.2 = (f32[120,512]{1,0:T(8,128)S(1)}, f32[120,512]{1,0:T(8,128)S(1)}, u32[]{:S(2)}, u32[]{:S(2)}) collective-permute-start(f32[120,512]{1,0:T(8,128)S(1)} %add.44.refs_0_), channel_id=1, source_target_pairs={{0,4},{4,0},{8,12},{12,8},{16,20},{20,16},{24,28},{28,24},{1,5},{5... | collective-permute-start | bytes 737288 | tf_op jit(solution)/shard_map/ppermute | solution.py:205
  37.4 24.4 %collective-permute-start.5 = (f32[480,512]{1,0:T(8,128)S(1)}, f32[480,512]{1,0:T(8,128)S(1)}, u32[]{:S(2)}, u32[]{:S(2)}) collective-permute-start(f32[480,512]{1,0:T(8,128)S(1)} %get-tuple-element.37.in_square), channel_id=1, source_target_pairs={{0,1},{1,0},{2,3},{3,2},{4,5},{5,4},{6,7},{7,6},{8,9},{9,8},{10,11... | collective-permute-start | bytes 2949128 | tf_op jit(solution)/shard_map/ppermute | solution.py:205
  38.0 23.8 %collective-permute-start.11 = (f32[240,384]{1,0:T(8,128)S(1)}, f32[240,384]{1,0:T(8,128)S(1)}, u32[]{:S(2)}, u32[]{:S(2)}) collective-permute-start(f32[240,384]{1,0:T(8,128)S(1)} %get-tuple-element.32.refs_1_), channel_id=1, source_target_pairs={{0,4},{4,0},{8,12},{12,8},{16,20},{20,16},{24,28},{28,24},{1,5},{5... | collective-permute-start | bytes 1105928 | tf_op jit(solution)/shard_map/ppermute | solution.py:205
  39.4 22.4 %collective-permute-start.12 = (f32[240,384]{1,0:T(8,128)S(1)}, f32[240,384]{1,0:T(8,128)S(1)}, u32[]{:S(2)}, u32[]{:S(2)}) collective-permute-start(f32[240,384]{1,0:T(8,128)S(1)} %get-tuple-element.33.refs_2_), channel_id=1, source_target_pairs={{0,8},{4,12},{8,0},{12,4},{16,24},{20,28},{24,16},{28,20},{1,9},{5... | collective-permute-start | bytes 1105928 | tf_op jit(solution)/shard_map/ppermute | solution.py:205
  41.0 20.8 %collective-permute-start.13 = (f32[240,384]{1,0:T(8,128)S(1)}, f32[240,384]{1,0:T(8,128)S(1)}, u32[]{:S(2)}, u32[]{:S(2)}) collective-permute-start(f32[240,384]{1,0:T(8,128)S(1)} %get-tuple-element.34.refs_3_), channel_id=1, source_target_pairs={{0,12},{4,8},{8,4},{12,0},{16,28},{20,24},{24,20},{28,16},{1,13},{... | collective-permute-start | bytes 1105928 | tf_op jit(solution)/shard_map/ppermute | solution.py:205
  41.5 18.7 %collective-permute-start.7 = (f32[320,128]{1,0:T(8,128)S(1)}, f32[320,128]{1,0:T(8,128)S(1)}, u32[]{:S(2)}, u32[]{:S(2)}) collective-permute-start(f32[320,128]{1,0:T(8,128)S(1)} %add.45), channel_id=1, source_target_pairs={{0,16},{4,20},{8,24},{12,28},{16,0},{20,4},{24,8},{28,12},{1,17},{... | collective-permute-start | bytes 491528 | tf_op jit(solution)/shard_map/ppermute | solution.py:205
  60.2 8.5 %collective-permute-start.9 = (f32[320,128]{1,0:T(8,128)S(1)}, f32[320,128]{1,0:T(8,128)S(1)}, u32[]{:S(2)}, u32[]{:S(2)}) collective-permute-start(f32[320,128]{1,0:T(8,128)S(1)} %add.46.a), channel_id=1, source_target_pairs={{0,2},{1,3},{2,0},{3,1},{4,6},{5,7},{6,4},{7,5},{8,10},{9,11},{10,... | collective-permute-start | bytes 491528 | tf_op jit(solution)/shard_map/ppermute | solution.py:205
  65.2 27.6 %collective-permute-start.15 = (f32[128,512]{1,0:T(8,128)S(1)}, f32[128,512]{1,0:T(8,128)S(1)}, u32[]{:S(2)}, u32[]{:S(2)}) collective-permute-start(f32[128,512]{1,0:T(8,128)S(1)} %get-tuple-element.45), channel_id=1, source_target_pairs={{0,16},{4,20},{8,24},{12,28},{16,0},{20,4},{24,8},{28,12},{1,17},{... | collective-permute-start | bytes 786440 | tf_op jit(solution)/shard_map/ppermute | solution.py:205
  68.6 29.8 %collective-permute-start.16 = (f32[128,512]{1,0:T(8,128)S(1)}, f32[128,512]{1,0:T(8,128)S(1)}, u32[]{:S(2)}, u32[]{:S(2)}) collective-permute-start(f32[128,512]{1,0:T(8,128)S(1)} %get-tuple-element.49), channel_id=1, source_target_pairs={{0,16},{4,20},{8,24},{12,28},{16,0},{20,4},{24,8},{28,12},{1,17},{... | collective-permute-start | bytes 786440 | tf_op jit(solution)/shard_map/ppermute | solution.py:205
  68.7 29.8 %collective-permute-start.8 = (f32[320,128]{1,0:T(8,128)S(1)}, f32[320,128]{1,0:T(8,128)S(1)}, u32[]{:S(2)}, u32[]{:S(2)}) collective-permute-start(f32[320,128]{1,0:T(8,128)S(1)} %add.46.a), channel_id=1, source_target_pairs={{0,1},{1,0},{2,3},{3,2},{4,5},{5,4},{6,7},{7,6},{8,9},{9,8},{10,11... | collective-permute-start | bytes 491528 | tf_op jit(solution)/shard_map/ppermute | solution.py:205
  68.7 30.4 %collective-permute-start.10 = (f32[320,128]{1,0:T(8,128)S(1)}, f32[320,128]{1,0:T(8,128)S(1)}, u32[]{:S(2)}, u32[]{:S(2)}) collective-permute-start(f32[320,128]{1,0:T(8,128)S(1)} %collective-permute-done.9.c), channel_id=1, source_target_pairs={{0,1},{1,0},{2,3},{3,2},{4,5},{5,4},{6,7},{7,6},{8,9},{9,8},{10,11... | collective-permute-start | bytes 491528 | tf_op jit(solution)/shard_map/ppermute | solution.py:205
  69.2 38.1 %collective-permute-start.14 = (f32[128,512]{1,0:T(8,128)S(1)}, f32[128,512]{1,0:T(8,128)S(1)}, u32[]{:S(2)}, u32[]{:S(2)}) collective-permute-start(f32[128,512]{1,0:T(8,128)S(1)} %get-tuple-element.40.token), channel_id=1, source_target_pairs={{0,16},{4,20},{8,24},{12,28},{16,0},{20,4},{24,8},{28,12},{1,17},{... | collective-permute-start | bytes 786440 | tf_op jit(solution)/shard_map/ppermute | solution.py:205
  92.9 45.3 %collective-permute-start.26 = (f32[128,512]{1,0:T(8,128)S(1)}, f32[128,512]{1,0:T(8,128)S(1)}, u32[]{:S(2)}, u32[]{:S(2)}) collective-permute-start(f32[128,512]{1,0:T(8,128)S(1)} %add.48.token.refs_5_.refs_8_), channel_id=1, source_target_pairs={{0,12},{4,8},{8,4},{12,0},{16,28},{20,24},{24,20},{28,16},{1,13},{... | collective-permute-start | bytes 786440 | tf_op jit(solution)/shard_map/ppermute | solution.py:205
  98.4 40.3 %collective-permute-start.25 = (f32[128,512]{1,0:T(8,128)S(1)}, f32[128,512]{1,0:T(8,128)S(1)}, u32[]{:S(2)}, u32[]{:S(2)}) collective-permute-start(f32[128,512]{1,0:T(8,128)S(1)} %add.48.token.refs_5_.refs_8_), channel_id=1, source_target_pairs={{0,8},{4,12},{8,0},{12,4},{16,24},{20,28},{24,16},{28,20},{1,9},{5... | collective-permute-start | bytes 786440 | tf_op jit(solution)/shard_map/ppermute | solution.py:205
  98.5 43.2 %collective-permute-start.24 = (f32[128,512]{1,0:T(8,128)S(1)}, f32[128,512]{1,0:T(8,128)S(1)}, u32[]{:S(2)}, u32[]{:S(2)}) collective-permute-start(f32[128,512]{1,0:T(8,128)S(1)} %add.48.token.refs_5_.refs_8_), channel_id=1, source_target_pairs={{0,4},{4,0},{8,12},{12,8},{16,20},{20,16},{24,28},{28,24},{1,5},{5... | collective-permute-start | bytes 786440 | tf_op jit(solution)/shard_map/ppermute | solution.py:205
  99.2 42.5 %collective-permute-start.29 = (f32[128,512]{1,0:T(8,128)S(1)}, f32[128,512]{1,0:T(8,128)S(1)}, u32[]{:S(2)}, u32[]{:S(2)}) collective-permute-start(f32[128,512]{1,0:T(8,128)S(1)} %add.49.refs_6_.refs_12_), channel_id=1, source_target_pairs={{0,12},{4,8},{8,4},{12,0},{16,28},{20,24},{24,20},{28,16},{1,13},{... | collective-permute-start | bytes 786440 | tf_op jit(solution)/shard_map/ppermute | solution.py:205
  138.1 9.2 %collective-permute-start.28 = (f32[128,512]{1,0:T(8,128)S(1)}, f32[128,512]{1,0:T(8,128)S(1)}, u32[]{:S(2)}, u32[]{:S(2)}) collective-permute-start(f32[128,512]{1,0:T(8,128)S(1)} %add.49.refs_6_.refs_12_), channel_id=1, source_target_pairs={{0,8},{4,12},{8,0},{12,4},{16,24},{20,28},{24,16},{28,20},{1,9},{5... | collective-permute-start | bytes 786440 | tf_op jit(solution)/shard_map/ppermute | solution.py:205
  138.2 11.8 %collective-permute-start.27 = (f32[128,512]{1,0:T(8,128)S(1)}, f32[128,512]{1,0:T(8,128)S(1)}, u32[]{:S(2)}, u32[]{:S(2)}) collective-permute-start(f32[128,512]{1,0:T(8,128)S(1)} %add.49.refs_6_.refs_12_), channel_id=1, source_target_pairs={{0,4},{4,0},{8,12},{12,8},{16,20},{20,16},{24,28},{28,24},{1,5},{5... | collective-permute-start | bytes 786440 | tf_op jit(solution)/shard_map/ppermute | solution.py:205
  138.8 12.9 %collective-permute-start.23 = (f32[128,512]{1,0:T(8,128)S(1)}, f32[128,512]{1,0:T(8,128)S(1)}, u32[]{:S(2)}, u32[]{:S(2)}) collective-permute-start(f32[128,512]{1,0:T(8,128)S(1)} %add.47.token.refs_4_), channel_id=1, source_target_pairs={{0,12},{4,8},{8,4},{12,0},{16,28},{20,24},{24,20},{28,16},{1,13},{... | collective-permute-start | bytes 786440 | tf_op jit(solution)/shard_map/ppermute | solution.py:205
  141.6 12.8 %collective-permute-start.22 = (f32[128,512]{1,0:T(8,128)S(1)}, f32[128,512]{1,0:T(8,128)S(1)}, u32[]{:S(2)}, u32[]{:S(2)}) collective-permute-start(f32[128,512]{1,0:T(8,128)S(1)} %add.47.token.refs_4_), channel_id=1, source_target_pairs={{0,8},{4,12},{8,0},{12,4},{16,24},{20,28},{24,16},{28,20},{1,9},{5... | collective-permute-start | bytes 786440 | tf_op jit(solution)/shard_map/ppermute | solution.py:205
  141.7 12.8 %collective-permute-start.21 = (f32[128,512]{1,0:T(8,128)S(1)}, f32[128,512]{1,0:T(8,128)S(1)}, u32[]{:S(2)}, u32[]{:S(2)}) collective-permute-start(f32[128,512]{1,0:T(8,128)S(1)} %add.47.token.refs_4_), channel_id=1, source_target_pairs={{0,4},{4,0},{8,12},{12,8},{16,20},{20,16},{24,28},{28,24},{1,5},{5... | collective-permute-start | bytes 786440 | tf_op jit(solution)/shard_map/ppermute | solution.py:205
  (9 other events, 22.0 us)

commit v3 on v2

--- a/solution.py
+++ b/solution.py
@@ -137,42 +137,36 @@
     )(gram)
 
 
-def first_kernel(bits, a, b, c, d, token, out, work, stack, block):
+def first_kernel(bits, a, b, c, d, out, work, stack, block):
     place_gram(bits, [a, b, c, d, stack], work)
     factor_step(0, work, out, block)
 
 
-def first_step(bits, shares, size, token):
+def first_step(bits, shares, size):
     blocks = sum(x.shape[0] for x in shares)
     return kernel(
         first_kernel,
-        [
-            jax.ShapeDtypeStruct((lanes, size), jnp.float32),
-            jax.ShapeDtypeStruct((size, size), jnp.float32),
-        ],
-        [smem] + [vmem] * 4 + [anywhere],
+        [shape(lanes, size), shape(size, size)],
+        [smem] + [vmem] * 4,
         [pltpu.VMEM((blocks, lanes), jnp.float32), pltpu.VMEM((lanes, lanes), jnp.float32)],
         "factor_first",
-    )(bits, *shares, token)
-
-
-def later_kernel(b, before, token, out, work, block):
+    )(bits, *shares)
+
+
+def later_kernel(b, before, out, work, block):
     work[...] = before[...]
     factor_step(b, work, out, block)
 
 
-def later_step(b, work, token):
+def later_step(b, work):
     size = work.shape[0]
     return kernel(
         functools.partial(later_kernel, b),
-        [
-            jax.ShapeDtypeStruct((lanes, size), jnp.float32),
-            jax.ShapeDtypeStruct((size, size), jnp.float32),
-        ],
-        [vmem, anywhere],
+        [shape(lanes, size), shape(size, size)],
+        [vmem],
         [pltpu.VMEM((lanes, lanes), jnp.float32)],
         "factor_later",
-    )(work, token)
+    )(work)
 
 
 def share_norms(right_rows):
@@ -224,78 +218,103 @@
     kept[...] = total[pl.ds(pl.multiple_of(bits[0] * half, 8), half), :]
 
 
+def add_kernel(*refs):
+    refs[-1][...] = refs[0][...] + refs[1][...]
+
+
+def add_after(a, b, *tokens):
+    return kernel(
+        add_kernel, shape(*a.shape), [vmem] * 2 + [anywhere] * len(tokens), [], "add_after"
+    )(a, b, *tokens)
+
+
 def gram_kernel(bits, *refs):
-    rows, (in_square, sent, kept, stack) = refs[:square], refs[square:]
-    half, rank = rows[0].shape
+    parts, (sent, kept, rows, stack) = refs[:square], refs[square:]
+    half, rank = parts[0].shape
     share = sent.shape[0]
-    for k, part in enumerate(rows):
-        in_square[k * half : (k + 1) * half, :] = part[...]
+    for k, part in enumerate(parts):
+        rows[k * half : (k + 1) * half, :] = part[...]
     at = 0
     for first in range(0, rank, lanes):
-        left, right = in_square[:, first:], in_square[:, first : first + lanes]
+        left, right = rows[:, first:], rows[:, first : first + lanes]
         stack[at : at + rank - first, :] = dot(left, right, ((0,), (0,)))
         at += rank - first
-    sent[...] = stack[pl.ds(pl.multiple_of((2 * bits[1] + 1 - bits[0]) * share, 8), share), :]
-    kept[...] = stack[pl.ds(pl.multiple_of((2 * bits[1] + bits[0]) * share, 8), share), :]
-
-
-def raw_kernel(bits, in_square, other, *refs):
-    columns, pieces, (left, right) = refs[:square], refs[square:-2], refs[-2:]
+    for out, core in ((kept, bits[0]), (sent, 1 - bits[0])):
+        index = (2 * bits[1] + core) * square + bits[2]
+        out[...] = stack[pl.ds(pl.multiple_of(index * share, 8), share), :]
+
+
+def order_kernel(bits, *refs):
+    out = refs[-1]
+    share = refs[0].shape[0]
+    for k in range(square):
+        out[pl.ds(pl.multiple_of((bits[2] ^ k) * share, 8), share), :] = refs[k][...]
+
+
+def raw_kernel(bits, *refs):
+    mine, others, columns = refs[:square], refs[square : 2 * square], refs[2 * square : 3 * square]
+    sent, kept, left, right, raw = refs[3 * square :]
     rows = columns[0].shape[0]
     half = rows // 2
     for k in range(square):
-        own = slice(k * half, (k + 1) * half)
         left[k * rows : (k + 1) * rows, :] = columns[k][...]
-        right[pl.ds(pl.multiple_of(k * rows + bits[0] * half, 8), half), :] = in_square[own, :]
-        right[pl.ds(pl.multiple_of(k * rows + (1 - bits[0]) * half, 8), half), :] = other[own, :]
-    step = pieces[0].shape[0]
-    raw = dot(left[...], right[...], ((0,), (0,)))
-    for at, piece in enumerate(pieces):
-        piece[...] = raw[at * step : (at + 1) * step]
-
-
-def left_kernel(bits, in_square, other, *refs):
-    count = refs[-2].shape[0] // lanes
-    inverses, refs = refs[:count], refs[count:]
-    own, (left, squares, inverse, rows) = refs[:-4], refs[-4:]
-    half = left.shape[0] // 2
+        right[pl.ds(pl.multiple_of(k * rows + bits[0] * half, 8), half), :] = mine[k][...]
+        right[pl.ds(pl.multiple_of(k * rows + (1 - bits[0]) * half, 8), half), :] = others[k][...]
+    raw[...] = dot(left[...], right[...], ((0,), (0,)))
+    count = kept.shape[0]
+    kept[...] = raw[pl.ds(pl.multiple_of(bits[4] * count, 8), count), :]
+    sent[...] = raw[pl.ds(pl.multiple_of((1 - bits[4]) * count, 8), count), :]
+
+
+def left_kernel(scale, bits, mine, other, *refs):
+    inverses, (left, left_scaled, inverse, rows) = refs[:-4], refs[-4:]
+    half = mine.shape[0]
     for b, part in enumerate(inverses):
         inverse[b * lanes : (b + 1) * lanes, :] = part[...]
-    rows[pl.ds(pl.multiple_of(bits[0] * half, 8), half), :] = in_square[:half, :]
-    rows[pl.ds(pl.multiple_of((1 - bits[0]) * half, 8), half), :] = other[:half, :]
-    total = None
-    for part in own:
+    rows[pl.ds(pl.multiple_of(bits[0] * half, 8), half), :] = mine[...]
+    rows[pl.ds(pl.multiple_of((1 - bits[0]) * half, 8), half), :] = other[...]
+    left[...] = dot(rows[...], inverse[...], ((1,), (1,)))
+    left_scaled[...] = left[...] * scale
+
+
+def norm_kernel(own, received, inverse, *refs):
+    out = refs[-1]
+    count = own.shape[0]
+    total = jnp.zeros((1, own.shape[1]), jnp.float32)
+    for part in (own, received):
         right = dot(part[...], inverse[...], ((1,), (1,)))
-        part_total = jnp.sum(right * right, axis=0, keepdims=True)
-        total = part_total if total is None else total + part_total
-    squares[...] = total
-    left[...] = dot(rows[...], inverse[...], ((1,), (1,)))
-
-
-def plane_kernel(scale, left, inverse, left_scaled, plane):
-    left_scaled[...] = left[...] * scale
+        total = total + jnp.sum(right * right, axis=0, keepdims=True)
+    out[:count, :] = received[...]
+    row = lax.broadcasted_iota(jnp.int32, (8, own.shape[1]), 0)
+    out[count:, :] = jnp.where(row == 0, total, 0.0)
+
+
+def momentum_kernel(bits, left, inverse, *refs):
+    pieces, own, received = refs[:square], refs[square : 2 * square], refs[2 * square : 3 * square]
+    new_momentum, raw, plane = refs[3 * square :]
+    rows, width = pieces[0].shape
+    half = own[0].shape[0]
     plane[...] = dot(left[...], inverse[...])
-
-
-def last_kernel(factor, steps, bits, squares, left, inverse, plane, *refs):
-    pieces, refs = refs[:square], refs[square:]
-    raws, (new_momentum, update, next_basis, raw, planes) = refs[: square * steps], refs[square * steps :]
-    rows, width = pieces[0].shape
-    step = raws[0].shape[0]
-    column_norm = jnp.sqrt(squares[...] + epsilon)
-    planes[:rows, :] = plane[...]
-    planes[rows:, :] = dot(left[...] * (factor / column_norm), inverse[...])
     for k in range(square):
         first = (bits[2] ^ k) * width
         new_momentum[:, pl.ds(pl.multiple_of(first, lanes), width)] = pieces[k][...]
-        for i in range(steps):
-            raw[pl.ds(pl.multiple_of(first + i * step, lanes), step), :] = raws[i * square + k][...]
-    cols, chunk = raw.shape[0], raw.shape[1]
+        at = pl.multiple_of(first + bits[4] * half, 8)
+        raw[pl.ds(at, half), :] = own[k][...]
+        at = pl.multiple_of(first + (1 - bits[4]) * half, 8)
+        raw[pl.ds(at, half), :] = received[k][:half, :]
+    cols, chunk = raw.shape
     for first in range(0, cols, chunk):
         at = slice(first, min(first + chunk, cols))
-        both = dot(planes[...], raw[at, :], ((1,), (1,)))
-        new_momentum[:, at] = new_momentum[:, at] - 0.5 * both[:rows]
-        update[:, at] = both[rows:].astype(jnp.bfloat16)
+        new_momentum[:, at] = new_momentum[:, at] - 0.5 * dot(plane[...], raw[at, :], ((1,), (1,)))
+
+
+def update_kernel(factor, bits, squares, left, inverse, raw, update, next_basis, plane):
+    column_norm = jnp.sqrt(squares[...] + epsilon)
+    plane[...] = dot(left[...] * (factor / column_norm), inverse[...])
+    cols, chunk = raw.shape
+    for first in range(0, cols, chunk):
+        at = slice(first, min(first + chunk, cols))
+        update[:, at] = dot(plane[...], raw[at, :], ((1,), (1,))).astype(jnp.bfloat16)
     count = next_basis.shape[0]
     own = raw[pl.ds(pl.multiple_of(bits[3] * count, 8), count), :]
     next_basis[...] = dot(own, inverse[...], ((1,), (1,))) / column_norm
@@ -304,7 +323,8 @@
 def in_squares(momentum, gradient, right_basis):
     device = lax.axis_index("fsdp")
     tensor = lax.axis_index("tensor")
-    bits = jnp.stack([tensor % 2, tensor // 2, device % square, device]).astype(jnp.int32)
+    bits = jnp.stack([tensor % 2, tensor // 2, device % square, device, device // square])
+    bits = bits.astype(jnp.int32)
     rows, cols = momentum.shape
     rank = right_basis.shape[1]
     half, width = rows // 2, cols // square
@@ -324,80 +344,83 @@
         "part_left",
     )(bits, right_basis, *pieces)
     mine = kept + swap(sent, "tensor", 1)
-    mine = mine + swap(mine, "tensor", 2)
+    mine = add_after(mine, swap(mine, "tensor", 2), *columns[1:])
     gathered = [mine] + [swap(mine, "fsdp", k) for k in range(1, square)]
-
-    count = rank // lanes
-    stacked = count * (count + 1) // 2 * lanes
-    share = stacked // 4
-    in_square, sent, kept = kernel(
-        gram_kernel,
-        [shape(square * half, rank), shape(share, lanes), shape(share, lanes)],
-        [smem] + [vmem] * square,
-        [pltpu.VMEM((stacked, lanes), jnp.float32)],
-        "part_gram",
-    )(bits, *gathered)
-    other = swap(in_square, "tensor", 1)
-    quarter = kept + swap(sent, "tensor", 1)
-    quarter = quarter + swap(quarter, "fsdp", square)
-    over_planes = swap(quarter, "tensor", 2)
-    shares = [quarter, swap(quarter, "tensor", 1), over_planes, swap(over_planes, "tensor", 1)]
-
-    steps = width // lanes
-    parts = kernel(
+    others = [swap(part, "tensor", 1) for part in gathered]
+
+    sent, kept = kernel(
         raw_kernel,
-        [shape(lanes, rank)] * steps,
-        [smem] + [vmem] * (2 + square),
+        [shape(width // 2, rank)] * 2,
+        [smem] + [vmem] * (3 * square),
         [
             pltpu.VMEM((square * rows, width), jnp.float32),
             pltpu.VMEM((square * rows, rank), jnp.float32),
+            pltpu.VMEM((width, rank), jnp.float32),
         ],
         "part_raw",
-    )(bits, in_square, other, *columns)
-    own, raws = [], []
-    for part in parts:
-        part = part + swap(part, "fsdp", square)
-        own.append(part)
-        raws += [part] + [swap(part, "fsdp", k) for k in range(1, square)]
+    )(bits, *gathered, *others, *columns)
+    own = kept + swap(sent, "fsdp", square)
+
+    count = rank // lanes
+    stacked = count * (count + 1) // 2 * lanes
+    share = stacked // (4 * square)
+    sent, kept = kernel(
+        gram_kernel,
+        [shape(share, lanes)] * 2,
+        [smem] + [vmem] * square,
+        [pltpu.VMEM((square * half, rank), jnp.float32), pltpu.VMEM((stacked, lanes), jnp.float32)],
+        "part_gram",
+    )(bits, *gathered)
+    part = kept + swap(sent, "tensor", 1)
+    part = part + swap(part, "fsdp", square)
+    quarter = kernel(
+        order_kernel, shape(square * share, lanes), [smem] + [vmem] * square, [], "order"
+    )(bits, part, *[swap(part, "fsdp", k) for k in range(1, square)])
+    over_planes = swap(quarter, "tensor", 2)
+    shares = [quarter, swap(quarter, "tensor", 1), over_planes, swap(over_planes, "tensor", 1)]
 
     factors = []
-    out, work = first_step(bits, shares, rank, parts[0])
+    out, work = first_step(bits, shares, rank)
     factors.append(out)
     for b in range(1, count):
-        out, work = later_step(b, work, own[min(b // 2, len(own) - 1)])
+        out, work = later_step(b, work)
         factors.append(out)
-
-    left, squares, inverse = kernel(
-        left_kernel,
-        [shape(rows, rank), shape(1, rank), shape(rank, rank)],
-        [smem] + [vmem] * (2 + count + steps),
+    left, left_scaled, inverse = kernel(
+        functools.partial(left_kernel, math.sqrt(total_rows)),
+        [shape(rows, rank), shape(rows, rank), shape(rank, rank)],
+        [smem] + [vmem] * (2 + count),
         [pltpu.VMEM((rows, rank), jnp.float32)],
         "left",
-    )(bits, in_square, other, *factors, *own)
-    for axis, last in (("tensor", lax.axis_size("tensor")), ("fsdp", square)):
-        flip = 1
-        while flip < last:
-            squares = squares + swap(squares, axis, flip)
-            flip *= 2
-    left_scaled, plane = kernel(
-        functools.partial(plane_kernel, math.sqrt(total_rows)),
-        [shape(rows, rank)] * 2,
-        [vmem] * 2,
+    )(bits, mine, others[0], *factors)
+
+    received = swap(own, "fsdp", square)
+    own_rows = [own] + [swap(own, "fsdp", k) for k in range(1, square)]
+    with_norms = kernel(
+        norm_kernel,
+        shape(width // 2 + 8, rank),
+        [vmem] * 3 + [anywhere] * (square - 1),
         [],
-        "plane",
-    )(left, inverse)
-
-    new_momentum, update, next_basis = kernel(
-        functools.partial(last_kernel, math.sqrt(total_rows / total_cols), steps),
-        [
-            shape(rows, cols),
-            shape(rows, cols, dtype=jnp.bfloat16),
-            shape(cols // lax.axis_size("fsdp"), rank),
-        ],
-        [smem] + [vmem] * (4 + square + square * steps),
-        [pltpu.VMEM((cols, rank), jnp.float32), pltpu.VMEM((2 * rows, rank), jnp.float32)],
-        "last",
-    )(bits, squares, left, inverse, plane, *pieces, *raws)
+        "norms",
+    )(own, received, inverse, *own_rows[1:])
+    received_rows = [with_norms] + [swap(with_norms, "fsdp", k) for k in range(1, square)]
+    squares = sum(part[width // 2 : width // 2 + 1] for part in received_rows)
+    squares = squares + swap(squares, "tensor", 1)
+    squares = squares + swap(squares, "tensor", 2)
+
+    new_momentum, raw = kernel(
+        momentum_kernel,
+        [shape(rows, cols), shape(cols, rank)],
+        [smem] + [vmem] * (2 + 3 * square),
+        [pltpu.VMEM((rows, rank), jnp.float32)],
+        "new_momentum",
+    )(bits, left, inverse, *pieces, *own_rows, *received_rows)
+    update, next_basis = kernel(
+        functools.partial(update_kernel, math.sqrt(total_rows / total_cols)),
+        [shape(rows, cols, dtype=jnp.bfloat16), shape(cols // lax.axis_size("fsdp"), rank)],
+        [smem] + [vmem] * 4,
+        [pltpu.VMEM((rows, rank), jnp.float32)],
+        "update",
+    )(bits, squares, left, inverse, raw)
     return (update, new_momentum, left_scaled, next_basis)
 
 

time: 163 us -> 151 us (0.926)
  waiting for transfers between devices: 81 us -> 68.4 us
  Pallas kernels: 44.9 us -> 47.2 us
  starting transfers between devices: 31.2 us -> 29.5 us
    ppermute x30, waiting for transfers between devices: 81 us -> 68.4 us  [swap(): lax.ppermute(value, axis, [(i, i ^ flip) for i in range(lax.axis_size(axi...]
    pallas_call x9 -> x12, Pallas kernels: 40.2 us -> 42.5 us  [the longest x3 14 us: later_step(): kernel(functools.partial(later_kernel, b), [shape(lanes, size), shape(siz...]
    ppermute x30, starting transfers between devices: 31.2 us -> 29.5 us  [swap(): lax.ppermute(value, axis, [(i, i ^ flip) for i in range(lax.axis_size(axi...]
  transfers between devices with their start and end apart: 30 -> 30, of which waited for: 15 -> 19; matrix products, arithmetic and copies ran while one was open for 0% -> 0% of each run, Pallas kernels for 18% -> 20%
where the time goes in v3:
time: 151 us
  waiting for transfers between devices  68.4 us (45%)
  Pallas kernels  47.2 us (31%)
  starting transfers between devices  29.5 us (20%)
  local copies, waits for them, and re-layouts  4.46 us (3%)
    ppermute x30, waiting for transfers between devices, swap(): lax.ppermute(value, axis, [(i, i ^ flip) for i in range(lax.axis_size(axi...  68.4 us
    ppermute x30, starting transfers between devices, swap(): lax.ppermute(value, axis, [(i, i ^ flip) for i in range(lax.axis_size(axi...  29.5 us
    pallas_call x3, Pallas kernels, later_step(): kernel(functools.partial(later_kernel, b), [shape(lanes, size), shape(siz...  14 us
    pallas_call x1, Pallas kernels, in_squares(): kernel(functools.partial(update_kernel, math.sqrt(total_rows / total_cols...  6.05 us
    pallas_call x1, Pallas kernels, in_squares(): kernel(momentum_kernel, [shape(rows, cols), shape(cols, rank)], [smem] +...  5.56 us
    pallas_call x1, Pallas kernels, first_step(): kernel(first_kernel, [shape(lanes, size), shape(size, size)], [smem] + [v...  5.24 us
    unnamed x6, local copies, waits for them, and re-layouts  4.37 us
    pallas_call x1, Pallas kernels, in_squares(): kernel(part_left_kernel, [shape(half, rank)] * 2, [smem] + [vmem] * (1 +...  3.95 us
  transfers between devices with their start and end apart: 30, of which 19 were waited for; matrix products, arithmetic and copies ran while one was open for 0% of the time, Pallas kernels for 20%

profile of v3, /device:TPU:0, one launch (start us, length us, event | category | flops | bytes accessed | tf_op | source)
XLA Modules:
  0.0 150.5 jit_solution(18076257092236437644)
XLA Ops:
  5.8 4.0 %part_left.1 = (f32[120,512]{1,0:T(8,128)S(1)}, f32[120,512]{1,0:T(8,128)S(1)}) custom-call(s32[5]{0:T(128)S(1)} %stack.23.bits, f32[1536,512]{1,0:T(8,128)S(1)} %copy-done, f32[240,384]{1,0:T(8,128)S(1)} %get-tuple-element.28.refs_0_.refs_8_, f32[240,384]{1,0:T(8,128)S(1)} %get-tuple-element.29.refs_1_, f32[240,384]{1,0:T(8,128)S(1)} %get-tuple-element.30.refs_2_, ...), custom_call_target="tpu_custom_call" | custom-call | tf_op jit(solution)/shard_map/part_left/pallas_call | solution.py:339
  10.3 2.6 %collective-permute-start.2 = (f32[240,384]{1,0:T(8,128)S(1)}, f32[240,384]{1,0:T(8,128)S(1)}, u32[]{:S(2)}, u32[]{:S(2)}) collective-permute-start(f32[240,384]{1,0:T(8,128)S(1)} %get-tuple-element.29.refs_1_), channel_id=1, source_target_pairs={{0,4},{4,0},{8,12},{12,8},{16,20},{20,16},{24,28},{28,24},{1,5},{5... | collective-permute-start | bytes 1105928 | tf_op jit(solution)/shard_map/ppermute | solution.py:199
  16.5 5.6 %collective-permute-done.2.refs_2_.refs_9_ = f32[240,384]{1,0:T(8,128)S(1)} collective-permute-done((f32[240,384]{1,0:T(8,128)S(1)}, f32[240,384]{1,0:T(8,128)S(1)}, u32[]{:S(2)}, u32[]{:S(2)}) %collective-permute-start.2) | collective-permute-done | bytes 368672 | tf_op jit(solution)/shard_map/ppermute | solution.py:199
  22.1 2.3 %collective-permute-done.3.refs_3_.refs_10_ = f32[240,384]{1,0:T(8,128)S(1)} collective-permute-done((f32[240,384]{1,0:T(8,128)S(1)}, f32[240,384]{1,0:T(8,128)S(1)}, u32[]{:S(2)}, u32[]{:S(2)}) %collective-permute-start.3) | collective-permute-done | bytes 368672 | tf_op jit(solution)/shard_map/ppermute | solution.py:199
  24.3 6.9 %collective-permute-done.4.refs_4_.refs_11_ = f32[240,384]{1,0:T(8,128)S(1)} collective-permute-done((f32[240,384]{1,0:T(8,128)S(1)}, f32[240,384]{1,0:T(8,128)S(1)}, u32[]{:S(2)}, u32[]{:S(2)}) %collective-permute-start.4) | collective-permute-done | bytes 368672 | tf_op jit(solution)/shard_map/ppermute | solution.py:199
  34.9 5.4 %collective-permute-done.6.refs_2_ = f32[120,512]{1,0:T(8,128)S(1)} collective-permute-done((f32[120,512]{1,0:T(8,128)S(1)}, f32[120,512]{1,0:T(8,128)S(1)}, u32[]{:S(2)}, u32[]{:S(2)}) %collective-permute-start.6) | collective-permute-done | bytes 245792 | tf_op jit(solution)/shard_map/ppermute | solution.py:199
  40.2 4.8 %collective-permute-done.7.refs_3_ = f32[120,512]{1,0:T(8,128)S(1)} collective-permute-done((f32[120,512]{1,0:T(8,128)S(1)}, f32[120,512]{1,0:T(8,128)S(1)}, u32[]{:S(2)}, u32[]{:S(2)}) %collective-permute-start.7) | collective-permute-done | bytes 245792 | tf_op jit(solution)/shard_map/ppermute | solution.py:199
  47.9 3.4 %part_raw.1 = (f32[192,512]{1,0:T(8,128)S(1)}, f32[192,512]{1,0:T(8,128)S(1)}) custom-call(s32[5]{0:T(128)S(1)} %stack.23.bits, f32[120,512]{1,0:T(8,128)S(1)} %add_after.1.refs_0_.mine, f32[120,512]{1,0:T(8,128)S(1)} %collective-permute-done.5.refs_1_, f32[120,512]{1,0:T(8,128)S(1)} %collective-permute-done.6.refs_2_, ...), custom_call_target="tpu_custom_call" | custom-call | tf_op jit(solution)/shard_map/part_raw/pallas_call | solution.py:351
  51.3 2.7 %collective-permute-start.12 = (f32[192,512]{1,0:T(8,128)S(1)}, f32[192,512]{1,0:T(8,128)S(1)}, u32[]{:S(2)}, u32[]{:S(2)}) collective-permute-start(f32[192,512]{1,0:T(8,128)S(1)} %get-tuple-element.35), channel_id=1, source_target_pairs={{0,16},{4,20},{8,24},{12,28},{16,0},{20,4},{24,8},{28,12},{1,17},{... | collective-permute-start | bytes 1179656 | tf_op jit(solution)/shard_map/ppermute | solution.py:199
  54.0 3.0 %part_gram.1 = (f32[80,128]{1,0:T(8,128)S(1)}, f32[80,128]{1,0:T(8,128)S(1)}) custom-call(s32[5]{0:T(128)S(1)} %stack.23.bits, f32[120,512]{1,0:T(8,128)S(1)} %add_after.1.refs_0_.mine, f32[120,512]{1,0:T(8,128)S(1)} %collective-permute-done.5.refs_1_, f32[120,512]{1,0:T(8,128)S(1)} %collective-permute-done.6.refs_2_, ...), custom_call_target="tpu_custom_call" | custom-call | tf_op jit(solution)/shard_map/part_gram/pallas_call | solution.py:367
  58.6 15.0 %collective-permute-done.15 = f32[80,128]{1,0:T(8,128)S(1)} collective-permute-done((f32[80,128]{1,0:T(8,128)S(1)}, f32[80,128]{1,0:T(8,128)S(1)}, u32[]{:S(2)}, u32[]{:S(2)}) %collective-permute-start.15) | collective-permute-done | bytes 40992 | tf_op jit(solution)/shard_map/ppermute | solution.py:199
  74.8 2.3 %collective-permute-start.18 = (f32[80,128]{1,0:T(8,128)S(1)}, f32[80,128]{1,0:T(8,128)S(1)}, u32[]{:S(2)}, u32[]{:S(2)}) collective-permute-start(f32[80,128]{1,0:T(8,128)S(1)} %add.41.refs_0_), channel_id=1, source_target_pairs={{0,12},{4,8},{8,4},{12,0},{16,28},{20,24},{24,20},{28,16},{1,13},{... | collective-permute-start | bytes 122888 | tf_op jit(solution)/shard_map/ppermute | solution.py:199
  81.9 3.4 %collective-permute-start.13 = (f32[192,512]{1,0:T(8,128)S(1)}, f32[192,512]{1,0:T(8,128)S(1)}, u32[]{:S(2)}, u32[]{:S(2)}) collective-permute-start(f32[192,512]{1,0:T(8,128)S(1)} %add.39.own.refs_4_), channel_id=1, source_target_pairs={{0,16},{4,20},{8,24},{12,28},{16,0},{20,4},{24,8},{28,12},{1,17},{... | collective-permute-start | bytes 1179656 | tf_op jit(solution)/shard_map/ppermute | solution.py:199
  91.7 5.2 %factor_first.1 = (f32[128,512]{1,0:T(8,128)S(1)}, f32[512,512]{1,0:T(8,128)S(1)}) custom-call(s32[5]{0:T(128)S(1)} %stack.23.bits, f32[320,128]{1,0:T(8,128)S(1)} %order.1.a, f32[320,128]{1,0:T(8,128)S(1)} %collective-permute-done.19.b, f32[320,128]{1,0:T(8,128)S(1)} %collective-permute-done.20.c, f32[320,128]{1,0:T(8,128)S(1)} %collective-permute-done.21.d), custom_call_target="tpu_custom_call" | custom-call | tf_op jit(solution)/shard_map/factor_first/pallas_call | solution.py:147
  96.9 4.6 %factor_later.3 = (f32[128,512]{1,0:T(8,128)S(1)}, f32[512,512]{1,0:T(8,128)S(1)}) custom-call(f32[512,512]{1,0:T(8,128)S(1)} %get-tuple-element.39.before), custom_call_target="tpu_custom_call" | custom-call | tf_op jit(solution)/shard_map/factor_later/pallas_call | solution.py:163
  101.5 4.3 %factor_later.4 = (f32[128,512]{1,0:T(8,128)S(1)}, f32[512,512]{1,0:T(8,128)S(1)}) custom-call(f32[512,512]{1,0:T(8,128)S(1)} %get-tuple-element.41.before), custom_call_target="tpu_custom_call" | custom-call | tf_op jit(solution)/shard_map/factor_later/pallas_call | solution.py:163
  105.7 5.2 %factor_later.5 = (f32[128,512]{1,0:T(8,128)S(1)}, f32[512,512]{1,0:T(8,128)}) custom-call(f32[512,512]{1,0:T(8,128)S(1)} %get-tuple-element.43.before), custom_call_target="tpu_custom_call" | custom-call | tf_op jit(solution)/shard_map/factor_later/pallas_call | solution.py:163
  110.9 2.4 %left.1 = (f32[240,512]{1,0:T(8,128)S(1)}, f32[240,512]{1,0:T(8,128)}, f32[512,512]{1,0:T(8,128)S(1)}) custom-call(s32[5]{0:T(128)S(1)} %stack.23.bits, f32[120,512]{1,0:T(8,128)S(1)} %add_after.1.refs_0_.mine, f32[120,512]{1,0:T(8,128)S(1)} %collective-permute-done.8.refs_4_.other, f32[128,512]{1,0:T(8,128)S(1)} %get-tuple-element.38.refs_0_, ...), custom_call_target="tpu_custom_call" | custom-call | tf_op jit(solution)/shard_map/left/pallas_call | solution.py:388
  113.4 2.3 %norms.1.refs_8_ = f32[200,512]{1,0:T(8,128)S(1)} custom-call(f32[192,512]{1,0:T(8,128)S(1)} %add.39.own.refs_4_, f32[192,512]{1,0:T(8,128)S(1)} %collective-permute-done.13.received, f32[512,512]{1,0:T(8,128)S(1)} %get-tuple-element.45.inverse, f32[192,512]{1,0:T(8,128)S(1)} %collective-permute-done.22.refs_0_.refs_5_, ...), custom_call_target="tpu_custom_call" | custom-call | tf_op jit(solution)/shard_map/norms/pallas_call | solution.py:398
  119.2 8.0 %collective-permute-done.25.refs_9_ = f32[200,512]{1,0:T(8,128)S(1)} collective-permute-done((f32[200,512]{1,0:T(8,128)S(1)}, f32[200,512]{1,0:T(8,128)S(1)}, u32[]{:S(2)}, u32[]{:S(2)}) %collective-permute-start.25) | collective-permute-done | bytes 409632 | tf_op jit(solution)/shard_map/ppermute | solution.py:199
  127.3 2.3 %collective-permute-done.26.refs_10_ = f32[200,512]{1,0:T(8,128)S(1)} collective-permute-done((f32[200,512]{1,0:T(8,128)S(1)}, f32[200,512]{1,0:T(8,128)S(1)}, u32[]{:S(2)}, u32[]{:S(2)}) %collective-permute-start.26) | collective-permute-done | bytes 409632 | tf_op jit(solution)/shard_map/ppermute | solution.py:199
  129.6 7.6 %collective-permute-done.27.refs_11_ = f32[200,512]{1,0:T(8,128)S(1)} collective-permute-done((f32[200,512]{1,0:T(8,128)S(1)}, f32[200,512]{1,0:T(8,128)S(1)}, u32[]{:S(2)}, u32[]{:S(2)}) %collective-permute-start.27) | collective-permute-done | bytes 409632 | tf_op jit(solution)/shard_map/ppermute | solution.py:199
  138.9 5.6 %new_momentum.1 = (f32[240,1536]{1,0:T(8,128)}, f32[1536,512]{1,0:T(8,128)S(1)}) custom-call(s32[5]{0:T(128)S(1)} %stack.23.bits, f32[240,512]{1,0:T(8,128)S(1)} %get-tuple-element.46.left, f32[512,512]{1,0:T(8,128)S(1)} %get-tuple-element.45.inverse, f32[240,384]{1,0:T(8,128)S(1)} %get-tuple-element.28.refs_0_.refs_8_, ...), custom_call_target="tpu_custom_call" | custom-call | tf_op jit(solution)/shard_map/new_momentum/pallas_call | solution.py:410
  144.5 6.0 %update.1 = (bf16[240,1536]{1,0:T(8,128)(2,1)}, f32[192,512]{1,0:T(8,128)}) custom-call(s32[5]{0:T(128)S(1)} %stack.23.bits, f32[1,512]{1,0:T(1,128)S(1)} %add.46.squares, f32[240,512]{1,0:T(8,128)S(1)} %get-tuple-element.46.left, f32[512,512]{1,0:T(8,128)S(1)} %get-tuple-element.45.inverse, f32[1536,512]{1,0:T(8,128)S(1)} %get-tuple-element.47.raw), custom_call_target="tpu_custom_call" | custom-call | tf_op jit(solution)/shard_map/update/pallas_call | solution.py:417
  (64 shorter events, 34.9 us)
Async XLA Ops:
  9.8 4.7 %collective-permute-start = (f32[120,512]{1,0:T(8,128)S(1)}, f32[120,512]{1,0:T(8,128)S(1)}, u32[]{:S(2)}, u32[]{:S(2)}) collective-permute-start(f32[120,512]{1,0:T(8,128)S(1)} %get-tuple-element.33), channel_id=1, source_target_pairs={{0,1},{1,0},{2,3},{3,2},{4,5},{5,4},{6,7},{7,6},{8,9},{9,8},{10,11... | collective-permute-start | bytes 737288 | tf_op jit(solution)/shard_map/ppermute | solution.py:199
  10.3 11.8 %collective-permute-start.2 = (f32[240,384]{1,0:T(8,128)S(1)}, f32[240,384]{1,0:T(8,128)S(1)}, u32[]{:S(2)}, u32[]{:S(2)}) collective-permute-start(f32[240,384]{1,0:T(8,128)S(1)} %get-tuple-element.29.refs_1_), channel_id=1, source_target_pairs={{0,4},{4,0},{8,12},{12,8},{16,20},{20,16},{24,28},{28,24},{1,5},{5... | collective-permute-start | bytes 1105928 | tf_op jit(solution)/shard_map/ppermute | solution.py:199
  12.9 11.4 %collective-permute-start.3 = (f32[240,384]{1,0:T(8,128)S(1)}, f32[240,384]{1,0:T(8,128)S(1)}, u32[]{:S(2)}, u32[]{:S(2)}) collective-permute-start(f32[240,384]{1,0:T(8,128)S(1)} %get-tuple-element.30.refs_2_), channel_id=1, source_target_pairs={{0,8},{4,12},{8,0},{12,4},{16,24},{20,28},{24,16},{28,20},{1,9},{5... | collective-permute-start | bytes 1105928 | tf_op jit(solution)/shard_map/ppermute | solution.py:199
  14.5 16.8 %collective-permute-start.4 = (f32[240,384]{1,0:T(8,128)S(1)}, f32[240,384]{1,0:T(8,128)S(1)}, u32[]{:S(2)}, u32[]{:S(2)}) collective-permute-start(f32[240,384]{1,0:T(8,128)S(1)} %get-tuple-element.31.refs_3_), channel_id=1, source_target_pairs={{0,12},{4,8},{8,4},{12,0},{16,28},{20,24},{24,20},{28,16},{1,13},{... | collective-permute-start | bytes 1105928 | tf_op jit(solution)/shard_map/ppermute | solution.py:199
  14.5 16.7 %collective-permute-start.1 = (f32[120,512]{1,0:T(8,128)S(1)}, f32[120,512]{1,0:T(8,128)S(1)}, u32[]{:S(2)}, u32[]{:S(2)}) collective-permute-start(f32[120,512]{1,0:T(8,128)S(1)} %add.38.refs_0_), channel_id=1, source_target_pairs={{0,2},{1,3},{2,0},{3,1},{4,6},{5,7},{6,4},{7,5},{8,10},{9,11},{10,... | collective-permute-start | bytes 737288 | tf_op jit(solution)/shard_map/ppermute | solution.py:199
  31.3 8.9 %collective-permute-start.6 = (f32[120,512]{1,0:T(8,128)S(1)}, f32[120,512]{1,0:T(8,128)S(1)}, u32[]{:S(2)}, u32[]{:S(2)}) collective-permute-start(f32[120,512]{1,0:T(8,128)S(1)} %add_after.1.refs_0_.mine), channel_id=1, source_target_pairs={{0,8},{4,12},{8,0},{12,4},{16,24},{20,28},{24,16},{28,20},{1,9},{5... | collective-permute-start | bytes 737288 | tf_op jit(solution)/shard_map/ppermute | solution.py:199
  33.1 11.9 %collective-permute-start.7 = (f32[120,512]{1,0:T(8,128)S(1)}, f32[120,512]{1,0:T(8,128)S(1)}, u32[]{:S(2)}, u32[]{:S(2)}) collective-permute-start(f32[120,512]{1,0:T(8,128)S(1)} %add_after.1.refs_0_.mine), channel_id=1, source_target_pairs={{0,12},{4,8},{8,4},{12,0},{16,28},{20,24},{24,20},{28,16},{1,13},{... | collective-permute-start | bytes 737288 | tf_op jit(solution)/shard_map/ppermute | solution.py:199
  34.5 11.9 %collective-permute-start.5 = (f32[120,512]{1,0:T(8,128)S(1)}, f32[120,512]{1,0:T(8,128)S(1)}, u32[]{:S(2)}, u32[]{:S(2)}) collective-permute-start(f32[120,512]{1,0:T(8,128)S(1)} %add_after.1.refs_0_.mine), channel_id=1, source_target_pairs={{0,4},{4,0},{8,12},{12,8},{16,20},{20,16},{24,28},{28,24},{1,5},{5... | collective-permute-start | bytes 737288 | tf_op jit(solution)/shard_map/ppermute | solution.py:199
  34.9 11.5 %collective-permute-start.8 = (f32[120,512]{1,0:T(8,128)S(1)}, f32[120,512]{1,0:T(8,128)S(1)}, u32[]{:S(2)}, u32[]{:S(2)}) collective-permute-start(f32[120,512]{1,0:T(8,128)S(1)} %add_after.1.refs_0_.mine), channel_id=1, source_target_pairs={{0,1},{1,0},{2,3},{3,2},{4,5},{5,4},{6,7},{7,6},{8,9},{9,8},{10,11... | collective-permute-start | bytes 737288 | tf_op jit(solution)/shard_map/ppermute | solution.py:199
  40.2 6.2 %collective-permute-start.10 = (f32[120,512]{1,0:T(8,128)S(1)}, f32[120,512]{1,0:T(8,128)S(1)}, u32[]{:S(2)}, u32[]{:S(2)}) collective-permute-start(f32[120,512]{1,0:T(8,128)S(1)} %collective-permute-done.6.refs_2_), channel_id=1, source_target_pairs={{0,1},{1,0},{2,3},{3,2},{4,5},{5,4},{6,7},{7,6},{8,9},{9,8},{10,11... | collective-permute-start | bytes 737288 | tf_op jit(solution)/shard_map/ppermute | solution.py:199
  51.3 30.6 %collective-permute-start.12 = (f32[192,512]{1,0:T(8,128)S(1)}, f32[192,512]{1,0:T(8,128)S(1)}, u32[]{:S(2)}, u32[]{:S(2)}) collective-permute-start(f32[192,512]{1,0:T(8,128)S(1)} %get-tuple-element.35), channel_id=1, source_target_pairs={{0,16},{4,20},{8,24},{12,28},{16,0},{20,4},{24,8},{28,12},{1,17},{... | collective-permute-start | bytes 1179656 | tf_op jit(solution)/shard_map/ppermute | solution.py:199
  58.2 15.4 %collective-permute-start.15 = (f32[80,128]{1,0:T(8,128)S(1)}, f32[80,128]{1,0:T(8,128)S(1)}, u32[]{:S(2)}, u32[]{:S(2)}) collective-permute-start(f32[80,128]{1,0:T(8,128)S(1)} %add.40), channel_id=1, source_target_pairs={{0,16},{4,20},{8,24},{12,28},{16,0},{20,4},{24,8},{28,12},{1,17},{... | collective-permute-start | bytes 122888 | tf_op jit(solution)/shard_map/ppermute | solution.py:199
  73.6 4.0 %collective-permute-start.16 = (f32[80,128]{1,0:T(8,128)S(1)}, f32[80,128]{1,0:T(8,128)S(1)}, u32[]{:S(2)}, u32[]{:S(2)}) collective-permute-start(f32[80,128]{1,0:T(8,128)S(1)} %add.41.refs_0_), channel_id=1, source_target_pairs={{0,4},{4,0},{8,12},{12,8},{16,20},{20,16},{24,28},{28,24},{1,5},{5... | collective-permute-start | bytes 122888 | tf_op jit(solution)/shard_map/ppermute | solution.py:199
  74.3 4.4 %collective-permute-start.17 = (f32[80,128]{1,0:T(8,128)S(1)}, f32[80,128]{1,0:T(8,128)S(1)}, u32[]{:S(2)}, u32[]{:S(2)}) collective-permute-start(f32[80,128]{1,0:T(8,128)S(1)} %add.41.refs_0_), channel_id=1, source_target_pairs={{0,8},{4,12},{8,0},{12,4},{16,24},{20,28},{24,16},{28,20},{1,9},{5... | collective-permute-start | bytes 122888 | tf_op jit(solution)/shard_map/ppermute | solution.py:199
  74.8 4.9 %collective-permute-start.18 = (f32[80,128]{1,0:T(8,128)S(1)}, f32[80,128]{1,0:T(8,128)S(1)}, u32[]{:S(2)}, u32[]{:S(2)}) collective-permute-start(f32[80,128]{1,0:T(8,128)S(1)} %add.41.refs_0_), channel_id=1, source_target_pairs={{0,12},{4,8},{8,4},{12,0},{16,28},{20,24},{24,20},{28,16},{1,13},{... | collective-permute-start | bytes 122888 | tf_op jit(solution)/shard_map/ppermute | solution.py:199
  80.3 8.6 %collective-permute-start.20 = (f32[320,128]{1,0:T(8,128)S(1)}, f32[320,128]{1,0:T(8,128)S(1)}, u32[]{:S(2)}, u32[]{:S(2)}) collective-permute-start(f32[320,128]{1,0:T(8,128)S(1)} %order.1.a), channel_id=1, source_target_pairs={{0,2},{1,3},{2,0},{3,1},{4,6},{5,7},{6,4},{7,5},{8,10},{9,11},{10,... | collective-permute-start | bytes 491528 | tf_op jit(solution)/shard_map/ppermute | solution.py:199
  81.9 31.4 %collective-permute-start.13 = (f32[192,512]{1,0:T(8,128)S(1)}, f32[192,512]{1,0:T(8,128)S(1)}, u32[]{:S(2)}, u32[]{:S(2)}) collective-permute-start(f32[192,512]{1,0:T(8,128)S(1)} %add.39.own.refs_4_), channel_id=1, source_target_pairs={{0,16},{4,20},{8,24},{12,28},{16,0},{20,4},{24,8},{28,12},{1,17},{... | collective-permute-start | bytes 1179656 | tf_op jit(solution)/shard_map/ppermute | solution.py:199
  85.4 28.0 %collective-permute-start.22 = (f32[192,512]{1,0:T(8,128)S(1)}, f32[192,512]{1,0:T(8,128)S(1)}, u32[]{:S(2)}, u32[]{:S(2)}) collective-permute-start(f32[192,512]{1,0:T(8,128)S(1)} %add.39.own.refs_4_), channel_id=1, source_target_pairs={{0,4},{4,0},{8,12},{12,8},{16,20},{20,16},{24,28},{28,24},{1,5},{5... | collective-permute-start | bytes 1179656 | tf_op jit(solution)/shard_map/ppermute | solution.py:199
  86.9 26.5 %collective-permute-start.23 = (f32[192,512]{1,0:T(8,128)S(1)}, f32[192,512]{1,0:T(8,128)S(1)}, u32[]{:S(2)}, u32[]{:S(2)}) collective-permute-start(f32[192,512]{1,0:T(8,128)S(1)} %add.39.own.refs_4_), channel_id=1, source_target_pairs={{0,8},{4,12},{8,0},{12,4},{16,24},{20,28},{24,16},{28,20},{1,9},{5... | collective-permute-start | bytes 1179656 | tf_op jit(solution)/shard_map/ppermute | solution.py:199
  86.9 26.5 %collective-permute-start.24 = (f32[192,512]{1,0:T(8,128)S(1)}, f32[192,512]{1,0:T(8,128)S(1)}, u32[]{:S(2)}, u32[]{:S(2)}) collective-permute-start(f32[192,512]{1,0:T(8,128)S(1)} %add.39.own.refs_4_), channel_id=1, source_target_pairs={{0,12},{4,8},{8,4},{12,0},{16,28},{20,24},{24,20},{28,16},{1,13},{... | collective-permute-start | bytes 1179656 | tf_op jit(solution)/shard_map/ppermute | solution.py:199
  115.7 11.6 %collective-permute-start.25 = (f32[200,512]{1,0:T(8,128)S(1)}, f32[200,512]{1,0:T(8,128)S(1)}, u32[]{:S(2)}, u32[]{:S(2)}) collective-permute-start(f32[200,512]{1,0:T(8,128)S(1)} %norms.1.refs_8_), channel_id=1, source_target_pairs={{0,4},{4,0},{8,12},{12,8},{16,20},{20,16},{24,28},{28,24},{1,5},{5... | collective-permute-start | bytes 1228808 | tf_op jit(solution)/shard_map/ppermute | solution.py:199
  117.2 12.3 %collective-permute-start.26 = (f32[200,512]{1,0:T(8,128)S(1)}, f32[200,512]{1,0:T(8,128)S(1)}, u32[]{:S(2)}, u32[]{:S(2)}) collective-permute-start(f32[200,512]{1,0:T(8,128)S(1)} %norms.1.refs_8_), channel_id=1, source_target_pairs={{0,8},{4,12},{8,0},{12,4},{16,24},{20,28},{24,16},{28,20},{1,9},{5... | collective-permute-start | bytes 1228808 | tf_op jit(solution)/shard_map/ppermute | solution.py:199
  117.2 20.0 %collective-permute-start.27 = (f32[200,512]{1,0:T(8,128)S(1)}, f32[200,512]{1,0:T(8,128)S(1)}, u32[]{:S(2)}, u32[]{:S(2)}) collective-permute-start(f32[200,512]{1,0:T(8,128)S(1)} %norms.1.refs_8_), channel_id=1, source_target_pairs={{0,12},{4,8},{8,4},{12,0},{16,28},{20,24},{24,20},{28,16},{1,13},{... | collective-permute-start | bytes 1228808 | tf_op jit(solution)/shard_map/ppermute | solution.py:199
  138.4 6.1 %collective-permute-start.29 = (f32[1,512]{1,0:T(1,128)S(1)}, f32[1,512]{1,0:T(1,128)S(1)}, u32[]{:S(2)}, u32[]{:S(2)}) collective-permute-start(f32[1,512]{1,0:T(1,128)S(1)} %add.45), channel_id=1, source_target_pairs={{0,2},{1,3},{2,0},{3,1},{4,6},{5,7},{6,4},{7,5},{8,10},{9,11},{10,... | collective-permute-start | bytes 6152 | tf_op jit(solution)/shard_map/ppermute | solution.py:199
  (9 other events, 12.6 us)

commit v4 on v3

--- a/solution.py
+++ b/solution.py
@@ -26,20 +26,36 @@
 anywhere = pl.BlockSpec(memory_space=pl.ANY)
 
 
-def kernel(body, out_shape, in_specs, scratch, name):
+def kernel(body, out_shape, in_specs, scratch, name, cost=0):
     return pl.pallas_call(
         body,
         out_shape=out_shape,
         in_specs=in_specs,
         scratch_shapes=scratch,
         compiler_params=pltpu.CompilerParams(vmem_limit_bytes=32 * 2**20),
-        cost_estimate=pl.CostEstimate(flops=0, bytes_accessed=0, transcendentals=0),
+        cost_estimate=pl.CostEstimate(flops=0, bytes_accessed=cost, transcendentals=0),
         name=name,
     )
 
 
 def shape(*dims, dtype=jnp.float32):
     return jax.ShapeDtypeStruct(dims, dtype)
+
+
+def split(value):
+    high = value.astype(jnp.bfloat16)
+    return high, (value - high.astype(jnp.float32)).astype(jnp.bfloat16)
+
+
+def dot_three(a, b):
+    a_high, a_low = split(a)
+    b_high, b_low = split(b)
+    return lax.dot_general(
+        jnp.concatenate([a_high, a_high, a_low], axis=1),
+        jnp.concatenate([b_high, b_low, b_high], axis=1),
+        (((1,), (1,)), ((), ())),
+        preferred_element_type=jnp.float32,
+    )
 
 
 def factor_block(block):
@@ -153,20 +169,20 @@
     )(bits, *shares)
 
 
-def later_kernel(b, before, out, work, block):
+def later_kernel(b, before, token, out, work, block):
     work[...] = before[...]
     factor_step(b, work, out, block)
 
 
-def later_step(b, work):
+def later_step(b, work, token):
     size = work.shape[0]
     return kernel(
         functools.partial(later_kernel, b),
         [shape(lanes, size), shape(size, size)],
-        [vmem],
+        [vmem, anywhere],
         [pltpu.VMEM((lanes, lanes), jnp.float32)],
         "factor_later",
-    )(work)
+    )(work, token)
 
 
 def share_norms(right_rows):
@@ -251,7 +267,7 @@
         out[pl.ds(pl.multiple_of((bits[2] ^ k) * share, 8), share), :] = refs[k][...]
 
 
-def raw_kernel(bits, *refs):
+def raw_kernel(bits, token, *refs):
     mine, others, columns = refs[:square], refs[square : 2 * square], refs[2 * square : 3 * square]
     sent, kept, left, right, raw = refs[3 * square :]
     rows = columns[0].shape[0]
@@ -278,46 +294,72 @@
 
 
 def norm_kernel(own, received, inverse, *refs):
-    out = refs[-1]
+    own_right, out = refs[-2:]
     count = own.shape[0]
-    total = jnp.zeros((1, own.shape[1]), jnp.float32)
-    for part in (own, received):
-        right = dot(part[...], inverse[...], ((1,), (1,)))
-        total = total + jnp.sum(right * right, axis=0, keepdims=True)
-    out[:count, :] = received[...]
+    own_right[...] = dot(own[...], inverse[...], ((1,), (1,)))
+    right = dot(received[...], inverse[...], ((1,), (1,)))
+    out[:count, :] = right
+    total = jnp.sum(right * right, axis=0, keepdims=True)
+    total = total + jnp.sum(own_right[...] * own_right[...], axis=0, keepdims=True)
     row = lax.broadcasted_iota(jnp.int32, (8, own.shape[1]), 0)
     out[count:, :] = jnp.where(row == 0, total, 0.0)
 
 
-def momentum_kernel(bits, left, inverse, *refs):
-    pieces, own, received = refs[:square], refs[square : 2 * square], refs[2 * square : 3 * square]
-    new_momentum, raw, plane = refs[3 * square :]
-    rows, width = pieces[0].shape
-    half = own[0].shape[0]
-    plane[...] = dot(left[...], inverse[...])
+def own_kernel(left, inverse, own_right, *refs):
+    rows, (rights, products) = refs[:-2], refs[-2:]
+    count = own_right.shape[0]
     for k in range(square):
-        first = (bits[2] ^ k) * width
-        new_momentum[:, pl.ds(pl.multiple_of(first, lanes), width)] = pieces[k][...]
-        at = pl.multiple_of(first + bits[4] * half, 8)
-        raw[pl.ds(at, half), :] = own[k][...]
-        at = pl.multiple_of(first + (1 - bits[4]) * half, 8)
-        raw[pl.ds(at, half), :] = received[k][:half, :]
-    cols, chunk = raw.shape
-    for first in range(0, cols, chunk):
-        at = slice(first, min(first + chunk, cols))
-        new_momentum[:, at] = new_momentum[:, at] - 0.5 * dot(plane[...], raw[at, :], ((1,), (1,)))
-
-
-def update_kernel(factor, bits, squares, left, inverse, raw, update, next_basis, plane):
-    column_norm = jnp.sqrt(squares[...] + epsilon)
-    plane[...] = dot(left[...] * (factor / column_norm), inverse[...])
-    cols, chunk = raw.shape
-    for first in range(0, cols, chunk):
-        at = slice(first, min(first + chunk, cols))
-        update[:, at] = dot(plane[...], raw[at, :], ((1,), (1,))).astype(jnp.bfloat16)
+        if k == 0:
+            right = own_right[...]
+        else:
+            right = dot(rows[k - 1][...], inverse[...], ((1,), (1,)))
+        rights[k * count : (k + 1) * count, :] = right
+    for k in range(square):
+        products[k] = dot_three(left[...], rights[k * count : (k + 1) * count, :])
+
+
+def momentum_kernel(bits, left, products, *refs):
+    pieces, received = refs[:square], refs[square : 2 * square]
+    new_momentum = refs[-1]
+    width = pieces[0].shape[1]
+    half = width // 2
+    for k in range(square):
+        at = pl.ds(pl.multiple_of((bits[2] ^ k) * width, lanes), width)
+        other = dot_three(left[...], received[k][:half, :])
+        lower = jnp.concatenate([products[k], other], axis=1)
+        upper = jnp.concatenate([other, products[k]], axis=1)
+        new_momentum[:, at] = pieces[k][...] - 0.5 * jnp.where(bits[4] == 0, lower, upper)
+
+
+def squares_kernel(row, *refs):
+    total = refs[0][row : row + 1, :]
+    for part in refs[1:square]:
+        total = total + part[row : row + 1, :]
+    refs[-1][...] = total
+
+
+def update_kernel(factor, bits, squares, left, rights, *refs):
+    received, (update, next_basis, right) = refs[:square], refs[square:]
+    rows = left.shape[0]
+    cols = update.shape[1]
+    width = cols // square
+    half = width // 2
+    inverse_norm = 1.0 / jnp.sqrt(squares[...] + epsilon)
+    for k in range(square):
+        at = pl.multiple_of(k * width + bits[4] * half, 8)
+        right[pl.ds(at, half), :] = rights[k * half : (k + 1) * half, :]
+        at = pl.multiple_of(k * width + (1 - bits[4]) * half, 8)
+        right[pl.ds(at, half), :] = received[k][:half, :]
+    scaled = left[...] * (factor * inverse_norm)
+    for k in range(0, square, 2):
+        both = dot_three(scaled, right[k * width : (k + 2) * width, :]).astype(jnp.bfloat16)
+        for i in range(2):
+            at = pl.ds(pl.multiple_of((bits[2] ^ (k + i)) * width, lanes), width)
+            update[:, at] = both[:, i * width : (i + 1) * width]
     count = next_basis.shape[0]
-    own = raw[pl.ds(pl.multiple_of(bits[3] * count, 8), count), :]
-    next_basis[...] = dot(own, inverse[...], ((1,), (1,))) / column_norm
+    place = ((bits[3] // 2) ^ bits[2]) * width + (bits[3] % 2) * half
+    own = right[pl.ds(pl.multiple_of(place, 8), count), :]
+    next_basis[...] = own / jnp.sqrt(squares[...] + epsilon)
 
 
 def in_squares(momentum, gradient, right_basis):
@@ -348,30 +390,30 @@
     gathered = [mine] + [swap(mine, "fsdp", k) for k in range(1, square)]
     others = [swap(part, "tensor", 1) for part in gathered]
 
+    count = rank // lanes
+    stacked = count * (count + 1) // 2 * lanes
+    share = stacked // (4 * square)
+    gram_sent, gram_kept = kernel(
+        gram_kernel,
+        [shape(share, lanes)] * 2,
+        [smem] + [vmem] * square,
+        [pltpu.VMEM((square * half, rank), jnp.float32), pltpu.VMEM((stacked, lanes), jnp.float32)],
+        "part_gram",
+    )(bits, *gathered)
+    part = gram_kept + swap(gram_sent, "tensor", 1)
+
     sent, kept = kernel(
         raw_kernel,
         [shape(width // 2, rank)] * 2,
-        [smem] + [vmem] * (3 * square),
+        [smem, anywhere] + [vmem] * (3 * square),
         [
             pltpu.VMEM((square * rows, width), jnp.float32),
             pltpu.VMEM((square * rows, rank), jnp.float32),
             pltpu.VMEM((width, rank), jnp.float32),
         ],
         "part_raw",
-    )(bits, *gathered, *others, *columns)
-    own = kept + swap(sent, "fsdp", square)
-
-    count = rank // lanes
-    stacked = count * (count + 1) // 2 * lanes
-    share = stacked // (4 * square)
-    sent, kept = kernel(
-        gram_kernel,
-        [shape(share, lanes)] * 2,
-        [smem] + [vmem] * square,
-        [pltpu.VMEM((square * half, rank), jnp.float32), pltpu.VMEM((stacked, lanes), jnp.float32)],
-        "part_gram",
-    )(bits, *gathered)
-    part = kept + swap(sent, "tensor", 1)
+    )(bits, part, *gathered, *others, *columns)
+
     part = part + swap(part, "fsdp", square)
     quarter = kernel(
         order_kernel, shape(square * share, lanes), [smem] + [vmem] * square, [], "order"
@@ -382,8 +424,12 @@
     factors = []
     out, work = first_step(bits, shares, rank)
     factors.append(out)
+    token = out
     for b in range(1, count):
-        out, work = later_step(b, work)
+        if b == (count + 1) // 2:
+            own = add_after(kept, swap(sent, "fsdp", square), out)
+            token = own
+        out, work = later_step(b, work, token)
         factors.append(out)
     left, left_scaled, inverse = kernel(
         functools.partial(left_kernel, math.sqrt(total_rows)),
@@ -395,32 +441,47 @@
 
     received = swap(own, "fsdp", square)
     own_rows = [own] + [swap(own, "fsdp", k) for k in range(1, square)]
-    with_norms = kernel(
+    own_right, with_norms = kernel(
         norm_kernel,
-        shape(width // 2 + 8, rank),
+        [shape(width // 2, rank), shape(width // 2 + 8, rank)],
         [vmem] * 3 + [anywhere] * (square - 1),
         [],
         "norms",
     )(own, received, inverse, *own_rows[1:])
     received_rows = [with_norms] + [swap(with_norms, "fsdp", k) for k in range(1, square)]
-    squares = sum(part[width // 2 : width // 2 + 1] for part in received_rows)
+    rights, products = kernel(
+        own_kernel,
+        [shape(square * (width // 2), rank), shape(square, rows, width // 2)],
+        [vmem] * (2 + square),
+        [],
+        "own_part",
+        cost=2**24,
+    )(left, inverse, own_right, *own_rows[1:])
+    squares = kernel(
+        functools.partial(squares_kernel, width // 2),
+        shape(1, rank),
+        [vmem] * square + [anywhere],
+        [],
+        "squares",
+    )(*received_rows, products)
     squares = squares + swap(squares, "tensor", 1)
     squares = squares + swap(squares, "tensor", 2)
 
-    new_momentum, raw = kernel(
+    new_momentum = kernel(
         momentum_kernel,
-        [shape(rows, cols), shape(cols, rank)],
-        [smem] + [vmem] * (2 + 3 * square),
-        [pltpu.VMEM((rows, rank), jnp.float32)],
+        shape(rows, cols),
+        [smem] + [vmem] * (2 + 2 * square),
+        [],
         "new_momentum",
-    )(bits, left, inverse, *pieces, *own_rows, *received_rows)
+        cost=2**22,
+    )(bits, left, products, *pieces, *received_rows)
     update, next_basis = kernel(
         functools.partial(update_kernel, math.sqrt(total_rows / total_cols)),
         [shape(rows, cols, dtype=jnp.bfloat16), shape(cols // lax.axis_size("fsdp"), rank)],
-        [smem] + [vmem] * 4,
-        [pltpu.VMEM((rows, rank), jnp.float32)],
+        [smem] + [vmem] * (3 + square),
+        [pltpu.VMEM((cols, rank), jnp.float32)],
         "update",
-    )(bits, squares, left, inverse, raw)
+    )(bits, squares, left, rights, *received_rows)
     return (update, new_momentum, left_scaled, next_basis)
 
 

time: 151 us -> 146 us (0.967)
  waiting for transfers between devices: 68.4 us -> 60.6 us
  starting transfers between devices: 29.5 us -> 34.7 us
  Pallas kernels: 47.2 us -> 45.6 us
    ppermute x30, waiting for transfers between devices: 68.4 us -> 60.6 us  [swap(): lax.ppermute(value, axis, [(i, i ^ flip) for i in range(lax.axis_size(axi...]
    ppermute x30, starting transfers between devices: 29.5 us -> 34.7 us  [swap(): lax.ppermute(value, axis, [(i, i ^ flip) for i in range(lax.axis_size(axi...]
    pallas_call x1, Pallas kernels: 6.05 us -> 3.13 us  [in_squares(): kernel(functools.partial(update_kernel, math.sqrt(total_rows / total_cols...]
    pallas_call x3 -> x5, Pallas kernels: 11.2 us -> 12.5 us  [the longest x1 4.04 us: in_squares(): kernel(own_kernel, [shape(square * (width // 2), rank), shape(square, row...]
  transfers between devices with their start and end apart: 30 -> 30, of which waited for: 19 -> 17; matrix products, arithmetic and copies ran while one was open for 0% -> 0% of each run, Pallas kernels for 20% -> 24%
where the time goes in v4:
time: 146 us
  waiting for transfers between devices  60.6 us (42%)
  Pallas kernels  45.6 us (31%)
  starting transfers between devices  34.7 us (24%)
  local copies, waits for them, and re-layouts  4.46 us (3%)
    ppermute x30, waiting for transfers between devices, swap(): lax.ppermute(value, axis, [(i, i ^ flip) for i in range(lax.axis_size(axi...  60.6 us
    ppermute x30, starting transfers between devices, swap(): lax.ppermute(value, axis, [(i, i ^ flip) for i in range(lax.axis_size(axi...  34.7 us
    pallas_call x3, Pallas kernels, later_step(): kernel(functools.partial(later_kernel, b), [shape(lanes, size), shape(siz...  14 us
    pallas_call x1, Pallas kernels, first_step(): kernel(first_kernel, [shape(lanes, size), shape(size, size)], [smem] + [v...  5.24 us
    unnamed x6, local copies, waits for them, and re-layouts  4.37 us
    pallas_call x1, Pallas kernels, in_squares(): kernel(own_kernel, [shape(square * (width // 2), rank), shape(square, row...  4.04 us
    pallas_call x1, Pallas kernels, in_squares(): kernel(part_left_kernel, [shape(half, rank)] * 2, [smem] + [vmem] * (1 +...  3.94 us
    pallas_call x1, Pallas kernels, in_squares(): kernel(raw_kernel, [shape(width // 2, rank)] * 2, [smem, anywhere] + [vme...  3.4 us
  transfers between devices with their start and end apart: 30, of which 17 were waited for; matrix products, arithmetic and copies ran while one was open for 0% of the time, Pallas kernels for 24%

profile of v4, /device:TPU:0, one launch (start us, length us, event | category | flops | bytes accessed | tf_op | source)
XLA Modules:
  0.0 146.2 jit_solution(18278118174583953490)
XLA Ops:
  5.8 3.9 %part_left.1 = (f32[120,512]{1,0:T(8,128)S(1)}, f32[120,512]{1,0:T(8,128)S(1)}) custom-call(s32[5]{0:T(128)S(1)} %stack.23.bits, f32[1536,512]{1,0:T(8,128)S(1)} %copy-done, f32[240,384]{1,0:T(8,128)S(1)} %get-tuple-element.30.refs_0_.refs_8_, f32[240,384]{1,0:T(8,128)S(1)} %get-tuple-element.31.refs_1_, f32[240,384]{1,0:T(8,128)S(1)} %get-tuple-element.32.refs_2_, ...), custom_call_target="tpu_custom_call" | custom-call | tf_op jit(solution)/shard_map/part_left/pallas_call | solution.py:381
  16.5 5.5 %collective-permute-done.2.refs_2_.refs_9_ = f32[240,384]{1,0:T(8,128)S(1)} collective-permute-done((f32[240,384]{1,0:T(8,128)S(1)}, f32[240,384]{1,0:T(8,128)S(1)}, u32[]{:S(2)}, u32[]{:S(2)}) %collective-permute-start.2) | collective-permute-done | bytes 368672 | tf_op jit(solution)/shard_map/ppermute | solution.py:215
  24.3 6.9 %collective-permute-done.4.refs_4_.refs_11_ = f32[240,384]{1,0:T(8,128)S(1)} collective-permute-done((f32[240,384]{1,0:T(8,128)S(1)}, f32[240,384]{1,0:T(8,128)S(1)}, u32[]{:S(2)}, u32[]{:S(2)}) %collective-permute-start.4) | collective-permute-done | bytes 368672 | tf_op jit(solution)/shard_map/ppermute | solution.py:215
  31.3 2.7 %collective-permute-start.7 = (f32[120,512]{1,0:T(8,128)S(1)}, f32[120,512]{1,0:T(8,128)S(1)}, u32[]{:S(2)}, u32[]{:S(2)}) collective-permute-start(f32[120,512]{1,0:T(8,128)S(1)} %add_after.2.refs_0_.mine), channel_id=1, source_target_pairs={{0,12},{4,8},{8,4},{12,0},{16,28},{20,24},{24,20},{28,16},{1,13},{... | collective-permute-start | bytes 737288 | tf_op jit(solution)/shard_map/ppermute | solution.py:215
  34.8 6.3 %collective-permute-done.7.refs_3_ = f32[120,512]{1,0:T(8,128)S(1)} collective-permute-done((f32[120,512]{1,0:T(8,128)S(1)}, f32[120,512]{1,0:T(8,128)S(1)}, u32[]{:S(2)}, u32[]{:S(2)}) %collective-permute-start.7) | collective-permute-done | bytes 245792 | tf_op jit(solution)/shard_map/ppermute | solution.py:215
  41.2 3.8 %collective-permute-done.6.refs_2_ = f32[120,512]{1,0:T(8,128)S(1)} collective-permute-done((f32[120,512]{1,0:T(8,128)S(1)}, f32[120,512]{1,0:T(8,128)S(1)}, u32[]{:S(2)}, u32[]{:S(2)}) %collective-permute-start.6) | collective-permute-done | bytes 245792 | tf_op jit(solution)/shard_map/ppermute | solution.py:215
  45.5 3.0 %part_gram.1 = (f32[80,128]{1,0:T(8,128)S(1)}, f32[80,128]{1,0:T(8,128)S(1)}) custom-call(s32[5]{0:T(128)S(1)} %stack.23.bits, f32[120,512]{1,0:T(8,128)S(1)} %add_after.2.refs_0_.mine, f32[120,512]{1,0:T(8,128)S(1)} %collective-permute-done.5.refs_1_, f32[120,512]{1,0:T(8,128)S(1)} %collective-permute-done.6.refs_2_, ...), custom_call_target="tpu_custom_call" | custom-call | tf_op jit(solution)/shard_map/part_gram/pallas_call | solution.py:396
  49.7 2.6 %collective-permute-start.14 = (f32[80,128]{1,0:T(8,128)S(1)}, f32[80,128]{1,0:T(8,128)S(1)}, u32[]{:S(2)}, u32[]{:S(2)}) collective-permute-start(f32[80,128]{1,0:T(8,128)S(1)} %add.27.token), channel_id=1, source_target_pairs={{0,16},{4,20},{8,24},{12,28},{16,0},{20,4},{24,8},{28,12},{1,17},{... | collective-permute-start | bytes 122888 | tf_op jit(solution)/shard_map/ppermute | solution.py:215
  52.3 3.4 %part_raw.1 = (f32[192,512]{1,0:T(8,128)S(1)}, f32[192,512]{1,0:T(8,128)S(1)}) custom-call(s32[5]{0:T(128)S(1)} %stack.23.bits, f32[80,128]{1,0:T(8,128)S(1)} %add.27.token, f32[120,512]{1,0:T(8,128)S(1)} %add_after.2.refs_0_.mine, f32[120,512]{1,0:T(8,128)S(1)} %collective-permute-done.5.refs_1_, f32[120,512]{1,0:T(8,128)S(1)} %collective-permute-done.6.refs_2_, ...), custom_call_target="tpu_custom_call" | custom-call | tf_op jit(solution)/shard_map/part_raw/pallas_call | solution.py:405
  59.7 6.2 %collective-permute-done.17.refs_3_ = f32[80,128]{1,0:T(8,128)S(1)} collective-permute-done((f32[80,128]{1,0:T(8,128)S(1)}, f32[80,128]{1,0:T(8,128)S(1)}, u32[]{:S(2)}, u32[]{:S(2)}) %collective-permute-start.17) | collective-permute-done | bytes 40992 | tf_op jit(solution)/shard_map/ppermute | solution.py:215
  68.5 3.8 %collective-permute-done.19.c = f32[320,128]{1,0:T(8,128)S(1)} collective-permute-done((f32[320,128]{1,0:T(8,128)S(1)}, f32[320,128]{1,0:T(8,128)S(1)}, u32[]{:S(2)}, u32[]{:S(2)}) %collective-permute-start.19) | collective-permute-done | bytes 163872 | tf_op jit(solution)/shard_map/ppermute | solution.py:215
  73.7 5.2 %factor_first.1 = (f32[128,512]{1,0:T(8,128)S(1)}, f32[512,512]{1,0:T(8,128)S(1)}) custom-call(s32[5]{0:T(128)S(1)} %stack.23.bits, f32[320,128]{1,0:T(8,128)S(1)} %order.1.a, f32[320,128]{1,0:T(8,128)S(1)} %collective-permute-done.18.b, f32[320,128]{1,0:T(8,128)S(1)} %collective-permute-done.19.c, f32[320,128]{1,0:T(8,128)S(1)} %collective-permute-done.20.d), custom_call_target="tpu_custom_call" | custom-call | tf_op jit(solution)/shard_map/factor_first/pallas_call | solution.py:163
  79.0 4.6 %factor_later.3 = (f32[128,512]{1,0:T(8,128)S(1)}, f32[512,512]{1,0:T(8,128)S(1)}) custom-call(f32[512,512]{1,0:T(8,128)S(1)} %get-tuple-element.40.before, f32[128,512]{1,0:T(8,128)S(1)} %get-tuple-element.41.token.refs_0_), custom_call_target="tpu_custom_call" | custom-call | tf_op jit(solution)/shard_map/factor_later/pallas_call | solution.py:179
  83.6 3.3 %collective-permute-start.24 = (f32[192,512]{1,0:T(8,128)S(1)}, f32[192,512]{1,0:T(8,128)S(1)}, u32[]{:S(2)}, u32[]{:S(2)}) collective-permute-start(f32[192,512]{1,0:T(8,128)S(1)} %add_after.3.token.own), channel_id=1, source_target_pairs={{0,12},{4,8},{8,4},{12,0},{16,28},{20,24},{24,20},{28,16},{1,13},{... | collective-permute-start | bytes 1179656 | tf_op jit(solution)/shard_map/ppermute | solution.py:215
  87.9 4.2 %collective-permute-start.21 = (f32[192,512]{1,0:T(8,128)S(1)}, f32[192,512]{1,0:T(8,128)S(1)}, u32[]{:S(2)}, u32[]{:S(2)}) collective-permute-start(f32[192,512]{1,0:T(8,128)S(1)} %add_after.3.token.own), channel_id=1, source_target_pairs={{0,16},{4,20},{8,24},{12,28},{16,0},{20,4},{24,8},{28,12},{1,17},{... | collective-permute-start | bytes 1179656 | tf_op jit(solution)/shard_map/ppermute | solution.py:215
  92.0 4.3 %factor_later.4 = (f32[128,512]{1,0:T(8,128)S(1)}, f32[512,512]{1,0:T(8,128)S(1)}) custom-call(f32[512,512]{1,0:T(8,128)S(1)} %get-tuple-element.43.before, f32[192,512]{1,0:T(8,128)S(1)} %add_after.3.token.own), custom_call_target="tpu_custom_call" | custom-call | tf_op jit(solution)/shard_map/factor_later/pallas_call | solution.py:179
  96.3 5.2 %factor_later.5 = (f32[128,512]{1,0:T(8,128)S(1)}, f32[512,512]{1,0:T(8,128)}) custom-call(f32[512,512]{1,0:T(8,128)S(1)} %get-tuple-element.45.before, f32[192,512]{1,0:T(8,128)S(1)} %add_after.3.token.own), custom_call_target="tpu_custom_call" | custom-call | tf_op jit(solution)/shard_map/factor_later/pallas_call | solution.py:179
  105.2 7.5 %collective-permute-done.23.refs_1_ = f32[192,512]{1,0:T(8,128)S(1)} collective-permute-done((f32[192,512]{1,0:T(8,128)S(1)}, f32[192,512]{1,0:T(8,128)S(1)}, u32[]{:S(2)}, u32[]{:S(2)}) %collective-permute-start.23) | collective-permute-done | bytes 393248 | tf_op jit(solution)/shard_map/ppermute | solution.py:215
  114.9 4.8 %collective-permute-start.27 = (f32[200,512]{1,0:T(8,128)S(1)}, f32[200,512]{1,0:T(8,128)S(1)}, u32[]{:S(2)}, u32[]{:S(2)}) collective-permute-start(f32[200,512]{1,0:T(8,128)S(1)} %get-tuple-element.48.refs_0_.refs_4_), channel_id=1, source_target_pairs={{0,12},{4,8},{8,4},{12,0},{16,28},{20,24},{24,20},{28,16},{1,13},{... | collective-permute-start | bytes 1228808 | tf_op jit(solution)/shard_map/ppermute | solution.py:215
  120.8 4.0 %own_part.1 = (f32[768,512]{1,0:T(8,128)S(1)}, f32[4,240,192]{2,1,0:T(8,128)S(1)}) custom-call(f32[240,512]{1,0:T(8,128)S(1)} %get-tuple-element.49.left, f32[512,512]{1,0:T(8,128)S(1)} %get-tuple-element.47.inverse, f32[192,512]{1,0:T(8,128)S(1)} %get-tuple-element.50.own_right, f32[192,512]{1,0:T(8,128)S(1)} %collective-permute-done.22.refs_0_, ...), custom_call_target="tpu_custom_call" | custom-call | bytes 16777216 | tf_op jit(solution)/shard_map/own_part/pallas_call | solution.py:452
  124.8 5.4 %collective-permute-done.27.refs_3_.refs_7_ = f32[200,512]{1,0:T(8,128)S(1)} collective-permute-done((f32[200,512]{1,0:T(8,128)S(1)}, f32[200,512]{1,0:T(8,128)S(1)}, u32[]{:S(2)}, u32[]{:S(2)}) %collective-permute-start.27) | collective-permute-done | bytes 409632 | tf_op jit(solution)/shard_map/ppermute | solution.py:215
  130.2 6.9 %collective-permute-done.26.refs_2_.refs_6_ = f32[200,512]{1,0:T(8,128)S(1)} collective-permute-done((f32[200,512]{1,0:T(8,128)S(1)}, f32[200,512]{1,0:T(8,128)S(1)}, u32[]{:S(2)}, u32[]{:S(2)}) %collective-permute-start.26) | collective-permute-done | bytes 409632 | tf_op jit(solution)/shard_map/ppermute | solution.py:215
  140.2 2.9 %new_momentum.1 = f32[240,1536]{1,0:T(8,128)} custom-call(s32[5]{0:T(128)S(1)} %stack.23.bits, f32[240,512]{1,0:T(8,128)S(1)} %get-tuple-element.49.left, f32[4,240,192]{2,1,0:T(8,128)S(1)} %get-tuple-element.51.refs_4_.products, f32[240,384]{1,0:T(8,128)S(1)} %get-tuple-element.30.refs_0_.refs_8_, f32[240,384]{1,0:T(8,128)S(1)} %get-tuple-element.31.refs_1_, ...), custom_call_target="tpu_custom_call" | custom-call | bytes 4194304 | tf_op jit(solution)/shard_map/new_momentum/pallas_call | solution.py:470
  143.1 3.1 %update.1 = (bf16[240,1536]{1,0:T(8,128)(2,1)}, f32[192,512]{1,0:T(8,128)}) custom-call(s32[5]{0:T(128)S(1)} %stack.23.bits, f32[1,512]{1,0:T(1,128)S(1)} %add.30.squares, f32[240,512]{1,0:T(8,128)S(1)} %get-tuple-element.49.left, f32[768,512]{1,0:T(8,128)S(1)} %get-tuple-element.52.rights, f32[200,512]{1,0:T(8,128)S(1)} %get-tuple-element.48.refs_0_.refs_4_, ...), custom_call_target="tpu_custom_call" | custom-call | tf_op jit(solution)/shard_map/update/pallas_call | solution.py:478
  (65 shorter events, 35.8 us)
Async XLA Ops:
  10.3 11.7 %collective-permute-start.2 = (f32[240,384]{1,0:T(8,128)S(1)}, f32[240,384]{1,0:T(8,128)S(1)}, u32[]{:S(2)}, u32[]{:S(2)}) collective-permute-start(f32[240,384]{1,0:T(8,128)S(1)} %get-tuple-element.31.refs_1_), channel_id=1, source_target_pairs={{0,4},{4,0},{8,12},{12,8},{16,20},{20,16},{24,28},{28,24},{1,5},{5... | collective-permute-start | bytes 1105928 | tf_op jit(solution)/shard_map/ppermute | solution.py:215
  12.9 11.4 %collective-permute-start.3 = (f32[240,384]{1,0:T(8,128)S(1)}, f32[240,384]{1,0:T(8,128)S(1)}, u32[]{:S(2)}, u32[]{:S(2)}) collective-permute-start(f32[240,384]{1,0:T(8,128)S(1)} %get-tuple-element.32.refs_2_), channel_id=1, source_target_pairs={{0,8},{4,12},{8,0},{12,4},{16,24},{20,28},{24,16},{28,20},{1,9},{5... | collective-permute-start | bytes 1105928 | tf_op jit(solution)/shard_map/ppermute | solution.py:215
  14.5 16.8 %collective-permute-start.4 = (f32[240,384]{1,0:T(8,128)S(1)}, f32[240,384]{1,0:T(8,128)S(1)}, u32[]{:S(2)}, u32[]{:S(2)}) collective-permute-start(f32[240,384]{1,0:T(8,128)S(1)} %get-tuple-element.33.refs_3_), channel_id=1, source_target_pairs={{0,12},{4,8},{8,4},{12,0},{16,28},{20,24},{24,20},{28,16},{1,13},{... | collective-permute-start | bytes 1105928 | tf_op jit(solution)/shard_map/ppermute | solution.py:215
  14.5 16.7 %collective-permute-start.1 = (f32[120,512]{1,0:T(8,128)S(1)}, f32[120,512]{1,0:T(8,128)S(1)}, u32[]{:S(2)}, u32[]{:S(2)}) collective-permute-start(f32[120,512]{1,0:T(8,128)S(1)} %add.26.refs_0_), channel_id=1, source_target_pairs={{0,2},{1,3},{2,0},{3,1},{4,6},{5,7},{6,4},{7,5},{8,10},{9,11},{10,... | collective-permute-start | bytes 737288 | tf_op jit(solution)/shard_map/ppermute | solution.py:215
  31.3 9.9 %collective-permute-start.7 = (f32[120,512]{1,0:T(8,128)S(1)}, f32[120,512]{1,0:T(8,128)S(1)}, u32[]{:S(2)}, u32[]{:S(2)}) collective-permute-start(f32[120,512]{1,0:T(8,128)S(1)} %add_after.2.refs_0_.mine), channel_id=1, source_target_pairs={{0,12},{4,8},{8,4},{12,0},{16,28},{20,24},{24,20},{28,16},{1,13},{... | collective-permute-start | bytes 737288 | tf_op jit(solution)/shard_map/ppermute | solution.py:215
  34.0 10.9 %collective-permute-start.6 = (f32[120,512]{1,0:T(8,128)S(1)}, f32[120,512]{1,0:T(8,128)S(1)}, u32[]{:S(2)}, u32[]{:S(2)}) collective-permute-start(f32[120,512]{1,0:T(8,128)S(1)} %add_after.2.refs_0_.mine), channel_id=1, source_target_pairs={{0,8},{4,12},{8,0},{12,4},{16,24},{20,28},{24,16},{28,20},{1,9},{5... | collective-permute-start | bytes 737288 | tf_op jit(solution)/shard_map/ppermute | solution.py:215
  34.5 10.6 %collective-permute-start.5 = (f32[120,512]{1,0:T(8,128)S(1)}, f32[120,512]{1,0:T(8,128)S(1)}, u32[]{:S(2)}, u32[]{:S(2)}) collective-permute-start(f32[120,512]{1,0:T(8,128)S(1)} %add_after.2.refs_0_.mine), channel_id=1, source_target_pairs={{0,4},{4,0},{8,12},{12,8},{16,20},{20,16},{24,28},{28,24},{1,5},{5... | collective-permute-start | bytes 737288 | tf_op jit(solution)/shard_map/ppermute | solution.py:215
  34.8 17.5 %collective-permute-start.9 = (f32[120,512]{1,0:T(8,128)S(1)}, f32[120,512]{1,0:T(8,128)S(1)}, u32[]{:S(2)}, u32[]{:S(2)}) collective-permute-start(f32[120,512]{1,0:T(8,128)S(1)} %add_after.2.refs_0_.mine), channel_id=1, source_target_pairs={{0,1},{1,0},{2,3},{3,2},{4,5},{5,4},{6,7},{7,6},{8,9},{9,8},{10,11... | collective-permute-start | bytes 737288 | tf_op jit(solution)/shard_map/ppermute | solution.py:215
  41.1 11.2 %collective-permute-start.12 = (f32[120,512]{1,0:T(8,128)S(1)}, f32[120,512]{1,0:T(8,128)S(1)}, u32[]{:S(2)}, u32[]{:S(2)}) collective-permute-start(f32[120,512]{1,0:T(8,128)S(1)} %collective-permute-done.7.refs_3_), channel_id=1, source_target_pairs={{0,1},{1,0},{2,3},{3,2},{4,5},{5,4},{6,7},{7,6},{8,9},{9,8},{10,11... | collective-permute-start | bytes 737288 | tf_op jit(solution)/shard_map/ppermute | solution.py:215
  44.9 7.4 %collective-permute-start.11 = (f32[120,512]{1,0:T(8,128)S(1)}, f32[120,512]{1,0:T(8,128)S(1)}, u32[]{:S(2)}, u32[]{:S(2)}) collective-permute-start(f32[120,512]{1,0:T(8,128)S(1)} %collective-permute-done.6.refs_2_), channel_id=1, source_target_pairs={{0,1},{1,0},{2,3},{3,2},{4,5},{5,4},{6,7},{7,6},{8,9},{9,8},{10,11... | collective-permute-start | bytes 737288 | tf_op jit(solution)/shard_map/ppermute | solution.py:215
  45.0 7.3 %collective-permute-start.10 = (f32[120,512]{1,0:T(8,128)S(1)}, f32[120,512]{1,0:T(8,128)S(1)}, u32[]{:S(2)}, u32[]{:S(2)}) collective-permute-start(f32[120,512]{1,0:T(8,128)S(1)} %collective-permute-done.5.refs_1_), channel_id=1, source_target_pairs={{0,1},{1,0},{2,3},{3,2},{4,5},{5,4},{6,7},{7,6},{8,9},{9,8},{10,11... | collective-permute-start | bytes 737288 | tf_op jit(solution)/shard_map/ppermute | solution.py:215
  49.7 6.4 %collective-permute-start.14 = (f32[80,128]{1,0:T(8,128)S(1)}, f32[80,128]{1,0:T(8,128)S(1)}, u32[]{:S(2)}, u32[]{:S(2)}) collective-permute-start(f32[80,128]{1,0:T(8,128)S(1)} %add.27.token), channel_id=1, source_target_pairs={{0,16},{4,20},{8,24},{12,28},{16,0},{20,4},{24,8},{28,12},{1,17},{... | collective-permute-start | bytes 122888 | tf_op jit(solution)/shard_map/ppermute | solution.py:215
  55.8 27.8 %collective-permute-start.13 = (f32[192,512]{1,0:T(8,128)S(1)}, f32[192,512]{1,0:T(8,128)S(1)}, u32[]{:S(2)}, u32[]{:S(2)}) collective-permute-start(f32[192,512]{1,0:T(8,128)S(1)} %get-tuple-element.39), channel_id=1, source_target_pairs={{0,16},{4,20},{8,24},{12,28},{16,0},{20,4},{24,8},{28,12},{1,17},{... | collective-permute-start | bytes 1179656 | tf_op jit(solution)/shard_map/ppermute | solution.py:215
  56.2 9.8 %collective-permute-start.17 = (f32[80,128]{1,0:T(8,128)S(1)}, f32[80,128]{1,0:T(8,128)S(1)}, u32[]{:S(2)}, u32[]{:S(2)}) collective-permute-start(f32[80,128]{1,0:T(8,128)S(1)} %add.28.refs_0_), channel_id=1, source_target_pairs={{0,12},{4,8},{8,4},{12,0},{16,28},{20,24},{24,20},{28,16},{1,13},{... | collective-permute-start | bytes 122888 | tf_op jit(solution)/shard_map/ppermute | solution.py:215
  58.3 8.1 %collective-permute-start.16 = (f32[80,128]{1,0:T(8,128)S(1)}, f32[80,128]{1,0:T(8,128)S(1)}, u32[]{:S(2)}, u32[]{:S(2)}) collective-permute-start(f32[80,128]{1,0:T(8,128)S(1)} %add.28.refs_0_), channel_id=1, source_target_pairs={{0,8},{4,12},{8,0},{12,4},{16,24},{20,28},{24,16},{28,20},{1,9},{5... | collective-permute-start | bytes 122888 | tf_op jit(solution)/shard_map/ppermute | solution.py:215
  58.8 7.6 %collective-permute-start.15 = (f32[80,128]{1,0:T(8,128)S(1)}, f32[80,128]{1,0:T(8,128)S(1)}, u32[]{:S(2)}, u32[]{:S(2)}) collective-permute-start(f32[80,128]{1,0:T(8,128)S(1)} %add.28.refs_0_), channel_id=1, source_target_pairs={{0,4},{4,0},{8,12},{12,8},{16,20},{20,16},{24,28},{28,24},{1,5},{5... | collective-permute-start | bytes 122888 | tf_op jit(solution)/shard_map/ppermute | solution.py:215
  66.9 5.4 %collective-permute-start.19 = (f32[320,128]{1,0:T(8,128)S(1)}, f32[320,128]{1,0:T(8,128)S(1)}, u32[]{:S(2)}, u32[]{:S(2)}) collective-permute-start(f32[320,128]{1,0:T(8,128)S(1)} %order.1.a), channel_id=1, source_target_pairs={{0,2},{1,3},{2,0},{3,1},{4,6},{5,7},{6,4},{7,5},{8,10},{9,11},{10,... | collective-permute-start | bytes 491528 | tf_op jit(solution)/shard_map/ppermute | solution.py:215
  83.6 21.6 %collective-permute-start.24 = (f32[192,512]{1,0:T(8,128)S(1)}, f32[192,512]{1,0:T(8,128)S(1)}, u32[]{:S(2)}, u32[]{:S(2)}) collective-permute-start(f32[192,512]{1,0:T(8,128)S(1)} %add_after.3.token.own), channel_id=1, source_target_pairs={{0,12},{4,8},{8,4},{12,0},{16,28},{20,24},{24,20},{28,16},{1,13},{... | collective-permute-start | bytes 1179656 | tf_op jit(solution)/shard_map/ppermute | solution.py:215
  86.9 25.9 %collective-permute-start.23 = (f32[192,512]{1,0:T(8,128)S(1)}, f32[192,512]{1,0:T(8,128)S(1)}, u32[]{:S(2)}, u32[]{:S(2)}) collective-permute-start(f32[192,512]{1,0:T(8,128)S(1)} %add_after.3.token.own), channel_id=1, source_target_pairs={{0,8},{4,12},{8,0},{12,4},{16,24},{20,28},{24,16},{28,20},{1,9},{5... | collective-permute-start | bytes 1179656 | tf_op jit(solution)/shard_map/ppermute | solution.py:215
  86.9 25.9 %collective-permute-start.22 = (f32[192,512]{1,0:T(8,128)S(1)}, f32[192,512]{1,0:T(8,128)S(1)}, u32[]{:S(2)}, u32[]{:S(2)}) collective-permute-start(f32[192,512]{1,0:T(8,128)S(1)} %add_after.3.token.own), channel_id=1, source_target_pairs={{0,4},{4,0},{8,12},{12,8},{16,20},{20,16},{24,28},{28,24},{1,5},{5... | collective-permute-start | bytes 1179656 | tf_op jit(solution)/shard_map/ppermute | solution.py:215
  87.9 24.9 %collective-permute-start.21 = (f32[192,512]{1,0:T(8,128)S(1)}, f32[192,512]{1,0:T(8,128)S(1)}, u32[]{:S(2)}, u32[]{:S(2)}) collective-permute-start(f32[192,512]{1,0:T(8,128)S(1)} %add_after.3.token.own), channel_id=1, source_target_pairs={{0,16},{4,20},{8,24},{12,28},{16,0},{20,4},{24,8},{28,12},{1,17},{... | collective-permute-start | bytes 1179656 | tf_op jit(solution)/shard_map/ppermute | solution.py:215
  114.9 15.2 %collective-permute-start.27 = (f32[200,512]{1,0:T(8,128)S(1)}, f32[200,512]{1,0:T(8,128)S(1)}, u32[]{:S(2)}, u32[]{:S(2)}) collective-permute-start(f32[200,512]{1,0:T(8,128)S(1)} %get-tuple-element.48.refs_0_.refs_4_), channel_id=1, source_target_pairs={{0,12},{4,8},{8,4},{12,0},{16,28},{20,24},{24,20},{28,16},{1,13},{... | collective-permute-start | bytes 1228808 | tf_op jit(solution)/shard_map/ppermute | solution.py:215
  119.8 17.3 %collective-permute-start.26 = (f32[200,512]{1,0:T(8,128)S(1)}, f32[200,512]{1,0:T(8,128)S(1)}, u32[]{:S(2)}, u32[]{:S(2)}) collective-permute-start(f32[200,512]{1,0:T(8,128)S(1)} %get-tuple-element.48.refs_0_.refs_4_), channel_id=1, source_target_pairs={{0,8},{4,12},{8,0},{12,4},{16,24},{20,28},{24,16},{28,20},{1,9},{5... | collective-permute-start | bytes 1228808 | tf_op jit(solution)/shard_map/ppermute | solution.py:215
  119.8 17.7 %collective-permute-start.25 = (f32[200,512]{1,0:T(8,128)S(1)}, f32[200,512]{1,0:T(8,128)S(1)}, u32[]{:S(2)}, u32[]{:S(2)}) collective-permute-start(f32[200,512]{1,0:T(8,128)S(1)} %get-tuple-element.48.refs_0_.refs_4_), channel_id=1, source_target_pairs={{0,4},{4,0},{8,12},{12,8},{16,20},{20,16},{24,28},{28,24},{1,5},{5... | collective-permute-start | bytes 1228808 | tf_op jit(solution)/shard_map/ppermute | solution.py:215
  (9 other events, 21.1 us)

commit v5 on v4

--- a/solution.py
+++ b/solution.py
@@ -47,15 +47,18 @@
     return high, (value - high.astype(jnp.float32)).astype(jnp.bfloat16)
 
 
+def three_left(value):
+    high, low = split(value)
+    return jnp.concatenate([high, high, low], axis=1)
+
+
+def three_right(value):
+    high, low = split(value)
+    return jnp.concatenate([high, low, high], axis=1)
+
+
 def dot_three(a, b):
-    a_high, a_low = split(a)
-    b_high, b_low = split(b)
-    return lax.dot_general(
-        jnp.concatenate([a_high, a_high, a_low], axis=1),
-        jnp.concatenate([b_high, b_low, b_high], axis=1),
-        (((1,), (1,)), ((), ())),
-        preferred_element_type=jnp.float32,
-    )
+    return lax.dot_general(a, b, (((1,), (1,)), ((), ())), preferred_element_type=jnp.float32)
 
 
 def factor_block(block):
@@ -234,6 +237,11 @@
     kept[...] = total[pl.ds(pl.multiple_of(bits[0] * half, 8), half), :]
 
 
+def core_add_kernel(bits, kept, both, out):
+    half = kept.shape[0]
+    out[...] = kept[...] + both[pl.ds(pl.multiple_of((1 - bits[0]) * half, 8), half), :]
+
+
 def add_kernel(*refs):
     refs[-1][...] = refs[0][...] + refs[1][...]
 
@@ -251,20 +259,22 @@
     for k, part in enumerate(parts):
         rows[k * half : (k + 1) * half, :] = part[...]
     at = 0
-    for first in range(0, rank, lanes):
-        left, right = rows[:, first:], rows[:, first : first + lanes]
-        stack[at : at + rank - first, :] = dot(left, right, ((0,), (0,)))
-        at += rank - first
+    for first in range(0, rank, 2 * lanes):
+        last = min(first + 2 * lanes, rank)
+        product = dot(rows[:, first:], rows[:, first:last], ((0,), (0,)))
+        for j in range(0, last - first, lanes):
+            stack[at : at + rank - first - j, :] = product[j:, j : j + lanes]
+            at += rank - first - j
     for out, core in ((kept, bits[0]), (sent, 1 - bits[0])):
-        index = (2 * bits[1] + core) * square + bits[2]
+        index = (2 * bits[1] + core) * 2 + bits[2] % 2
         out[...] = stack[pl.ds(pl.multiple_of(index * share, 8), share), :]
 
 
 def order_kernel(bits, *refs):
     out = refs[-1]
     share = refs[0].shape[0]
-    for k in range(square):
-        out[pl.ds(pl.multiple_of((bits[2] ^ k) * share, 8), share), :] = refs[k][...]
+    for k in range(2):
+        out[pl.ds(pl.multiple_of((bits[2] % 2 ^ k) * share, 8), share), :] = refs[k][...]
 
 
 def raw_kernel(bits, token, *refs):
@@ -306,26 +316,29 @@
 
 
 def own_kernel(left, inverse, own_right, *refs):
-    rows, (rights, products) = refs[:-2], refs[-2:]
+    rows, (rights, splits, products) = refs[:-3], refs[-3:]
     count = own_right.shape[0]
+    rights[:count, :] = own_right[...]
+    for k in range(1, square):
+        right = dot(rows[k - 1][...], inverse[...], ((1,), (1,)))
+        rights[k * count : (k + 1) * count, :] = right
+    splits[...] = three_right(rights[...])
+    product = dot_three(three_left(left[...]), splits[...])
     for k in range(square):
-        if k == 0:
-            right = own_right[...]
-        else:
-            right = dot(rows[k - 1][...], inverse[...], ((1,), (1,)))
-        rights[k * count : (k + 1) * count, :] = right
-    for k in range(square):
-        products[k] = dot_three(left[...], rights[k * count : (k + 1) * count, :])
+        products[k] = product[:, k * count : (k + 1) * count]
 
 
 def momentum_kernel(bits, left, products, *refs):
     pieces, received = refs[:square], refs[square : 2 * square]
-    new_momentum = refs[-1]
+    new_momentum, splits = refs[-2:]
     width = pieces[0].shape[1]
     half = width // 2
     for k in range(square):
+        splits[k * half : (k + 1) * half, :] = three_right(received[k][:half, :])
+    product = dot_three(three_left(left[...]), splits[...])
+    for k in range(square):
         at = pl.ds(pl.multiple_of((bits[2] ^ k) * width, lanes), width)
-        other = dot_three(left[...], received[k][:half, :])
+        other = product[:, k * half : (k + 1) * half]
         lower = jnp.concatenate([products[k], other], axis=1)
         upper = jnp.concatenate([other, products[k]], axis=1)
         new_momentum[:, at] = pieces[k][...] - 0.5 * jnp.where(bits[4] == 0, lower, upper)
@@ -338,28 +351,27 @@
     refs[-1][...] = total
 
 
-def update_kernel(factor, bits, squares, left, rights, *refs):
-    received, (update, next_basis, right) = refs[:square], refs[square:]
-    rows = left.shape[0]
-    cols = update.shape[1]
-    width = cols // square
-    half = width // 2
-    inverse_norm = 1.0 / jnp.sqrt(squares[...] + epsilon)
+def update_kernel(factor, bits, squares, left, rights, own_splits, splits, *refs):
+    received, (update, next_basis) = refs[:square], refs[square:]
+    half = next_basis.shape[0]
+    width = 2 * half
+    norm = jnp.sqrt(squares[...] + epsilon)
+    scaled = three_left(left[...] * (factor / norm))
+    mine = dot_three(scaled, own_splits[...])
+    other = dot_three(scaled, splits[...])
     for k in range(square):
-        at = pl.multiple_of(k * width + bits[4] * half, 8)
-        right[pl.ds(at, half), :] = rights[k * half : (k + 1) * half, :]
-        at = pl.multiple_of(k * width + (1 - bits[4]) * half, 8)
-        right[pl.ds(at, half), :] = received[k][:half, :]
-    scaled = left[...] * (factor * inverse_norm)
-    for k in range(0, square, 2):
-        both = dot_three(scaled, right[k * width : (k + 2) * width, :]).astype(jnp.bfloat16)
-        for i in range(2):
-            at = pl.ds(pl.multiple_of((bits[2] ^ (k + i)) * width, lanes), width)
-            update[:, at] = both[:, i * width : (i + 1) * width]
-    count = next_basis.shape[0]
-    place = ((bits[3] // 2) ^ bits[2]) * width + (bits[3] % 2) * half
-    own = right[pl.ds(pl.multiple_of(place, 8), count), :]
-    next_basis[...] = own / jnp.sqrt(squares[...] + epsilon)
+        at = pl.ds(pl.multiple_of((bits[2] ^ k) * width, lanes), width)
+        parts = slice(k * half, (k + 1) * half)
+        lower = jnp.concatenate([mine[:, parts], other[:, parts]], axis=1)
+        upper = jnp.concatenate([other[:, parts], mine[:, parts]], axis=1)
+        update[:, at] = jnp.where(bits[4] == 0, lower, upper).astype(jnp.bfloat16)
+    for k in range(square):
+
+        @pl.when((bits[3] // 2) ^ bits[2] == k)
+        def _():
+            mine_rows = rights[k * half : (k + 1) * half, :]
+            rows = jnp.where(bits[3] % 2 == bits[4], mine_rows, received[k][:half, :])
+            next_basis[...] = rows / norm
 
 
 def in_squares(momentum, gradient, right_basis):
@@ -385,14 +397,18 @@
         [pltpu.VMEM((rows, rank), jnp.float32)],
         "part_left",
     )(bits, right_basis, *pieces)
-    mine = kept + swap(sent, "tensor", 1)
+    cores = [[i, i + 1] for i in range(0, lax.axis_size("tensor"), 2)]
+    both = lax.all_gather(sent, "tensor", axis=0, tiled=True, axis_index_groups=cores)
+    mine = kernel(core_add_kernel, shape(half, rank), [smem, vmem, vmem], [], "core_add")(
+        bits, kept, both
+    )
     mine = add_after(mine, swap(mine, "tensor", 2), *columns[1:])
     gathered = [mine] + [swap(mine, "fsdp", k) for k in range(1, square)]
     others = [swap(part, "tensor", 1) for part in gathered]
 
     count = rank // lanes
     stacked = count * (count + 1) // 2 * lanes
-    share = stacked // (4 * square)
+    share = stacked // 8
     gram_sent, gram_kept = kernel(
         gram_kernel,
         [shape(share, lanes)] * 2,
@@ -414,10 +430,10 @@
         "part_raw",
     )(bits, part, *gathered, *others, *columns)
 
-    part = part + swap(part, "fsdp", square)
+    part = add_after(part, swap(part, "fsdp", square), kept)
     quarter = kernel(
-        order_kernel, shape(square * share, lanes), [smem] + [vmem] * square, [], "order"
-    )(bits, part, *[swap(part, "fsdp", k) for k in range(1, square)])
+        order_kernel, shape(2 * share, lanes), [smem] + [vmem] * 2, [], "order"
+    )(bits, part, swap(part, "fsdp", 1))
     over_planes = swap(quarter, "tensor", 2)
     shares = [quarter, swap(quarter, "tensor", 1), over_planes, swap(over_planes, "tensor", 1)]
 
@@ -449,9 +465,13 @@
         "norms",
     )(own, received, inverse, *own_rows[1:])
     received_rows = [with_norms] + [swap(with_norms, "fsdp", k) for k in range(1, square)]
-    rights, products = kernel(
+    rights, own_splits, products = kernel(
         own_kernel,
-        [shape(square * (width // 2), rank), shape(square, rows, width // 2)],
+        [
+            shape(cols // 2, rank),
+            shape(cols // 2, 3 * rank, dtype=jnp.bfloat16),
+            shape(square, rows, width // 2),
+        ],
         [vmem] * (2 + square),
         [],
         "own_part",
@@ -467,9 +487,9 @@
     squares = squares + swap(squares, "tensor", 1)
     squares = squares + swap(squares, "tensor", 2)
 
-    new_momentum = kernel(
+    new_momentum, splits = kernel(
         momentum_kernel,
-        shape(rows, cols),
+        [shape(rows, cols), shape(cols // 2, 3 * rank, dtype=jnp.bfloat16)],
         [smem] + [vmem] * (2 + 2 * square),
         [],
         "new_momentum",
@@ -478,10 +498,10 @@
     update, next_basis = kernel(
         functools.partial(update_kernel, math.sqrt(total_rows / total_cols)),
         [shape(rows, cols, dtype=jnp.bfloat16), shape(cols // lax.axis_size("fsdp"), rank)],
-        [smem] + [vmem] * (3 + square),
-        [pltpu.VMEM((cols, rank), jnp.float32)],
+        [smem] + [vmem] * (5 + square),
+        [],
         "update",
-    )(bits, squares, left, rights, *received_rows)
+    )(bits, squares, left, rights, own_splits, splits, *received_rows)
     return (update, new_momentum, left_scaled, next_basis)
 
 

time: 146 us -> 136 us (0.932)
  starting transfers between devices: 34.7 us -> 27.2 us
  waiting for transfers between devices: 60.6 us -> 54.9 us
  blocking collectives: 0 us -> 2.34 us
    ppermute x30 -> x27, starting transfers between devices: 34.7 us -> 27.2 us  [swap(): lax.ppermute(value, axis, [(i, i ^ flip) for i in range(lax.axis_size(axi...]
    ppermute x30 -> x27, waiting for transfers between devices: 60.6 us -> 54.9 us  [swap(): lax.ppermute(value, axis, [(i, i ^ flip) for i in range(lax.axis_size(axi...]
    all_gather x0 -> x1, blocking collectives: none -> 2.34 us  [in_squares(): lax.all_gather(sent, 'tensor', axis=0, tiled=True, axis_index_groups=cores)]
    pallas_call x3 -> x4, Pallas kernels: 7.5 us -> 8.43 us  [the longest x1 4.35 us: in_squares(): kernel(own_kernel, [shape(cols // 2, rank), shape(cols // 2, 3 * rank, dt...]
  transfers between devices with their start and end apart: 30 -> 27, of which waited for: 17 -> 16; matrix products, arithmetic and copies ran while one was open for 0% -> 0% of each run, Pallas kernels for 24% -> 29%
where the time goes in v5:
time: 136 us; the launch traced here: 135 us
  waiting for transfers between devices  54.9 us (40%)
  Pallas kernels  45.6 us (34%)
  starting transfers between devices  27.2 us (20%)
  local copies, waits for them, and re-layouts  4.46 us (3%)
  blocking collectives  2.34 us (2%)
    ppermute x27, waiting for transfers between devices, swap(): lax.ppermute(value, axis, [(i, i ^ flip) for i in range(lax.axis_size(axi...  54.9 us
    ppermute x27, starting transfers between devices, swap(): lax.ppermute(value, axis, [(i, i ^ flip) for i in range(lax.axis_size(axi...  27.2 us
    pallas_call x3, Pallas kernels, later_step(): kernel(functools.partial(later_kernel, b), [shape(lanes, size), shape(siz...  14 us
    pallas_call x1, Pallas kernels, first_step(): kernel(first_kernel, [shape(lanes, size), shape(size, size)], [smem] + [v...  5.06 us
    unnamed x6, local copies, waits for them, and re-layouts  4.38 us
    pallas_call x1, Pallas kernels, in_squares(): kernel(own_kernel, [shape(cols // 2, rank), shape(cols // 2, 3 * rank, dt...  4.35 us
    pallas_call x1, Pallas kernels, in_squares(): kernel(part_left_kernel, [shape(half, rank)] * 2, [smem] + [vmem] * (1 +...  3.94 us
    pallas_call x1, Pallas kernels, in_squares(): kernel(raw_kernel, [shape(width // 2, rank)] * 2, [smem, anywhere] + [vme...  3.42 us
  transfers between devices with their start and end apart: 27, of which 16 were waited for; matrix products, arithmetic and copies ran while one was open for 0% of the time, Pallas kernels for 29%

profile of v5, /device:TPU:0, one launch (start us, length us, event | category | flops | bytes accessed | tf_op | source)
XLA Modules:
  0.0 135.3 jit_solution(18111871822956257418)
XLA Ops:
  3.9 3.0 %collective-permute-start.1 = (f32[240,384]{1,0:T(8,128)S(1)}, f32[240,384]{1,0:T(8,128)S(1)}, u32[]{:S(2)}, u32[]{:S(2)}) collective-permute-start(f32[240,384]{1,0:T(8,128)S(1)} %get-tuple-element.34.refs_1_), channel_id=1, source_target_pairs={{0,4},{4,0},{8,12},{12,8},{16,20},{20,16},{24,28},{28,24},{1,5},{5... | collective-permute-start | bytes 1105928 | tf_op jit(solution)/shard_map/ppermute | solution.py:218
  10.4 3.9 %part_left.1 = (f32[120,512]{1,0:T(8,128)S(1)}, f32[120,512]{1,0:T(8,128)S(1)}) custom-call(s32[5]{0:T(128)S(1)} %stack.23.bits, f32[1536,512]{1,0:T(8,128)S(1)} %copy-done, f32[240,384]{1,0:T(8,128)S(1)} %get-tuple-element.33.refs_0_.refs_8_, f32[240,384]{1,0:T(8,128)S(1)} %get-tuple-element.34.refs_1_, f32[240,384]{1,0:T(8,128)S(1)} %get-tuple-element.35.refs_2_, ...), custom_call_target="tpu_custom_call" | custom-call | tf_op jit(solution)/shard_map/part_left/pallas_call | solution.py:393
  14.4 2.3 %all_gather.3.both = f32[240,512]{1,0:T(8,128)S(1)} all-gather(f32[120,512]{1,0:T(8,128)S(1)} %get-tuple-element.38), channel_id=1, replica_groups={{0,1},{2,3},{4,5},{6,7},{8,9},{10,11},{12,13},{14,15},{16,17},{18,19},{..., dimensions={0}, use_global_device_ids=true | all-gather | bytes 737280 | tf_op jit(solution)/shard_map/all_gather | solution.py:401
  19.3 6.3 %collective-permute-done.refs_1_ = f32[120,512]{1,0:T(8,128)S(1)} collective-permute-done((f32[120,512]{1,0:T(8,128)S(1)}, f32[120,512]{1,0:T(8,128)S(1)}, u32[]{:S(2)}, u32[]{:S(2)}) %collective-permute-start) | collective-permute-done | bytes 245792 | tf_op jit(solution)/shard_map/ppermute | solution.py:218
  29.2 5.4 %collective-permute-done.5.refs_2_ = f32[120,512]{1,0:T(8,128)S(1)} collective-permute-done((f32[120,512]{1,0:T(8,128)S(1)}, f32[120,512]{1,0:T(8,128)S(1)}, u32[]{:S(2)}, u32[]{:S(2)}) %collective-permute-start.5) | collective-permute-done | bytes 245792 | tf_op jit(solution)/shard_map/ppermute | solution.py:218
  34.6 4.8 %collective-permute-done.6.refs_3_ = f32[120,512]{1,0:T(8,128)S(1)} collective-permute-done((f32[120,512]{1,0:T(8,128)S(1)}, f32[120,512]{1,0:T(8,128)S(1)}, u32[]{:S(2)}, u32[]{:S(2)}) %collective-permute-start.6) | collective-permute-done | bytes 245792 | tf_op jit(solution)/shard_map/ppermute | solution.py:218
  44.3 2.7 %collective-permute-start.13 = (f32[160,128]{1,0:T(8,128)S(1)}, f32[160,128]{1,0:T(8,128)S(1)}, u32[]{:S(2)}, u32[]{:S(2)}) collective-permute-start(f32[160,128]{1,0:T(8,128)S(1)} %add.20.token.refs_0_), channel_id=1, source_target_pairs={{0,16},{4,20},{8,24},{12,28},{16,0},{20,4},{24,8},{28,12},{1,17},{... | collective-permute-start | bytes 245768 | tf_op jit(solution)/shard_map/ppermute | solution.py:218
  47.0 3.4 %part_raw.1 = (f32[192,512]{1,0:T(8,128)S(1)}, f32[192,512]{1,0:T(8,128)S(1)}) custom-call(s32[5]{0:T(128)S(1)} %stack.23.bits, f32[160,128]{1,0:T(8,128)S(1)} %add.20.token.refs_0_, f32[120,512]{1,0:T(8,128)S(1)} %add_after.3.refs_0_.mine, f32[120,512]{1,0:T(8,128)S(1)} %collective-permute-done.4.refs_1_, f32[120,512]{1,0:T(8,128)S(1)} %collective-permute-done.5.refs_2_, ...), custom_call_target="tpu_custom_call" | custom-call | tf_op jit(solution)/shard_map/part_raw/pallas_call | solution.py:421
  53.3 3.0 %collective-permute-done.14.refs_1_ = f32[160,128]{1,0:T(8,128)S(1)} collective-permute-done((f32[160,128]{1,0:T(8,128)S(1)}, f32[160,128]{1,0:T(8,128)S(1)}, u32[]{:S(2)}, u32[]{:S(2)}) %collective-permute-start.14) | collective-permute-done | bytes 81952 | tf_op jit(solution)/shard_map/ppermute | solution.py:218
  58.4 3.8 %collective-permute-done.16.c = f32[320,128]{1,0:T(8,128)S(1)} collective-permute-done((f32[320,128]{1,0:T(8,128)S(1)}, f32[320,128]{1,0:T(8,128)S(1)}, u32[]{:S(2)}, u32[]{:S(2)}) %collective-permute-start.16) | collective-permute-done | bytes 163872 | tf_op jit(solution)/shard_map/ppermute | solution.py:218
  63.6 5.1 %factor_first.1 = (f32[128,512]{1,0:T(8,128)S(1)}, f32[512,512]{1,0:T(8,128)S(1)}) custom-call(s32[5]{0:T(128)S(1)} %stack.23.bits, f32[320,128]{1,0:T(8,128)S(1)} %order.1.a, f32[320,128]{1,0:T(8,128)S(1)} %collective-permute-done.15.b, f32[320,128]{1,0:T(8,128)S(1)} %collective-permute-done.16.c, f32[320,128]{1,0:T(8,128)S(1)} %collective-permute-done.17.d), custom_call_target="tpu_custom_call" | custom-call | tf_op jit(solution)/shard_map/factor_first/pallas_call | solution.py:166
  68.7 4.8 %factor_later.3 = (f32[128,512]{1,0:T(8,128)S(1)}, f32[512,512]{1,0:T(8,128)S(1)}) custom-call(f32[512,512]{1,0:T(8,128)S(1)} %get-tuple-element.43.before, f32[128,512]{1,0:T(8,128)S(1)} %get-tuple-element.44.token.refs_0_), custom_call_target="tpu_custom_call" | custom-call | tf_op jit(solution)/shard_map/factor_later/pallas_call | solution.py:182
  75.0 3.1 %collective-permute-start.20 = (f32[192,512]{1,0:T(8,128)S(1)}, f32[192,512]{1,0:T(8,128)S(1)}, u32[]{:S(2)}, u32[]{:S(2)}) collective-permute-start(f32[192,512]{1,0:T(8,128)S(1)} %add_after.5.token.own), channel_id=1, source_target_pairs={{0,8},{4,12},{8,0},{12,4},{16,24},{20,28},{24,16},{28,20},{1,9},{5... | collective-permute-start | bytes 1179656 | tf_op jit(solution)/shard_map/ppermute | solution.py:218
  79.1 4.3 %factor_later.4 = (f32[128,512]{1,0:T(8,128)S(1)}, f32[512,512]{1,0:T(8,128)S(1)}) custom-call(f32[512,512]{1,0:T(8,128)S(1)} %get-tuple-element.46.before, f32[192,512]{1,0:T(8,128)S(1)} %add_after.5.token.own), custom_call_target="tpu_custom_call" | custom-call | tf_op jit(solution)/shard_map/factor_later/pallas_call | solution.py:182
  83.4 5.0 %factor_later.5 = (f32[128,512]{1,0:T(8,128)S(1)}, f32[512,512]{1,0:T(8,128)}) custom-call(f32[512,512]{1,0:T(8,128)S(1)} %get-tuple-element.48.before, f32[192,512]{1,0:T(8,128)S(1)} %add_after.5.token.own), custom_call_target="tpu_custom_call" | custom-call | tf_op jit(solution)/shard_map/factor_later/pallas_call | solution.py:182
  88.3 2.4 %left.1 = (f32[240,512]{1,0:T(8,128)S(1)}, f32[240,512]{1,0:T(8,128)}, f32[512,512]{1,0:T(8,128)S(1)}) custom-call(s32[5]{0:T(128)S(1)} %stack.23.bits, f32[120,512]{1,0:T(8,128)S(1)} %add_after.3.refs_0_.mine, f32[120,512]{1,0:T(8,128)S(1)} %collective-permute-done.8.refs_4_.other, f32[128,512]{1,0:T(8,128)S(1)} %get-tuple-element.44.token.refs_0_, ...), custom_call_target="tpu_custom_call" | custom-call | tf_op jit(solution)/shard_map/left/pallas_call | solution.py:450
  90.8 3.4 %collective-permute-done.18.received = f32[192,512]{1,0:T(8,128)S(1)} collective-permute-done((f32[192,512]{1,0:T(8,128)S(1)}, f32[192,512]{1,0:T(8,128)S(1)}, u32[]{:S(2)}, u32[]{:S(2)}) %collective-permute-start.18) | collective-permute-done | bytes 393248 | tf_op jit(solution)/shard_map/ppermute | solution.py:218
  95.6 8.2 %collective-permute-done.21.refs_2_ = f32[192,512]{1,0:T(8,128)S(1)} collective-permute-done((f32[192,512]{1,0:T(8,128)S(1)}, f32[192,512]{1,0:T(8,128)S(1)}, u32[]{:S(2)}, u32[]{:S(2)}) %collective-permute-start.21) | collective-permute-done | bytes 393248 | tf_op jit(solution)/shard_map/ppermute | solution.py:218
  106.7 2.9 %collective-permute-start.24 = (f32[200,512]{1,0:T(8,128)S(1)}, f32[200,512]{1,0:T(8,128)S(1)}, u32[]{:S(2)}, u32[]{:S(2)}) collective-permute-start(f32[200,512]{1,0:T(8,128)S(1)} %get-tuple-element.51.refs_0_.refs_4_), channel_id=1, source_target_pairs={{0,12},{4,8},{8,4},{12,0},{16,28},{20,24},{24,20},{28,16},{1,13},{... | collective-permute-start | bytes 1228808 | tf_op jit(solution)/shard_map/ppermute | solution.py:218
  109.6 4.3 %own_part.1 = (f32[768,512]{1,0:T(8,128)S(1)}, bf16[768,1536]{1,0:T(8,128)(2,1)S(1)}, f32[4,240,192]{2,1,0:T(8,128)S(1)}) custom-call(f32[240,512]{1,0:T(8,128)S(1)} %get-tuple-element.52.left, f32[512,512]{1,0:T(8,128)S(1)} %get-tuple-element.50.inverse, f32[192,512]{1,0:T(8,128)S(1)} %get-tuple-element.53.own_right, ...), custom_call_target="tpu_custom_call" | custom-call | bytes 16777216 | tf_op jit(solution)/shard_map/own_part/pallas_call | solution.py:468
  114.0 3.7 %collective-permute-done.22.refs_1_.refs_5_ = f32[200,512]{1,0:T(8,128)S(1)} collective-permute-done((f32[200,512]{1,0:T(8,128)S(1)}, f32[200,512]{1,0:T(8,128)S(1)}, u32[]{:S(2)}, u32[]{:S(2)}) %collective-permute-start.22) | collective-permute-done | bytes 409632 | tf_op jit(solution)/shard_map/ppermute | solution.py:218
  119.1 7.4 %collective-permute-done.24.refs_3_.refs_7_ = f32[200,512]{1,0:T(8,128)S(1)} collective-permute-done((f32[200,512]{1,0:T(8,128)S(1)}, f32[200,512]{1,0:T(8,128)S(1)}, u32[]{:S(2)}, u32[]{:S(2)}) %collective-permute-start.24) | collective-permute-done | bytes 409632 | tf_op jit(solution)/shard_map/ppermute | solution.py:218
  129.1 3.0 %new_momentum.1 = (f32[240,1536]{1,0:T(8,128)}, bf16[768,1536]{1,0:T(8,128)(2,1)S(1)}) custom-call(s32[5]{0:T(128)S(1)} %stack.23.bits, f32[240,512]{1,0:T(8,128)S(1)} %get-tuple-element.52.left, f32[4,240,192]{2,1,0:T(8,128)S(1)} %get-tuple-element.54.refs_4_.products, f32[240,384]{1,0:T(8,128)S(1)} %get-tuple-element.33.refs_0_.refs_8_, ...), custom_call_target="tpu_custom_call" | custom-call | bytes 4194304 | tf_op jit(solution)/shard_map/new_momentum/pallas_call | solution.py:490
  132.1 3.2 %update.1 = (bf16[240,1536]{1,0:T(8,128)(2,1)}, f32[192,512]{1,0:T(8,128)}) custom-call(s32[5]{0:T(128)S(1)} %stack.23.bits, f32[1,512]{1,0:T(1,128)S(1)} %add.22.squares, f32[240,512]{1,0:T(8,128)S(1)} %get-tuple-element.52.left, f32[768,512]{1,0:T(8,128)S(1)} %get-tuple-element.55.rights, bf16[768,1536]{1,0:T(8,128)(2,1)S(1)} %get-tuple-element.56.own_splits, ...), custom_call_target="tpu_custom_call" | custom-call | tf_op jit(solution)/shard_map/update/pallas_call | solution.py:498
  (60 shorter events, 35.2 us)
Async XLA Ops:
  3.9 21.6 %collective-permute-start.1 = (f32[240,384]{1,0:T(8,128)S(1)}, f32[240,384]{1,0:T(8,128)S(1)}, u32[]{:S(2)}, u32[]{:S(2)}) collective-permute-start(f32[240,384]{1,0:T(8,128)S(1)} %get-tuple-element.34.refs_1_), channel_id=1, source_target_pairs={{0,4},{4,0},{8,12},{12,8},{16,20},{20,16},{24,28},{28,24},{1,5},{5... | collective-permute-start | bytes 1105928 | tf_op jit(solution)/shard_map/ppermute | solution.py:218
  7.0 18.6 %collective-permute-start.2 = (f32[240,384]{1,0:T(8,128)S(1)}, f32[240,384]{1,0:T(8,128)S(1)}, u32[]{:S(2)}, u32[]{:S(2)}) collective-permute-start(f32[240,384]{1,0:T(8,128)S(1)} %get-tuple-element.35.refs_2_), channel_id=1, source_target_pairs={{0,8},{4,12},{8,0},{12,4},{16,24},{20,28},{24,16},{28,20},{1,9},{5... | collective-permute-start | bytes 1105928 | tf_op jit(solution)/shard_map/ppermute | solution.py:218
  8.5 17.0 %collective-permute-start.3 = (f32[240,384]{1,0:T(8,128)S(1)}, f32[240,384]{1,0:T(8,128)S(1)}, u32[]{:S(2)}, u32[]{:S(2)}) collective-permute-start(f32[240,384]{1,0:T(8,128)S(1)} %get-tuple-element.36.refs_3_), channel_id=1, source_target_pairs={{0,12},{4,8},{8,4},{12,0},{16,28},{20,24},{24,20},{28,16},{1,13},{... | collective-permute-start | bytes 1105928 | tf_op jit(solution)/shard_map/ppermute | solution.py:218
  17.3 8.3 %collective-permute-start = (f32[120,512]{1,0:T(8,128)S(1)}, f32[120,512]{1,0:T(8,128)S(1)}, u32[]{:S(2)}, u32[]{:S(2)}) collective-permute-start(f32[120,512]{1,0:T(8,128)S(1)} %core_add.1.refs_0_), channel_id=1, source_target_pairs={{0,2},{1,3},{2,0},{3,1},{4,6},{5,7},{6,4},{7,5},{8,10},{9,11},{10,... | collective-permute-start | bytes 737288 | tf_op jit(solution)/shard_map/ppermute | solution.py:218
  25.6 9.0 %collective-permute-start.5 = (f32[120,512]{1,0:T(8,128)S(1)}, f32[120,512]{1,0:T(8,128)S(1)}, u32[]{:S(2)}, u32[]{:S(2)}) collective-permute-start(f32[120,512]{1,0:T(8,128)S(1)} %add_after.3.refs_0_.mine), channel_id=1, source_target_pairs={{0,8},{4,12},{8,0},{12,4},{16,24},{20,28},{24,16},{28,20},{1,9},{5... | collective-permute-start | bytes 737288 | tf_op jit(solution)/shard_map/ppermute | solution.py:218
  27.5 11.9 %collective-permute-start.6 = (f32[120,512]{1,0:T(8,128)S(1)}, f32[120,512]{1,0:T(8,128)S(1)}, u32[]{:S(2)}, u32[]{:S(2)}) collective-permute-start(f32[120,512]{1,0:T(8,128)S(1)} %add_after.3.refs_0_.mine), channel_id=1, source_target_pairs={{0,12},{4,8},{8,4},{12,0},{16,28},{20,24},{24,20},{28,16},{1,13},{... | collective-permute-start | bytes 737288 | tf_op jit(solution)/shard_map/ppermute | solution.py:218
  28.8 11.9 %collective-permute-start.4 = (f32[120,512]{1,0:T(8,128)S(1)}, f32[120,512]{1,0:T(8,128)S(1)}, u32[]{:S(2)}, u32[]{:S(2)}) collective-permute-start(f32[120,512]{1,0:T(8,128)S(1)} %add_after.3.refs_0_.mine), channel_id=1, source_target_pairs={{0,4},{4,0},{8,12},{12,8},{16,20},{20,16},{24,28},{28,24},{1,5},{5... | collective-permute-start | bytes 737288 | tf_op jit(solution)/shard_map/ppermute | solution.py:218
  29.2 17.8 %collective-permute-start.8 = (f32[120,512]{1,0:T(8,128)S(1)}, f32[120,512]{1,0:T(8,128)S(1)}, u32[]{:S(2)}, u32[]{:S(2)}) collective-permute-start(f32[120,512]{1,0:T(8,128)S(1)} %add_after.3.refs_0_.mine), channel_id=1, source_target_pairs={{0,1},{1,0},{2,3},{3,2},{4,5},{5,4},{6,7},{7,6},{8,9},{9,8},{10,11... | collective-permute-start | bytes 737288 | tf_op jit(solution)/shard_map/ppermute | solution.py:218
  34.5 12.4 %collective-permute-start.10 = (f32[120,512]{1,0:T(8,128)S(1)}, f32[120,512]{1,0:T(8,128)S(1)}, u32[]{:S(2)}, u32[]{:S(2)}) collective-permute-start(f32[120,512]{1,0:T(8,128)S(1)} %collective-permute-done.5.refs_2_), channel_id=1, source_target_pairs={{0,1},{1,0},{2,3},{3,2},{4,5},{5,4},{6,7},{7,6},{8,9},{9,8},{10,11... | collective-permute-start | bytes 737288 | tf_op jit(solution)/shard_map/ppermute | solution.py:218
  39.4 7.6 %collective-permute-start.11 = (f32[120,512]{1,0:T(8,128)S(1)}, f32[120,512]{1,0:T(8,128)S(1)}, u32[]{:S(2)}, u32[]{:S(2)}) collective-permute-start(f32[120,512]{1,0:T(8,128)S(1)} %collective-permute-done.6.refs_3_), channel_id=1, source_target_pairs={{0,1},{1,0},{2,3},{3,2},{4,5},{5,4},{6,7},{7,6},{8,9},{9,8},{10,11... | collective-permute-start | bytes 737288 | tf_op jit(solution)/shard_map/ppermute | solution.py:218
  40.7 6.3 %collective-permute-start.9 = (f32[120,512]{1,0:T(8,128)S(1)}, f32[120,512]{1,0:T(8,128)S(1)}, u32[]{:S(2)}, u32[]{:S(2)}) collective-permute-start(f32[120,512]{1,0:T(8,128)S(1)} %collective-permute-done.4.refs_1_), channel_id=1, source_target_pairs={{0,1},{1,0},{2,3},{3,2},{4,5},{5,4},{6,7},{7,6},{8,9},{9,8},{10,11... | collective-permute-start | bytes 737288 | tf_op jit(solution)/shard_map/ppermute | solution.py:218
  44.3 7.4 %collective-permute-start.13 = (f32[160,128]{1,0:T(8,128)S(1)}, f32[160,128]{1,0:T(8,128)S(1)}, u32[]{:S(2)}, u32[]{:S(2)}) collective-permute-start(f32[160,128]{1,0:T(8,128)S(1)} %add.20.token.refs_0_), channel_id=1, source_target_pairs={{0,16},{4,20},{8,24},{12,28},{16,0},{20,4},{24,8},{28,12},{1,17},{... | collective-permute-start | bytes 245768 | tf_op jit(solution)/shard_map/ppermute | solution.py:218
  51.7 4.5 %collective-permute-start.14 = (f32[160,128]{1,0:T(8,128)S(1)}, f32[160,128]{1,0:T(8,128)S(1)}, u32[]{:S(2)}, u32[]{:S(2)}) collective-permute-start(f32[160,128]{1,0:T(8,128)S(1)} %add_after.4.refs_0_), channel_id=1, source_target_pairs={{0,4},{4,0},{8,12},{12,8},{16,20},{20,16},{24,28},{28,24},{1,5},{5... | collective-permute-start | bytes 245768 | tf_op jit(solution)/shard_map/ppermute | solution.py:218
  52.4 21.1 %collective-permute-start.12 = (f32[192,512]{1,0:T(8,128)S(1)}, f32[192,512]{1,0:T(8,128)S(1)}, u32[]{:S(2)}, u32[]{:S(2)}) collective-permute-start(f32[192,512]{1,0:T(8,128)S(1)} %get-tuple-element.42), channel_id=1, source_target_pairs={{0,16},{4,20},{8,24},{12,28},{16,0},{20,4},{24,8},{28,12},{1,17},{... | collective-permute-start | bytes 1179656 | tf_op jit(solution)/shard_map/ppermute | solution.py:218
  56.8 5.4 %collective-permute-start.16 = (f32[320,128]{1,0:T(8,128)S(1)}, f32[320,128]{1,0:T(8,128)S(1)}, u32[]{:S(2)}, u32[]{:S(2)}) collective-permute-start(f32[320,128]{1,0:T(8,128)S(1)} %order.1.a), channel_id=1, source_target_pairs={{0,2},{1,3},{2,0},{3,1},{4,6},{5,7},{6,4},{7,5},{8,10},{9,11},{10,... | collective-permute-start | bytes 491528 | tf_op jit(solution)/shard_map/ppermute | solution.py:218
  58.4 3.8 %collective-permute-start.15 = (f32[320,128]{1,0:T(8,128)S(1)}, f32[320,128]{1,0:T(8,128)S(1)}, u32[]{:S(2)}, u32[]{:S(2)}) collective-permute-start(f32[320,128]{1,0:T(8,128)S(1)} %order.1.a), channel_id=1, source_target_pairs={{0,1},{1,0},{2,3},{3,2},{4,5},{5,4},{6,7},{7,6},{8,9},{9,8},{10,11... | collective-permute-start | bytes 491528 | tf_op jit(solution)/shard_map/ppermute | solution.py:218
  73.5 20.7 %collective-permute-start.18 = (f32[192,512]{1,0:T(8,128)S(1)}, f32[192,512]{1,0:T(8,128)S(1)}, u32[]{:S(2)}, u32[]{:S(2)}) collective-permute-start(f32[192,512]{1,0:T(8,128)S(1)} %add_after.5.token.own), channel_id=1, source_target_pairs={{0,16},{4,20},{8,24},{12,28},{16,0},{20,4},{24,8},{28,12},{1,17},{... | collective-permute-start | bytes 1179656 | tf_op jit(solution)/shard_map/ppermute | solution.py:218
  74.5 19.7 %collective-permute-start.19 = (f32[192,512]{1,0:T(8,128)S(1)}, f32[192,512]{1,0:T(8,128)S(1)}, u32[]{:S(2)}, u32[]{:S(2)}) collective-permute-start(f32[192,512]{1,0:T(8,128)S(1)} %add_after.5.token.own), channel_id=1, source_target_pairs={{0,4},{4,0},{8,12},{12,8},{16,20},{20,16},{24,28},{28,24},{1,5},{5... | collective-permute-start | bytes 1179656 | tf_op jit(solution)/shard_map/ppermute | solution.py:218
  75.0 20.6 %collective-permute-start.20 = (f32[192,512]{1,0:T(8,128)S(1)}, f32[192,512]{1,0:T(8,128)S(1)}, u32[]{:S(2)}, u32[]{:S(2)}) collective-permute-start(f32[192,512]{1,0:T(8,128)S(1)} %add_after.5.token.own), channel_id=1, source_target_pairs={{0,8},{4,12},{8,0},{12,4},{16,24},{20,28},{24,16},{28,20},{1,9},{5... | collective-permute-start | bytes 1179656 | tf_op jit(solution)/shard_map/ppermute | solution.py:218
  78.2 25.7 %collective-permute-start.21 = (f32[192,512]{1,0:T(8,128)S(1)}, f32[192,512]{1,0:T(8,128)S(1)}, u32[]{:S(2)}, u32[]{:S(2)}) collective-permute-start(f32[192,512]{1,0:T(8,128)S(1)} %add_after.5.token.own), channel_id=1, source_target_pairs={{0,12},{4,8},{8,4},{12,0},{16,28},{20,24},{24,20},{28,16},{1,13},{... | collective-permute-start | bytes 1179656 | tf_op jit(solution)/shard_map/ppermute | solution.py:218
  106.0 11.6 %collective-permute-start.22 = (f32[200,512]{1,0:T(8,128)S(1)}, f32[200,512]{1,0:T(8,128)S(1)}, u32[]{:S(2)}, u32[]{:S(2)}) collective-permute-start(f32[200,512]{1,0:T(8,128)S(1)} %get-tuple-element.51.refs_0_.refs_4_), channel_id=1, source_target_pairs={{0,4},{4,0},{8,12},{12,8},{16,20},{20,16},{24,28},{28,24},{1,5},{5... | collective-permute-start | bytes 1228808 | tf_op jit(solution)/shard_map/ppermute | solution.py:218
  106.7 12.4 %collective-permute-start.23 = (f32[200,512]{1,0:T(8,128)S(1)}, f32[200,512]{1,0:T(8,128)S(1)}, u32[]{:S(2)}, u32[]{:S(2)}) collective-permute-start(f32[200,512]{1,0:T(8,128)S(1)} %get-tuple-element.51.refs_0_.refs_4_), channel_id=1, source_target_pairs={{0,8},{4,12},{8,0},{12,4},{16,24},{20,28},{24,16},{28,20},{1,9},{5... | collective-permute-start | bytes 1228808 | tf_op jit(solution)/shard_map/ppermute | solution.py:218
  106.7 19.8 %collective-permute-start.24 = (f32[200,512]{1,0:T(8,128)S(1)}, f32[200,512]{1,0:T(8,128)S(1)}, u32[]{:S(2)}, u32[]{:S(2)}) collective-permute-start(f32[200,512]{1,0:T(8,128)S(1)} %get-tuple-element.51.refs_0_.refs_4_), channel_id=1, source_target_pairs={{0,12},{4,8},{8,4},{12,0},{16,28},{20,24},{24,20},{28,16},{1,13},{... | collective-permute-start | bytes 1228808 | tf_op jit(solution)/shard_map/ppermute | solution.py:218
  127.6 4.5 %collective-permute-start.26 = (f32[1,512]{1,0:T(1,128)S(1)}, f32[1,512]{1,0:T(1,128)S(1)}, u32[]{:S(2)}, u32[]{:S(2)}) collective-permute-start(f32[1,512]{1,0:T(1,128)S(1)} %add.21), channel_id=1, source_target_pairs={{0,2},{1,3},{2,0},{3,1},{4,6},{5,7},{6,4},{7,5},{8,10},{9,11},{10,... | collective-permute-start | bytes 6152 | tf_op jit(solution)/shard_map/ppermute | solution.py:218
  (6 other events, 8.4 us)

commit v6 on v5

--- a/solution.py
+++ b/solution.py
@@ -26,10 +26,12 @@
 anywhere = pl.BlockSpec(memory_space=pl.ANY)
 
 
-def kernel(body, out_shape, in_specs, scratch, name, cost=0):
+def kernel(body, out_shape, in_specs, scratch, name, cost=0, out_specs=None):
+    extra = {} if out_specs is None else {"out_specs": out_specs}
     return pl.pallas_call(
         body,
         out_shape=out_shape,
+        **extra,
         in_specs=in_specs,
         scratch_shapes=scratch,
         compiler_params=pltpu.CompilerParams(vmem_limit_bytes=32 * 2**20),
@@ -270,13 +272,6 @@
         out[...] = stack[pl.ds(pl.multiple_of(index * share, 8), share), :]
 
 
-def order_kernel(bits, *refs):
-    out = refs[-1]
-    share = refs[0].shape[0]
-    for k in range(2):
-        out[pl.ds(pl.multiple_of((bits[2] % 2 ^ k) * share, 8), share), :] = refs[k][...]
-
-
 def raw_kernel(bits, token, *refs):
     mine, others, columns = refs[:square], refs[square : 2 * square], refs[2 * square : 3 * square]
     sent, kept, left, right, raw = refs[3 * square :]
@@ -292,8 +287,8 @@
     sent[...] = raw[pl.ds(pl.multiple_of((1 - bits[4]) * count, 8), count), :]
 
 
-def left_kernel(scale, bits, mine, other, *refs):
-    inverses, (left, left_scaled, inverse, rows) = refs[:-4], refs[-4:]
+def left_kernel(scale, bits, mine, other, own, *refs):
+    inverses, (left, left_scaled, inverse, own_right, rows) = refs[:-5], refs[-5:]
     half = mine.shape[0]
     for b, part in enumerate(inverses):
         inverse[b * lanes : (b + 1) * lanes, :] = part[...]
@@ -301,17 +296,16 @@
     rows[pl.ds(pl.multiple_of((1 - bits[0]) * half, 8), half), :] = other[...]
     left[...] = dot(rows[...], inverse[...], ((1,), (1,)))
     left_scaled[...] = left[...] * scale
-
-
-def norm_kernel(own, received, inverse, *refs):
-    own_right, out = refs[-2:]
-    count = own.shape[0]
     own_right[...] = dot(own[...], inverse[...], ((1,), (1,)))
+
+
+def norm_kernel(own_right, received, inverse, one, two, out):
+    count = own_right.shape[0]
     right = dot(received[...], inverse[...], ((1,), (1,)))
     out[:count, :] = right
     total = jnp.sum(right * right, axis=0, keepdims=True)
     total = total + jnp.sum(own_right[...] * own_right[...], axis=0, keepdims=True)
-    row = lax.broadcasted_iota(jnp.int32, (8, own.shape[1]), 0)
+    row = lax.broadcasted_iota(jnp.int32, (8, own_right.shape[1]), 0)
     out[count:, :] = jnp.where(row == 0, total, 0.0)
 
 
@@ -319,29 +313,47 @@
     rows, (rights, splits, products) = refs[:-3], refs[-3:]
     count = own_right.shape[0]
     rights[:count, :] = own_right[...]
-    for k in range(1, square):
-        right = dot(rows[k - 1][...], inverse[...], ((1,), (1,)))
-        rights[k * count : (k + 1) * count, :] = right
+    for k, part in enumerate(rows):
+        at = slice((k + 1) * count, (k + 2) * count)
+        rights[at, :] = dot(part[...], inverse[...], ((1,), (1,)))
     splits[...] = three_right(rights[...])
     product = dot_three(three_left(left[...]), splits[...])
-    for k in range(square):
+    for k in range(len(rows) + 1):
         products[k] = product[:, k * count : (k + 1) * count]
 
 
-def momentum_kernel(bits, left, products, *refs):
+def diagonal_kernel(left, inverse, first, second, right, splits, product):
+    middle = first.shape[0]
+    right[:middle, :] = dot(first[...], inverse[...], ((1,), (1,)))
+    right[middle:, :] = dot(second[...], inverse[...], ((1,), (1,)))
+    splits[...] = three_right(right[...])
+    product[...] = dot_three(three_left(left[...]), splits[...])
+
+
+def momentum_kernel(bits, left, products, last_product, *refs):
     pieces, received = refs[:square], refs[square : 2 * square]
-    new_momentum, splits = refs[-2:]
+    new_momentum, splits, ready, sent = refs[-4:]
     width = pieces[0].shape[1]
     half = width // 2
+    scaled = three_left(left[...])
+    copies = []
     for k in range(square):
-        splits[k * half : (k + 1) * half, :] = three_right(received[k][:half, :])
-    product = dot_three(three_left(left[...]), splits[...])
-    for k in range(square):
-        at = pl.ds(pl.multiple_of((bits[2] ^ k) * width, lanes), width)
-        other = product[:, k * half : (k + 1) * half]
-        lower = jnp.concatenate([products[k], other], axis=1)
-        upper = jnp.concatenate([other, products[k]], axis=1)
-        new_momentum[:, at] = pieces[k][...] - 0.5 * jnp.where(bits[4] == 0, lower, upper)
+        parts = slice(k * half, (k + 1) * half)
+        splits[parts, :] = three_right(received[k][:half, :])
+        if k % 2 == 0:
+            continue
+        both = dot_three(scaled, splits[(k - 1) * half : (k + 1) * half, :])
+        for i in (k - 1, k):
+            other = both[:, (i - k + 1) * half : (i - k + 2) * half]
+            mine = products[i] if i < square - 1 else last_product[...]
+            lower = jnp.concatenate([mine, other], axis=1)
+            upper = jnp.concatenate([other, mine], axis=1)
+            ready[i] = pieces[i][...] - 0.5 * jnp.where(bits[4] == 0, lower, upper)
+            at = pl.ds(pl.multiple_of((bits[2] ^ i) * width, lanes), width)
+            copies.append(pltpu.make_async_copy(ready.at[i], new_momentum.at[:, at], sent.at[i]))
+            copies[i].start()
+    for copy in copies:
+        copy.wait()
 
 
 def squares_kernel(row, *refs):
@@ -351,27 +363,35 @@
     refs[-1][...] = total
 
 
-def update_kernel(factor, bits, squares, left, rights, own_splits, splits, *refs):
-    received, (update, next_basis) = refs[:square], refs[square:]
-    half = next_basis.shape[0]
+def update_kernel(factor, bits, squares, left, rights, last_right, own_splits, last_split, splits, *refs):
+    received, (update, next_basis, ready, basis_ready, sent) = refs[:square], refs[square:]
+    half = basis_ready.shape[0]
     width = 2 * half
     norm = jnp.sqrt(squares[...] + epsilon)
-    scaled = three_left(left[...] * (factor / norm))
-    mine = dot_three(scaled, own_splits[...])
-    other = dot_three(scaled, splits[...])
-    for k in range(square):
-        at = pl.ds(pl.multiple_of((bits[2] ^ k) * width, lanes), width)
-        parts = slice(k * half, (k + 1) * half)
-        lower = jnp.concatenate([mine[:, parts], other[:, parts]], axis=1)
-        upper = jnp.concatenate([other[:, parts], mine[:, parts]], axis=1)
-        update[:, at] = jnp.where(bits[4] == 0, lower, upper).astype(jnp.bfloat16)
     for k in range(square):
 
         @pl.when((bits[3] // 2) ^ bits[2] == k)
         def _():
-            mine_rows = rights[k * half : (k + 1) * half, :]
+            mine_rows = rights[k * half : (k + 1) * half, :] if k < square - 1 else last_right[...]
             rows = jnp.where(bits[3] % 2 == bits[4], mine_rows, received[k][:half, :])
-            next_basis[...] = rows / norm
+            basis_ready[...] = rows / norm
+
+    copies = [pltpu.make_async_copy(basis_ready, next_basis, sent.at[square])]
+    copies[0].start()
+    scaled = three_left(left[...] * (factor / norm))
+    for k in range(square):
+        parts = slice(k * half, (k + 1) * half)
+        mine = dot_three(scaled, own_splits[parts, :] if k < square - 1 else last_split[...])
+        other = dot_three(scaled, splits[parts, :])
+        lower = jnp.concatenate([mine, other], axis=1)
+        upper = jnp.concatenate([other, mine], axis=1)
+        ready[k] = jnp.where(bits[4] == 0, lower, upper).astype(jnp.bfloat16)
+        at = pl.ds(pl.multiple_of((bits[2] ^ k) * width, lanes), width)
+        copy = pltpu.make_async_copy(ready.at[k], update.at[:, at], sent.at[k])
+        copy.start()
+        copies.append(copy)
+    for copy in copies:
+        copy.wait()
 
 
 def in_squares(momentum, gradient, right_basis):
@@ -431,9 +451,8 @@
     )(bits, part, *gathered, *others, *columns)
 
     part = add_after(part, swap(part, "fsdp", square), kept)
-    quarter = kernel(
-        order_kernel, shape(2 * share, lanes), [smem] + [vmem] * 2, [], "order"
-    )(bits, part, swap(part, "fsdp", 1))
+    chips = [[i, i + 1] for i in range(0, lax.axis_size("fsdp"), 2)]
+    quarter = lax.all_gather(part, "fsdp", axis=0, tiled=True, axis_index_groups=chips)
     over_planes = swap(quarter, "tensor", 2)
     shares = [quarter, swap(quarter, "tensor", 1), over_planes, swap(over_planes, "tensor", 1)]
 
@@ -447,61 +466,77 @@
             token = own
         out, work = later_step(b, work, token)
         factors.append(out)
-    left, left_scaled, inverse = kernel(
+    left, left_scaled, inverse, own_right = kernel(
         functools.partial(left_kernel, math.sqrt(total_rows)),
-        [shape(rows, rank), shape(rows, rank), shape(rank, rank)],
-        [smem] + [vmem] * (2 + count),
+        [shape(rows, rank), shape(rows, rank), shape(rank, rank), shape(width // 2, rank)],
+        [smem] + [vmem] * (3 + count),
         [pltpu.VMEM((rows, rank), jnp.float32)],
         "left",
-    )(bits, mine, others[0], *factors)
+    )(bits, mine, others[0], own, *factors)
 
     received = swap(own, "fsdp", square)
-    own_rows = [own] + [swap(own, "fsdp", k) for k in range(1, square)]
-    own_right, with_norms = kernel(
-        norm_kernel,
-        [shape(width // 2, rank), shape(width // 2 + 8, rank)],
-        [vmem] * 3 + [anywhere] * (square - 1),
-        [],
-        "norms",
-    )(own, received, inverse, *own_rows[1:])
+    beside = [swap(own, "fsdp", k) for k in (1, 2)]
+    with_norms = kernel(
+        norm_kernel, shape(width // 2 + 8, rank), [vmem] * 3 + [anywhere] * 2, [], "norms"
+    )(own_right, received, inverse, *beside)
     received_rows = [with_norms] + [swap(with_norms, "fsdp", k) for k in range(1, square)]
+    middle = width // 4
+    diagonal = [swap(beside[1][:middle], "fsdp", 1), swap(beside[0][middle:], "fsdp", 2)]
     rights, own_splits, products = kernel(
         own_kernel,
         [
-            shape(cols // 2, rank),
-            shape(cols // 2, 3 * rank, dtype=jnp.bfloat16),
-            shape(square, rows, width // 2),
+            shape(3 * (width // 2), rank),
+            shape(3 * (width // 2), 3 * rank, dtype=jnp.bfloat16),
+            shape(3, rows, width // 2),
         ],
-        [vmem] * (2 + square),
+        [vmem] * 5,
         [],
         "own_part",
         cost=2**24,
-    )(left, inverse, own_right, *own_rows[1:])
+    )(left, inverse, own_right, *beside)
+    last_right, last_split, last_product = kernel(
+        diagonal_kernel,
+        [
+            shape(width // 2, rank),
+            shape(width // 2, 3 * rank, dtype=jnp.bfloat16),
+            shape(rows, width // 2),
+        ],
+        [vmem] * 4,
+        [],
+        "diagonal_part",
+        cost=2**22,
+    )(left, inverse, *diagonal)
     squares = kernel(
         functools.partial(squares_kernel, width // 2),
         shape(1, rank),
-        [vmem] * square + [anywhere],
+        [vmem] * square + [anywhere] * 2,
         [],
         "squares",
-    )(*received_rows, products)
+    )(*received_rows, products, last_product)
     squares = squares + swap(squares, "tensor", 1)
     squares = squares + swap(squares, "tensor", 2)
 
     new_momentum, splits = kernel(
         momentum_kernel,
         [shape(rows, cols), shape(cols // 2, 3 * rank, dtype=jnp.bfloat16)],
-        [smem] + [vmem] * (2 + 2 * square),
-        [],
+        [smem] + [vmem] * (3 + 2 * square),
+        [pltpu.VMEM((square, rows, width), jnp.float32), pltpu.SemaphoreType.DMA((square,))],
         "new_momentum",
         cost=2**22,
-    )(bits, left, products, *pieces, *received_rows)
+        out_specs=[anywhere, vmem],
+    )(bits, left, products, last_product, *pieces, *received_rows)
     update, next_basis = kernel(
         functools.partial(update_kernel, math.sqrt(total_rows / total_cols)),
         [shape(rows, cols, dtype=jnp.bfloat16), shape(cols // lax.axis_size("fsdp"), rank)],
-        [smem] + [vmem] * (5 + square),
-        [],
+        [smem] + [vmem] * (7 + square),
+        [
+            pltpu.VMEM((square, rows, width), jnp.bfloat16),
+            pltpu.VMEM((width // 2, rank), jnp.float32),
+            pltpu.SemaphoreType.DMA((square + 1,)),
+        ],
         "update",
-    )(bits, squares, left, rights, own_splits, splits, *received_rows)
+        out_specs=[anywhere, anywhere],
+    )(bits, squares, left, rights, last_right, own_splits, last_split, splits, *received_rows)
     return (update, new_momentum, left_scaled, next_basis)
 
 

time: 136 us -> 133 us (0.978)
  waiting for transfers between devices: 54.9 us -> 47.6 us
  blocking collectives: 2.34 us -> 7.46 us
    ppermute x27, waiting for transfers between devices: 54.9 us -> 47.6 us  [swap(): lax.ppermute(value, axis, [(i, i ^ flip) for i in range(lax.axis_size(axi...]
    all_gather x0 -> x1, blocking collectives: none -> 5.3 us  [in_squares(): lax.all_gather(part, 'fsdp', axis=0, tiled=True, axis_index_groups=chips)]
  transfers between devices with their start and end apart: 27 -> 27, of which waited for: 16 -> 13; matrix products, arithmetic and copies ran while one was open for 0% -> 0% of each run, Pallas kernels for 29% -> 30%
where the time goes in v6:
time: 133 us
  waiting for transfers between devices  47.6 us (36%)
  Pallas kernels  45.5 us (34%)
  starting transfers between devices  26.7 us (20%)
  blocking collectives  7.46 us (6%)
  local copies, waits for them, and re-layouts  4.49 us (3%)
    ppermute x27, waiting for transfers between devices, swap(): lax.ppermute(value, axis, [(i, i ^ flip) for i in range(lax.axis_size(axi...  47.6 us
    ppermute x27, starting transfers between devices, swap(): lax.ppermute(value, axis, [(i, i ^ flip) for i in range(lax.axis_size(axi...  26.7 us
    pallas_call x3, Pallas kernels, later_step(): kernel(functools.partial(later_kernel, b), [shape(lanes, size), shape(siz...  14 us
    all_gather x1, blocking collectives, in_squares(): lax.all_gather(part, 'fsdp', axis=0, tiled=True, axis_index_groups=chips)  5.3 us
    pallas_call x1, Pallas kernels, first_step(): kernel(first_kernel, [shape(lanes, size), shape(size, size)], [smem] + [v...  5.06 us
    unnamed x6, local copies, waits for them, and re-layouts  4.38 us
    pallas_call x1, Pallas kernels, in_squares(): kernel(part_left_kernel, [shape(half, rank)] * 2, [smem] + [vmem] * (1 +...  3.94 us
    pallas_call x1, Pallas kernels, in_squares(): kernel(raw_kernel, [shape(width // 2, rank)] * 2, [smem, anywhere] + [vme...  3.41 us
  transfers between devices with their start and end apart: 27, of which 13 were waited for; matrix products, arithmetic and copies ran while one was open for 0% of the time, Pallas kernels for 30%

profile of v6, /device:TPU:0, one launch (start us, length us, event | category | flops | bytes accessed | tf_op | source)
XLA Modules:
  0.0 132.9 jit_solution(7508227138158167664)
XLA Ops:
  3.9 3.0 %collective-permute-start.1 = (f32[240,384]{1,0:T(8,128)S(1)}, f32[240,384]{1,0:T(8,128)S(1)}, u32[]{:S(2)}, u32[]{:S(2)}) collective-permute-start(f32[240,384]{1,0:T(8,128)S(1)} %get-tuple-element.36.refs_1_), channel_id=1, source_target_pairs={{0,4},{4,0},{8,12},{12,8},{16,20},{20,16},{24,28},{28,24},{1,5},{5... | collective-permute-start | bytes 1105928 | tf_op jit(solution)/shard_map/ppermute | solution.py:220
  10.4 3.9 %part_left.1 = (f32[120,512]{1,0:T(8,128)S(1)}, f32[120,512]{1,0:T(8,128)S(1)}) custom-call(s32[5]{0:T(128)S(1)} %stack.23.bits, f32[1536,512]{1,0:T(8,128)S(1)} %copy-done, f32[240,384]{1,0:T(8,128)S(1)} %get-tuple-element.35.refs_0_.refs_8_, f32[240,384]{1,0:T(8,128)S(1)} %get-tuple-element.36.refs_1_, f32[240,384]{1,0:T(8,128)S(1)} %get-tuple-element.37.refs_2_, ...), custom_call_target="tpu_custom_call" | custom-call | tf_op jit(solution)/shard_map/part_left/pallas_call | solution.py:413
  14.4 2.2 %all_gather.6.both = f32[240,512]{1,0:T(8,128)S(1)} all-gather(f32[120,512]{1,0:T(8,128)S(1)} %get-tuple-element.40), channel_id=1, replica_groups={{0,1},{2,3},{4,5},{6,7},{8,9},{10,11},{12,13},{14,15},{16,17},{18,19},{..., dimensions={0}, use_global_device_ids=true | all-gather | bytes 737280 | tf_op jit(solution)/shard_map/all_gather | solution.py:421
  19.1 6.3 %collective-permute-done.refs_1_ = f32[120,512]{1,0:T(8,128)S(1)} collective-permute-done((f32[120,512]{1,0:T(8,128)S(1)}, f32[120,512]{1,0:T(8,128)S(1)}, u32[]{:S(2)}, u32[]{:S(2)}) %collective-permute-start) | collective-permute-done | bytes 245792 | tf_op jit(solution)/shard_map/ppermute | solution.py:220
  29.0 5.4 %collective-permute-done.6.refs_2_ = f32[120,512]{1,0:T(8,128)S(1)} collective-permute-done((f32[120,512]{1,0:T(8,128)S(1)}, f32[120,512]{1,0:T(8,128)S(1)}, u32[]{:S(2)}, u32[]{:S(2)}) %collective-permute-start.6) | collective-permute-done | bytes 245792 | tf_op jit(solution)/shard_map/ppermute | solution.py:220
  34.4 4.8 %collective-permute-done.7.refs_3_ = f32[120,512]{1,0:T(8,128)S(1)} collective-permute-done((f32[120,512]{1,0:T(8,128)S(1)}, f32[120,512]{1,0:T(8,128)S(1)}, u32[]{:S(2)}, u32[]{:S(2)}) %collective-permute-start.7) | collective-permute-done | bytes 245792 | tf_op jit(solution)/shard_map/ppermute | solution.py:220
  40.5 2.1 %part_gram.1 = (f32[160,128]{1,0:T(8,128)S(1)}, f32[160,128]{1,0:T(8,128)S(1)}) custom-call(s32[5]{0:T(128)S(1)} %stack.23.bits, f32[120,512]{1,0:T(8,128)S(1)} %add_after.3.refs_0_.mine, f32[120,512]{1,0:T(8,128)S(1)} %collective-permute-done.5.refs_1_, f32[120,512]{1,0:T(8,128)S(1)} %collective-permute-done.6.refs_2_, ...), custom_call_target="tpu_custom_call" | custom-call | tf_op jit(solution)/shard_map/part_gram/pallas_call | solution.py:432
  44.1 2.7 %collective-permute-start.13 = (f32[160,128]{1,0:T(8,128)S(1)}, f32[160,128]{1,0:T(8,128)S(1)}, u32[]{:S(2)}, u32[]{:S(2)}) collective-permute-start(f32[160,128]{1,0:T(8,128)S(1)} %add.20.token.refs_0_), channel_id=1, source_target_pairs={{0,16},{4,20},{8,24},{12,28},{16,0},{20,4},{24,8},{28,12},{1,17},{... | collective-permute-start | bytes 245768 | tf_op jit(solution)/shard_map/ppermute | solution.py:220
  46.8 3.4 %part_raw.1 = (f32[192,512]{1,0:T(8,128)S(1)}, f32[192,512]{1,0:T(8,128)S(1)}) custom-call(s32[5]{0:T(128)S(1)} %stack.23.bits, f32[160,128]{1,0:T(8,128)S(1)} %add.20.token.refs_0_, f32[120,512]{1,0:T(8,128)S(1)} %add_after.3.refs_0_.mine, f32[120,512]{1,0:T(8,128)S(1)} %collective-permute-done.5.refs_1_, f32[120,512]{1,0:T(8,128)S(1)} %collective-permute-done.6.refs_2_, ...), custom_call_target="tpu_custom_call" | custom-call | tf_op jit(solution)/shard_map/part_raw/pallas_call | solution.py:441
  51.6 5.3 %all_gather.7.a = f32[320,128]{1,0:T(8,128)S(1)} all-gather(f32[160,128]{1,0:T(8,128)S(1)} %add_after.4), channel_id=1, replica_groups={{0,4},{8,12},{16,20},{24,28},{1,5},{9,13},{17,21},{25,29},{2,6},{10,14}..., dimensions={0}, use_global_device_ids=true | all-gather | bytes 245760 | tf_op jit(solution)/shard_map/all_gather | solution.py:455
  58.4 3.8 %collective-permute-done.15.c = f32[320,128]{1,0:T(8,128)S(1)} collective-permute-done((f32[320,128]{1,0:T(8,128)S(1)}, f32[320,128]{1,0:T(8,128)S(1)}, u32[]{:S(2)}, u32[]{:S(2)}) %collective-permute-start.15) | collective-permute-done | bytes 163872 | tf_op jit(solution)/shard_map/ppermute | solution.py:220
  63.6 5.1 %factor_first.1 = (f32[128,512]{1,0:T(8,128)S(1)}, f32[512,512]{1,0:T(8,128)S(1)}) custom-call(s32[5]{0:T(128)S(1)} %stack.23.bits, f32[320,128]{1,0:T(8,128)S(1)} %all_gather.7.a, f32[320,128]{1,0:T(8,128)S(1)} %collective-permute-done.14.b, f32[320,128]{1,0:T(8,128)S(1)} %collective-permute-done.15.c, f32[320,128]{1,0:T(8,128)S(1)} %collective-permute-done.16.d), custom_call_target="tpu_custom_call" | custom-call | tf_op jit(solution)/shard_map/factor_first/pallas_call | solution.py:168
  68.6 4.6 %factor_later.3 = (f32[128,512]{1,0:T(8,128)S(1)}, f32[512,512]{1,0:T(8,128)S(1)}) custom-call(f32[512,512]{1,0:T(8,128)S(1)} %get-tuple-element.45.before, f32[128,512]{1,0:T(8,128)S(1)} %get-tuple-element.46.token.refs_0_), custom_call_target="tpu_custom_call" | custom-call | tf_op jit(solution)/shard_map/factor_later/pallas_call | solution.py:184
  74.6 3.4 %collective-permute-start.17 = (f32[192,512]{1,0:T(8,128)S(1)}, f32[192,512]{1,0:T(8,128)S(1)}, u32[]{:S(2)}, u32[]{:S(2)}) collective-permute-start(f32[192,512]{1,0:T(8,128)S(1)} %add_after.5.token.own), channel_id=1, source_target_pairs={{0,16},{4,20},{8,24},{12,28},{16,0},{20,4},{24,8},{28,12},{1,17},{... | collective-permute-start | bytes 1179656 | tf_op jit(solution)/shard_map/ppermute | solution.py:220
  77.9 4.3 %factor_later.4 = (f32[128,512]{1,0:T(8,128)S(1)}, f32[512,512]{1,0:T(8,128)S(1)}) custom-call(f32[512,512]{1,0:T(8,128)S(1)} %get-tuple-element.48.before, f32[192,512]{1,0:T(8,128)S(1)} %add_after.5.token.own), custom_call_target="tpu_custom_call" | custom-call | tf_op jit(solution)/shard_map/factor_later/pallas_call | solution.py:184
  82.2 5.2 %factor_later.5 = (f32[128,512]{1,0:T(8,128)S(1)}, f32[512,512]{1,0:T(8,128)}) custom-call(f32[512,512]{1,0:T(8,128)S(1)} %get-tuple-element.50.before, f32[192,512]{1,0:T(8,128)S(1)} %add_after.5.token.own), custom_call_target="tpu_custom_call" | custom-call | tf_op jit(solution)/shard_map/factor_later/pallas_call | solution.py:184
  87.4 2.9 %left.1 = (f32[240,512]{1,0:T(8,128)S(1)}, f32[240,512]{1,0:T(8,128)}, f32[512,512]{1,0:T(8,128)S(1)}, f32[192,512]{1,0:T(8,128)S(1)}) custom-call(s32[5]{0:T(128)S(1)} %stack.23.bits, f32[120,512]{1,0:T(8,128)S(1)} %add_after.3.refs_0_.mine, f32[120,512]{1,0:T(8,128)S(1)} %collective-permute-done.4.refs_4_.other, f32[192,512]{1,0:T(8,128)S(1)} %add_after.5.token.own, ...), custom_call_target="tpu_custom_call" | custom-call | tf_op jit(solution)/shard_map/left/pallas_call | solution.py:469
  90.3 2.2 %collective-permute-done.19.two.refs_1_ = f32[192,512]{1,0:T(8,128)S(1)} collective-permute-done((f32[192,512]{1,0:T(8,128)S(1)}, f32[192,512]{1,0:T(8,128)S(1)}, u32[]{:S(2)}, u32[]{:S(2)}) %collective-permute-start.19) | collective-permute-done | bytes 393248 | tf_op jit(solution)/shard_map/ppermute | solution.py:220
  92.5 2.8 %collective-permute-done.17.received = f32[192,512]{1,0:T(8,128)S(1)} collective-permute-done((f32[192,512]{1,0:T(8,128)S(1)}, f32[192,512]{1,0:T(8,128)S(1)}, u32[]{:S(2)}, u32[]{:S(2)}) %collective-permute-start.17) | collective-permute-done | bytes 393248 | tf_op jit(solution)/shard_map/ppermute | solution.py:220
  101.7 2.9 %own_part.1 = (f32[576,512]{1,0:T(8,128)S(1)}, bf16[576,1536]{1,0:T(8,128)(2,1)S(1)}, f32[3,240,192]{2,1,0:T(8,128)S(1)}) custom-call(f32[240,512]{1,0:T(8,128)S(1)} %get-tuple-element.54.left, f32[512,512]{1,0:T(8,128)S(1)} %get-tuple-element.53.inverse, f32[192,512]{1,0:T(8,128)S(1)} %get-tuple-element.52.own_right, ...), custom_call_target="tpu_custom_call" | custom-call | bytes 16777216 | tf_op jit(solution)/shard_map/own_part/pallas_call | solution.py:485
  104.6 15.1 %collective-permute-done.23.first = f32[96,512]{1,0:T(8,128)S(1)} collective-permute-done((f32[96,512]{1,0:T(8,128)S(1)}, f32[96,512]{1,0:T(8,128)S(1)}, u32[]{:S(2)}, u32[]{:S(2)}) %collective-permute-start.23) | collective-permute-done | bytes 196640 | tf_op jit(solution)/shard_map/ppermute | solution.py:220
  121.2 2.7 %diagonal_part.1 = (f32[192,512]{1,0:T(8,128)S(1)}, bf16[192,1536]{1,0:T(8,128)(2,1)S(1)}, f32[240,192]{1,0:T(8,128)S(1)}) custom-call(f32[240,512]{1,0:T(8,128)S(1)} %get-tuple-element.54.left, f32[512,512]{1,0:T(8,128)S(1)} %get-tuple-element.53.inverse, f32[96,512]{1,0:T(8,128)S(1)} %collective-permute-done.23.first, ...), custom_call_target="tpu_custom_call" | custom-call | bytes 4194304 | tf_op jit(solution)/shard_map/diagonal_part/pallas_call | solution.py:497
  126.7 2.8 %new_momentum.1 = (f32[240,1536]{1,0:T(8,128)}, bf16[768,1536]{1,0:T(8,128)(2,1)S(1)}) custom-call(s32[5]{0:T(128)S(1)} %stack.23.bits, f32[240,512]{1,0:T(8,128)S(1)} %get-tuple-element.54.left, f32[3,240,192]{2,1,0:T(8,128)S(1)} %get-tuple-element.55.refs_4_.products, f32[240,192]{1,0:T(8,128)S(1)} %get-tuple-element.56.refs_5_.last_product, ...), custom_call_target="tpu_custom_call" | custom-call | bytes 4194304 | tf_op jit(solution)/shard_map/new_momentum/pallas_call | solution.py:519
  129.5 3.2 %update.1 = (bf16[240,1536]{1,0:T(8,128)(2,1)}, f32[192,512]{1,0:T(8,128)}) custom-call(s32[5]{0:T(128)S(1)} %stack.23.bits, f32[1,512]{1,0:T(1,128)S(1)} %add.22.squares, f32[240,512]{1,0:T(8,128)S(1)} %get-tuple-element.54.left, f32[576,512]{1,0:T(8,128)S(1)} %get-tuple-element.57.rights, f32[192,512]{1,0:T(8,128)S(1)} %get-tuple-element.58.last_right, ...), custom_call_target="tpu_custom_call" | custom-call | tf_op jit(solution)/shard_map/update/pallas_call | solution.py:528
  (63 shorter events, 32.0 us)
Async XLA Ops:
  3.9 21.4 %collective-permute-start.1 = (f32[240,384]{1,0:T(8,128)S(1)}, f32[240,384]{1,0:T(8,128)S(1)}, u32[]{:S(2)}, u32[]{:S(2)}) collective-permute-start(f32[240,384]{1,0:T(8,128)S(1)} %get-tuple-element.36.refs_1_), channel_id=1, source_target_pairs={{0,4},{4,0},{8,12},{12,8},{16,20},{20,16},{24,28},{28,24},{1,5},{5... | collective-permute-start | bytes 1105928 | tf_op jit(solution)/shard_map/ppermute | solution.py:220
  7.0 18.4 %collective-permute-start.2 = (f32[240,384]{1,0:T(8,128)S(1)}, f32[240,384]{1,0:T(8,128)S(1)}, u32[]{:S(2)}, u32[]{:S(2)}) collective-permute-start(f32[240,384]{1,0:T(8,128)S(1)} %get-tuple-element.37.refs_2_), channel_id=1, source_target_pairs={{0,8},{4,12},{8,0},{12,4},{16,24},{20,28},{24,16},{28,20},{1,9},{5... | collective-permute-start | bytes 1105928 | tf_op jit(solution)/shard_map/ppermute | solution.py:220
  8.5 16.8 %collective-permute-start.3 = (f32[240,384]{1,0:T(8,128)S(1)}, f32[240,384]{1,0:T(8,128)S(1)}, u32[]{:S(2)}, u32[]{:S(2)}) collective-permute-start(f32[240,384]{1,0:T(8,128)S(1)} %get-tuple-element.38.refs_3_), channel_id=1, source_target_pairs={{0,12},{4,8},{8,4},{12,0},{16,28},{20,24},{24,20},{28,16},{1,13},{... | collective-permute-start | bytes 1105928 | tf_op jit(solution)/shard_map/ppermute | solution.py:220
  17.1 8.3 %collective-permute-start = (f32[120,512]{1,0:T(8,128)S(1)}, f32[120,512]{1,0:T(8,128)S(1)}, u32[]{:S(2)}, u32[]{:S(2)}) collective-permute-start(f32[120,512]{1,0:T(8,128)S(1)} %core_add.1.refs_0_), channel_id=1, source_target_pairs={{0,2},{1,3},{2,0},{3,1},{4,6},{5,7},{6,4},{7,5},{8,10},{9,11},{10,... | collective-permute-start | bytes 737288 | tf_op jit(solution)/shard_map/ppermute | solution.py:220
  25.4 9.0 %collective-permute-start.6 = (f32[120,512]{1,0:T(8,128)S(1)}, f32[120,512]{1,0:T(8,128)S(1)}, u32[]{:S(2)}, u32[]{:S(2)}) collective-permute-start(f32[120,512]{1,0:T(8,128)S(1)} %add_after.3.refs_0_.mine), channel_id=1, source_target_pairs={{0,8},{4,12},{8,0},{12,4},{16,24},{20,28},{24,16},{28,20},{1,9},{5... | collective-permute-start | bytes 737288 | tf_op jit(solution)/shard_map/ppermute | solution.py:220
  27.3 11.9 %collective-permute-start.7 = (f32[120,512]{1,0:T(8,128)S(1)}, f32[120,512]{1,0:T(8,128)S(1)}, u32[]{:S(2)}, u32[]{:S(2)}) collective-permute-start(f32[120,512]{1,0:T(8,128)S(1)} %add_after.3.refs_0_.mine), channel_id=1, source_target_pairs={{0,12},{4,8},{8,4},{12,0},{16,28},{20,24},{24,20},{28,16},{1,13},{... | collective-permute-start | bytes 737288 | tf_op jit(solution)/shard_map/ppermute | solution.py:220
  28.7 11.9 %collective-permute-start.5 = (f32[120,512]{1,0:T(8,128)S(1)}, f32[120,512]{1,0:T(8,128)S(1)}, u32[]{:S(2)}, u32[]{:S(2)}) collective-permute-start(f32[120,512]{1,0:T(8,128)S(1)} %add_after.3.refs_0_.mine), channel_id=1, source_target_pairs={{0,4},{4,0},{8,12},{12,8},{16,20},{20,16},{24,28},{28,24},{1,5},{5... | collective-permute-start | bytes 737288 | tf_op jit(solution)/shard_map/ppermute | solution.py:220
  29.0 17.8 %collective-permute-start.4 = (f32[120,512]{1,0:T(8,128)S(1)}, f32[120,512]{1,0:T(8,128)S(1)}, u32[]{:S(2)}, u32[]{:S(2)}) collective-permute-start(f32[120,512]{1,0:T(8,128)S(1)} %add_after.3.refs_0_.mine), channel_id=1, source_target_pairs={{0,1},{1,0},{2,3},{3,2},{4,5},{5,4},{6,7},{7,6},{8,9},{9,8},{10,11... | collective-permute-start | bytes 737288 | tf_op jit(solution)/shard_map/ppermute | solution.py:220
  34.4 12.4 %collective-permute-start.10 = (f32[120,512]{1,0:T(8,128)S(1)}, f32[120,512]{1,0:T(8,128)S(1)}, u32[]{:S(2)}, u32[]{:S(2)}) collective-permute-start(f32[120,512]{1,0:T(8,128)S(1)} %collective-permute-done.6.refs_2_), channel_id=1, source_target_pairs={{0,1},{1,0},{2,3},{3,2},{4,5},{5,4},{6,7},{7,6},{8,9},{9,8},{10,11... | collective-permute-start | bytes 737288 | tf_op jit(solution)/shard_map/ppermute | solution.py:220
  39.2 7.6 %collective-permute-start.11 = (f32[120,512]{1,0:T(8,128)S(1)}, f32[120,512]{1,0:T(8,128)S(1)}, u32[]{:S(2)}, u32[]{:S(2)}) collective-permute-start(f32[120,512]{1,0:T(8,128)S(1)} %collective-permute-done.7.refs_3_), channel_id=1, source_target_pairs={{0,1},{1,0},{2,3},{3,2},{4,5},{5,4},{6,7},{7,6},{8,9},{9,8},{10,11... | collective-permute-start | bytes 737288 | tf_op jit(solution)/shard_map/ppermute | solution.py:220
  40.5 6.3 %collective-permute-start.9 = (f32[120,512]{1,0:T(8,128)S(1)}, f32[120,512]{1,0:T(8,128)S(1)}, u32[]{:S(2)}, u32[]{:S(2)}) collective-permute-start(f32[120,512]{1,0:T(8,128)S(1)} %collective-permute-done.5.refs_1_), channel_id=1, source_target_pairs={{0,1},{1,0},{2,3},{3,2},{4,5},{5,4},{6,7},{7,6},{8,9},{9,8},{10,11... | collective-permute-start | bytes 737288 | tf_op jit(solution)/shard_map/ppermute | solution.py:220
  44.1 7.4 %collective-permute-start.13 = (f32[160,128]{1,0:T(8,128)S(1)}, f32[160,128]{1,0:T(8,128)S(1)}, u32[]{:S(2)}, u32[]{:S(2)}) collective-permute-start(f32[160,128]{1,0:T(8,128)S(1)} %add.20.token.refs_0_), channel_id=1, source_target_pairs={{0,16},{4,20},{8,24},{12,28},{16,0},{20,4},{24,8},{28,12},{1,17},{... | collective-permute-start | bytes 245768 | tf_op jit(solution)/shard_map/ppermute | solution.py:220
  50.2 23.0 %collective-permute-start.12 = (f32[192,512]{1,0:T(8,128)S(1)}, f32[192,512]{1,0:T(8,128)S(1)}, u32[]{:S(2)}, u32[]{:S(2)}) collective-permute-start(f32[192,512]{1,0:T(8,128)S(1)} %get-tuple-element.44), channel_id=1, source_target_pairs={{0,16},{4,20},{8,24},{12,28},{16,0},{20,4},{24,8},{28,12},{1,17},{... | collective-permute-start | bytes 1179656 | tf_op jit(solution)/shard_map/ppermute | solution.py:220
  56.9 5.3 %collective-permute-start.15 = (f32[320,128]{1,0:T(8,128)S(1)}, f32[320,128]{1,0:T(8,128)S(1)}, u32[]{:S(2)}, u32[]{:S(2)}) collective-permute-start(f32[320,128]{1,0:T(8,128)S(1)} %all_gather.7.a), channel_id=1, source_target_pairs={{0,2},{1,3},{2,0},{3,1},{4,6},{5,7},{6,4},{7,5},{8,10},{9,11},{10,... | collective-permute-start | bytes 491528 | tf_op jit(solution)/shard_map/ppermute | solution.py:220
  58.4 3.8 %collective-permute-start.14 = (f32[320,128]{1,0:T(8,128)S(1)}, f32[320,128]{1,0:T(8,128)S(1)}, u32[]{:S(2)}, u32[]{:S(2)}) collective-permute-start(f32[320,128]{1,0:T(8,128)S(1)} %all_gather.7.a), channel_id=1, source_target_pairs={{0,1},{1,0},{2,3},{3,2},{4,5},{5,4},{6,7},{7,6},{8,9},{9,8},{10,11... | collective-permute-start | bytes 491528 | tf_op jit(solution)/shard_map/ppermute | solution.py:220
  73.3 19.2 %collective-permute-start.19 = (f32[192,512]{1,0:T(8,128)S(1)}, f32[192,512]{1,0:T(8,128)S(1)}, u32[]{:S(2)}, u32[]{:S(2)}) collective-permute-start(f32[192,512]{1,0:T(8,128)S(1)} %add_after.5.token.own), channel_id=1, source_target_pairs={{0,8},{4,12},{8,0},{12,4},{16,24},{20,28},{24,16},{28,20},{1,9},{5... | collective-permute-start | bytes 1179656 | tf_op jit(solution)/shard_map/ppermute | solution.py:220
  74.0 18.4 %collective-permute-start.18 = (f32[192,512]{1,0:T(8,128)S(1)}, f32[192,512]{1,0:T(8,128)S(1)}, u32[]{:S(2)}, u32[]{:S(2)}) collective-permute-start(f32[192,512]{1,0:T(8,128)S(1)} %add_after.5.token.own), channel_id=1, source_target_pairs={{0,4},{4,0},{8,12},{12,8},{16,20},{20,16},{24,28},{28,24},{1,5},{5... | collective-permute-start | bytes 1179656 | tf_op jit(solution)/shard_map/ppermute | solution.py:220
  74.6 20.7 %collective-permute-start.17 = (f32[192,512]{1,0:T(8,128)S(1)}, f32[192,512]{1,0:T(8,128)S(1)}, u32[]{:S(2)}, u32[]{:S(2)}) collective-permute-start(f32[192,512]{1,0:T(8,128)S(1)} %add_after.5.token.own), channel_id=1, source_target_pairs={{0,16},{4,20},{8,24},{12,28},{16,0},{20,4},{24,8},{28,12},{1,17},{... | collective-permute-start | bytes 1179656 | tf_op jit(solution)/shard_map/ppermute | solution.py:220
  96.4 27.4 %collective-permute-start.20 = (f32[200,512]{1,0:T(8,128)S(1)}, f32[200,512]{1,0:T(8,128)S(1)}, u32[]{:S(2)}, u32[]{:S(2)}) collective-permute-start(f32[200,512]{1,0:T(8,128)S(1)} %norms.1.refs_0_.refs_4_), channel_id=1, source_target_pairs={{0,4},{4,0},{8,12},{12,8},{16,20},{20,16},{24,28},{28,24},{1,5},{5... | collective-permute-start | bytes 1228808 | tf_op jit(solution)/shard_map/ppermute | solution.py:220
  98.0 25.9 %collective-permute-start.21 = (f32[200,512]{1,0:T(8,128)S(1)}, f32[200,512]{1,0:T(8,128)S(1)}, u32[]{:S(2)}, u32[]{:S(2)}) collective-permute-start(f32[200,512]{1,0:T(8,128)S(1)} %norms.1.refs_0_.refs_4_), channel_id=1, source_target_pairs={{0,8},{4,12},{8,0},{12,4},{16,24},{20,28},{24,16},{28,20},{1,9},{5... | collective-permute-start | bytes 1228808 | tf_op jit(solution)/shard_map/ppermute | solution.py:220
  98.0 25.9 %collective-permute-start.22 = (f32[200,512]{1,0:T(8,128)S(1)}, f32[200,512]{1,0:T(8,128)S(1)}, u32[]{:S(2)}, u32[]{:S(2)}) collective-permute-start(f32[200,512]{1,0:T(8,128)S(1)} %norms.1.refs_0_.refs_4_), channel_id=1, source_target_pairs={{0,12},{4,8},{8,4},{12,0},{16,28},{20,24},{24,20},{28,16},{1,13},{... | collective-permute-start | bytes 1228808 | tf_op jit(solution)/shard_map/ppermute | solution.py:220
  100.0 19.7 %collective-permute-start.23 = (f32[96,512]{1,0:T(8,128)S(1)}, f32[96,512]{1,0:T(8,128)S(1)}, u32[]{:S(2)}, u32[]{:S(2)}) collective-permute-start(f32[96,512]{1,0:T(8,128)S(1)} %slice.8), channel_id=1, source_target_pairs={{0,4},{4,0},{8,12},{12,8},{16,20},{20,16},{24,28},{28,24},{1,5},{5... | collective-permute-start | bytes 589832 | tf_op jit(solution)/shard_map/ppermute | solution.py:220
  101.6 19.6 %collective-permute-start.24 = (f32[96,512]{1,0:T(8,128)S(1)}, f32[96,512]{1,0:T(8,128)S(1)}, u32[]{:S(2)}, u32[]{:S(2)}) collective-permute-start(f32[96,512]{1,0:T(8,128)S(1)} %slice.9), channel_id=1, source_target_pairs={{0,8},{4,12},{8,0},{12,4},{16,24},{20,28},{24,16},{28,20},{1,9},{5... | collective-permute-start | bytes 589832 | tf_op jit(solution)/shard_map/ppermute | solution.py:220
  125.2 4.3 %collective-permute-start.26 = (f32[1,512]{1,0:T(1,128)S(1)}, f32[1,512]{1,0:T(1,128)S(1)}, u32[]{:S(2)}, u32[]{:S(2)}) collective-permute-start(f32[1,512]{1,0:T(1,128)S(1)} %add.21), channel_id=1, source_target_pairs={{0,2},{1,3},{2,0},{3,1},{4,6},{5,7},{6,4},{7,5},{8,10},{9,11},{10,... | collective-permute-start | bytes 6152 | tf_op jit(solution)/shard_map/ppermute | solution.py:220
  (6 other events, 8.5 us)

commit v7 on v6

--- a/solution.py
+++ b/solution.py
@@ -26,11 +26,12 @@
 anywhere = pl.BlockSpec(memory_space=pl.ANY)
 
 
-def kernel(body, out_shape, in_specs, scratch, name, cost=0, out_specs=None):
+def kernel(body, out_shape, in_specs, scratch, name, cost=0, out_specs=None, aliases=None):
     extra = {} if out_specs is None else {"out_specs": out_specs}
     return pl.pallas_call(
         body,
         out_shape=out_shape,
+        input_output_aliases=aliases or {},
         **extra,
         in_specs=in_specs,
         scratch_shapes=scratch,
@@ -227,14 +228,9 @@
         piece[...] = momentum[:, at] + gradient[:, at].astype(jnp.float32)
 
 
-def part_left_kernel(bits, basis, *refs):
-    pieces, (sent, kept, total) = refs[:square], refs[square:]
-    width = pieces[0].shape[1]
+def part_left_kernel(bits, basis, momentum, gradient, token, sent, kept, total):
     half = sent.shape[0]
-    for k, piece in enumerate(pieces):
-        rows = pl.ds(pl.multiple_of((bits[2] ^ k) * width, lanes), width)
-        part = dot(piece[...], basis[rows, :])
-        total[...] = part if k == 0 else total[...] + part
+    total[...] = dot(momentum[...] + gradient[...].astype(jnp.float32), basis[...])
     sent[...] = total[pl.ds(pl.multiple_of((1 - bits[0]) * half, 8), half), :]
     kept[...] = total[pl.ds(pl.multiple_of(bits[0] * half, 8), half), :]
 
@@ -299,97 +295,111 @@
     own_right[...] = dot(own[...], inverse[...], ((1,), (1,)))
 
 
-def norm_kernel(own_right, received, inverse, one, two, out):
-    count = own_right.shape[0]
+def norm_kernel(own_right, received, inverse, one, two, out, squares):
     right = dot(received[...], inverse[...], ((1,), (1,)))
-    out[:count, :] = right
+    out[...] = right
     total = jnp.sum(right * right, axis=0, keepdims=True)
-    total = total + jnp.sum(own_right[...] * own_right[...], axis=0, keepdims=True)
-    row = lax.broadcasted_iota(jnp.int32, (8, own_right.shape[1]), 0)
-    out[count:, :] = jnp.where(row == 0, total, 0.0)
-
-
-def own_kernel(left, inverse, own_right, *refs):
-    rows, (rights, splits, products) = refs[:-3], refs[-3:]
+    squares[...] = total + jnp.sum(own_right[...] * own_right[...], axis=0, keepdims=True)
+
+
+def with_row(rows, squares, out):
+    count = rows.shape[0]
+    out[:count, :] = rows[...]
+    row = lax.broadcasted_iota(jnp.int32, (8, rows.shape[1]), 0)
+    out[count:, :] = jnp.where(row == 0, squares[...], 0.0)
+
+
+def pack_kernel(rows, squares, out):
+    with_row(rows, squares, out)
+
+
+def own_kernel(left, inverse, own_right, one, two, rights, splits, products):
     count = own_right.shape[0]
     rights[:count, :] = own_right[...]
-    for k, part in enumerate(rows):
+    for k, part in enumerate((one, two)):
         at = slice((k + 1) * count, (k + 2) * count)
         rights[at, :] = dot(part[...], inverse[...], ((1,), (1,)))
     splits[...] = three_right(rights[...])
     product = dot_three(three_left(left[...]), splits[...])
-    for k in range(len(rows) + 1):
+    for k in range(3):
         products[k] = product[:, k * count : (k + 1) * count]
 
 
-def diagonal_kernel(left, inverse, first, second, right, splits, product):
-    middle = first.shape[0]
-    right[:middle, :] = dot(first[...], inverse[...], ((1,), (1,)))
-    right[middle:, :] = dot(second[...], inverse[...], ((1,), (1,)))
-    splits[...] = three_right(right[...])
-    product[...] = dot_three(three_left(left[...]), splits[...])
-
-
-def momentum_kernel(bits, left, products, last_product, *refs):
-    pieces, received = refs[:square], refs[square : 2 * square]
-    new_momentum, splits, ready, sent = refs[-4:]
+def columns_of(bits, k, width):
+    return pl.ds(pl.multiple_of((bits[2] ^ k) * width, lanes), width)
+
+
+def in_order(bits, mine, other):
+    lower = jnp.concatenate([mine, other], axis=1)
+    return jnp.where(bits[4] == 0, lower, jnp.concatenate([other, mine], axis=1))
+
+
+def momentum_kernel(bits, left, rights, squares, products, *refs):
+    pieces, received, (new_momentum, splits, first, second, ready, sent) = refs[:3], refs[3:6], refs[6:]
     width = pieces[0].shape[1]
     half = width // 2
-    scaled = three_left(left[...])
+    middle = half // 2
+    with_row(rights.at[2 * half : 2 * half + middle], squares, first)
+    with_row(rights.at[half + middle : 2 * half], squares, second)
+    for k in range(3):
+        splits[k * half : (k + 1) * half, :] = three_right(received[k][...])
+    both = dot_three(three_left(left[...]), splits[...])
     copies = []
-    for k in range(square):
-        parts = slice(k * half, (k + 1) * half)
-        splits[parts, :] = three_right(received[k][:half, :])
-        if k % 2 == 0:
-            continue
-        both = dot_three(scaled, splits[(k - 1) * half : (k + 1) * half, :])
-        for i in (k - 1, k):
-            other = both[:, (i - k + 1) * half : (i - k + 2) * half]
-            mine = products[i] if i < square - 1 else last_product[...]
-            lower = jnp.concatenate([mine, other], axis=1)
-            upper = jnp.concatenate([other, mine], axis=1)
-            ready[i] = pieces[i][...] - 0.5 * jnp.where(bits[4] == 0, lower, upper)
-            at = pl.ds(pl.multiple_of((bits[2] ^ i) * width, lanes), width)
-            copies.append(pltpu.make_async_copy(ready.at[i], new_momentum.at[:, at], sent.at[i]))
-            copies[i].start()
+    for k in range(3):
+        other = both[:, k * half : (k + 1) * half]
+        ready[k] = pieces[k][...] - 0.5 * in_order(bits, products[k], other)
+        target = new_momentum.at[:, columns_of(bits, k, width)]
+        copies.append(pltpu.make_async_copy(ready.at[k], target, sent.at[k]))
+        copies[k].start()
     for copy in copies:
         copy.wait()
 
 
-def squares_kernel(row, *refs):
-    total = refs[0][row : row + 1, :]
-    for part in refs[1:square]:
-        total = total + part[row : row + 1, :]
-    refs[-1][...] = total
-
-
-def update_kernel(factor, bits, squares, left, rights, last_right, own_splits, last_split, splits, *refs):
-    received, (update, next_basis, ready, basis_ready, sent) = refs[:square], refs[square:]
-    half = basis_ready.shape[0]
-    width = 2 * half
-    norm = jnp.sqrt(squares[...] + epsilon)
+def last_kernel(factor, bits, squares, left, rights, own_splits, splits, *refs):
+    received, (first, second, piece, _, new_momentum, update, next_basis), scratch = (
+        refs[:square],
+        refs[square : square + 7],
+        refs[square + 7 :],
+    )
+    last_right, last_splits, ready, scaled_ready, basis_ready, sent = scratch
+    half, width = basis_ready.shape[0], piece.shape[1]
+    middle = half // 2
+    total = squares[...] + received[square - 1][half : half + 1, :]
+    total = total + first[middle : middle + 1, :] + second[middle : middle + 1, :]
+    norm = jnp.sqrt(total + epsilon)
+    copies = []
+
+    def send(source, target, index):
+        copies.append(pltpu.make_async_copy(source, target, sent.at[index]))
+        copies[-1].start()
+
+    last_right[:middle, :] = first[:middle, :]
+    last_right[middle:, :] = second[:middle, :]
+    last_splits[:half, :] = three_right(last_right[...])
+    last_splits[half:, :] = three_right(received[square - 1][:half, :])
+    both = dot_three(three_left(left[...]), last_splits[...])
+    ready[...] = piece[...] - 0.5 * in_order(bits, both[:, :half], both[:, half:])
+    send(ready, new_momentum.at[:, columns_of(bits, square - 1, width)], square)
     for k in range(square):
 
         @pl.when((bits[3] // 2) ^ bits[2] == k)
         def _():
-            mine_rows = rights[k * half : (k + 1) * half, :] if k < square - 1 else last_right[...]
-            rows = jnp.where(bits[3] % 2 == bits[4], mine_rows, received[k][:half, :])
-            basis_ready[...] = rows / norm
-
-    copies = [pltpu.make_async_copy(basis_ready, next_basis, sent.at[square])]
-    copies[0].start()
+            mine = rights[k * half : (k + 1) * half, :] if k < square - 1 else last_right[...]
+            mine = jnp.where(bits[3] % 2 == bits[4], mine, received[k][:half, :])
+            basis_ready[...] = mine / norm
+
+    send(basis_ready, next_basis, square + 1)
     scaled = three_left(left[...] * (factor / norm))
     for k in range(square):
-        parts = slice(k * half, (k + 1) * half)
-        mine = dot_three(scaled, own_splits[parts, :] if k < square - 1 else last_split[...])
-        other = dot_three(scaled, splits[parts, :])
-        lower = jnp.concatenate([mine, other], axis=1)
-        upper = jnp.concatenate([other, mine], axis=1)
-        ready[k] = jnp.where(bits[4] == 0, lower, upper).astype(jnp.bfloat16)
-        at = pl.ds(pl.multiple_of((bits[2] ^ k) * width, lanes), width)
-        copy = pltpu.make_async_copy(ready.at[k], update.at[:, at], sent.at[k])
-        copy.start()
-        copies.append(copy)
+        if k < square - 1:
+            parts = slice(k * half, (k + 1) * half)
+            mine = dot_three(scaled, own_splits[parts, :])
+            other = dot_three(scaled, splits[parts, :])
+        else:
+            both = dot_three(scaled, last_splits[...])
+            mine, other = both[:, :half], both[:, half:]
+        scaled_ready[k] = in_order(bits, mine, other).astype(jnp.bfloat16)
+        send(scaled_ready.at[k], update.at[:, columns_of(bits, k, width)], k)
     for copy in copies:
         copy.wait()
 
@@ -413,10 +423,10 @@
     sent, kept = kernel(
         part_left_kernel,
         [shape(half, rank)] * 2,
-        [smem] + [vmem] * (1 + square),
+        [smem] + [vmem] * 3 + [anywhere],
         [pltpu.VMEM((rows, rank), jnp.float32)],
         "part_left",
-    )(bits, right_basis, *pieces)
+    )(bits, right_basis, momentum, gradient, pieces[0])
     cores = [[i, i + 1] for i in range(0, lax.axis_size("tensor"), 2)]
     both = lax.all_gather(sent, "tensor", axis=0, tiled=True, axis_index_groups=cores)
     mine = kernel(core_add_kernel, shape(half, rank), [smem, vmem, vmem], [], "core_add")(
@@ -461,7 +471,7 @@
     factors.append(out)
     token = out
     for b in range(1, count):
-        if b == (count + 1) // 2:
+        if b == 1:
             own = add_after(kept, swap(sent, "fsdp", square), out)
             token = own
         out, work = later_step(b, work, token)
@@ -476,67 +486,73 @@
 
     received = swap(own, "fsdp", square)
     beside = [swap(own, "fsdp", k) for k in (1, 2)]
-    with_norms = kernel(
-        norm_kernel, shape(width // 2 + 8, rank), [vmem] * 3 + [anywhere] * 2, [], "norms"
+    half_width = width // 2
+    received_right, squares = kernel(
+        norm_kernel,
+        [shape(half_width, rank), shape(1, rank)],
+        [vmem] * 3 + [anywhere] * 2,
+        [],
+        "norms",
     )(own_right, received, inverse, *beside)
-    received_rows = [with_norms] + [swap(with_norms, "fsdp", k) for k in range(1, square)]
-    middle = width // 4
-    diagonal = [swap(beside[1][:middle], "fsdp", 1), swap(beside[0][middle:], "fsdp", 2)]
+    for flip in (1, 2):
+        squares = squares + swap(squares, "tensor", flip)
+    packed = kernel(pack_kernel, shape(half_width + 8, rank), [vmem] * 2, [], "pack")(
+        received_right, squares
+    )
+    received_rows = [received_right] + [swap(received_right, "fsdp", k) for k in (1, 2)]
+    received_rows += [swap(packed, "fsdp", 3)]
+
     rights, own_splits, products = kernel(
         own_kernel,
         [
-            shape(3 * (width // 2), rank),
-            shape(3 * (width // 2), 3 * rank, dtype=jnp.bfloat16),
-            shape(3, rows, width // 2),
+            shape(3 * half_width, rank),
+            shape(3 * half_width, 3 * rank, dtype=jnp.bfloat16),
+            shape(3, rows, half_width),
         ],
         [vmem] * 5,
         [],
         "own_part",
         cost=2**24,
     )(left, inverse, own_right, *beside)
-    last_right, last_split, last_product = kernel(
-        diagonal_kernel,
+
+    new_momentum, splits, first, second = kernel(
+        momentum_kernel,
         [
-            shape(width // 2, rank),
-            shape(width // 2, 3 * rank, dtype=jnp.bfloat16),
-            shape(rows, width // 2),
+            shape(rows, cols),
+            shape(3 * half_width, 3 * rank, dtype=jnp.bfloat16),
+            shape(half_width // 2 + 8, rank),
+            shape(half_width // 2 + 8, rank),
         ],
-        [vmem] * 4,
-        [],
-        "diagonal_part",
-        cost=2**22,
-    )(left, inverse, *diagonal)
-    squares = kernel(
-        functools.partial(squares_kernel, width // 2),
-        shape(1, rank),
-        [vmem] * square + [anywhere] * 2,
-        [],
-        "squares",
-    )(*received_rows, products, last_product)
-    squares = squares + swap(squares, "tensor", 1)
-    squares = squares + swap(squares, "tensor", 2)
-
-    new_momentum, splits = kernel(
-        momentum_kernel,
-        [shape(rows, cols), shape(cols // 2, 3 * rank, dtype=jnp.bfloat16)],
-        [smem] + [vmem] * (3 + 2 * square),
-        [pltpu.VMEM((square, rows, width), jnp.float32), pltpu.SemaphoreType.DMA((square,))],
+        [smem] + [vmem] * 10,
+        [pltpu.VMEM((3, rows, width), jnp.float32), pltpu.SemaphoreType.DMA((3,))],
         "new_momentum",
-        cost=2**22,
-        out_specs=[anywhere, vmem],
-    )(bits, left, products, last_product, *pieces, *received_rows)
-    update, next_basis = kernel(
-        functools.partial(update_kernel, math.sqrt(total_rows / total_cols)),
-        [shape(rows, cols, dtype=jnp.bfloat16), shape(cols // lax.axis_size("fsdp"), rank)],
-        [smem] + [vmem] * (7 + square),
+        cost=2**24,
+        out_specs=[anywhere] + [vmem] * 3,
+    )(bits, left, rights, squares, products, *pieces[:3], *received_rows[:3])
+    first, second = swap(first, "fsdp", 1), swap(second, "fsdp", 2)
+    new_momentum, update, next_basis = kernel(
+        functools.partial(last_kernel, math.sqrt(total_rows / total_cols)),
         [
+            shape(rows, cols),
+            shape(rows, cols, dtype=jnp.bfloat16),
+            shape(cols // lax.axis_size("fsdp"), rank),
+        ],
+        [smem] + [vmem] * (8 + square) + [anywhere],
+        [
+            pltpu.VMEM((half_width, rank), jnp.float32),
+            pltpu.VMEM((2 * half_width, 3 * rank), jnp.bfloat16),
+            pltpu.VMEM((rows, width), jnp.float32),
             pltpu.VMEM((square, rows, width), jnp.bfloat16),
-            pltpu.VMEM((width // 2, rank), jnp.float32),
-            pltpu.SemaphoreType.DMA((square + 1,)),
+            pltpu.VMEM((half_width, rank), jnp.float32),
+            pltpu.SemaphoreType.DMA((square + 2,)),
         ],
-        "update",
-        out_specs=[anywhere, anywhere],
-    )(bits, squares, left, rights, last_right, own_splits, last_split, splits, *received_rows)
+        "last",
+        out_specs=[anywhere] * 3,
+        aliases={9 + square: 0},
+    )(
+        *(bits, squares, left, rights, own_splits, splits, *received_rows),
+        *(first, second, pieces[3], new_momentum),
+    )
     return (update, new_momentum, left_scaled, next_basis)
 
 

time: 133 us -> 123 us (0.925)
  waiting for transfers between devices: 47.6 us -> 33.2 us
  starting transfers between devices: 26.7 us -> 33.8 us
  Pallas kernels: 45.5 us -> 42.6 us
    ppermute x27, waiting for transfers between devices: 47.6 us -> 33.2 us  [swap(): lax.ppermute(value, axis, [(i, i ^ flip) for i in range(lax.axis_size(axi...]
    ppermute x27, starting transfers between devices: 26.7 us -> 33.8 us  [swap(): lax.ppermute(value, axis, [(i, i ^ flip) for i in range(lax.axis_size(axi...]
    pallas_call x7 -> x6, Pallas kernels: 16.7 us -> 13.8 us  [the longest x1 3.95 us: in_squares(): kernel(functools.partial(last_kernel, math.sqrt(total_rows / total_cols))...]
where the time goes in v7:
time: 123 us
  Pallas kernels  42.6 us (35%)
  starting transfers between devices  33.8 us (27%)
  waiting for transfers between devices  33.2 us (27%)
  blocking collectives  7.46 us (6%)
  local copies, waits for them, and re-layouts  4.46 us (4%)
    ppermute x27, starting transfers between devices, swap(): lax.ppermute(value, axis, [(i, i ^ flip) for i in range(lax.axis_size(axi...  33.8 us
    ppermute x27, waiting for transfers between devices, swap(): lax.ppermute(value, axis, [(i, i ^ flip) for i in range(lax.axis_size(axi...  33.2 us
    pallas_call x3, Pallas kernels, later_step(): kernel(functools.partial(later_kernel, b), [shape(lanes, size), shape(siz...  14 us
    all_gather x1, blocking collectives, in_squares(): lax.all_gather(part, 'fsdp', axis=0, tiled=True, axis_index_groups=chips)  5.3 us
    pallas_call x1, Pallas kernels, first_step(): kernel(first_kernel, [shape(lanes, size), shape(size, size)], [smem] + [v...  5.07 us
    unnamed x6, local copies, waits for them, and re-layouts  4.38 us
    pallas_call x1, Pallas kernels, in_squares(): kernel(functools.partial(last_kernel, math.sqrt(total_rows / total_cols))...  3.95 us
    pallas_call x1, Pallas kernels, in_squares(): kernel(raw_kernel, [shape(width // 2, rank)] * 2, [smem, anywhere] + [vme...  3.42 us
  transfers between devices with their start and end apart: 27, of which 13 were waited for; matrix products, arithmetic and copies ran while one was open for 0% of the time, Pallas kernels for 30%

profile of v7, /device:TPU:0, one launch (start us, length us, event | category | flops | bytes accessed | tf_op | source)
XLA Modules:
  0.0 122.6 jit_solution(9868527869249866126)
XLA Ops:
  3.9 3.0 %collective-permute-start.1 = (f32[240,384]{1,0:T(8,128)S(1)}, f32[240,384]{1,0:T(8,128)S(1)}, u32[]{:S(2)}, u32[]{:S(2)}) collective-permute-start(f32[240,384]{1,0:T(8,128)S(1)} %get-tuple-element.40.refs_1_), channel_id=1, source_target_pairs={{0,4},{4,0},{8,12},{12,8},{16,20},{20,16},{24,28},{28,24},{1,5},{5... | collective-permute-start | bytes 1105928 | tf_op jit(solution)/shard_map/ppermute | solution.py:221
  10.4 3.4 %part_left.1 = (f32[120,512]{1,0:T(8,128)S(1)}, f32[120,512]{1,0:T(8,128)S(1)}) custom-call(s32[5]{0:T(128)S(1)} %stack.23.bits, f32[1536,512]{1,0:T(8,128)S(1)} %copy-done.1, f32[240,1536]{1,0:T(8,128)S(1)} %copy-done, bf16[240,1536]{1,0:T(8,128)(2,1)S(1)} %copy-done.2, f32[240,384]{1,0:T(8,128)S(1)} %get-tuple-element.37.token.refs_8_.refs_0_), custom_call_target="tpu_custom_call" | custom-call | tf_op jit(solution)/shard_map/part_left/pallas_call | solution.py:423
  13.8 2.2 %all_gather.6.both = f32[240,512]{1,0:T(8,128)S(1)} all-gather(f32[120,512]{1,0:T(8,128)S(1)} %get-tuple-element.39), channel_id=1, replica_groups={{0,1},{2,3},{4,5},{6,7},{8,9},{10,11},{12,13},{14,15},{16,17},{18,19},{..., dimensions={0}, use_global_device_ids=true | all-gather | bytes 737280 | tf_op jit(solution)/shard_map/all_gather | solution.py:431
  18.5 6.3 %collective-permute-done.refs_1_ = f32[120,512]{1,0:T(8,128)S(1)} collective-permute-done((f32[120,512]{1,0:T(8,128)S(1)}, f32[120,512]{1,0:T(8,128)S(1)}, u32[]{:S(2)}, u32[]{:S(2)}) %collective-permute-start) | collective-permute-done | bytes 245792 | tf_op jit(solution)/shard_map/ppermute | solution.py:221
  24.8 2.8 %collective-permute-start.7 = (f32[120,512]{1,0:T(8,128)S(1)}, f32[120,512]{1,0:T(8,128)S(1)}, u32[]{:S(2)}, u32[]{:S(2)}) collective-permute-start(f32[120,512]{1,0:T(8,128)S(1)} %add_after.3.refs_0_.mine), channel_id=1, source_target_pairs={{0,12},{4,8},{8,4},{12,0},{16,28},{20,24},{24,20},{28,16},{1,13},{... | collective-permute-start | bytes 737288 | tf_op jit(solution)/shard_map/ppermute | solution.py:221
  28.4 6.3 %collective-permute-done.7.refs_3_ = f32[120,512]{1,0:T(8,128)S(1)} collective-permute-done((f32[120,512]{1,0:T(8,128)S(1)}, f32[120,512]{1,0:T(8,128)S(1)}, u32[]{:S(2)}, u32[]{:S(2)}) %collective-permute-start.7) | collective-permute-done | bytes 245792 | tf_op jit(solution)/shard_map/ppermute | solution.py:221
  34.7 3.8 %collective-permute-done.6.refs_2_ = f32[120,512]{1,0:T(8,128)S(1)} collective-permute-done((f32[120,512]{1,0:T(8,128)S(1)}, f32[120,512]{1,0:T(8,128)S(1)}, u32[]{:S(2)}, u32[]{:S(2)}) %collective-permute-start.6) | collective-permute-done | bytes 245792 | tf_op jit(solution)/shard_map/ppermute | solution.py:221
  39.0 2.1 %part_gram.1 = (f32[160,128]{1,0:T(8,128)S(1)}, f32[160,128]{1,0:T(8,128)S(1)}) custom-call(s32[5]{0:T(128)S(1)} %stack.23.bits, f32[120,512]{1,0:T(8,128)S(1)} %add_after.3.refs_0_.mine, f32[120,512]{1,0:T(8,128)S(1)} %collective-permute-done.5.refs_1_, f32[120,512]{1,0:T(8,128)S(1)} %collective-permute-done.6.refs_2_, ...), custom_call_target="tpu_custom_call" | custom-call | tf_op jit(solution)/shard_map/part_gram/pallas_call | solution.py:442
  42.5 2.6 %collective-permute-start.13 = (f32[160,128]{1,0:T(8,128)S(1)}, f32[160,128]{1,0:T(8,128)S(1)}, u32[]{:S(2)}, u32[]{:S(2)}) collective-permute-start(f32[160,128]{1,0:T(8,128)S(1)} %add.20.token.refs_0_), channel_id=1, source_target_pairs={{0,16},{4,20},{8,24},{12,28},{16,0},{20,4},{24,8},{28,12},{1,17},{... | collective-permute-start | bytes 245768 | tf_op jit(solution)/shard_map/ppermute | solution.py:221
  45.2 3.4 %part_raw.1 = (f32[192,512]{1,0:T(8,128)S(1)}, f32[192,512]{1,0:T(8,128)S(1)}) custom-call(s32[5]{0:T(128)S(1)} %stack.23.bits, f32[160,128]{1,0:T(8,128)S(1)} %add.20.token.refs_0_, f32[120,512]{1,0:T(8,128)S(1)} %add_after.3.refs_0_.mine, f32[120,512]{1,0:T(8,128)S(1)} %collective-permute-done.5.refs_1_, f32[120,512]{1,0:T(8,128)S(1)} %collective-permute-done.6.refs_2_, ...), custom_call_target="tpu_custom_call" | custom-call | tf_op jit(solution)/shard_map/part_raw/pallas_call | solution.py:451
  49.7 5.3 %all_gather.7.a = f32[320,128]{1,0:T(8,128)S(1)} all-gather(f32[160,128]{1,0:T(8,128)S(1)} %add_after.4), channel_id=1, replica_groups={{0,4},{8,12},{16,20},{24,28},{1,5},{9,13},{17,21},{25,29},{2,6},{10,14}..., dimensions={0}, use_global_device_ids=true | all-gather | bytes 245760 | tf_op jit(solution)/shard_map/all_gather | solution.py:465
  56.5 3.8 %collective-permute-done.15.c = f32[320,128]{1,0:T(8,128)S(1)} collective-permute-done((f32[320,128]{1,0:T(8,128)S(1)}, f32[320,128]{1,0:T(8,128)S(1)}, u32[]{:S(2)}, u32[]{:S(2)}) %collective-permute-start.15) | collective-permute-done | bytes 163872 | tf_op jit(solution)/shard_map/ppermute | solution.py:221
  61.7 5.1 %factor_first.1 = (f32[128,512]{1,0:T(8,128)S(1)}, f32[512,512]{1,0:T(8,128)S(1)}) custom-call(s32[5]{0:T(128)S(1)} %stack.23.bits, f32[320,128]{1,0:T(8,128)S(1)} %all_gather.7.a, f32[320,128]{1,0:T(8,128)S(1)} %collective-permute-done.14.b, f32[320,128]{1,0:T(8,128)S(1)} %collective-permute-done.15.c, f32[320,128]{1,0:T(8,128)S(1)} %collective-permute-done.16.d), custom_call_target="tpu_custom_call" | custom-call | tf_op jit(solution)/shard_map/factor_first/pallas_call | solution.py:169
  72.2 4.6 %factor_later.3 = (f32[128,512]{1,0:T(8,128)S(1)}, f32[512,512]{1,0:T(8,128)S(1)}) custom-call(f32[512,512]{1,0:T(8,128)S(1)} %get-tuple-element.48.before, f32[192,512]{1,0:T(8,128)S(1)} %add_after.5.token.own), custom_call_target="tpu_custom_call" | custom-call | tf_op jit(solution)/shard_map/factor_later/pallas_call | solution.py:185
  76.8 4.3 %factor_later.4 = (f32[128,512]{1,0:T(8,128)S(1)}, f32[512,512]{1,0:T(8,128)S(1)}) custom-call(f32[512,512]{1,0:T(8,128)S(1)} %get-tuple-element.50.before, f32[192,512]{1,0:T(8,128)S(1)} %add_after.5.token.own), custom_call_target="tpu_custom_call" | custom-call | tf_op jit(solution)/shard_map/factor_later/pallas_call | solution.py:185
  81.1 5.2 %factor_later.5 = (f32[128,512]{1,0:T(8,128)S(1)}, f32[512,512]{1,0:T(8,128)}) custom-call(f32[512,512]{1,0:T(8,128)S(1)} %get-tuple-element.52.before, f32[192,512]{1,0:T(8,128)S(1)} %add_after.5.token.own), custom_call_target="tpu_custom_call" | custom-call | tf_op jit(solution)/shard_map/factor_later/pallas_call | solution.py:185
  86.3 2.9 %left.1 = (f32[240,512]{1,0:T(8,128)S(1)}, f32[240,512]{1,0:T(8,128)}, f32[512,512]{1,0:T(8,128)S(1)}, f32[192,512]{1,0:T(8,128)S(1)}) custom-call(s32[5]{0:T(128)S(1)} %stack.23.bits, f32[120,512]{1,0:T(8,128)S(1)} %add_after.3.refs_0_.mine, f32[120,512]{1,0:T(8,128)S(1)} %collective-permute-done.4.refs_4_.other, f32[192,512]{1,0:T(8,128)S(1)} %add_after.5.token.own, ...), custom_call_target="tpu_custom_call" | custom-call | tf_op jit(solution)/shard_map/left/pallas_call | solution.py:479
  94.3 2.1 %collective-permute-done.21 = f32[1,512]{1,0:T(1,128)S(1)} collective-permute-done((f32[1,512]{1,0:T(1,128)S(1)}, f32[1,512]{1,0:T(1,128)S(1)}, u32[]{:S(2)}, u32[]{:S(2)}) %collective-permute-start.21) | collective-permute-done | bytes 2080 | tf_op jit(solution)/shard_map/ppermute | solution.py:221
  96.4 2.8 %collective-permute-start.24 = (f32[200,512]{1,0:T(8,128)S(1)}, f32[200,512]{1,0:T(8,128)S(1)}, u32[]{:S(2)}, u32[]{:S(2)}) collective-permute-start(f32[200,512]{1,0:T(8,128)S(1)} %pack.1), channel_id=1, source_target_pairs={{0,12},{4,8},{8,4},{12,0},{16,28},{20,24},{24,20},{28,16},{1,13},{... | collective-permute-start | bytes 1228808 | tf_op jit(solution)/shard_map/ppermute | solution.py:221
  99.3 2.9 %own_part.1 = (f32[576,512]{1,0:T(8,128)S(1)}, bf16[576,1536]{1,0:T(8,128)(2,1)S(1)}, f32[3,240,192]{2,1,0:T(8,128)S(1)}) custom-call(f32[240,512]{1,0:T(8,128)S(1)} %get-tuple-element.57.left, f32[512,512]{1,0:T(8,128)S(1)} %get-tuple-element.55.inverse, f32[192,512]{1,0:T(8,128)S(1)} %get-tuple-element.54.own_right, ...), custom_call_target="tpu_custom_call" | custom-call | bytes 16777216 | tf_op jit(solution)/shard_map/own_part/pallas_call | solution.py:505
  102.2 2.4 %new_momentum.1 = (f32[240,1536]{1,0:T(8,128)}, bf16[576,1536]{1,0:T(8,128)(2,1)S(1)}, f32[104,512]{1,0:T(8,128)S(1)}, f32[104,512]{1,0:T(8,128)S(1)}) custom-call(s32[5]{0:T(128)S(1)} %stack.23.bits, f32[240,512]{1,0:T(8,128)S(1)} %get-tuple-element.57.left, f32[576,512]{1,0:T(8,128)S(1)} %get-tuple-element.58.rights, f32[1,512]{1,0:T(1,128)S(1)} %add.22.squares, ...), custom_call_target="tpu_custom_call" | custom-call | bytes 16777216 | tf_op jit(solution)/shard_map/new_momentum/pallas_call | solution.py:518
  105.4 9.2 %collective-permute-start.26 = (f32[104,512]{1,0:T(8,128)S(1)}, f32[104,512]{1,0:T(8,128)S(1)}, u32[]{:S(2)}, u32[]{:S(2)}) collective-permute-start(f32[104,512]{1,0:T(8,128)S(1)} %get-tuple-element.64), channel_id=1, source_target_pairs={{0,8},{4,12},{8,0},{12,4},{16,24},{20,28},{24,16},{28,20},{1,9},{5... | collective-permute-start | bytes 638984 | tf_op jit(solution)/shard_map/ppermute | solution.py:221
  114.6 3.8 %collective-permute-done.26.refs_5_ = f32[104,512]{1,0:T(8,128)S(1)} collective-permute-done((f32[104,512]{1,0:T(8,128)S(1)}, f32[104,512]{1,0:T(8,128)S(1)}, u32[]{:S(2)}, u32[]{:S(2)}) %collective-permute-start.26) | collective-permute-done | bytes 213024 | tf_op jit(solution)/shard_map/ppermute | solution.py:221
  118.5 3.9 %last.1 = (f32[240,1536]{1,0:T(8,128)}, bf16[240,1536]{1,0:T(8,128)(2,1)}, f32[192,512]{1,0:T(8,128)}) custom-call(s32[5]{0:T(128)S(1)} %stack.23.bits, f32[1,512]{1,0:T(1,128)S(1)} %add.22.squares, f32[240,512]{1,0:T(8,128)S(1)} %get-tuple-element.57.left, f32[576,512]{1,0:T(8,128)S(1)} %get-tuple-element.58.rights, ...), custom_call_target="tpu_custom_call", output_to_operand_aliasing={{0}: (13, {})} | custom-call | tf_op jit(solution)/shard_map/last/pallas_call | solution.py:533
  (60 shorter events, 27.5 us)
Async XLA Ops:
  3.9 20.8 %collective-permute-start.1 = (f32[240,384]{1,0:T(8,128)S(1)}, f32[240,384]{1,0:T(8,128)S(1)}, u32[]{:S(2)}, u32[]{:S(2)}) collective-permute-start(f32[240,384]{1,0:T(8,128)S(1)} %get-tuple-element.40.refs_1_), channel_id=1, source_target_pairs={{0,4},{4,0},{8,12},{12,8},{16,20},{20,16},{24,28},{28,24},{1,5},{5... | collective-permute-start | bytes 1105928 | tf_op jit(solution)/shard_map/ppermute | solution.py:221
  6.9 17.9 %collective-permute-start.2 = (f32[240,384]{1,0:T(8,128)S(1)}, f32[240,384]{1,0:T(8,128)S(1)}, u32[]{:S(2)}, u32[]{:S(2)}) collective-permute-start(f32[240,384]{1,0:T(8,128)S(1)} %get-tuple-element.41.refs_2_), channel_id=1, source_target_pairs={{0,8},{4,12},{8,0},{12,4},{16,24},{20,28},{24,16},{28,20},{1,9},{5... | collective-permute-start | bytes 1105928 | tf_op jit(solution)/shard_map/ppermute | solution.py:221
  8.5 16.3 %collective-permute-start.3 = (f32[240,384]{1,0:T(8,128)S(1)}, f32[240,384]{1,0:T(8,128)S(1)}, u32[]{:S(2)}, u32[]{:S(2)}) collective-permute-start(f32[240,384]{1,0:T(8,128)S(1)} %get-tuple-element.42.refs_6_), channel_id=1, source_target_pairs={{0,12},{4,8},{8,4},{12,0},{16,28},{20,24},{24,20},{28,16},{1,13},{... | collective-permute-start | bytes 1105928 | tf_op jit(solution)/shard_map/ppermute | solution.py:221
  16.5 8.3 %collective-permute-start = (f32[120,512]{1,0:T(8,128)S(1)}, f32[120,512]{1,0:T(8,128)S(1)}, u32[]{:S(2)}, u32[]{:S(2)}) collective-permute-start(f32[120,512]{1,0:T(8,128)S(1)} %core_add.1.refs_0_), channel_id=1, source_target_pairs={{0,2},{1,3},{2,0},{3,1},{4,6},{5,7},{6,4},{7,5},{8,10},{9,11},{10,... | collective-permute-start | bytes 737288 | tf_op jit(solution)/shard_map/ppermute | solution.py:221
  24.8 9.9 %collective-permute-start.7 = (f32[120,512]{1,0:T(8,128)S(1)}, f32[120,512]{1,0:T(8,128)S(1)}, u32[]{:S(2)}, u32[]{:S(2)}) collective-permute-start(f32[120,512]{1,0:T(8,128)S(1)} %add_after.3.refs_0_.mine), channel_id=1, source_target_pairs={{0,12},{4,8},{8,4},{12,0},{16,28},{20,24},{24,20},{28,16},{1,13},{... | collective-permute-start | bytes 737288 | tf_op jit(solution)/shard_map/ppermute | solution.py:221
  27.6 10.9 %collective-permute-start.6 = (f32[120,512]{1,0:T(8,128)S(1)}, f32[120,512]{1,0:T(8,128)S(1)}, u32[]{:S(2)}, u32[]{:S(2)}) collective-permute-start(f32[120,512]{1,0:T(8,128)S(1)} %add_after.3.refs_0_.mine), channel_id=1, source_target_pairs={{0,8},{4,12},{8,0},{12,4},{16,24},{20,28},{24,16},{28,20},{1,9},{5... | collective-permute-start | bytes 737288 | tf_op jit(solution)/shard_map/ppermute | solution.py:221
  28.1 10.5 %collective-permute-start.5 = (f32[120,512]{1,0:T(8,128)S(1)}, f32[120,512]{1,0:T(8,128)S(1)}, u32[]{:S(2)}, u32[]{:S(2)}) collective-permute-start(f32[120,512]{1,0:T(8,128)S(1)} %add_after.3.refs_0_.mine), channel_id=1, source_target_pairs={{0,4},{4,0},{8,12},{12,8},{16,20},{20,16},{24,28},{28,24},{1,5},{5... | collective-permute-start | bytes 737288 | tf_op jit(solution)/shard_map/ppermute | solution.py:221
  28.4 16.7 %collective-permute-start.4 = (f32[120,512]{1,0:T(8,128)S(1)}, f32[120,512]{1,0:T(8,128)S(1)}, u32[]{:S(2)}, u32[]{:S(2)}) collective-permute-start(f32[120,512]{1,0:T(8,128)S(1)} %add_after.3.refs_0_.mine), channel_id=1, source_target_pairs={{0,1},{1,0},{2,3},{3,2},{4,5},{5,4},{6,7},{7,6},{8,9},{9,8},{10,11... | collective-permute-start | bytes 737288 | tf_op jit(solution)/shard_map/ppermute | solution.py:221
  34.7 10.4 %collective-permute-start.11 = (f32[120,512]{1,0:T(8,128)S(1)}, f32[120,512]{1,0:T(8,128)S(1)}, u32[]{:S(2)}, u32[]{:S(2)}) collective-permute-start(f32[120,512]{1,0:T(8,128)S(1)} %collective-permute-done.7.refs_3_), channel_id=1, source_target_pairs={{0,1},{1,0},{2,3},{3,2},{4,5},{5,4},{6,7},{7,6},{8,9},{9,8},{10,11... | collective-permute-start | bytes 737288 | tf_op jit(solution)/shard_map/ppermute | solution.py:221
  38.5 6.6 %collective-permute-start.10 = (f32[120,512]{1,0:T(8,128)S(1)}, f32[120,512]{1,0:T(8,128)S(1)}, u32[]{:S(2)}, u32[]{:S(2)}) collective-permute-start(f32[120,512]{1,0:T(8,128)S(1)} %collective-permute-done.6.refs_2_), channel_id=1, source_target_pairs={{0,1},{1,0},{2,3},{3,2},{4,5},{5,4},{6,7},{7,6},{8,9},{9,8},{10,11... | collective-permute-start | bytes 737288 | tf_op jit(solution)/shard_map/ppermute | solution.py:221
  38.5 6.6 %collective-permute-start.9 = (f32[120,512]{1,0:T(8,128)S(1)}, f32[120,512]{1,0:T(8,128)S(1)}, u32[]{:S(2)}, u32[]{:S(2)}) collective-permute-start(f32[120,512]{1,0:T(8,128)S(1)} %collective-permute-done.5.refs_1_), channel_id=1, source_target_pairs={{0,1},{1,0},{2,3},{3,2},{4,5},{5,4},{6,7},{7,6},{8,9},{9,8},{10,11... | collective-permute-start | bytes 737288 | tf_op jit(solution)/shard_map/ppermute | solution.py:221
  42.5 7.2 %collective-permute-start.13 = (f32[160,128]{1,0:T(8,128)S(1)}, f32[160,128]{1,0:T(8,128)S(1)}, u32[]{:S(2)}, u32[]{:S(2)}) collective-permute-start(f32[160,128]{1,0:T(8,128)S(1)} %add.20.token.refs_0_), channel_id=1, source_target_pairs={{0,16},{4,20},{8,24},{12,28},{16,0},{20,4},{24,8},{28,12},{1,17},{... | collective-permute-start | bytes 245768 | tf_op jit(solution)/shard_map/ppermute | solution.py:221
  48.6 20.3 %collective-permute-start.12 = (f32[192,512]{1,0:T(8,128)S(1)}, f32[192,512]{1,0:T(8,128)S(1)}, u32[]{:S(2)}, u32[]{:S(2)}) collective-permute-start(f32[192,512]{1,0:T(8,128)S(1)} %get-tuple-element.46), channel_id=1, source_target_pairs={{0,16},{4,20},{8,24},{12,28},{16,0},{20,4},{24,8},{28,12},{1,17},{... | collective-permute-start | bytes 1179656 | tf_op jit(solution)/shard_map/ppermute | solution.py:221
  55.0 5.3 %collective-permute-start.15 = (f32[320,128]{1,0:T(8,128)S(1)}, f32[320,128]{1,0:T(8,128)S(1)}, u32[]{:S(2)}, u32[]{:S(2)}) collective-permute-start(f32[320,128]{1,0:T(8,128)S(1)} %all_gather.7.a), channel_id=1, source_target_pairs={{0,2},{1,3},{2,0},{3,1},{4,6},{5,7},{6,4},{7,5},{8,10},{9,11},{10,... | collective-permute-start | bytes 491528 | tf_op jit(solution)/shard_map/ppermute | solution.py:221
  56.5 3.8 %collective-permute-start.14 = (f32[320,128]{1,0:T(8,128)S(1)}, f32[320,128]{1,0:T(8,128)S(1)}, u32[]{:S(2)}, u32[]{:S(2)}) collective-permute-start(f32[320,128]{1,0:T(8,128)S(1)} %all_gather.7.a), channel_id=1, source_target_pairs={{0,1},{1,0},{2,3},{3,2},{4,5},{5,4},{6,7},{7,6},{8,9},{9,8},{10,11... | collective-permute-start | bytes 491528 | tf_op jit(solution)/shard_map/ppermute | solution.py:221
  68.9 20.2 %collective-permute-start.19 = (f32[192,512]{1,0:T(8,128)S(1)}, f32[192,512]{1,0:T(8,128)S(1)}, u32[]{:S(2)}, u32[]{:S(2)}) collective-permute-start(f32[192,512]{1,0:T(8,128)S(1)} %add_after.5.token.own), channel_id=1, source_target_pairs={{0,8},{4,12},{8,0},{12,4},{16,24},{20,28},{24,16},{28,20},{1,9},{5... | collective-permute-start | bytes 1179656 | tf_op jit(solution)/shard_map/ppermute | solution.py:221
  69.0 20.2 %collective-permute-start.18 = (f32[192,512]{1,0:T(8,128)S(1)}, f32[192,512]{1,0:T(8,128)S(1)}, u32[]{:S(2)}, u32[]{:S(2)}) collective-permute-start(f32[192,512]{1,0:T(8,128)S(1)} %add_after.5.token.own), channel_id=1, source_target_pairs={{0,4},{4,0},{8,12},{12,8},{16,20},{20,16},{24,28},{28,24},{1,5},{5... | collective-permute-start | bytes 1179656 | tf_op jit(solution)/shard_map/ppermute | solution.py:221
  70.3 19.3 %collective-permute-start.17 = (f32[192,512]{1,0:T(8,128)S(1)}, f32[192,512]{1,0:T(8,128)S(1)}, u32[]{:S(2)}, u32[]{:S(2)}) collective-permute-start(f32[192,512]{1,0:T(8,128)S(1)} %add_after.5.token.own), channel_id=1, source_target_pairs={{0,16},{4,20},{8,24},{12,28},{16,0},{20,4},{24,8},{28,12},{1,17},{... | collective-permute-start | bytes 1179656 | tf_op jit(solution)/shard_map/ppermute | solution.py:221
  90.8 11.3 %collective-permute-start.23 = (f32[192,512]{1,0:T(8,128)S(1)}, f32[192,512]{1,0:T(8,128)S(1)}, u32[]{:S(2)}, u32[]{:S(2)}) collective-permute-start(f32[192,512]{1,0:T(8,128)S(1)} %get-tuple-element.61.refs_3_.rows.refs_0_), channel_id=1, source_target_pairs={{0,8},{4,12},{8,0},{12,4},{16,24},{20,28},{24,16},{28,20},{1,9},{5... | collective-permute-start | bytes 1179656 | tf_op jit(solution)/shard_map/ppermute | solution.py:221
  90.9 11.3 %collective-permute-start.22 = (f32[192,512]{1,0:T(8,128)S(1)}, f32[192,512]{1,0:T(8,128)S(1)}, u32[]{:S(2)}, u32[]{:S(2)}) collective-permute-start(f32[192,512]{1,0:T(8,128)S(1)} %get-tuple-element.61.refs_3_.rows.refs_0_), channel_id=1, source_target_pairs={{0,4},{4,0},{8,12},{12,8},{16,20},{20,16},{24,28},{28,24},{1,5},{5... | collective-permute-start | bytes 1179656 | tf_op jit(solution)/shard_map/ppermute | solution.py:221
  92.8 3.6 %collective-permute-start.21 = (f32[1,512]{1,0:T(1,128)S(1)}, f32[1,512]{1,0:T(1,128)S(1)}, u32[]{:S(2)}, u32[]{:S(2)}) collective-permute-start(f32[1,512]{1,0:T(1,128)S(1)} %add.21), channel_id=1, source_target_pairs={{0,2},{1,3},{2,0},{3,1},{4,6},{5,7},{6,4},{7,5},{8,10},{9,11},{10,... | collective-permute-start | bytes 6152 | tf_op jit(solution)/shard_map/ppermute | solution.py:221
  96.4 18.2 %collective-permute-start.24 = (f32[200,512]{1,0:T(8,128)S(1)}, f32[200,512]{1,0:T(8,128)S(1)}, u32[]{:S(2)}, u32[]{:S(2)}) collective-permute-start(f32[200,512]{1,0:T(8,128)S(1)} %pack.1), channel_id=1, source_target_pairs={{0,12},{4,8},{8,4},{12,0},{16,28},{20,24},{24,20},{28,16},{1,13},{... | collective-permute-start | bytes 1228808 | tf_op jit(solution)/shard_map/ppermute | solution.py:221
  104.6 10.1 %collective-permute-start.25 = (f32[104,512]{1,0:T(8,128)S(1)}, f32[104,512]{1,0:T(8,128)S(1)}, u32[]{:S(2)}, u32[]{:S(2)}) collective-permute-start(f32[104,512]{1,0:T(8,128)S(1)} %get-tuple-element.63), channel_id=1, source_target_pairs={{0,4},{4,0},{8,12},{12,8},{16,20},{20,16},{24,28},{28,24},{1,5},{5... | collective-permute-start | bytes 638984 | tf_op jit(solution)/shard_map/ppermute | solution.py:221
  105.4 13.1 %collective-permute-start.26 = (f32[104,512]{1,0:T(8,128)S(1)}, f32[104,512]{1,0:T(8,128)S(1)}, u32[]{:S(2)}, u32[]{:S(2)}) collective-permute-start(f32[104,512]{1,0:T(8,128)S(1)} %get-tuple-element.64), channel_id=1, source_target_pairs={{0,8},{4,12},{8,0},{12,4},{16,24},{20,28},{24,16},{28,20},{1,9},{5... | collective-permute-start | bytes 638984 | tf_op jit(solution)/shard_map/ppermute | solution.py:221
  (6 other events, 8.3 us)

commit v8 on v7

--- a/solution.py
+++ b/solution.py
@@ -302,23 +302,23 @@
     squares[...] = total + jnp.sum(own_right[...] * own_right[...], axis=0, keepdims=True)
 
 
-def with_row(rows, squares, out):
-    count = rows.shape[0]
-    out[:count, :] = rows[...]
-    row = lax.broadcasted_iota(jnp.int32, (8, rows.shape[1]), 0)
-    out[count:, :] = jnp.where(row == 0, squares[...], 0.0)
-
-
-def pack_kernel(rows, squares, out):
-    with_row(rows, squares, out)
-
-
-def own_kernel(left, inverse, own_right, one, two, rights, splits, products):
+def forward_kernel(one, two, squares, one_here, two_here, first, second):
+    middle = second.shape[0]
+    first[:middle, :] = two[:middle, :]
+    row = lax.broadcasted_iota(jnp.int32, (8, two.shape[1]), 0)
+    first[middle:, :] = jnp.where(row == 0, squares[...], 0.0)
+    second[...] = one[middle:, :]
+
+
+def own_kernel(left, inverse, own_right, one, two, rights, first, second, splits, products):
     count = own_right.shape[0]
+    middle = count // 2
     rights[:count, :] = own_right[...]
     for k, part in enumerate((one, two)):
         at = slice((k + 1) * count, (k + 2) * count)
         rights[at, :] = dot(part[...], inverse[...], ((1,), (1,)))
+    first[...] = rights[2 * count : 2 * count + middle, :]
+    second[...] = rights[count + middle : 2 * count, :]
     splits[...] = three_right(rights[...])
     product = dot_three(three_left(left[...]), splits[...])
     for k in range(3):
@@ -334,13 +334,10 @@
     return jnp.where(bits[4] == 0, lower, jnp.concatenate([other, mine], axis=1))
 
 
-def momentum_kernel(bits, left, rights, squares, products, *refs):
-    pieces, received, (new_momentum, splits, first, second, ready, sent) = refs[:3], refs[3:6], refs[6:]
+def momentum_kernel(bits, left, products, *refs):
+    pieces, received, (new_momentum, splits, ready, sent) = refs[:3], refs[3:6], refs[6:]
     width = pieces[0].shape[1]
     half = width // 2
-    middle = half // 2
-    with_row(rights.at[2 * half : 2 * half + middle], squares, first)
-    with_row(rights.at[half + middle : 2 * half], squares, second)
     for k in range(3):
         splits[k * half : (k + 1) * half, :] = three_right(received[k][...])
     both = dot_three(three_left(left[...]), splits[...])
@@ -356,27 +353,27 @@
 
 
 def last_kernel(factor, bits, squares, left, rights, own_splits, splits, *refs):
-    received, (first, second, piece, _, new_momentum, update, next_basis), scratch = (
-        refs[:square],
-        refs[square : square + 7],
-        refs[square + 7 :],
-    )
-    last_right, last_splits, ready, scaled_ready, basis_ready, sent = scratch
+    received, (own_first, own_second, first, second, piece, _, new_momentum, update, next_basis), scratch = (
+        refs[:3],
+        refs[3:12],
+        refs[12:],
+    )
+    last_own, last_received, last_splits, ready, scaled_ready, basis_ready, sent = scratch
     half, width = basis_ready.shape[0], piece.shape[1]
     middle = half // 2
-    total = squares[...] + received[square - 1][half : half + 1, :]
-    total = total + first[middle : middle + 1, :] + second[middle : middle + 1, :]
-    norm = jnp.sqrt(total + epsilon)
+    norm = jnp.sqrt(squares[...] + first[middle : middle + 1, :] + epsilon)
     copies = []
 
     def send(source, target, index):
         copies.append(pltpu.make_async_copy(source, target, sent.at[index]))
         copies[-1].start()
 
-    last_right[:middle, :] = first[:middle, :]
-    last_right[middle:, :] = second[:middle, :]
-    last_splits[:half, :] = three_right(last_right[...])
-    last_splits[half:, :] = three_right(received[square - 1][:half, :])
+    last_own[:middle, :] = own_first[...]
+    last_own[middle:, :] = own_second[...]
+    last_received[:middle, :] = first[:middle, :]
+    last_received[middle:, :] = second[...]
+    last_splits[:half, :] = three_right(last_own[...])
+    last_splits[half:, :] = three_right(last_received[...])
     both = dot_three(three_left(left[...]), last_splits[...])
     ready[...] = piece[...] - 0.5 * in_order(bits, both[:, :half], both[:, half:])
     send(ready, new_momentum.at[:, columns_of(bits, square - 1, width)], square)
@@ -384,9 +381,10 @@
 
         @pl.when((bits[3] // 2) ^ bits[2] == k)
         def _():
-            mine = rights[k * half : (k + 1) * half, :] if k < square - 1 else last_right[...]
-            mine = jnp.where(bits[3] % 2 == bits[4], mine, received[k][:half, :])
-            basis_ready[...] = mine / norm
+            last = k == square - 1
+            mine = last_own[...] if last else rights[k * half : (k + 1) * half, :]
+            other = last_received[...] if last else received[k][...]
+            basis_ready[...] = jnp.where(bits[3] % 2 == bits[4], mine, other) / norm
 
     send(basis_ready, next_basis, square + 1)
     scaled = three_left(left[...] * (factor / norm))
@@ -494,18 +492,17 @@
         [],
         "norms",
     )(own_right, received, inverse, *beside)
-    for flip in (1, 2):
-        squares = squares + swap(squares, "tensor", flip)
-    packed = kernel(pack_kernel, shape(half_width + 8, rank), [vmem] * 2, [], "pack")(
-        received_right, squares
-    )
     received_rows = [received_right] + [swap(received_right, "fsdp", k) for k in (1, 2)]
-    received_rows += [swap(packed, "fsdp", 3)]
-
-    rights, own_splits, products = kernel(
+    for axis, flip in (("tensor", 1), ("tensor", 2), ("fsdp", 2)):
+        squares = squares + swap(squares, axis, flip)
+
+    half_rows = shape(half_width // 2, rank)
+    rights, own_first, own_second, own_splits, products = kernel(
         own_kernel,
         [
             shape(3 * half_width, rank),
+            half_rows,
+            half_rows,
             shape(3 * half_width, 3 * rank, dtype=jnp.bfloat16),
             shape(3, rows, half_width),
         ],
@@ -514,22 +511,25 @@
         "own_part",
         cost=2**24,
     )(left, inverse, own_right, *beside)
-
-    new_momentum, splits, first, second = kernel(
+    own_first, own_second = swap(own_first, "fsdp", 1), swap(own_second, "fsdp", 2)
+    first, second = kernel(
+        forward_kernel,
+        [shape(half_width // 2 + 8, rank), half_rows],
+        [vmem] * 3 + [anywhere] * 2,
+        [],
+        "forward",
+    )(received_rows[1], received_rows[2], squares, own_first, own_second)
+    first, second = swap(first, "fsdp", 1), swap(second, "fsdp", 2)
+
+    new_momentum, splits = kernel(
         momentum_kernel,
-        [
-            shape(rows, cols),
-            shape(3 * half_width, 3 * rank, dtype=jnp.bfloat16),
-            shape(half_width // 2 + 8, rank),
-            shape(half_width // 2 + 8, rank),
-        ],
-        [smem] + [vmem] * 10,
+        [shape(rows, cols), shape(3 * half_width, 3 * rank, dtype=jnp.bfloat16)],
+        [smem] + [vmem] * 8,
         [pltpu.VMEM((3, rows, width), jnp.float32), pltpu.SemaphoreType.DMA((3,))],
         "new_momentum",
         cost=2**24,
-        out_specs=[anywhere] + [vmem] * 3,
-    )(bits, left, rights, squares, products, *pieces[:3], *received_rows[:3])
-    first, second = swap(first, "fsdp", 1), swap(second, "fsdp", 2)
+        out_specs=[anywhere, vmem],
+    )(bits, left, products, *pieces[:3], *received_rows)
     new_momentum, update, next_basis = kernel(
         functools.partial(last_kernel, math.sqrt(total_rows / total_cols)),
         [
@@ -537,8 +537,9 @@
             shape(rows, cols, dtype=jnp.bfloat16),
             shape(cols // lax.axis_size("fsdp"), rank),
         ],
-        [smem] + [vmem] * (8 + square) + [anywhere],
+        [smem] + [vmem] * 13 + [anywhere],
         [
+            pltpu.VMEM((half_width, rank), jnp.float32),
             pltpu.VMEM((half_width, rank), jnp.float32),
             pltpu.VMEM((2 * half_width, 3 * rank), jnp.bfloat16),
             pltpu.VMEM((rows, width), jnp.float32),
@@ -548,10 +549,10 @@
         ],
         "last",
         out_specs=[anywhere] * 3,
-        aliases={9 + square: 0},
+        aliases={14: 0},
     )(
         *(bits, squares, left, rights, own_splits, splits, *received_rows),
-        *(first, second, pieces[3], new_momentum),
+        *(own_first, own_second, first, second, pieces[3], new_momentum),
     )
     return (update, new_momentum, left_scaled, next_basis)
 

time: 123 us -> 117 us (0.951)
  starting transfers between devices: 33.8 us -> 25.6 us
  waiting for transfers between devices: 33.2 us -> 35.7 us
    ppermute x27 -> x29, starting transfers between devices: 33.8 us -> 25.6 us  [swap(): lax.ppermute(value, axis, [(i, i ^ flip) for i in range(lax.axis_size(axi...]
    ppermute x27 -> x29, waiting for transfers between devices: 33.2 us -> 35.7 us  [swap(): lax.ppermute(value, axis, [(i, i ^ flip) for i in range(lax.axis_size(axi...]
  transfers between devices with their start and end apart: 27 -> 29, of which waited for: 13 -> 13; matrix products, arithmetic and copies ran while one was open for 0% -> 0% of each run, Pallas kernels for 30% -> 31%
where the time goes in v8:
time: 117 us
  Pallas kernels  42.6 us (36%)
  waiting for transfers between devices  35.7 us (31%)
  starting transfers between devices  25.6 us (22%)
  blocking collectives  7.46 us (6%)
  local copies, waits for them, and re-layouts  4.46 us (4%)
    ppermute x29, waiting for transfers between devices, swap(): lax.ppermute(value, axis, [(i, i ^ flip) for i in range(lax.axis_size(axi...  35.7 us
    ppermute x29, starting transfers between devices, swap(): lax.ppermute(value, axis, [(i, i ^ flip) for i in range(lax.axis_size(axi...  25.6 us
    pallas_call x3, Pallas kernels, later_step(): kernel(functools.partial(later_kernel, b), [shape(lanes, size), shape(siz...  14 us
    all_gather x1, blocking collectives, in_squares(): lax.all_gather(part, 'fsdp', axis=0, tiled=True, axis_index_groups=chips)  5.3 us
    pallas_call x1, Pallas kernels, first_step(): kernel(first_kernel, [shape(lanes, size), shape(size, size)], [smem] + [v...  5.07 us
    unnamed x6, local copies, waits for them, and re-layouts  4.38 us
    pallas_call x1, Pallas kernels, in_squares(): kernel(functools.partial(last_kernel, math.sqrt(total_rows / total_cols))...  3.97 us
    pallas_call x1, Pallas kernels, in_squares(): kernel(raw_kernel, [shape(width // 2, rank)] * 2, [smem, anywhere] + [vme...  3.41 us
  transfers between devices with their start and end apart: 29, of which 13 were waited for; matrix products, arithmetic and copies ran while one was open for 0% of the time, Pallas kernels for 31%

profile of v8, /device:TPU:0, one launch (start us, length us, event | category | flops | bytes accessed | tf_op | source)
XLA Modules:
  0.0 116.9 jit_solution(3234907278189756346)
XLA Ops:
  3.9 3.0 %collective-permute-start.1 = (f32[240,384]{1,0:T(8,128)S(1)}, f32[240,384]{1,0:T(8,128)S(1)}, u32[]{:S(2)}, u32[]{:S(2)}) collective-permute-start(f32[240,384]{1,0:T(8,128)S(1)} %get-tuple-element.42.refs_1_), channel_id=1, source_target_pairs={{0,4},{4,0},{8,12},{12,8},{16,20},{20,16},{24,28},{28,24},{1,5},{5... | collective-permute-start | bytes 1105928 | tf_op jit(solution)/shard_map/ppermute | solution.py:221
  10.4 3.4 %part_left.1 = (f32[120,512]{1,0:T(8,128)S(1)}, f32[120,512]{1,0:T(8,128)S(1)}) custom-call(s32[5]{0:T(128)S(1)} %stack.23.bits, f32[1536,512]{1,0:T(8,128)S(1)} %copy-done.1, f32[240,1536]{1,0:T(8,128)S(1)} %copy-done, bf16[240,1536]{1,0:T(8,128)(2,1)S(1)} %copy-done.2, f32[240,384]{1,0:T(8,128)S(1)} %get-tuple-element.39.token.refs_8_.refs_0_), custom_call_target="tpu_custom_call" | custom-call | tf_op jit(solution)/shard_map/part_left/pallas_call | solution.py:421
  13.8 2.2 %all_gather.6.both = f32[240,512]{1,0:T(8,128)S(1)} all-gather(f32[120,512]{1,0:T(8,128)S(1)} %get-tuple-element.41), channel_id=1, replica_groups={{0,1},{2,3},{4,5},{6,7},{8,9},{10,11},{12,13},{14,15},{16,17},{18,19},{..., dimensions={0}, use_global_device_ids=true | all-gather | bytes 737280 | tf_op jit(solution)/shard_map/all_gather | solution.py:429
  18.5 6.3 %collective-permute-done.refs_1_ = f32[120,512]{1,0:T(8,128)S(1)} collective-permute-done((f32[120,512]{1,0:T(8,128)S(1)}, f32[120,512]{1,0:T(8,128)S(1)}, u32[]{:S(2)}, u32[]{:S(2)}) %collective-permute-start) | collective-permute-done | bytes 245792 | tf_op jit(solution)/shard_map/ppermute | solution.py:221
  24.8 2.8 %collective-permute-start.7 = (f32[120,512]{1,0:T(8,128)S(1)}, f32[120,512]{1,0:T(8,128)S(1)}, u32[]{:S(2)}, u32[]{:S(2)}) collective-permute-start(f32[120,512]{1,0:T(8,128)S(1)} %add_after.3.refs_0_.mine), channel_id=1, source_target_pairs={{0,12},{4,8},{8,4},{12,0},{16,28},{20,24},{24,20},{28,16},{1,13},{... | collective-permute-start | bytes 737288 | tf_op jit(solution)/shard_map/ppermute | solution.py:221
  28.4 6.3 %collective-permute-done.7.refs_3_ = f32[120,512]{1,0:T(8,128)S(1)} collective-permute-done((f32[120,512]{1,0:T(8,128)S(1)}, f32[120,512]{1,0:T(8,128)S(1)}, u32[]{:S(2)}, u32[]{:S(2)}) %collective-permute-start.7) | collective-permute-done | bytes 245792 | tf_op jit(solution)/shard_map/ppermute | solution.py:221
  34.7 3.8 %collective-permute-done.6.refs_2_ = f32[120,512]{1,0:T(8,128)S(1)} collective-permute-done((f32[120,512]{1,0:T(8,128)S(1)}, f32[120,512]{1,0:T(8,128)S(1)}, u32[]{:S(2)}, u32[]{:S(2)}) %collective-permute-start.6) | collective-permute-done | bytes 245792 | tf_op jit(solution)/shard_map/ppermute | solution.py:221
  39.0 2.1 %part_gram.1 = (f32[160,128]{1,0:T(8,128)S(1)}, f32[160,128]{1,0:T(8,128)S(1)}) custom-call(s32[5]{0:T(128)S(1)} %stack.23.bits, f32[120,512]{1,0:T(8,128)S(1)} %add_after.3.refs_0_.mine, f32[120,512]{1,0:T(8,128)S(1)} %collective-permute-done.5.refs_1_, f32[120,512]{1,0:T(8,128)S(1)} %collective-permute-done.6.refs_2_, ...), custom_call_target="tpu_custom_call" | custom-call | tf_op jit(solution)/shard_map/part_gram/pallas_call | solution.py:440
  42.5 2.6 %collective-permute-start.13 = (f32[160,128]{1,0:T(8,128)S(1)}, f32[160,128]{1,0:T(8,128)S(1)}, u32[]{:S(2)}, u32[]{:S(2)}) collective-permute-start(f32[160,128]{1,0:T(8,128)S(1)} %add.23.token.refs_0_), channel_id=1, source_target_pairs={{0,16},{4,20},{8,24},{12,28},{16,0},{20,4},{24,8},{28,12},{1,17},{... | collective-permute-start | bytes 245768 | tf_op jit(solution)/shard_map/ppermute | solution.py:221
  45.2 3.4 %part_raw.1 = (f32[192,512]{1,0:T(8,128)S(1)}, f32[192,512]{1,0:T(8,128)S(1)}) custom-call(s32[5]{0:T(128)S(1)} %stack.23.bits, f32[160,128]{1,0:T(8,128)S(1)} %add.23.token.refs_0_, f32[120,512]{1,0:T(8,128)S(1)} %add_after.3.refs_0_.mine, f32[120,512]{1,0:T(8,128)S(1)} %collective-permute-done.5.refs_1_, f32[120,512]{1,0:T(8,128)S(1)} %collective-permute-done.6.refs_2_, ...), custom_call_target="tpu_custom_call" | custom-call | tf_op jit(solution)/shard_map/part_raw/pallas_call | solution.py:449
  49.7 5.3 %all_gather.7.a = f32[320,128]{1,0:T(8,128)S(1)} all-gather(f32[160,128]{1,0:T(8,128)S(1)} %add_after.4), channel_id=1, replica_groups={{0,4},{8,12},{16,20},{24,28},{1,5},{9,13},{17,21},{25,29},{2,6},{10,14}..., dimensions={0}, use_global_device_ids=true | all-gather | bytes 245760 | tf_op jit(solution)/shard_map/all_gather | solution.py:463
  56.5 3.8 %collective-permute-done.15.c = f32[320,128]{1,0:T(8,128)S(1)} collective-permute-done((f32[320,128]{1,0:T(8,128)S(1)}, f32[320,128]{1,0:T(8,128)S(1)}, u32[]{:S(2)}, u32[]{:S(2)}) %collective-permute-start.15) | collective-permute-done | bytes 163872 | tf_op jit(solution)/shard_map/ppermute | solution.py:221
  61.7 5.1 %factor_first.1 = (f32[128,512]{1,0:T(8,128)S(1)}, f32[512,512]{1,0:T(8,128)S(1)}) custom-call(s32[5]{0:T(128)S(1)} %stack.23.bits, f32[320,128]{1,0:T(8,128)S(1)} %all_gather.7.a, f32[320,128]{1,0:T(8,128)S(1)} %collective-permute-done.14.b, f32[320,128]{1,0:T(8,128)S(1)} %collective-permute-done.15.c, f32[320,128]{1,0:T(8,128)S(1)} %collective-permute-done.16.d), custom_call_target="tpu_custom_call" | custom-call | tf_op jit(solution)/shard_map/factor_first/pallas_call | solution.py:169
  66.8 2.1 %collective-permute-done.12.refs_1_ = f32[192,512]{1,0:T(8,128)S(1)} collective-permute-done((f32[192,512]{1,0:T(8,128)S(1)}, f32[192,512]{1,0:T(8,128)S(1)}, u32[]{:S(2)}, u32[]{:S(2)}) %collective-permute-start.12) | collective-permute-done | bytes 393248 | tf_op jit(solution)/shard_map/ppermute | solution.py:221
  72.3 4.6 %factor_later.3 = (f32[128,512]{1,0:T(8,128)S(1)}, f32[512,512]{1,0:T(8,128)S(1)}) custom-call(f32[512,512]{1,0:T(8,128)S(1)} %get-tuple-element.50.before, f32[192,512]{1,0:T(8,128)S(1)} %add_after.5.token.own), custom_call_target="tpu_custom_call" | custom-call | tf_op jit(solution)/shard_map/factor_later/pallas_call | solution.py:185
  76.8 4.3 %factor_later.4 = (f32[128,512]{1,0:T(8,128)S(1)}, f32[512,512]{1,0:T(8,128)S(1)}) custom-call(f32[512,512]{1,0:T(8,128)S(1)} %get-tuple-element.52.before, f32[192,512]{1,0:T(8,128)S(1)} %add_after.5.token.own), custom_call_target="tpu_custom_call" | custom-call | tf_op jit(solution)/shard_map/factor_later/pallas_call | solution.py:185
  81.1 5.2 %factor_later.5 = (f32[128,512]{1,0:T(8,128)S(1)}, f32[512,512]{1,0:T(8,128)}) custom-call(f32[512,512]{1,0:T(8,128)S(1)} %get-tuple-element.54.before, f32[192,512]{1,0:T(8,128)S(1)} %add_after.5.token.own), custom_call_target="tpu_custom_call" | custom-call | tf_op jit(solution)/shard_map/factor_later/pallas_call | solution.py:185
  86.3 2.9 %left.1 = (f32[240,512]{1,0:T(8,128)S(1)}, f32[240,512]{1,0:T(8,128)}, f32[512,512]{1,0:T(8,128)S(1)}, f32[192,512]{1,0:T(8,128)S(1)}) custom-call(s32[5]{0:T(128)S(1)} %stack.23.bits, f32[120,512]{1,0:T(8,128)S(1)} %add_after.3.refs_0_.mine, f32[120,512]{1,0:T(8,128)S(1)} %collective-permute-done.4.refs_4_.other, f32[192,512]{1,0:T(8,128)S(1)} %add_after.5.token.own, ...), custom_call_target="tpu_custom_call" | custom-call | tf_op jit(solution)/shard_map/left/pallas_call | solution.py:477
  91.7 2.9 %own_part.1 = (f32[576,512]{1,0:T(8,128)S(1)}, f32[96,512]{1,0:T(8,128)S(1)}, f32[96,512]{1,0:T(8,128)S(1)}, bf16[576,1536]{1,0:T(8,128)(2,1)S(1)}, f32[3,240,192]{2,1,0:T(8,128)S(1)}) custom-call(f32[240,512]{1,0:T(8,128)S(1)} %get-tuple-element.59.left, f32[512,512]{1,0:T(8,128)S(1)} %get-tuple-element.57.inverse, ...), custom_call_target="tpu_custom_call" | custom-call | bytes 16777216 | tf_op jit(solution)/shard_map/own_part/pallas_call | solution.py:500
  100.6 2.1 %collective-permute-done.21 = f32[1,512]{1,0:T(1,128)S(1)} collective-permute-done((f32[1,512]{1,0:T(1,128)S(1)}, f32[1,512]{1,0:T(1,128)S(1)}, u32[]{:S(2)}, u32[]{:S(2)}) %collective-permute-start.21) | collective-permute-done | bytes 2080 | tf_op jit(solution)/shard_map/ppermute | solution.py:221
  102.8 3.5 %collective-permute-done.22 = f32[1,512]{1,0:T(1,128)S(1)} collective-permute-done((f32[1,512]{1,0:T(1,128)S(1)}, f32[1,512]{1,0:T(1,128)S(1)}, u32[]{:S(2)}, u32[]{:S(2)}) %collective-permute-start.22) | collective-permute-done | bytes 2080 | tf_op jit(solution)/shard_map/ppermute | solution.py:221
  107.6 2.4 %new_momentum.1 = (f32[240,1536]{1,0:T(8,128)}, bf16[576,1536]{1,0:T(8,128)(2,1)S(1)}) custom-call(s32[5]{0:T(128)S(1)} %stack.23.bits, f32[240,512]{1,0:T(8,128)S(1)} %get-tuple-element.59.left, f32[3,240,192]{2,1,0:T(8,128)S(1)} %get-tuple-element.62.products, f32[240,384]{1,0:T(8,128)S(1)} %get-tuple-element.39.token.refs_8_.refs_0_, ...), custom_call_target="tpu_custom_call" | custom-call | bytes 16777216 | tf_op jit(solution)/shard_map/new_momentum/pallas_call | solution.py:524
  110.0 2.8 %collective-permute-done.28.refs_6_ = f32[96,512]{1,0:T(8,128)S(1)} collective-permute-done((f32[96,512]{1,0:T(8,128)S(1)}, f32[96,512]{1,0:T(8,128)S(1)}, u32[]{:S(2)}, u32[]{:S(2)}) %collective-permute-start.28) | collective-permute-done | bytes 196640 | tf_op jit(solution)/shard_map/ppermute | solution.py:221
  112.8 4.0 %last.1 = (f32[240,1536]{1,0:T(8,128)}, bf16[240,1536]{1,0:T(8,128)(2,1)}, f32[192,512]{1,0:T(8,128)}) custom-call(s32[5]{0:T(128)S(1)} %stack.23.bits, f32[1,512]{1,0:T(1,128)S(1)} %add.26.squares, f32[240,512]{1,0:T(8,128)S(1)} %get-tuple-element.59.left, f32[576,512]{1,0:T(8,128)S(1)} %get-tuple-element.60.rights, ...), custom_call_target="tpu_custom_call", output_to_operand_aliasing={{0}: (14, {})} | custom-call | tf_op jit(solution)/shard_map/last/pallas_call | solution.py:533
  (65 shorter events, 29.3 us)
Async XLA Ops:
  3.9 20.8 %collective-permute-start.1 = (f32[240,384]{1,0:T(8,128)S(1)}, f32[240,384]{1,0:T(8,128)S(1)}, u32[]{:S(2)}, u32[]{:S(2)}) collective-permute-start(f32[240,384]{1,0:T(8,128)S(1)} %get-tuple-element.42.refs_1_), channel_id=1, source_target_pairs={{0,4},{4,0},{8,12},{12,8},{16,20},{20,16},{24,28},{28,24},{1,5},{5... | collective-permute-start | bytes 1105928 | tf_op jit(solution)/shard_map/ppermute | solution.py:221
  6.9 17.8 %collective-permute-start.2 = (f32[240,384]{1,0:T(8,128)S(1)}, f32[240,384]{1,0:T(8,128)S(1)}, u32[]{:S(2)}, u32[]{:S(2)}) collective-permute-start(f32[240,384]{1,0:T(8,128)S(1)} %get-tuple-element.43.refs_2_), channel_id=1, source_target_pairs={{0,8},{4,12},{8,0},{12,4},{16,24},{20,28},{24,16},{28,20},{1,9},{5... | collective-permute-start | bytes 1105928 | tf_op jit(solution)/shard_map/ppermute | solution.py:221
  8.5 16.3 %collective-permute-start.3 = (f32[240,384]{1,0:T(8,128)S(1)}, f32[240,384]{1,0:T(8,128)S(1)}, u32[]{:S(2)}, u32[]{:S(2)}) collective-permute-start(f32[240,384]{1,0:T(8,128)S(1)} %get-tuple-element.44.refs_7_), channel_id=1, source_target_pairs={{0,12},{4,8},{8,4},{12,0},{16,28},{20,24},{24,20},{28,16},{1,13},{... | collective-permute-start | bytes 1105928 | tf_op jit(solution)/shard_map/ppermute | solution.py:221
  16.5 8.3 %collective-permute-start = (f32[120,512]{1,0:T(8,128)S(1)}, f32[120,512]{1,0:T(8,128)S(1)}, u32[]{:S(2)}, u32[]{:S(2)}) collective-permute-start(f32[120,512]{1,0:T(8,128)S(1)} %core_add.1.refs_0_), channel_id=1, source_target_pairs={{0,2},{1,3},{2,0},{3,1},{4,6},{5,7},{6,4},{7,5},{8,10},{9,11},{10,... | collective-permute-start | bytes 737288 | tf_op jit(solution)/shard_map/ppermute | solution.py:221
  24.8 9.9 %collective-permute-start.7 = (f32[120,512]{1,0:T(8,128)S(1)}, f32[120,512]{1,0:T(8,128)S(1)}, u32[]{:S(2)}, u32[]{:S(2)}) collective-permute-start(f32[120,512]{1,0:T(8,128)S(1)} %add_after.3.refs_0_.mine), channel_id=1, source_target_pairs={{0,12},{4,8},{8,4},{12,0},{16,28},{20,24},{24,20},{28,16},{1,13},{... | collective-permute-start | bytes 737288 | tf_op jit(solution)/shard_map/ppermute | solution.py:221
  27.6 10.9 %collective-permute-start.6 = (f32[120,512]{1,0:T(8,128)S(1)}, f32[120,512]{1,0:T(8,128)S(1)}, u32[]{:S(2)}, u32[]{:S(2)}) collective-permute-start(f32[120,512]{1,0:T(8,128)S(1)} %add_after.3.refs_0_.mine), channel_id=1, source_target_pairs={{0,8},{4,12},{8,0},{12,4},{16,24},{20,28},{24,16},{28,20},{1,9},{5... | collective-permute-start | bytes 737288 | tf_op jit(solution)/shard_map/ppermute | solution.py:221
  28.1 10.5 %collective-permute-start.5 = (f32[120,512]{1,0:T(8,128)S(1)}, f32[120,512]{1,0:T(8,128)S(1)}, u32[]{:S(2)}, u32[]{:S(2)}) collective-permute-start(f32[120,512]{1,0:T(8,128)S(1)} %add_after.3.refs_0_.mine), channel_id=1, source_target_pairs={{0,4},{4,0},{8,12},{12,8},{16,20},{20,16},{24,28},{28,24},{1,5},{5... | collective-permute-start | bytes 737288 | tf_op jit(solution)/shard_map/ppermute | solution.py:221
  28.4 16.7 %collective-permute-start.4 = (f32[120,512]{1,0:T(8,128)S(1)}, f32[120,512]{1,0:T(8,128)S(1)}, u32[]{:S(2)}, u32[]{:S(2)}) collective-permute-start(f32[120,512]{1,0:T(8,128)S(1)} %add_after.3.refs_0_.mine), channel_id=1, source_target_pairs={{0,1},{1,0},{2,3},{3,2},{4,5},{5,4},{6,7},{7,6},{8,9},{9,8},{10,11... | collective-permute-start | bytes 737288 | tf_op jit(solution)/shard_map/ppermute | solution.py:221
  34.7 10.4 %collective-permute-start.11 = (f32[120,512]{1,0:T(8,128)S(1)}, f32[120,512]{1,0:T(8,128)S(1)}, u32[]{:S(2)}, u32[]{:S(2)}) collective-permute-start(f32[120,512]{1,0:T(8,128)S(1)} %collective-permute-done.7.refs_3_), channel_id=1, source_target_pairs={{0,1},{1,0},{2,3},{3,2},{4,5},{5,4},{6,7},{7,6},{8,9},{9,8},{10,11... | collective-permute-start | bytes 737288 | tf_op jit(solution)/shard_map/ppermute | solution.py:221
  38.5 6.6 %collective-permute-start.10 = (f32[120,512]{1,0:T(8,128)S(1)}, f32[120,512]{1,0:T(8,128)S(1)}, u32[]{:S(2)}, u32[]{:S(2)}) collective-permute-start(f32[120,512]{1,0:T(8,128)S(1)} %collective-permute-done.6.refs_2_), channel_id=1, source_target_pairs={{0,1},{1,0},{2,3},{3,2},{4,5},{5,4},{6,7},{7,6},{8,9},{9,8},{10,11... | collective-permute-start | bytes 737288 | tf_op jit(solution)/shard_map/ppermute | solution.py:221
  38.5 6.6 %collective-permute-start.9 = (f32[120,512]{1,0:T(8,128)S(1)}, f32[120,512]{1,0:T(8,128)S(1)}, u32[]{:S(2)}, u32[]{:S(2)}) collective-permute-start(f32[120,512]{1,0:T(8,128)S(1)} %collective-permute-done.5.refs_1_), channel_id=1, source_target_pairs={{0,1},{1,0},{2,3},{3,2},{4,5},{5,4},{6,7},{7,6},{8,9},{9,8},{10,11... | collective-permute-start | bytes 737288 | tf_op jit(solution)/shard_map/ppermute | solution.py:221
  42.5 7.2 %collective-permute-start.13 = (f32[160,128]{1,0:T(8,128)S(1)}, f32[160,128]{1,0:T(8,128)S(1)}, u32[]{:S(2)}, u32[]{:S(2)}) collective-permute-start(f32[160,128]{1,0:T(8,128)S(1)} %add.23.token.refs_0_), channel_id=1, source_target_pairs={{0,16},{4,20},{8,24},{12,28},{16,0},{20,4},{24,8},{28,12},{1,17},{... | collective-permute-start | bytes 245768 | tf_op jit(solution)/shard_map/ppermute | solution.py:221
  48.6 20.3 %collective-permute-start.12 = (f32[192,512]{1,0:T(8,128)S(1)}, f32[192,512]{1,0:T(8,128)S(1)}, u32[]{:S(2)}, u32[]{:S(2)}) collective-permute-start(f32[192,512]{1,0:T(8,128)S(1)} %get-tuple-element.48), channel_id=1, source_target_pairs={{0,16},{4,20},{8,24},{12,28},{16,0},{20,4},{24,8},{28,12},{1,17},{... | collective-permute-start | bytes 1179656 | tf_op jit(solution)/shard_map/ppermute | solution.py:221
  55.0 5.3 %collective-permute-start.15 = (f32[320,128]{1,0:T(8,128)S(1)}, f32[320,128]{1,0:T(8,128)S(1)}, u32[]{:S(2)}, u32[]{:S(2)}) collective-permute-start(f32[320,128]{1,0:T(8,128)S(1)} %all_gather.7.a), channel_id=1, source_target_pairs={{0,2},{1,3},{2,0},{3,1},{4,6},{5,7},{6,4},{7,5},{8,10},{9,11},{10,... | collective-permute-start | bytes 491528 | tf_op jit(solution)/shard_map/ppermute | solution.py:221
  56.5 3.8 %collective-permute-start.14 = (f32[320,128]{1,0:T(8,128)S(1)}, f32[320,128]{1,0:T(8,128)S(1)}, u32[]{:S(2)}, u32[]{:S(2)}) collective-permute-start(f32[320,128]{1,0:T(8,128)S(1)} %all_gather.7.a), channel_id=1, source_target_pairs={{0,1},{1,0},{2,3},{3,2},{4,5},{5,4},{6,7},{7,6},{8,9},{9,8},{10,11... | collective-permute-start | bytes 491528 | tf_op jit(solution)/shard_map/ppermute | solution.py:221
  68.9 20.2 %collective-permute-start.19 = (f32[192,512]{1,0:T(8,128)S(1)}, f32[192,512]{1,0:T(8,128)S(1)}, u32[]{:S(2)}, u32[]{:S(2)}) collective-permute-start(f32[192,512]{1,0:T(8,128)S(1)} %add_after.5.token.own), channel_id=1, source_target_pairs={{0,8},{4,12},{8,0},{12,4},{16,24},{20,28},{24,16},{28,20},{1,9},{5... | collective-permute-start | bytes 1179656 | tf_op jit(solution)/shard_map/ppermute | solution.py:221
  69.0 20.2 %collective-permute-start.18 = (f32[192,512]{1,0:T(8,128)S(1)}, f32[192,512]{1,0:T(8,128)S(1)}, u32[]{:S(2)}, u32[]{:S(2)}) collective-permute-start(f32[192,512]{1,0:T(8,128)S(1)} %add_after.5.token.own), channel_id=1, source_target_pairs={{0,4},{4,0},{8,12},{12,8},{16,20},{20,16},{24,28},{28,24},{1,5},{5... | collective-permute-start | bytes 1179656 | tf_op jit(solution)/shard_map/ppermute | solution.py:221
  70.3 19.3 %collective-permute-start.17 = (f32[192,512]{1,0:T(8,128)S(1)}, f32[192,512]{1,0:T(8,128)S(1)}, u32[]{:S(2)}, u32[]{:S(2)}) collective-permute-start(f32[192,512]{1,0:T(8,128)S(1)} %add_after.5.token.own), channel_id=1, source_target_pairs={{0,16},{4,20},{8,24},{12,28},{16,0},{20,4},{24,8},{28,12},{1,17},{... | collective-permute-start | bytes 1179656 | tf_op jit(solution)/shard_map/ppermute | solution.py:221
  90.9 15.4 %collective-permute-start.24 = (f32[192,512]{1,0:T(8,128)S(1)}, f32[192,512]{1,0:T(8,128)S(1)}, u32[]{:S(2)}, u32[]{:S(2)}) collective-permute-start(f32[192,512]{1,0:T(8,128)S(1)} %get-tuple-element.63.refs_3_.refs_0_), channel_id=1, source_target_pairs={{0,8},{4,12},{8,0},{12,4},{16,24},{20,28},{24,16},{28,20},{1,9},{5... | collective-permute-start | bytes 1179656 | tf_op jit(solution)/shard_map/ppermute | solution.py:221
  90.9 15.4 %collective-permute-start.23 = (f32[192,512]{1,0:T(8,128)S(1)}, f32[192,512]{1,0:T(8,128)S(1)}, u32[]{:S(2)}, u32[]{:S(2)}) collective-permute-start(f32[192,512]{1,0:T(8,128)S(1)} %get-tuple-element.63.refs_3_.refs_0_), channel_id=1, source_target_pairs={{0,4},{4,0},{8,12},{12,8},{16,20},{20,16},{24,28},{28,24},{1,5},{5... | collective-permute-start | bytes 1179656 | tf_op jit(solution)/shard_map/ppermute | solution.py:221
  94.6 11.7 %collective-permute-start.25 = (f32[96,512]{1,0:T(8,128)S(1)}, f32[96,512]{1,0:T(8,128)S(1)}, u32[]{:S(2)}, u32[]{:S(2)}) collective-permute-start(f32[96,512]{1,0:T(8,128)S(1)} %get-tuple-element.65), channel_id=1, source_target_pairs={{0,4},{4,0},{8,12},{12,8},{16,20},{20,16},{24,28},{28,24},{1,5},{5... | collective-permute-start | bytes 589832 | tf_op jit(solution)/shard_map/ppermute | solution.py:221
  96.0 10.3 %collective-permute-start.26 = (f32[96,512]{1,0:T(8,128)S(1)}, f32[96,512]{1,0:T(8,128)S(1)}, u32[]{:S(2)}, u32[]{:S(2)}) collective-permute-start(f32[96,512]{1,0:T(8,128)S(1)} %get-tuple-element.66), channel_id=1, source_target_pairs={{0,8},{4,12},{8,0},{12,4},{16,24},{20,28},{24,16},{28,20},{1,9},{5... | collective-permute-start | bytes 589832 | tf_op jit(solution)/shard_map/ppermute | solution.py:221
  106.3 6.4 %collective-permute-start.27 = (f32[104,512]{1,0:T(8,128)S(1)}, f32[104,512]{1,0:T(8,128)S(1)}, u32[]{:S(2)}, u32[]{:S(2)}) collective-permute-start(f32[104,512]{1,0:T(8,128)S(1)} %get-tuple-element.67), channel_id=1, source_target_pairs={{0,4},{4,0},{8,12},{12,8},{16,20},{20,16},{24,28},{28,24},{1,5},{5... | collective-permute-start | bytes 638984 | tf_op jit(solution)/shard_map/ppermute | solution.py:221
  107.1 5.7 %collective-permute-start.28 = (f32[96,512]{1,0:T(8,128)S(1)}, f32[96,512]{1,0:T(8,128)S(1)}, u32[]{:S(2)}, u32[]{:S(2)}) collective-permute-start(f32[96,512]{1,0:T(8,128)S(1)} %get-tuple-element.68), channel_id=1, source_target_pairs={{0,8},{4,12},{8,0},{12,4},{16,24},{20,28},{24,16},{28,20},{1,9},{5... | collective-permute-start | bytes 589832 | tf_op jit(solution)/shard_map/ppermute | solution.py:221
  (8 other events, 15.4 us)

commit v9 on v8

--- a/solution.py
+++ b/solution.py
@@ -175,20 +175,24 @@
     )(bits, *shares)
 
 
-def later_kernel(b, before, token, out, work, block):
+def later_kernel(before, first, own, inverse, own_right, squares, work, block):
     work[...] = before[...]
-    factor_step(b, work, out, block)
-
-
-def later_step(b, work, token):
+    inverse[:lanes, :] = first[...]
+    for b in range(1, work.shape[0] // lanes):
+        factor_step(b, work, inverse.at[b * lanes : (b + 1) * lanes], block)
+    own_right[...] = dot(own[...], inverse[...], ((1,), (1,)))
+    squares[...] = jnp.sum(own_right[...] * own_right[...], axis=0, keepdims=True)
+
+
+def later_steps(work, first, own):
     size = work.shape[0]
     return kernel(
-        functools.partial(later_kernel, b),
-        [shape(lanes, size), shape(size, size)],
-        [vmem, anywhere],
-        [pltpu.VMEM((lanes, lanes), jnp.float32)],
+        later_kernel,
+        [shape(size, size), shape(*own.shape), shape(1, size)],
+        [vmem] * 3,
+        [pltpu.VMEM((size, size), jnp.float32), pltpu.VMEM((lanes, lanes), jnp.float32)],
         "factor_later",
-    )(work, token)
+    )(work, first, own)
 
 
 def share_norms(right_rows):
@@ -283,46 +287,40 @@
     sent[...] = raw[pl.ds(pl.multiple_of((1 - bits[4]) * count, 8), count), :]
 
 
-def left_kernel(scale, bits, mine, other, own, *refs):
-    inverses, (left, left_scaled, inverse, own_right, rows) = refs[:-5], refs[-5:]
+def norm_kernel(inverse, before, one, two, received, out, squares):
+    right = dot(received[...], inverse[...], ((1,), (1,)))
+    out[...] = right
+    squares[...] = before[...] + jnp.sum(right * right, axis=0, keepdims=True)
+
+
+def beside_kernel(inverse, one, two, squares, rights, first, second):
+    count = one.shape[0]
+    middle = count // 2
+    rights[:count, :] = dot(one[...], inverse[...], ((1,), (1,)))
+    rights[count:, :] = dot(two[...], inverse[...], ((1,), (1,)))
+    first[...] = rights[count : count + middle, :]
+    with_row(rights.at[middle:count], squares[...], second)
+
+
+def with_row(rows, value, out):
+    count = rows.shape[0]
+    out[:count, :] = rows[...]
+    row = lax.broadcasted_iota(jnp.int32, (8, rows.shape[1]), 0)
+    out[count:, :] = jnp.where(row == 0, value, 0.0)
+
+
+def left_kernel(bits, mine, other, inverse, left, rows):
     half = mine.shape[0]
-    for b, part in enumerate(inverses):
-        inverse[b * lanes : (b + 1) * lanes, :] = part[...]
     rows[pl.ds(pl.multiple_of(bits[0] * half, 8), half), :] = mine[...]
     rows[pl.ds(pl.multiple_of((1 - bits[0]) * half, 8), half), :] = other[...]
     left[...] = dot(rows[...], inverse[...], ((1,), (1,)))
-    left_scaled[...] = left[...] * scale
-    own_right[...] = dot(own[...], inverse[...], ((1,), (1,)))
-
-
-def norm_kernel(own_right, received, inverse, one, two, out, squares):
-    right = dot(received[...], inverse[...], ((1,), (1,)))
-    out[...] = right
-    total = jnp.sum(right * right, axis=0, keepdims=True)
-    squares[...] = total + jnp.sum(own_right[...] * own_right[...], axis=0, keepdims=True)
-
-
-def forward_kernel(one, two, squares, one_here, two_here, first, second):
+
+
+def forward_kernel(one, two, squares, own_second, left, own_first, first, second, total):
     middle = second.shape[0]
-    first[:middle, :] = two[:middle, :]
-    row = lax.broadcasted_iota(jnp.int32, (8, two.shape[1]), 0)
-    first[middle:, :] = jnp.where(row == 0, squares[...], 0.0)
+    total[...] = squares[...] + own_second[middle : middle + 1, :]
+    with_row(two.at[:middle], total[...], first)
     second[...] = one[middle:, :]
-
-
-def own_kernel(left, inverse, own_right, one, two, rights, first, second, splits, products):
-    count = own_right.shape[0]
-    middle = count // 2
-    rights[:count, :] = own_right[...]
-    for k, part in enumerate((one, two)):
-        at = slice((k + 1) * count, (k + 2) * count)
-        rights[at, :] = dot(part[...], inverse[...], ((1,), (1,)))
-    first[...] = rights[2 * count : 2 * count + middle, :]
-    second[...] = rights[count + middle : 2 * count, :]
-    splits[...] = three_right(rights[...])
-    product = dot_three(three_left(left[...]), splits[...])
-    for k in range(3):
-        products[k] = product[:, k * count : (k + 1) * count]
 
 
 def columns_of(bits, k, width):
@@ -334,25 +332,31 @@
     return jnp.where(bits[4] == 0, lower, jnp.concatenate([other, mine], axis=1))
 
 
-def momentum_kernel(bits, left, products, *refs):
-    pieces, received, (new_momentum, splits, ready, sent) = refs[:3], refs[3:6], refs[6:]
+def momentum_kernel(scale, bits, left, own_right, rights, *refs):
+    pieces, received, refs = refs[:3], refs[3:6], refs[6:]
+    new_momentum, left_scaled, own_splits, splits, ready, left_ready, sent = refs
+    left_ready[...] = left[...] * scale
+    copies = [pltpu.make_async_copy(left_ready, left_scaled, sent.at[3])]
+    copies[0].start()
     width = pieces[0].shape[1]
     half = width // 2
+    own_splits[:half, :] = three_right(own_right[...])
+    own_splits[half:, :] = three_right(rights[...])
     for k in range(3):
         splits[k * half : (k + 1) * half, :] = three_right(received[k][...])
-    both = dot_three(three_left(left[...]), splits[...])
-    copies = []
+    scaled = three_left(left[...])
     for k in range(3):
-        other = both[:, k * half : (k + 1) * half]
-        ready[k] = pieces[k][...] - 0.5 * in_order(bits, products[k], other)
+        at = slice(k * half, (k + 1) * half)
+        mine, other = dot_three(scaled, own_splits[at, :]), dot_three(scaled, splits[at, :])
+        ready[k] = pieces[k][...] - 0.5 * in_order(bits, mine, other)
         target = new_momentum.at[:, columns_of(bits, k, width)]
         copies.append(pltpu.make_async_copy(ready.at[k], target, sent.at[k]))
-        copies[k].start()
+        copies[-1].start()
     for copy in copies:
         copy.wait()
 
 
-def last_kernel(factor, bits, squares, left, rights, own_splits, splits, *refs):
+def last_kernel(factor, bits, squares, left, own_right, rights, own_splits, splits, *refs):
     received, (own_first, own_second, first, second, piece, _, new_momentum, update, next_basis), scratch = (
         refs[:3],
         refs[3:12],
@@ -369,7 +373,7 @@
         copies[-1].start()
 
     last_own[:middle, :] = own_first[...]
-    last_own[middle:, :] = own_second[...]
+    last_own[middle:, :] = own_second[:middle, :]
     last_received[:middle, :] = first[:middle, :]
     last_received[middle:, :] = second[...]
     last_splits[:half, :] = three_right(last_own[...])
@@ -381,9 +385,9 @@
 
         @pl.when((bits[3] // 2) ^ bits[2] == k)
         def _():
-            last = k == square - 1
-            mine = last_own[...] if last else rights[k * half : (k + 1) * half, :]
-            other = last_received[...] if last else received[k][...]
+            beside = [rights[i * half : (i + 1) * half, :] for i in range(2)]
+            mine = [own_right[...], *beside, last_own[...]][k]
+            other = last_received[...] if k == square - 1 else received[k][...]
             basis_ready[...] = jnp.where(bits[3] % 2 == bits[4], mine, other) / norm
 
     send(basis_ready, next_basis, square + 1)
@@ -464,72 +468,65 @@
     over_planes = swap(quarter, "tensor", 2)
     shares = [quarter, swap(quarter, "tensor", 1), over_planes, swap(over_planes, "tensor", 1)]
 
-    factors = []
-    out, work = first_step(bits, shares, rank)
-    factors.append(out)
-    token = out
-    for b in range(1, count):
-        if b == 1:
-            own = add_after(kept, swap(sent, "fsdp", square), out)
-            token = own
-        out, work = later_step(b, work, token)
-        factors.append(out)
-    left, left_scaled, inverse, own_right = kernel(
-        functools.partial(left_kernel, math.sqrt(total_rows)),
-        [shape(rows, rank), shape(rows, rank), shape(rank, rank), shape(width // 2, rank)],
-        [smem] + [vmem] * (3 + count),
-        [pltpu.VMEM((rows, rank), jnp.float32)],
-        "left",
-    )(bits, mine, others[0], own, *factors)
-
+    first_block, work = first_step(bits, shares, rank)
+    own = add_after(kept, swap(sent, "fsdp", square), first_block)
+
+    half_width = width // 2
     received = swap(own, "fsdp", square)
     beside = [swap(own, "fsdp", k) for k in (1, 2)]
-    half_width = width // 2
+    inverse, own_right, squares = later_steps(work, first_block, own)
     received_right, squares = kernel(
         norm_kernel,
         [shape(half_width, rank), shape(1, rank)],
-        [vmem] * 3 + [anywhere] * 2,
+        [vmem] * 2 + [anywhere] * 2 + [vmem],
         [],
         "norms",
-    )(own_right, received, inverse, *beside)
+    )(inverse, squares, *beside, received)
     received_rows = [received_right] + [swap(received_right, "fsdp", k) for k in (1, 2)]
-    for axis, flip in (("tensor", 1), ("tensor", 2), ("fsdp", 2)):
-        squares = squares + swap(squares, axis, flip)
+    for flip in (1, 2):
+        squares = squares + swap(squares, "tensor", flip)
 
     half_rows = shape(half_width // 2, rank)
-    rights, own_first, own_second, own_splits, products = kernel(
-        own_kernel,
-        [
-            shape(3 * half_width, rank),
-            half_rows,
-            half_rows,
-            shape(3 * half_width, 3 * rank, dtype=jnp.bfloat16),
-            shape(3, rows, half_width),
-        ],
-        [vmem] * 5,
+    with_norms = shape(half_width // 2 + 8, rank)
+    rights, own_first, own_second = kernel(
+        beside_kernel,
+        [shape(2 * half_width, rank), half_rows, with_norms],
+        [vmem] * 4,
         [],
-        "own_part",
-        cost=2**24,
-    )(left, inverse, own_right, *beside)
+        "beside",
+    )(inverse, *beside, squares)
     own_first, own_second = swap(own_first, "fsdp", 1), swap(own_second, "fsdp", 2)
-    first, second = kernel(
+    left = kernel(
+        left_kernel,
+        shape(rows, rank),
+        [smem] + [vmem] * 3,
+        [pltpu.VMEM((rows, rank), jnp.float32)],
+        "left",
+        cost=2**23,
+    )(bits, mine, others[0], inverse)
+    first, second, squares = kernel(
         forward_kernel,
-        [shape(half_width // 2 + 8, rank), half_rows],
-        [vmem] * 3 + [anywhere] * 2,
+        [with_norms, half_rows, shape(1, rank)],
+        [vmem] * 4 + [anywhere] * 2,
         [],
         "forward",
-    )(received_rows[1], received_rows[2], squares, own_first, own_second)
+    )(received_rows[1], received_rows[2], squares, own_second, left, own_first)
     first, second = swap(first, "fsdp", 1), swap(second, "fsdp", 2)
 
-    new_momentum, splits = kernel(
-        momentum_kernel,
-        [shape(rows, cols), shape(3 * half_width, 3 * rank, dtype=jnp.bfloat16)],
-        [smem] + [vmem] * 8,
-        [pltpu.VMEM((3, rows, width), jnp.float32), pltpu.SemaphoreType.DMA((3,))],
+    splits_shape = shape(3 * half_width, 3 * rank, dtype=jnp.bfloat16)
+    new_momentum, left_scaled, own_splits, splits = kernel(
+        functools.partial(momentum_kernel, math.sqrt(total_rows)),
+        [shape(rows, cols), shape(rows, rank), splits_shape, splits_shape],
+        [smem] + [vmem] * 9,
+        [
+            pltpu.VMEM((3, rows, width), jnp.float32),
+            pltpu.VMEM((rows, rank), jnp.float32),
+            pltpu.SemaphoreType.DMA((4,)),
+        ],
         "new_momentum",
         cost=2**24,
-        out_specs=[anywhere, vmem],
-    )(bits, left, products, *pieces[:3], *received_rows)
+        out_specs=[anywhere] * 2 + [vmem] * 2,
+    )(bits, left, own_right, rights, *pieces[:3], *received_rows)
     new_momentum, update, next_basis = kernel(
         functools.partial(last_kernel, math.sqrt(total_rows / total_cols)),
         [
@@ -537,7 +534,7 @@
             shape(rows, cols, dtype=jnp.bfloat16),
             shape(cols // lax.axis_size("fsdp"), rank),
         ],
-        [smem] + [vmem] * 13 + [anywhere],
+        [smem] + [vmem] * 14 + [anywhere],
         [
             pltpu.VMEM((half_width, rank), jnp.float32),
             pltpu.VMEM((half_width, rank), jnp.float32),
@@ -549,9 +546,9 @@
         ],
         "last",
         out_specs=[anywhere] * 3,
-        aliases={14: 0},
+        aliases={15: 0},
     )(
-        *(bits, squares, left, rights, own_splits, splits, *received_rows),
+        *(bits, squares, left, own_right, rights, own_splits, splits, *received_rows),
         *(own_first, own_second, first, second, pieces[3], new_momentum),
     )
     return (update, new_momentum, left_scaled, next_basis)

time: 117 us -> 117 us (level)
  Pallas kernels: 42.6 us -> 40.6 us
    pallas_call x8 -> x6, Pallas kernels: 23.4 us -> 21.4 us  [the longest x1 13.5 us: later_steps(): kernel(later_kernel, [shape(size, size), shape(*own.shape), shape(1, size...]
    ppermute x29 -> x28, waiting for transfers between devices: 35.7 us -> 36.8 us  [swap(): lax.ppermute(value, axis, [(i, i ^ flip) for i in range(lax.axis_size(axi...]
    ppermute x29 -> x28, starting transfers between devices: 25.6 us -> 26.3 us  [swap(): lax.ppermute(value, axis, [(i, i ^ flip) for i in range(lax.axis_size(axi...]
  transfers between devices with their start and end apart: 29 -> 28, of which waited for: 13 -> 14; matrix products, arithmetic and copies ran while one was open for 0% -> 0% of each run, Pallas kernels for 31% -> 30%
where the time goes in v9:
time: 117 us
  Pallas kernels  40.6 us (35%)
  waiting for transfers between devices  36.8 us (31%)
  starting transfers between devices  26.3 us (22%)
  blocking collectives  7.46 us (6%)
  local copies, waits for them, and re-layouts  4.46 us (4%)
    ppermute x28, waiting for transfers between devices, swap(): lax.ppermute(value, axis, [(i, i ^ flip) for i in range(lax.axis_size(axi...  36.8 us
    ppermute x28, starting transfers between devices, swap(): lax.ppermute(value, axis, [(i, i ^ flip) for i in range(lax.axis_size(axi...  26.3 us
    pallas_call x1, Pallas kernels, later_steps(): kernel(later_kernel, [shape(size, size), shape(*own.shape), shape(1, size...  13.5 us
    all_gather x1, blocking collectives, in_squares(): lax.all_gather(part, 'fsdp', axis=0, tiled=True, axis_index_groups=chips)  5.3 us
    pallas_call x1, Pallas kernels, first_step(): kernel(first_kernel, [shape(lanes, size), shape(size, size)], [smem] + [v...  5.06 us
    unnamed x6, local copies, waits for them, and re-layouts  4.38 us
    pallas_call x1, Pallas kernels, in_squares(): kernel(functools.partial(last_kernel, math.sqrt(total_rows / total_cols))...  3.94 us
    pallas_call x1, Pallas kernels, in_squares(): kernel(raw_kernel, [shape(width // 2, rank)] * 2, [smem, anywhere] + [vme...  3.42 us
  transfers between devices with their start and end apart: 28, of which 14 were waited for; matrix products, arithmetic and copies ran while one was open for 0% of the time, Pallas kernels for 30%

profile of v9, /device:TPU:0, one launch (start us, length us, event | category | flops | bytes accessed | tf_op | source)
XLA Modules:
  0.0 116.6 jit_solution(17540401267391535725)
XLA Ops:
  3.9 3.0 %collective-permute-start.1 = (f32[240,384]{1,0:T(8,128)S(1)}, f32[240,384]{1,0:T(8,128)S(1)}, u32[]{:S(2)}, u32[]{:S(2)}) collective-permute-start(f32[240,384]{1,0:T(8,128)S(1)} %get-tuple-element.37.refs_1_), channel_id=1, source_target_pairs={{0,4},{4,0},{8,12},{12,8},{16,20},{20,16},{24,28},{28,24},{1,5},{5... | collective-permute-start | bytes 1105928 | tf_op jit(solution)/shard_map/ppermute | solution.py:225
  10.4 3.4 %part_left.1 = (f32[120,512]{1,0:T(8,128)S(1)}, f32[120,512]{1,0:T(8,128)S(1)}) custom-call(s32[5]{0:T(128)S(1)} %stack.23.bits, f32[1536,512]{1,0:T(8,128)S(1)} %copy-done.1, f32[240,1536]{1,0:T(8,128)S(1)} %copy-done, bf16[240,1536]{1,0:T(8,128)(2,1)S(1)} %copy-done.2, f32[240,384]{1,0:T(8,128)S(1)} %get-tuple-element.34.token.refs_8_.refs_0_), custom_call_target="tpu_custom_call" | custom-call | tf_op jit(solution)/shard_map/part_left/pallas_call | solution.py:425
  13.8 2.2 %all_gather.6.both = f32[240,512]{1,0:T(8,128)S(1)} all-gather(f32[120,512]{1,0:T(8,128)S(1)} %get-tuple-element.36), channel_id=1, replica_groups={{0,1},{2,3},{4,5},{6,7},{8,9},{10,11},{12,13},{14,15},{16,17},{18,19},{..., dimensions={0}, use_global_device_ids=true | all-gather | bytes 737280 | tf_op jit(solution)/shard_map/all_gather | solution.py:433
  16.5 2.0 %collective-permute-start = (f32[120,512]{1,0:T(8,128)S(1)}, f32[120,512]{1,0:T(8,128)S(1)}, u32[]{:S(2)}, u32[]{:S(2)}) collective-permute-start(f32[120,512]{1,0:T(8,128)S(1)} %core_add.1.refs_0_), channel_id=1, source_target_pairs={{0,2},{1,3},{2,0},{3,1},{4,6},{5,7},{6,4},{7,5},{8,10},{9,11},{10,... | collective-permute-start | bytes 737288 | tf_op jit(solution)/shard_map/ppermute | solution.py:225
  18.5 6.3 %collective-permute-done.refs_1_ = f32[120,512]{1,0:T(8,128)S(1)} collective-permute-done((f32[120,512]{1,0:T(8,128)S(1)}, f32[120,512]{1,0:T(8,128)S(1)}, u32[]{:S(2)}, u32[]{:S(2)}) %collective-permute-start) | collective-permute-done | bytes 245792 | tf_op jit(solution)/shard_map/ppermute | solution.py:225
  24.8 2.8 %collective-permute-start.6 = (f32[120,512]{1,0:T(8,128)S(1)}, f32[120,512]{1,0:T(8,128)S(1)}, u32[]{:S(2)}, u32[]{:S(2)}) collective-permute-start(f32[120,512]{1,0:T(8,128)S(1)} %add_after.3.refs_0_.mine), channel_id=1, source_target_pairs={{0,12},{4,8},{8,4},{12,0},{16,28},{20,24},{24,20},{28,16},{1,13},{... | collective-permute-start | bytes 737288 | tf_op jit(solution)/shard_map/ppermute | solution.py:225
  28.4 6.3 %collective-permute-done.6.refs_3_ = f32[120,512]{1,0:T(8,128)S(1)} collective-permute-done((f32[120,512]{1,0:T(8,128)S(1)}, f32[120,512]{1,0:T(8,128)S(1)}, u32[]{:S(2)}, u32[]{:S(2)}) %collective-permute-start.6) | collective-permute-done | bytes 245792 | tf_op jit(solution)/shard_map/ppermute | solution.py:225
  34.7 3.8 %collective-permute-done.5.refs_2_ = f32[120,512]{1,0:T(8,128)S(1)} collective-permute-done((f32[120,512]{1,0:T(8,128)S(1)}, f32[120,512]{1,0:T(8,128)S(1)}, u32[]{:S(2)}, u32[]{:S(2)}) %collective-permute-start.5) | collective-permute-done | bytes 245792 | tf_op jit(solution)/shard_map/ppermute | solution.py:225
  39.0 2.1 %part_gram.1 = (f32[160,128]{1,0:T(8,128)S(1)}, f32[160,128]{1,0:T(8,128)S(1)}) custom-call(s32[5]{0:T(128)S(1)} %stack.23.bits, f32[120,512]{1,0:T(8,128)S(1)} %add_after.3.refs_0_.mine, f32[120,512]{1,0:T(8,128)S(1)} %collective-permute-done.4.refs_1_, f32[120,512]{1,0:T(8,128)S(1)} %collective-permute-done.5.refs_2_, ...), custom_call_target="tpu_custom_call" | custom-call | tf_op jit(solution)/shard_map/part_gram/pallas_call | solution.py:444
  42.5 2.6 %collective-permute-start.8 = (f32[160,128]{1,0:T(8,128)S(1)}, f32[160,128]{1,0:T(8,128)S(1)}, u32[]{:S(2)}, u32[]{:S(2)}) collective-permute-start(f32[160,128]{1,0:T(8,128)S(1)} %add.20.token.refs_0_), channel_id=1, source_target_pairs={{0,16},{4,20},{8,24},{12,28},{16,0},{20,4},{24,8},{28,12},{1,17},{... | collective-permute-start | bytes 245768 | tf_op jit(solution)/shard_map/ppermute | solution.py:225
  45.2 3.4 %part_raw.1 = (f32[192,512]{1,0:T(8,128)S(1)}, f32[192,512]{1,0:T(8,128)S(1)}) custom-call(s32[5]{0:T(128)S(1)} %stack.23.bits, f32[160,128]{1,0:T(8,128)S(1)} %add.20.token.refs_0_, f32[120,512]{1,0:T(8,128)S(1)} %add_after.3.refs_0_.mine, f32[120,512]{1,0:T(8,128)S(1)} %collective-permute-done.4.refs_1_, f32[120,512]{1,0:T(8,128)S(1)} %collective-permute-done.5.refs_2_, ...), custom_call_target="tpu_custom_call" | custom-call | tf_op jit(solution)/shard_map/part_raw/pallas_call | solution.py:453
  49.7 5.3 %all_gather.7.a = f32[320,128]{1,0:T(8,128)S(1)} all-gather(f32[160,128]{1,0:T(8,128)S(1)} %add_after.4), channel_id=1, replica_groups={{0,4},{8,12},{16,20},{24,28},{1,5},{9,13},{17,21},{25,29},{2,6},{10,14}..., dimensions={0}, use_global_device_ids=true | all-gather | bytes 245760 | tf_op jit(solution)/shard_map/all_gather | solution.py:467
  56.5 3.8 %collective-permute-done.14.c = f32[320,128]{1,0:T(8,128)S(1)} collective-permute-done((f32[320,128]{1,0:T(8,128)S(1)}, f32[320,128]{1,0:T(8,128)S(1)}, u32[]{:S(2)}, u32[]{:S(2)}) %collective-permute-start.14) | collective-permute-done | bytes 163872 | tf_op jit(solution)/shard_map/ppermute | solution.py:225
  61.7 5.1 %factor_first.1 = (f32[128,512]{1,0:T(8,128)S(1)}, f32[512,512]{1,0:T(8,128)S(1)}) custom-call(s32[5]{0:T(128)S(1)} %stack.23.bits, f32[320,128]{1,0:T(8,128)S(1)} %all_gather.7.a, f32[320,128]{1,0:T(8,128)S(1)} %collective-permute-done.13.b, f32[320,128]{1,0:T(8,128)S(1)} %collective-permute-done.14.c, f32[320,128]{1,0:T(8,128)S(1)} %collective-permute-done.15.d), custom_call_target="tpu_custom_call" | custom-call | tf_op jit(solution)/shard_map/factor_first/pallas_call | solution.py:169
  66.8 2.1 %collective-permute-done.16.refs_1_ = f32[192,512]{1,0:T(8,128)S(1)} collective-permute-done((f32[192,512]{1,0:T(8,128)S(1)}, f32[192,512]{1,0:T(8,128)S(1)}, u32[]{:S(2)}, u32[]{:S(2)}) %collective-permute-start.16) | collective-permute-done | bytes 393248 | tf_op jit(solution)/shard_map/ppermute | solution.py:225
  69.0 2.0 %collective-permute-start.18 = (f32[192,512]{1,0:T(8,128)S(1)}, f32[192,512]{1,0:T(8,128)S(1)}, u32[]{:S(2)}, u32[]{:S(2)}) collective-permute-start(f32[192,512]{1,0:T(8,128)S(1)} %add_after.5.own), channel_id=1, source_target_pairs={{0,8},{4,12},{8,0},{12,4},{16,24},{20,28},{24,16},{28,20},{1,9},{5... | collective-permute-start | bytes 1179656 | tf_op jit(solution)/shard_map/ppermute | solution.py:225
  72.2 13.5 %factor_later.1 = (f32[512,512]{1,0:T(8,128)S(1)}, f32[192,512]{1,0:T(8,128)S(1)}, f32[1,512]{1,0:T(1,128)S(1)}) custom-call(f32[512,512]{1,0:T(8,128)S(1)} %get-tuple-element.43.before, f32[128,512]{1,0:T(8,128)S(1)} %get-tuple-element.44.refs_2_.first, f32[192,512]{1,0:T(8,128)S(1)} %add_after.5.own), custom_call_target="tpu_custom_call" | custom-call | tf_op jit(solution)/shard_map/factor_later/pallas_call | solution.py:189
  85.7 2.7 %collective-permute-done.19.received = f32[192,512]{1,0:T(8,128)S(1)} collective-permute-done((f32[192,512]{1,0:T(8,128)S(1)}, f32[192,512]{1,0:T(8,128)S(1)}, u32[]{:S(2)}, u32[]{:S(2)}) %collective-permute-start.19) | collective-permute-done | bytes 393248 | tf_op jit(solution)/shard_map/ppermute | solution.py:225
  93.8 2.1 %collective-permute-done.23 = f32[1,512]{1,0:T(1,128)S(1)} collective-permute-done((f32[1,512]{1,0:T(1,128)S(1)}, f32[1,512]{1,0:T(1,128)S(1)}, u32[]{:S(2)}, u32[]{:S(2)}) %collective-permute-start.23) | collective-permute-done | bytes 2080 | tf_op jit(solution)/shard_map/ppermute | solution.py:225
  95.9 2.2 %beside.1 = (f32[384,512]{1,0:T(8,128)S(1)}, f32[96,512]{1,0:T(8,128)S(1)}, f32[104,512]{1,0:T(8,128)S(1)}) custom-call(f32[512,512]{1,0:T(8,128)S(1)} %get-tuple-element.46.inverse, f32[192,512]{1,0:T(8,128)S(1)} %collective-permute-done.17.one, f32[192,512]{1,0:T(8,128)S(1)} %collective-permute-done.18.two, f32[1,512]{1,0:T(1,128)S(1)} %add.22.squares), custom_call_target="tpu_custom_call" | custom-call | tf_op jit(solution)/shard_map/beside/pallas_call | solution.py:491
  98.1 2.0 %collective-permute-start.24 = (f32[104,512]{1,0:T(8,128)S(1)}, f32[104,512]{1,0:T(8,128)S(1)}, u32[]{:S(2)}, u32[]{:S(2)}) collective-permute-start(f32[104,512]{1,0:T(8,128)S(1)} %get-tuple-element.50), channel_id=1, source_target_pairs={{0,8},{4,12},{8,0},{12,4},{16,24},{20,28},{24,16},{28,20},{1,9},{5... | collective-permute-start | bytes 638984 | tf_op jit(solution)/shard_map/ppermute | solution.py:225
  102.5 3.5 %collective-permute-done.25.own_first.refs_3_ = f32[96,512]{1,0:T(8,128)S(1)} collective-permute-done((f32[96,512]{1,0:T(8,128)S(1)}, f32[96,512]{1,0:T(8,128)S(1)}, u32[]{:S(2)}, u32[]{:S(2)}) %collective-permute-start.25) | collective-permute-done | bytes 196640 | tf_op jit(solution)/shard_map/ppermute | solution.py:225
  108.0 2.9 %new_momentum.1 = (f32[240,1536]{1,0:T(8,128)}, f32[240,512]{1,0:T(8,128)}, bf16[576,1536]{1,0:T(8,128)(2,1)S(1)}, bf16[576,1536]{1,0:T(8,128)(2,1)S(1)}) custom-call(s32[5]{0:T(128)S(1)} %stack.23.bits, f32[240,512]{1,0:T(8,128)S(1)} %left.1, f32[192,512]{1,0:T(8,128)S(1)} %get-tuple-element.53.own_right, f32[384,512]{1,0:T(8,128)S(1)} %get-tuple-element.54.rights, ...), custom_call_target="tpu_custom_call" | custom-call | bytes 16777216 | tf_op jit(solution)/shard_map/new_momentum/pallas_call | solution.py:517
  112.5 3.9 %last.1 = (f32[240,1536]{1,0:T(8,128)}, bf16[240,1536]{1,0:T(8,128)(2,1)}, f32[192,512]{1,0:T(8,128)}) custom-call(s32[5]{0:T(128)S(1)} %stack.23.bits, f32[1,512]{1,0:T(1,128)S(1)} %get-tuple-element.52.squares, f32[240,512]{1,0:T(8,128)S(1)} %left.1, f32[192,512]{1,0:T(8,128)S(1)} %get-tuple-element.53.own_right, ...), custom_call_target="tpu_custom_call", output_to_operand_aliasing={{0}: (15, {})} | custom-call | tf_op jit(solution)/shard_map/last/pallas_call | solution.py:530
  (60 shorter events, 26.8 us)
Async XLA Ops:
  3.9 20.8 %collective-permute-start.1 = (f32[240,384]{1,0:T(8,128)S(1)}, f32[240,384]{1,0:T(8,128)S(1)}, u32[]{:S(2)}, u32[]{:S(2)}) collective-permute-start(f32[240,384]{1,0:T(8,128)S(1)} %get-tuple-element.37.refs_1_), channel_id=1, source_target_pairs={{0,4},{4,0},{8,12},{12,8},{16,20},{20,16},{24,28},{28,24},{1,5},{5... | collective-permute-start | bytes 1105928 | tf_op jit(solution)/shard_map/ppermute | solution.py:225
  6.9 17.8 %collective-permute-start.2 = (f32[240,384]{1,0:T(8,128)S(1)}, f32[240,384]{1,0:T(8,128)S(1)}, u32[]{:S(2)}, u32[]{:S(2)}) collective-permute-start(f32[240,384]{1,0:T(8,128)S(1)} %get-tuple-element.38.refs_2_), channel_id=1, source_target_pairs={{0,8},{4,12},{8,0},{12,4},{16,24},{20,28},{24,16},{28,20},{1,9},{5... | collective-permute-start | bytes 1105928 | tf_op jit(solution)/shard_map/ppermute | solution.py:225
  8.5 16.3 %collective-permute-start.3 = (f32[240,384]{1,0:T(8,128)S(1)}, f32[240,384]{1,0:T(8,128)S(1)}, u32[]{:S(2)}, u32[]{:S(2)}) collective-permute-start(f32[240,384]{1,0:T(8,128)S(1)} %get-tuple-element.39.refs_7_), channel_id=1, source_target_pairs={{0,12},{4,8},{8,4},{12,0},{16,28},{20,24},{24,20},{28,16},{1,13},{... | collective-permute-start | bytes 1105928 | tf_op jit(solution)/shard_map/ppermute | solution.py:225
  16.5 8.3 %collective-permute-start = (f32[120,512]{1,0:T(8,128)S(1)}, f32[120,512]{1,0:T(8,128)S(1)}, u32[]{:S(2)}, u32[]{:S(2)}) collective-permute-start(f32[120,512]{1,0:T(8,128)S(1)} %core_add.1.refs_0_), channel_id=1, source_target_pairs={{0,2},{1,3},{2,0},{3,1},{4,6},{5,7},{6,4},{7,5},{8,10},{9,11},{10,... | collective-permute-start | bytes 737288 | tf_op jit(solution)/shard_map/ppermute | solution.py:225
  24.8 9.9 %collective-permute-start.6 = (f32[120,512]{1,0:T(8,128)S(1)}, f32[120,512]{1,0:T(8,128)S(1)}, u32[]{:S(2)}, u32[]{:S(2)}) collective-permute-start(f32[120,512]{1,0:T(8,128)S(1)} %add_after.3.refs_0_.mine), channel_id=1, source_target_pairs={{0,12},{4,8},{8,4},{12,0},{16,28},{20,24},{24,20},{28,16},{1,13},{... | collective-permute-start | bytes 737288 | tf_op jit(solution)/shard_map/ppermute | solution.py:225
  27.6 10.9 %collective-permute-start.5 = (f32[120,512]{1,0:T(8,128)S(1)}, f32[120,512]{1,0:T(8,128)S(1)}, u32[]{:S(2)}, u32[]{:S(2)}) collective-permute-start(f32[120,512]{1,0:T(8,128)S(1)} %add_after.3.refs_0_.mine), channel_id=1, source_target_pairs={{0,8},{4,12},{8,0},{12,4},{16,24},{20,28},{24,16},{28,20},{1,9},{5... | collective-permute-start | bytes 737288 | tf_op jit(solution)/shard_map/ppermute | solution.py:225
  28.1 10.5 %collective-permute-start.4 = (f32[120,512]{1,0:T(8,128)S(1)}, f32[120,512]{1,0:T(8,128)S(1)}, u32[]{:S(2)}, u32[]{:S(2)}) collective-permute-start(f32[120,512]{1,0:T(8,128)S(1)} %add_after.3.refs_0_.mine), channel_id=1, source_target_pairs={{0,4},{4,0},{8,12},{12,8},{16,20},{20,16},{24,28},{28,24},{1,5},{5... | collective-permute-start | bytes 737288 | tf_op jit(solution)/shard_map/ppermute | solution.py:225
  28.4 16.7 %collective-permute-start.9 = (f32[120,512]{1,0:T(8,128)S(1)}, f32[120,512]{1,0:T(8,128)S(1)}, u32[]{:S(2)}, u32[]{:S(2)}) collective-permute-start(f32[120,512]{1,0:T(8,128)S(1)} %add_after.3.refs_0_.mine), channel_id=1, source_target_pairs={{0,1},{1,0},{2,3},{3,2},{4,5},{5,4},{6,7},{7,6},{8,9},{9,8},{10,11... | collective-permute-start | bytes 737288 | tf_op jit(solution)/shard_map/ppermute | solution.py:225
  34.7 10.4 %collective-permute-start.12 = (f32[120,512]{1,0:T(8,128)S(1)}, f32[120,512]{1,0:T(8,128)S(1)}, u32[]{:S(2)}, u32[]{:S(2)}) collective-permute-start(f32[120,512]{1,0:T(8,128)S(1)} %collective-permute-done.6.refs_3_), channel_id=1, source_target_pairs={{0,1},{1,0},{2,3},{3,2},{4,5},{5,4},{6,7},{7,6},{8,9},{9,8},{10,11... | collective-permute-start | bytes 737288 | tf_op jit(solution)/shard_map/ppermute | solution.py:225
  38.5 6.6 %collective-permute-start.11 = (f32[120,512]{1,0:T(8,128)S(1)}, f32[120,512]{1,0:T(8,128)S(1)}, u32[]{:S(2)}, u32[]{:S(2)}) collective-permute-start(f32[120,512]{1,0:T(8,128)S(1)} %collective-permute-done.5.refs_2_), channel_id=1, source_target_pairs={{0,1},{1,0},{2,3},{3,2},{4,5},{5,4},{6,7},{7,6},{8,9},{9,8},{10,11... | collective-permute-start | bytes 737288 | tf_op jit(solution)/shard_map/ppermute | solution.py:225
  38.5 6.6 %collective-permute-start.10 = (f32[120,512]{1,0:T(8,128)S(1)}, f32[120,512]{1,0:T(8,128)S(1)}, u32[]{:S(2)}, u32[]{:S(2)}) collective-permute-start(f32[120,512]{1,0:T(8,128)S(1)} %collective-permute-done.4.refs_1_), channel_id=1, source_target_pairs={{0,1},{1,0},{2,3},{3,2},{4,5},{5,4},{6,7},{7,6},{8,9},{9,8},{10,11... | collective-permute-start | bytes 737288 | tf_op jit(solution)/shard_map/ppermute | solution.py:225
  42.5 7.2 %collective-permute-start.8 = (f32[160,128]{1,0:T(8,128)S(1)}, f32[160,128]{1,0:T(8,128)S(1)}, u32[]{:S(2)}, u32[]{:S(2)}) collective-permute-start(f32[160,128]{1,0:T(8,128)S(1)} %add.20.token.refs_0_), channel_id=1, source_target_pairs={{0,16},{4,20},{8,24},{12,28},{16,0},{20,4},{24,8},{28,12},{1,17},{... | collective-permute-start | bytes 245768 | tf_op jit(solution)/shard_map/ppermute | solution.py:225
  48.6 20.3 %collective-permute-start.16 = (f32[192,512]{1,0:T(8,128)S(1)}, f32[192,512]{1,0:T(8,128)S(1)}, u32[]{:S(2)}, u32[]{:S(2)}) collective-permute-start(f32[192,512]{1,0:T(8,128)S(1)} %get-tuple-element.45), channel_id=1, source_target_pairs={{0,16},{4,20},{8,24},{12,28},{16,0},{20,4},{24,8},{28,12},{1,17},{... | collective-permute-start | bytes 1179656 | tf_op jit(solution)/shard_map/ppermute | solution.py:225
  55.0 5.3 %collective-permute-start.14 = (f32[320,128]{1,0:T(8,128)S(1)}, f32[320,128]{1,0:T(8,128)S(1)}, u32[]{:S(2)}, u32[]{:S(2)}) collective-permute-start(f32[320,128]{1,0:T(8,128)S(1)} %all_gather.7.a), channel_id=1, source_target_pairs={{0,2},{1,3},{2,0},{3,1},{4,6},{5,7},{6,4},{7,5},{8,10},{9,11},{10,... | collective-permute-start | bytes 491528 | tf_op jit(solution)/shard_map/ppermute | solution.py:225
  56.5 3.8 %collective-permute-start.13 = (f32[320,128]{1,0:T(8,128)S(1)}, f32[320,128]{1,0:T(8,128)S(1)}, u32[]{:S(2)}, u32[]{:S(2)}) collective-permute-start(f32[320,128]{1,0:T(8,128)S(1)} %all_gather.7.a), channel_id=1, source_target_pairs={{0,1},{1,0},{2,3},{3,2},{4,5},{5,4},{6,7},{7,6},{8,9},{9,8},{10,11... | collective-permute-start | bytes 491528 | tf_op jit(solution)/shard_map/ppermute | solution.py:225
  68.9 19.5 %collective-permute-start.19 = (f32[192,512]{1,0:T(8,128)S(1)}, f32[192,512]{1,0:T(8,128)S(1)}, u32[]{:S(2)}, u32[]{:S(2)}) collective-permute-start(f32[192,512]{1,0:T(8,128)S(1)} %add_after.5.own), channel_id=1, source_target_pairs={{0,16},{4,20},{8,24},{12,28},{16,0},{20,4},{24,8},{28,12},{1,17},{... | collective-permute-start | bytes 1179656 | tf_op jit(solution)/shard_map/ppermute | solution.py:225
  69.0 19.5 %collective-permute-start.18 = (f32[192,512]{1,0:T(8,128)S(1)}, f32[192,512]{1,0:T(8,128)S(1)}, u32[]{:S(2)}, u32[]{:S(2)}) collective-permute-start(f32[192,512]{1,0:T(8,128)S(1)} %add_after.5.own), channel_id=1, source_target_pairs={{0,8},{4,12},{8,0},{12,4},{16,24},{20,28},{24,16},{28,20},{1,9},{5... | collective-permute-start | bytes 1179656 | tf_op jit(solution)/shard_map/ppermute | solution.py:225
  71.0 17.6 %collective-permute-start.17 = (f32[192,512]{1,0:T(8,128)S(1)}, f32[192,512]{1,0:T(8,128)S(1)}, u32[]{:S(2)}, u32[]{:S(2)}) collective-permute-start(f32[192,512]{1,0:T(8,128)S(1)} %add_after.5.own), channel_id=1, source_target_pairs={{0,4},{4,0},{8,12},{12,8},{16,20},{20,16},{24,28},{28,24},{1,5},{5... | collective-permute-start | bytes 1179656 | tf_op jit(solution)/shard_map/ppermute | solution.py:225
  89.7 16.2 %collective-permute-start.21 = (f32[192,512]{1,0:T(8,128)S(1)}, f32[192,512]{1,0:T(8,128)S(1)}, u32[]{:S(2)}, u32[]{:S(2)}) collective-permute-start(f32[192,512]{1,0:T(8,128)S(1)} %get-tuple-element.48.refs_3_.refs_0_), channel_id=1, source_target_pairs={{0,8},{4,12},{8,0},{12,4},{16,24},{20,28},{24,16},{28,20},{1,9},{5... | collective-permute-start | bytes 1179656 | tf_op jit(solution)/shard_map/ppermute | solution.py:225
  89.8 16.2 %collective-permute-start.20 = (f32[192,512]{1,0:T(8,128)S(1)}, f32[192,512]{1,0:T(8,128)S(1)}, u32[]{:S(2)}, u32[]{:S(2)}) collective-permute-start(f32[192,512]{1,0:T(8,128)S(1)} %get-tuple-element.48.refs_3_.refs_0_), channel_id=1, source_target_pairs={{0,4},{4,0},{8,12},{12,8},{16,20},{20,16},{24,28},{28,24},{1,5},{5... | collective-permute-start | bytes 1179656 | tf_op jit(solution)/shard_map/ppermute | solution.py:225
  98.1 7.9 %collective-permute-start.24 = (f32[104,512]{1,0:T(8,128)S(1)}, f32[104,512]{1,0:T(8,128)S(1)}, u32[]{:S(2)}, u32[]{:S(2)}) collective-permute-start(f32[104,512]{1,0:T(8,128)S(1)} %get-tuple-element.50), channel_id=1, source_target_pairs={{0,8},{4,12},{8,0},{12,4},{16,24},{20,28},{24,16},{28,20},{1,9},{5... | collective-permute-start | bytes 638984 | tf_op jit(solution)/shard_map/ppermute | solution.py:225
  100.1 5.8 %collective-permute-start.25 = (f32[96,512]{1,0:T(8,128)S(1)}, f32[96,512]{1,0:T(8,128)S(1)}, u32[]{:S(2)}, u32[]{:S(2)}) collective-permute-start(f32[96,512]{1,0:T(8,128)S(1)} %get-tuple-element.51), channel_id=1, source_target_pairs={{0,4},{4,0},{8,12},{12,8},{16,20},{20,16},{24,28},{28,24},{1,5},{5... | collective-permute-start | bytes 589832 | tf_op jit(solution)/shard_map/ppermute | solution.py:225
  106.0 6.5 %collective-permute-start.26 = (f32[104,512]{1,0:T(8,128)S(1)}, f32[104,512]{1,0:T(8,128)S(1)}, u32[]{:S(2)}, u32[]{:S(2)}) collective-permute-start(f32[104,512]{1,0:T(8,128)S(1)} %get-tuple-element.57), channel_id=1, source_target_pairs={{0,4},{4,0},{8,12},{12,8},{16,20},{20,16},{24,28},{28,24},{1,5},{5... | collective-permute-start | bytes 638984 | tf_op jit(solution)/shard_map/ppermute | solution.py:225
  106.8 5.7 %collective-permute-start.27 = (f32[96,512]{1,0:T(8,128)S(1)}, f32[96,512]{1,0:T(8,128)S(1)}, u32[]{:S(2)}, u32[]{:S(2)}) collective-permute-start(f32[96,512]{1,0:T(8,128)S(1)} %get-tuple-element.58), channel_id=1, source_target_pairs={{0,8},{4,12},{8,0},{12,4},{16,24},{20,28},{24,16},{28,20},{1,9},{5... | collective-permute-start | bytes 589832 | tf_op jit(solution)/shard_map/ppermute | solution.py:225
  (7 other events, 11.9 us)

commit v10 on v9

--- a/solution.py
+++ b/solution.py
@@ -293,13 +293,14 @@
     squares[...] = before[...] + jnp.sum(right * right, axis=0, keepdims=True)
 
 
-def beside_kernel(inverse, one, two, squares, rights, first, second):
+def beside_kernel(inverse, one, two, token, rights, first, second):
     count = one.shape[0]
     middle = count // 2
     rights[:count, :] = dot(one[...], inverse[...], ((1,), (1,)))
     rights[count:, :] = dot(two[...], inverse[...], ((1,), (1,)))
-    first[...] = rights[count : count + middle, :]
-    with_row(rights.at[middle:count], squares[...], second)
+    for out, at in ((first, count), (second, middle)):
+        out[:middle, :] = rights[at : at + middle, :]
+        out[middle:, :] = jnp.zeros((out.shape[0] - middle, out.shape[1]), jnp.float32)
 
 
 def with_row(rows, value, out):
@@ -316,10 +317,9 @@
     left[...] = dot(rows[...], inverse[...], ((1,), (1,)))
 
 
-def forward_kernel(one, two, squares, own_second, left, own_first, first, second, total):
+def forward_kernel(one, two, squares, first, second):
     middle = second.shape[0]
-    total[...] = squares[...] + own_second[middle : middle + 1, :]
-    with_row(two.at[:middle], total[...], first)
+    with_row(two.at[:middle], squares[...], first)
     second[...] = one[middle:, :]
 
 
@@ -357,7 +357,7 @@
 
 
 def last_kernel(factor, bits, squares, left, own_right, rights, own_splits, splits, *refs):
-    received, (own_first, own_second, first, second, piece, _, new_momentum, update, next_basis), scratch = (
+    received, (first, second, own_first, own_second, piece, _, new_momentum, update, next_basis), scratch = (
         refs[:3],
         refs[3:12],
         refs[12:],
@@ -372,7 +372,7 @@
         copies.append(pltpu.make_async_copy(source, target, sent.at[index]))
         copies[-1].start()
 
-    last_own[:middle, :] = own_first[...]
+    last_own[:middle, :] = own_first[:middle, :]
     last_own[middle:, :] = own_second[:middle, :]
     last_received[:middle, :] = first[:middle, :]
     last_received[middle:, :] = second[...]
@@ -488,14 +488,16 @@
 
     half_rows = shape(half_width // 2, rank)
     with_norms = shape(half_width // 2 + 8, rank)
+    padded = shape(half_width // 2 + 8, rank)
     rights, own_first, own_second = kernel(
         beside_kernel,
-        [shape(2 * half_width, rank), half_rows, with_norms],
-        [vmem] * 4,
+        [shape(2 * half_width, rank), padded, padded],
+        [vmem] * 3 + [anywhere],
         [],
         "beside",
     )(inverse, *beside, squares)
     own_first, own_second = swap(own_first, "fsdp", 1), swap(own_second, "fsdp", 2)
+    squares = squares + swap(squares, "fsdp", 2)
     left = kernel(
         left_kernel,
         shape(rows, rank),
@@ -504,13 +506,9 @@
         "left",
         cost=2**23,
     )(bits, mine, others[0], inverse)
-    first, second, squares = kernel(
-        forward_kernel,
-        [with_norms, half_rows, shape(1, rank)],
-        [vmem] * 4 + [anywhere] * 2,
-        [],
-        "forward",
-    )(received_rows[1], received_rows[2], squares, own_second, left, own_first)
+    first, second = kernel(
+        forward_kernel, [with_norms, half_rows], [vmem] * 3, [], "forward"
+    )(received_rows[1], received_rows[2], squares)
     first, second = swap(first, "fsdp", 1), swap(second, "fsdp", 2)
 
     splits_shape = shape(3 * half_width, 3 * rank, dtype=jnp.bfloat16)
@@ -549,7 +547,7 @@
         aliases={15: 0},
     )(
         *(bits, squares, left, own_right, rights, own_splits, splits, *received_rows),
-        *(own_first, own_second, first, second, pieces[3], new_momentum),
+        *(first, second, own_first, own_second, pieces[3], new_momentum),
     )
     return (update, new_momentum, left_scaled, next_basis)
 

time: 117 us -> 115 us (0.983)
  waiting for transfers between devices: 36.8 us -> 33.6 us
  starting transfers between devices: 26.3 us -> 27.9 us
    ppermute x28 -> x29, waiting for transfers between devices: 36.8 us -> 33.6 us  [swap(): lax.ppermute(value, axis, [(i, i ^ flip) for i in range(lax.axis_size(axi...]
    ppermute x28 -> x29, starting transfers between devices: 26.3 us -> 27.9 us  [swap(): lax.ppermute(value, axis, [(i, i ^ flip) for i in range(lax.axis_size(axi...]
  transfers between devices with their start and end apart: 28 -> 29, of which waited for: 14 -> 13; matrix products, arithmetic and copies ran while one was open for 0% -> 0% of each run, Pallas kernels for 30% -> 30%
where the time goes in v10:
time: 115 us
  Pallas kernels  40.7 us (35%)
  waiting for transfers between devices  33.6 us (29%)
  starting transfers between devices  27.9 us (24%)
  blocking collectives  7.46 us (6%)
  local copies, waits for them, and re-layouts  4.46 us (4%)
    ppermute x29, waiting for transfers between devices, swap(): lax.ppermute(value, axis, [(i, i ^ flip) for i in range(lax.axis_size(axi...  33.6 us
    ppermute x29, starting transfers between devices, swap(): lax.ppermute(value, axis, [(i, i ^ flip) for i in range(lax.axis_size(axi...  27.9 us
    pallas_call x1, Pallas kernels, later_steps(): kernel(later_kernel, [shape(size, size), shape(*own.shape), shape(1, size...  13.5 us
    all_gather x1, blocking collectives, in_squares(): lax.all_gather(part, 'fsdp', axis=0, tiled=True, axis_index_groups=chips)  5.3 us
    pallas_call x1, Pallas kernels, first_step(): kernel(first_kernel, [shape(lanes, size), shape(size, size)], [smem] + [v...  5.06 us
    unnamed x6, local copies, waits for them, and re-layouts  4.38 us
    pallas_call x1, Pallas kernels, in_squares(): kernel(functools.partial(last_kernel, math.sqrt(total_rows / total_cols))...  3.99 us
    pallas_call x1, Pallas kernels, in_squares(): kernel(raw_kernel, [shape(width // 2, rank)] * 2, [smem, anywhere] + [vme...  3.42 us
  transfers between devices with their start and end apart: 29, of which 13 were waited for; matrix products, arithmetic and copies ran while one was open for 0% of the time, Pallas kernels for 30%

profile of v10, /device:TPU:0, one launch (start us, length us, event | category | flops | bytes accessed | tf_op | source)
XLA Modules:
  0.0 115.2 jit_solution(15914655052414889740)
XLA Ops:
  3.9 3.0 %collective-permute-start.1 = (f32[240,384]{1,0:T(8,128)S(1)}, f32[240,384]{1,0:T(8,128)S(1)}, u32[]{:S(2)}, u32[]{:S(2)}) collective-permute-start(f32[240,384]{1,0:T(8,128)S(1)} %get-tuple-element.36.refs_1_), channel_id=1, source_target_pairs={{0,4},{4,0},{8,12},{12,8},{16,20},{20,16},{24,28},{28,24},{1,5},{5... | collective-permute-start | bytes 1105928 | tf_op jit(solution)/shard_map/ppermute | solution.py:225
  10.4 3.4 %part_left.1 = (f32[120,512]{1,0:T(8,128)S(1)}, f32[120,512]{1,0:T(8,128)S(1)}) custom-call(s32[5]{0:T(128)S(1)} %stack.23.bits, f32[1536,512]{1,0:T(8,128)S(1)} %copy-done.1, f32[240,1536]{1,0:T(8,128)S(1)} %copy-done, bf16[240,1536]{1,0:T(8,128)(2,1)S(1)} %copy-done.2, f32[240,384]{1,0:T(8,128)S(1)} %get-tuple-element.33.token.refs_8_.refs_0_), custom_call_target="tpu_custom_call" | custom-call | tf_op jit(solution)/shard_map/part_left/pallas_call | solution.py:425
  13.8 2.2 %all_gather.6.both = f32[240,512]{1,0:T(8,128)S(1)} all-gather(f32[120,512]{1,0:T(8,128)S(1)} %get-tuple-element.35), channel_id=1, replica_groups={{0,1},{2,3},{4,5},{6,7},{8,9},{10,11},{12,13},{14,15},{16,17},{18,19},{..., dimensions={0}, use_global_device_ids=true | all-gather | bytes 737280 | tf_op jit(solution)/shard_map/all_gather | solution.py:433
  16.5 2.0 %collective-permute-start = (f32[120,512]{1,0:T(8,128)S(1)}, f32[120,512]{1,0:T(8,128)S(1)}, u32[]{:S(2)}, u32[]{:S(2)}) collective-permute-start(f32[120,512]{1,0:T(8,128)S(1)} %core_add.1.refs_0_), channel_id=1, source_target_pairs={{0,2},{1,3},{2,0},{3,1},{4,6},{5,7},{6,4},{7,5},{8,10},{9,11},{10,... | collective-permute-start | bytes 737288 | tf_op jit(solution)/shard_map/ppermute | solution.py:225
  18.5 6.3 %collective-permute-done.refs_1_ = f32[120,512]{1,0:T(8,128)S(1)} collective-permute-done((f32[120,512]{1,0:T(8,128)S(1)}, f32[120,512]{1,0:T(8,128)S(1)}, u32[]{:S(2)}, u32[]{:S(2)}) %collective-permute-start) | collective-permute-done | bytes 245792 | tf_op jit(solution)/shard_map/ppermute | solution.py:225
  24.8 2.8 %collective-permute-start.6 = (f32[120,512]{1,0:T(8,128)S(1)}, f32[120,512]{1,0:T(8,128)S(1)}, u32[]{:S(2)}, u32[]{:S(2)}) collective-permute-start(f32[120,512]{1,0:T(8,128)S(1)} %add_after.3.refs_0_.mine), channel_id=1, source_target_pairs={{0,12},{4,8},{8,4},{12,0},{16,28},{20,24},{24,20},{28,16},{1,13},{... | collective-permute-start | bytes 737288 | tf_op jit(solution)/shard_map/ppermute | solution.py:225
  28.4 6.3 %collective-permute-done.6.refs_3_ = f32[120,512]{1,0:T(8,128)S(1)} collective-permute-done((f32[120,512]{1,0:T(8,128)S(1)}, f32[120,512]{1,0:T(8,128)S(1)}, u32[]{:S(2)}, u32[]{:S(2)}) %collective-permute-start.6) | collective-permute-done | bytes 245792 | tf_op jit(solution)/shard_map/ppermute | solution.py:225
  34.7 3.8 %collective-permute-done.5.refs_2_ = f32[120,512]{1,0:T(8,128)S(1)} collective-permute-done((f32[120,512]{1,0:T(8,128)S(1)}, f32[120,512]{1,0:T(8,128)S(1)}, u32[]{:S(2)}, u32[]{:S(2)}) %collective-permute-start.5) | collective-permute-done | bytes 245792 | tf_op jit(solution)/shard_map/ppermute | solution.py:225
  39.0 2.1 %part_gram.1 = (f32[160,128]{1,0:T(8,128)S(1)}, f32[160,128]{1,0:T(8,128)S(1)}) custom-call(s32[5]{0:T(128)S(1)} %stack.23.bits, f32[120,512]{1,0:T(8,128)S(1)} %add_after.3.refs_0_.mine, f32[120,512]{1,0:T(8,128)S(1)} %collective-permute-done.4.refs_1_, f32[120,512]{1,0:T(8,128)S(1)} %collective-permute-done.5.refs_2_, ...), custom_call_target="tpu_custom_call" | custom-call | tf_op jit(solution)/shard_map/part_gram/pallas_call | solution.py:444
  42.5 2.6 %collective-permute-start.8 = (f32[160,128]{1,0:T(8,128)S(1)}, f32[160,128]{1,0:T(8,128)S(1)}, u32[]{:S(2)}, u32[]{:S(2)}) collective-permute-start(f32[160,128]{1,0:T(8,128)S(1)} %add.23.token.refs_0_), channel_id=1, source_target_pairs={{0,16},{4,20},{8,24},{12,28},{16,0},{20,4},{24,8},{28,12},{1,17},{... | collective-permute-start | bytes 245768 | tf_op jit(solution)/shard_map/ppermute | solution.py:225
  45.2 3.4 %part_raw.1 = (f32[192,512]{1,0:T(8,128)S(1)}, f32[192,512]{1,0:T(8,128)S(1)}) custom-call(s32[5]{0:T(128)S(1)} %stack.23.bits, f32[160,128]{1,0:T(8,128)S(1)} %add.23.token.refs_0_, f32[120,512]{1,0:T(8,128)S(1)} %add_after.3.refs_0_.mine, f32[120,512]{1,0:T(8,128)S(1)} %collective-permute-done.4.refs_1_, f32[120,512]{1,0:T(8,128)S(1)} %collective-permute-done.5.refs_2_, ...), custom_call_target="tpu_custom_call" | custom-call | tf_op jit(solution)/shard_map/part_raw/pallas_call | solution.py:453
  49.7 5.3 %all_gather.7.a = f32[320,128]{1,0:T(8,128)S(1)} all-gather(f32[160,128]{1,0:T(8,128)S(1)} %add_after.4), channel_id=1, replica_groups={{0,4},{8,12},{16,20},{24,28},{1,5},{9,13},{17,21},{25,29},{2,6},{10,14}..., dimensions={0}, use_global_device_ids=true | all-gather | bytes 245760 | tf_op jit(solution)/shard_map/all_gather | solution.py:467
  56.5 3.8 %collective-permute-done.14.c = f32[320,128]{1,0:T(8,128)S(1)} collective-permute-done((f32[320,128]{1,0:T(8,128)S(1)}, f32[320,128]{1,0:T(8,128)S(1)}, u32[]{:S(2)}, u32[]{:S(2)}) %collective-permute-start.14) | collective-permute-done | bytes 163872 | tf_op jit(solution)/shard_map/ppermute | solution.py:225
  61.7 5.1 %factor_first.1 = (f32[128,512]{1,0:T(8,128)S(1)}, f32[512,512]{1,0:T(8,128)S(1)}) custom-call(s32[5]{0:T(128)S(1)} %stack.23.bits, f32[320,128]{1,0:T(8,128)S(1)} %all_gather.7.a, f32[320,128]{1,0:T(8,128)S(1)} %collective-permute-done.13.b, f32[320,128]{1,0:T(8,128)S(1)} %collective-permute-done.14.c, f32[320,128]{1,0:T(8,128)S(1)} %collective-permute-done.15.d), custom_call_target="tpu_custom_call" | custom-call | tf_op jit(solution)/shard_map/factor_first/pallas_call | solution.py:169
  66.8 2.1 %collective-permute-done.16.refs_1_ = f32[192,512]{1,0:T(8,128)S(1)} collective-permute-done((f32[192,512]{1,0:T(8,128)S(1)}, f32[192,512]{1,0:T(8,128)S(1)}, u32[]{:S(2)}, u32[]{:S(2)}) %collective-permute-start.16) | collective-permute-done | bytes 393248 | tf_op jit(solution)/shard_map/ppermute | solution.py:225
  69.0 2.0 %collective-permute-start.18 = (f32[192,512]{1,0:T(8,128)S(1)}, f32[192,512]{1,0:T(8,128)S(1)}, u32[]{:S(2)}, u32[]{:S(2)}) collective-permute-start(f32[192,512]{1,0:T(8,128)S(1)} %add_after.5.own), channel_id=1, source_target_pairs={{0,8},{4,12},{8,0},{12,4},{16,24},{20,28},{24,16},{28,20},{1,9},{5... | collective-permute-start | bytes 1179656 | tf_op jit(solution)/shard_map/ppermute | solution.py:225
  72.2 13.5 %factor_later.1 = (f32[512,512]{1,0:T(8,128)S(1)}, f32[192,512]{1,0:T(8,128)S(1)}, f32[1,512]{1,0:T(1,128)S(1)}) custom-call(f32[512,512]{1,0:T(8,128)S(1)} %get-tuple-element.42.before, f32[128,512]{1,0:T(8,128)S(1)} %get-tuple-element.43.refs_2_.first, f32[192,512]{1,0:T(8,128)S(1)} %add_after.5.own), custom_call_target="tpu_custom_call" | custom-call | tf_op jit(solution)/shard_map/factor_later/pallas_call | solution.py:189
  85.7 2.7 %collective-permute-done.19.received = f32[192,512]{1,0:T(8,128)S(1)} collective-permute-done((f32[192,512]{1,0:T(8,128)S(1)}, f32[192,512]{1,0:T(8,128)S(1)}, u32[]{:S(2)}, u32[]{:S(2)}) %collective-permute-start.19) | collective-permute-done | bytes 393248 | tf_op jit(solution)/shard_map/ppermute | solution.py:225
  93.8 2.1 %collective-permute-done.21 = f32[1,512]{1,0:T(1,128)S(1)} collective-permute-done((f32[1,512]{1,0:T(1,128)S(1)}, f32[1,512]{1,0:T(1,128)S(1)}, u32[]{:S(2)}, u32[]{:S(2)}) %collective-permute-start.21) | collective-permute-done | bytes 2080 | tf_op jit(solution)/shard_map/ppermute | solution.py:225
  95.9 1.9 %collective-permute-start.22 = (f32[1,512]{1,0:T(1,128)S(1)}, f32[1,512]{1,0:T(1,128)S(1)}, u32[]{:S(2)}, u32[]{:S(2)}) collective-permute-start(f32[1,512]{1,0:T(1,128)S(1)} %add.25.token), channel_id=1, source_target_pairs={{0,8},{4,12},{8,0},{12,4},{16,24},{20,28},{24,16},{28,20},{1,9},{5... | collective-permute-start | bytes 6152 | tf_op jit(solution)/shard_map/ppermute | solution.py:225
  97.9 2.2 %beside.1 = (f32[384,512]{1,0:T(8,128)S(1)}, f32[104,512]{1,0:T(8,128)S(1)}, f32[104,512]{1,0:T(8,128)S(1)}) custom-call(f32[512,512]{1,0:T(8,128)S(1)} %get-tuple-element.45.inverse, f32[192,512]{1,0:T(8,128)S(1)} %collective-permute-done.17.one, f32[192,512]{1,0:T(8,128)S(1)} %collective-permute-done.18.two, f32[1,512]{1,0:T(1,128)S(1)} %add.25.token), custom_call_target="tpu_custom_call" | custom-call | tf_op jit(solution)/shard_map/beside/pallas_call | solution.py:492
  102.4 2.1 %collective-permute-start.26 = (f32[96,512]{1,0:T(8,128)S(1)}, f32[96,512]{1,0:T(8,128)S(1)}, u32[]{:S(2)}, u32[]{:S(2)}) collective-permute-start(f32[96,512]{1,0:T(8,128)S(1)} %get-tuple-element.54), channel_id=1, source_target_pairs={{0,8},{4,12},{8,0},{12,4},{16,24},{20,28},{24,16},{28,20},{1,9},{5... | collective-permute-start | bytes 589832 | tf_op jit(solution)/shard_map/ppermute | solution.py:225
  106.1 3.0 %new_momentum.1 = (f32[240,1536]{1,0:T(8,128)}, f32[240,512]{1,0:T(8,128)}, bf16[576,1536]{1,0:T(8,128)(2,1)S(1)}, bf16[576,1536]{1,0:T(8,128)(2,1)S(1)}) custom-call(s32[5]{0:T(128)S(1)} %stack.23.bits, f32[240,512]{1,0:T(8,128)S(1)} %left.1, f32[192,512]{1,0:T(8,128)S(1)} %get-tuple-element.48.own_right, f32[384,512]{1,0:T(8,128)S(1)} %get-tuple-element.49.rights, ...), custom_call_target="tpu_custom_call" | custom-call | bytes 16777216 | tf_op jit(solution)/shard_map/new_momentum/pallas_call | solution.py:515
  111.0 4.0 %last.1 = (f32[240,1536]{1,0:T(8,128)}, bf16[240,1536]{1,0:T(8,128)(2,1)}, f32[192,512]{1,0:T(8,128)}) custom-call(s32[5]{0:T(128)S(1)} %stack.23.bits, f32[1,512]{1,0:T(1,128)S(1)} %add.26.squares, f32[240,512]{1,0:T(8,128)S(1)} %left.1, f32[192,512]{1,0:T(8,128)S(1)} %get-tuple-element.48.own_right, ...), custom_call_target="tpu_custom_call", output_to_operand_aliasing={{0}: (15, {})} | custom-call | tf_op jit(solution)/shard_map/last/pallas_call | solution.py:528
  (63 shorter events, 26.7 us)
Async XLA Ops:
  3.9 20.8 %collective-permute-start.1 = (f32[240,384]{1,0:T(8,128)S(1)}, f32[240,384]{1,0:T(8,128)S(1)}, u32[]{:S(2)}, u32[]{:S(2)}) collective-permute-start(f32[240,384]{1,0:T(8,128)S(1)} %get-tuple-element.36.refs_1_), channel_id=1, source_target_pairs={{0,4},{4,0},{8,12},{12,8},{16,20},{20,16},{24,28},{28,24},{1,5},{5... | collective-permute-start | bytes 1105928 | tf_op jit(solution)/shard_map/ppermute | solution.py:225
  6.9 17.8 %collective-permute-start.2 = (f32[240,384]{1,0:T(8,128)S(1)}, f32[240,384]{1,0:T(8,128)S(1)}, u32[]{:S(2)}, u32[]{:S(2)}) collective-permute-start(f32[240,384]{1,0:T(8,128)S(1)} %get-tuple-element.37.refs_2_), channel_id=1, source_target_pairs={{0,8},{4,12},{8,0},{12,4},{16,24},{20,28},{24,16},{28,20},{1,9},{5... | collective-permute-start | bytes 1105928 | tf_op jit(solution)/shard_map/ppermute | solution.py:225
  8.5 16.3 %collective-permute-start.3 = (f32[240,384]{1,0:T(8,128)S(1)}, f32[240,384]{1,0:T(8,128)S(1)}, u32[]{:S(2)}, u32[]{:S(2)}) collective-permute-start(f32[240,384]{1,0:T(8,128)S(1)} %get-tuple-element.38.refs_7_), channel_id=1, source_target_pairs={{0,12},{4,8},{8,4},{12,0},{16,28},{20,24},{24,20},{28,16},{1,13},{... | collective-permute-start | bytes 1105928 | tf_op jit(solution)/shard_map/ppermute | solution.py:225
  16.5 8.3 %collective-permute-start = (f32[120,512]{1,0:T(8,128)S(1)}, f32[120,512]{1,0:T(8,128)S(1)}, u32[]{:S(2)}, u32[]{:S(2)}) collective-permute-start(f32[120,512]{1,0:T(8,128)S(1)} %core_add.1.refs_0_), channel_id=1, source_target_pairs={{0,2},{1,3},{2,0},{3,1},{4,6},{5,7},{6,4},{7,5},{8,10},{9,11},{10,... | collective-permute-start | bytes 737288 | tf_op jit(solution)/shard_map/ppermute | solution.py:225
  24.8 9.9 %collective-permute-start.6 = (f32[120,512]{1,0:T(8,128)S(1)}, f32[120,512]{1,0:T(8,128)S(1)}, u32[]{:S(2)}, u32[]{:S(2)}) collective-permute-start(f32[120,512]{1,0:T(8,128)S(1)} %add_after.3.refs_0_.mine), channel_id=1, source_target_pairs={{0,12},{4,8},{8,4},{12,0},{16,28},{20,24},{24,20},{28,16},{1,13},{... | collective-permute-start | bytes 737288 | tf_op jit(solution)/shard_map/ppermute | solution.py:225
  27.6 10.9 %collective-permute-start.5 = (f32[120,512]{1,0:T(8,128)S(1)}, f32[120,512]{1,0:T(8,128)S(1)}, u32[]{:S(2)}, u32[]{:S(2)}) collective-permute-start(f32[120,512]{1,0:T(8,128)S(1)} %add_after.3.refs_0_.mine), channel_id=1, source_target_pairs={{0,8},{4,12},{8,0},{12,4},{16,24},{20,28},{24,16},{28,20},{1,9},{5... | collective-permute-start | bytes 737288 | tf_op jit(solution)/shard_map/ppermute | solution.py:225
  28.1 10.5 %collective-permute-start.4 = (f32[120,512]{1,0:T(8,128)S(1)}, f32[120,512]{1,0:T(8,128)S(1)}, u32[]{:S(2)}, u32[]{:S(2)}) collective-permute-start(f32[120,512]{1,0:T(8,128)S(1)} %add_after.3.refs_0_.mine), channel_id=1, source_target_pairs={{0,4},{4,0},{8,12},{12,8},{16,20},{20,16},{24,28},{28,24},{1,5},{5... | collective-permute-start | bytes 737288 | tf_op jit(solution)/shard_map/ppermute | solution.py:225
  28.4 16.7 %collective-permute-start.9 = (f32[120,512]{1,0:T(8,128)S(1)}, f32[120,512]{1,0:T(8,128)S(1)}, u32[]{:S(2)}, u32[]{:S(2)}) collective-permute-start(f32[120,512]{1,0:T(8,128)S(1)} %add_after.3.refs_0_.mine), channel_id=1, source_target_pairs={{0,1},{1,0},{2,3},{3,2},{4,5},{5,4},{6,7},{7,6},{8,9},{9,8},{10,11... | collective-permute-start | bytes 737288 | tf_op jit(solution)/shard_map/ppermute | solution.py:225
  34.7 10.4 %collective-permute-start.12 = (f32[120,512]{1,0:T(8,128)S(1)}, f32[120,512]{1,0:T(8,128)S(1)}, u32[]{:S(2)}, u32[]{:S(2)}) collective-permute-start(f32[120,512]{1,0:T(8,128)S(1)} %collective-permute-done.6.refs_3_), channel_id=1, source_target_pairs={{0,1},{1,0},{2,3},{3,2},{4,5},{5,4},{6,7},{7,6},{8,9},{9,8},{10,11... | collective-permute-start | bytes 737288 | tf_op jit(solution)/shard_map/ppermute | solution.py:225
  38.5 6.6 %collective-permute-start.11 = (f32[120,512]{1,0:T(8,128)S(1)}, f32[120,512]{1,0:T(8,128)S(1)}, u32[]{:S(2)}, u32[]{:S(2)}) collective-permute-start(f32[120,512]{1,0:T(8,128)S(1)} %collective-permute-done.5.refs_2_), channel_id=1, source_target_pairs={{0,1},{1,0},{2,3},{3,2},{4,5},{5,4},{6,7},{7,6},{8,9},{9,8},{10,11... | collective-permute-start | bytes 737288 | tf_op jit(solution)/shard_map/ppermute | solution.py:225
  38.5 6.6 %collective-permute-start.10 = (f32[120,512]{1,0:T(8,128)S(1)}, f32[120,512]{1,0:T(8,128)S(1)}, u32[]{:S(2)}, u32[]{:S(2)}) collective-permute-start(f32[120,512]{1,0:T(8,128)S(1)} %collective-permute-done.4.refs_1_), channel_id=1, source_target_pairs={{0,1},{1,0},{2,3},{3,2},{4,5},{5,4},{6,7},{7,6},{8,9},{9,8},{10,11... | collective-permute-start | bytes 737288 | tf_op jit(solution)/shard_map/ppermute | solution.py:225
  42.5 7.2 %collective-permute-start.8 = (f32[160,128]{1,0:T(8,128)S(1)}, f32[160,128]{1,0:T(8,128)S(1)}, u32[]{:S(2)}, u32[]{:S(2)}) collective-permute-start(f32[160,128]{1,0:T(8,128)S(1)} %add.23.token.refs_0_), channel_id=1, source_target_pairs={{0,16},{4,20},{8,24},{12,28},{16,0},{20,4},{24,8},{28,12},{1,17},{... | collective-permute-start | bytes 245768 | tf_op jit(solution)/shard_map/ppermute | solution.py:225
  48.6 20.3 %collective-permute-start.16 = (f32[192,512]{1,0:T(8,128)S(1)}, f32[192,512]{1,0:T(8,128)S(1)}, u32[]{:S(2)}, u32[]{:S(2)}) collective-permute-start(f32[192,512]{1,0:T(8,128)S(1)} %get-tuple-element.44), channel_id=1, source_target_pairs={{0,16},{4,20},{8,24},{12,28},{16,0},{20,4},{24,8},{28,12},{1,17},{... | collective-permute-start | bytes 1179656 | tf_op jit(solution)/shard_map/ppermute | solution.py:225
  55.0 5.3 %collective-permute-start.14 = (f32[320,128]{1,0:T(8,128)S(1)}, f32[320,128]{1,0:T(8,128)S(1)}, u32[]{:S(2)}, u32[]{:S(2)}) collective-permute-start(f32[320,128]{1,0:T(8,128)S(1)} %all_gather.7.a), channel_id=1, source_target_pairs={{0,2},{1,3},{2,0},{3,1},{4,6},{5,7},{6,4},{7,5},{8,10},{9,11},{10,... | collective-permute-start | bytes 491528 | tf_op jit(solution)/shard_map/ppermute | solution.py:225
  68.9 19.5 %collective-permute-start.19 = (f32[192,512]{1,0:T(8,128)S(1)}, f32[192,512]{1,0:T(8,128)S(1)}, u32[]{:S(2)}, u32[]{:S(2)}) collective-permute-start(f32[192,512]{1,0:T(8,128)S(1)} %add_after.5.own), channel_id=1, source_target_pairs={{0,16},{4,20},{8,24},{12,28},{16,0},{20,4},{24,8},{28,12},{1,17},{... | collective-permute-start | bytes 1179656 | tf_op jit(solution)/shard_map/ppermute | solution.py:225
  69.0 19.5 %collective-permute-start.18 = (f32[192,512]{1,0:T(8,128)S(1)}, f32[192,512]{1,0:T(8,128)S(1)}, u32[]{:S(2)}, u32[]{:S(2)}) collective-permute-start(f32[192,512]{1,0:T(8,128)S(1)} %add_after.5.own), channel_id=1, source_target_pairs={{0,8},{4,12},{8,0},{12,4},{16,24},{20,28},{24,16},{28,20},{1,9},{5... | collective-permute-start | bytes 1179656 | tf_op jit(solution)/shard_map/ppermute | solution.py:225
  71.0 17.6 %collective-permute-start.17 = (f32[192,512]{1,0:T(8,128)S(1)}, f32[192,512]{1,0:T(8,128)S(1)}, u32[]{:S(2)}, u32[]{:S(2)}) collective-permute-start(f32[192,512]{1,0:T(8,128)S(1)} %add_after.5.own), channel_id=1, source_target_pairs={{0,4},{4,0},{8,12},{12,8},{16,20},{20,16},{24,28},{28,24},{1,5},{5... | collective-permute-start | bytes 1179656 | tf_op jit(solution)/shard_map/ppermute | solution.py:225
  89.7 11.2 %collective-permute-start.24 = (f32[192,512]{1,0:T(8,128)S(1)}, f32[192,512]{1,0:T(8,128)S(1)}, u32[]{:S(2)}, u32[]{:S(2)}) collective-permute-start(f32[192,512]{1,0:T(8,128)S(1)} %get-tuple-element.50.refs_3_.refs_0_), channel_id=1, source_target_pairs={{0,8},{4,12},{8,0},{12,4},{16,24},{20,28},{24,16},{28,20},{1,9},{5... | collective-permute-start | bytes 1179656 | tf_op jit(solution)/shard_map/ppermute | solution.py:225
  89.8 11.2 %collective-permute-start.23 = (f32[192,512]{1,0:T(8,128)S(1)}, f32[192,512]{1,0:T(8,128)S(1)}, u32[]{:S(2)}, u32[]{:S(2)}) collective-permute-start(f32[192,512]{1,0:T(8,128)S(1)} %get-tuple-element.50.refs_3_.refs_0_), channel_id=1, source_target_pairs={{0,4},{4,0},{8,12},{12,8},{16,20},{20,16},{24,28},{28,24},{1,5},{5... | collective-permute-start | bytes 1179656 | tf_op jit(solution)/shard_map/ppermute | solution.py:225
  95.9 5.0 %collective-permute-start.22 = (f32[1,512]{1,0:T(1,128)S(1)}, f32[1,512]{1,0:T(1,128)S(1)}, u32[]{:S(2)}, u32[]{:S(2)}) collective-permute-start(f32[1,512]{1,0:T(1,128)S(1)} %add.25.token), channel_id=1, source_target_pairs={{0,8},{4,12},{8,0},{12,4},{16,24},{20,28},{24,16},{28,20},{1,9},{5... | collective-permute-start | bytes 6152 | tf_op jit(solution)/shard_map/ppermute | solution.py:225
  100.1 9.0 %collective-permute-start.27 = (f32[104,512]{1,0:T(8,128)S(1)}, f32[104,512]{1,0:T(8,128)S(1)}, u32[]{:S(2)}, u32[]{:S(2)}) collective-permute-start(f32[104,512]{1,0:T(8,128)S(1)} %get-tuple-element.55), channel_id=1, source_target_pairs={{0,4},{4,0},{8,12},{12,8},{16,20},{20,16},{24,28},{28,24},{1,5},{5... | collective-permute-start | bytes 638984 | tf_op jit(solution)/shard_map/ppermute | solution.py:225
  100.9 8.2 %collective-permute-start.28 = (f32[104,512]{1,0:T(8,128)S(1)}, f32[104,512]{1,0:T(8,128)S(1)}, u32[]{:S(2)}, u32[]{:S(2)}) collective-permute-start(f32[104,512]{1,0:T(8,128)S(1)} %get-tuple-element.56), channel_id=1, source_target_pairs={{0,8},{4,12},{8,0},{12,4},{16,24},{20,28},{24,16},{28,20},{1,9},{5... | collective-permute-start | bytes 638984 | tf_op jit(solution)/shard_map/ppermute | solution.py:225
  101.0 10.0 %collective-permute-start.25 = (f32[104,512]{1,0:T(8,128)S(1)}, f32[104,512]{1,0:T(8,128)S(1)}, u32[]{:S(2)}, u32[]{:S(2)}) collective-permute-start(f32[104,512]{1,0:T(8,128)S(1)} %get-tuple-element.53), channel_id=1, source_target_pairs={{0,4},{4,0},{8,12},{12,8},{16,20},{20,16},{24,28},{28,24},{1,5},{5... | collective-permute-start | bytes 638984 | tf_op jit(solution)/shard_map/ppermute | solution.py:225
  102.4 8.6 %collective-permute-start.26 = (f32[96,512]{1,0:T(8,128)S(1)}, f32[96,512]{1,0:T(8,128)S(1)}, u32[]{:S(2)}, u32[]{:S(2)}) collective-permute-start(f32[96,512]{1,0:T(8,128)S(1)} %get-tuple-element.54), channel_id=1, source_target_pairs={{0,8},{4,12},{8,0},{12,4},{16,24},{20,28},{24,16},{28,20},{1,9},{5... | collective-permute-start | bytes 589832 | tf_op jit(solution)/shard_map/ppermute | solution.py:225
  (8 other events, 15.7 us)

commit v11 on v10

--- a/solution.py
+++ b/solution.py
@@ -356,13 +356,19 @@
         copy.wait()
 
 
+def diagonal_kernel(left, one, two, rights, splits, product):
+    middle = rights.shape[0] // 2
+    rights[:middle, :] = one[:middle, :]
+    rights[middle:, :] = two[:middle, :]
+    splits[...] = three_right(rights[...])
+    product[...] = dot_three(three_left(left[...]), splits[...])
+
+
 def last_kernel(factor, bits, squares, left, own_right, rights, own_splits, splits, *refs):
-    received, (first, second, own_first, own_second, piece, _, new_momentum, update, next_basis), scratch = (
-        refs[:3],
-        refs[3:12],
-        refs[12:],
-    )
-    last_own, last_received, last_splits, ready, scaled_ready, basis_ready, sent = scratch
+    received, refs = refs[:3], refs[3:]
+    first, second, last_own, own_last_splits, last_product, piece, _ = refs[:7]
+    new_momentum, update, next_basis = refs[7:10]
+    last_received, last_splits, ready, scaled_ready, basis_ready, sent = refs[10:]
     half, width = basis_ready.shape[0], piece.shape[1]
     middle = half // 2
     norm = jnp.sqrt(squares[...] + first[middle : middle + 1, :] + epsilon)
@@ -372,14 +378,11 @@
         copies.append(pltpu.make_async_copy(source, target, sent.at[index]))
         copies[-1].start()
 
-    last_own[:middle, :] = own_first[:middle, :]
-    last_own[middle:, :] = own_second[:middle, :]
     last_received[:middle, :] = first[:middle, :]
     last_received[middle:, :] = second[...]
-    last_splits[:half, :] = three_right(last_own[...])
-    last_splits[half:, :] = three_right(last_received[...])
-    both = dot_three(three_left(left[...]), last_splits[...])
-    ready[...] = piece[...] - 0.5 * in_order(bits, both[:, :half], both[:, half:])
+    last_splits[...] = three_right(last_received[...])
+    other = dot_three(three_left(left[...]), last_splits[...])
+    ready[...] = piece[...] - 0.5 * in_order(bits, last_product[...], other)
     send(ready, new_momentum.at[:, columns_of(bits, square - 1, width)], square)
     for k in range(square):
 
@@ -398,8 +401,8 @@
             mine = dot_three(scaled, own_splits[parts, :])
             other = dot_three(scaled, splits[parts, :])
         else:
-            both = dot_three(scaled, last_splits[...])
-            mine, other = both[:, :half], both[:, half:]
+            mine = dot_three(scaled, own_last_splits[...])
+            other = dot_three(scaled, last_splits[...])
         scaled_ready[k] = in_order(bits, mine, other).astype(jnp.bfloat16)
         send(scaled_ready.at[k], update.at[:, columns_of(bits, k, width)], k)
     for copy in copies:
@@ -525,6 +528,17 @@
         cost=2**24,
         out_specs=[anywhere] * 2 + [vmem] * 2,
     )(bits, left, own_right, rights, *pieces[:3], *received_rows)
+    last_own = kernel(
+        diagonal_kernel,
+        [
+            shape(half_width, rank),
+            shape(half_width, 3 * rank, dtype=jnp.bfloat16),
+            shape(rows, half_width),
+        ],
+        [vmem] * 3,
+        [],
+        "diagonal",
+    )(left, own_first, own_second)
     new_momentum, update, next_basis = kernel(
         functools.partial(last_kernel, math.sqrt(total_rows / total_cols)),
         [
@@ -532,11 +546,10 @@
             shape(rows, cols, dtype=jnp.bfloat16),
             shape(cols // lax.axis_size("fsdp"), rank),
         ],
-        [smem] + [vmem] * 14 + [anywhere],
+        [smem] + [vmem] * 15 + [anywhere],
         [
             pltpu.VMEM((half_width, rank), jnp.float32),
-            pltpu.VMEM((half_width, rank), jnp.float32),
-            pltpu.VMEM((2 * half_width, 3 * rank), jnp.bfloat16),
+            pltpu.VMEM((half_width, 3 * rank), jnp.bfloat16),
             pltpu.VMEM((rows, width), jnp.float32),
             pltpu.VMEM((square, rows, width), jnp.bfloat16),
             pltpu.VMEM((half_width, rank), jnp.float32),
@@ -544,10 +557,10 @@
         ],
         "last",
         out_specs=[anywhere] * 3,
-        aliases={15: 0},
+        aliases={16: 0},
     )(
         *(bits, squares, left, own_right, rights, own_splits, splits, *received_rows),
-        *(first, second, own_first, own_second, pieces[3], new_momentum),
+        *(first, second, *last_own, pieces[3], new_momentum),
     )
     return (update, new_momentum, left_scaled, next_basis)
 

time: 115 us -> 116 us (level)
  transfers between devices with their start and end apart: 29 -> 29, of which waited for: 13 -> 14; matrix products, arithmetic and copies ran while one was open for 0% -> 0% of each run, Pallas kernels for 30% -> 30%
where the time goes in v11:
time: 116 us
  Pallas kernels  40.8 us (35%)
  waiting for transfers between devices  34.5 us (30%)
  starting transfers between devices  27.9 us (24%)
  blocking collectives  7.46 us (6%)
  local copies, waits for them, and re-layouts  4.46 us (4%)
    ppermute x29, waiting for transfers between devices, swap(): lax.ppermute(value, axis, [(i, i ^ flip) for i in range(lax.axis_size(axi...  34.5 us
    ppermute x29, starting transfers between devices, swap(): lax.ppermute(value, axis, [(i, i ^ flip) for i in range(lax.axis_size(axi...  27.9 us
    pallas_call x1, Pallas kernels, later_steps(): kernel(later_kernel, [shape(size, size), shape(*own.shape), shape(1, size...  13.5 us
    all_gather x1, blocking collectives, in_squares(): lax.all_gather(part, 'fsdp', axis=0, tiled=True, axis_index_groups=chips)  5.3 us
    pallas_call x1, Pallas kernels, first_step(): kernel(first_kernel, [shape(lanes, size), shape(size, size)], [smem] + [v...  5.06 us
    unnamed x6, local copies, waits for them, and re-layouts  4.38 us
    pallas_call x1, Pallas kernels, in_squares(): kernel(functools.partial(last_kernel, math.sqrt(total_rows / total_cols))...  3.69 us
    pallas_call x1, Pallas kernels, in_squares(): kernel(raw_kernel, [shape(width // 2, rank)] * 2, [smem, anywhere] + [vme...  3.42 us
  transfers between devices with their start and end apart: 29, of which 14 were waited for; matrix products, arithmetic and copies ran while one was open for 0% of the time, Pallas kernels for 30%

profile of v11, /device:TPU:0, one launch (start us, length us, event | category | flops | bytes accessed | tf_op | source)
XLA Modules:
  0.0 116.1 jit_solution(1809620892248223540)
XLA Ops:
  3.9 3.0 %collective-permute-start.1 = (f32[240,384]{1,0:T(8,128)S(1)}, f32[240,384]{1,0:T(8,128)S(1)}, u32[]{:S(2)}, u32[]{:S(2)}) collective-permute-start(f32[240,384]{1,0:T(8,128)S(1)} %get-tuple-element.39.refs_1_), channel_id=1, source_target_pairs={{0,4},{4,0},{8,12},{12,8},{16,20},{20,16},{24,28},{28,24},{1,5},{5... | collective-permute-start | bytes 1105928 | tf_op jit(solution)/shard_map/ppermute | solution.py:225
  10.4 3.4 %part_left.1 = (f32[120,512]{1,0:T(8,128)S(1)}, f32[120,512]{1,0:T(8,128)S(1)}) custom-call(s32[5]{0:T(128)S(1)} %stack.23.bits, f32[1536,512]{1,0:T(8,128)S(1)} %copy-done.1, f32[240,1536]{1,0:T(8,128)S(1)} %copy-done, bf16[240,1536]{1,0:T(8,128)(2,1)S(1)} %copy-done.2, f32[240,384]{1,0:T(8,128)S(1)} %get-tuple-element.36.token.refs_8_.refs_0_), custom_call_target="tpu_custom_call" | custom-call | tf_op jit(solution)/shard_map/part_left/pallas_call | solution.py:428
  13.8 2.2 %all_gather.6.both = f32[240,512]{1,0:T(8,128)S(1)} all-gather(f32[120,512]{1,0:T(8,128)S(1)} %get-tuple-element.38), channel_id=1, replica_groups={{0,1},{2,3},{4,5},{6,7},{8,9},{10,11},{12,13},{14,15},{16,17},{18,19},{..., dimensions={0}, use_global_device_ids=true | all-gather | bytes 737280 | tf_op jit(solution)/shard_map/all_gather | solution.py:436
  16.5 2.0 %collective-permute-start = (f32[120,512]{1,0:T(8,128)S(1)}, f32[120,512]{1,0:T(8,128)S(1)}, u32[]{:S(2)}, u32[]{:S(2)}) collective-permute-start(f32[120,512]{1,0:T(8,128)S(1)} %core_add.1.refs_0_), channel_id=1, source_target_pairs={{0,2},{1,3},{2,0},{3,1},{4,6},{5,7},{6,4},{7,5},{8,10},{9,11},{10,... | collective-permute-start | bytes 737288 | tf_op jit(solution)/shard_map/ppermute | solution.py:225
  18.5 6.3 %collective-permute-done.refs_1_ = f32[120,512]{1,0:T(8,128)S(1)} collective-permute-done((f32[120,512]{1,0:T(8,128)S(1)}, f32[120,512]{1,0:T(8,128)S(1)}, u32[]{:S(2)}, u32[]{:S(2)}) %collective-permute-start) | collective-permute-done | bytes 245792 | tf_op jit(solution)/shard_map/ppermute | solution.py:225
  24.8 2.8 %collective-permute-start.6 = (f32[120,512]{1,0:T(8,128)S(1)}, f32[120,512]{1,0:T(8,128)S(1)}, u32[]{:S(2)}, u32[]{:S(2)}) collective-permute-start(f32[120,512]{1,0:T(8,128)S(1)} %add_after.3.refs_0_.mine), channel_id=1, source_target_pairs={{0,12},{4,8},{8,4},{12,0},{16,28},{20,24},{24,20},{28,16},{1,13},{... | collective-permute-start | bytes 737288 | tf_op jit(solution)/shard_map/ppermute | solution.py:225
  28.4 6.3 %collective-permute-done.6.refs_3_ = f32[120,512]{1,0:T(8,128)S(1)} collective-permute-done((f32[120,512]{1,0:T(8,128)S(1)}, f32[120,512]{1,0:T(8,128)S(1)}, u32[]{:S(2)}, u32[]{:S(2)}) %collective-permute-start.6) | collective-permute-done | bytes 245792 | tf_op jit(solution)/shard_map/ppermute | solution.py:225
  34.7 3.8 %collective-permute-done.5.refs_2_ = f32[120,512]{1,0:T(8,128)S(1)} collective-permute-done((f32[120,512]{1,0:T(8,128)S(1)}, f32[120,512]{1,0:T(8,128)S(1)}, u32[]{:S(2)}, u32[]{:S(2)}) %collective-permute-start.5) | collective-permute-done | bytes 245792 | tf_op jit(solution)/shard_map/ppermute | solution.py:225
  39.0 2.1 %part_gram.1 = (f32[160,128]{1,0:T(8,128)S(1)}, f32[160,128]{1,0:T(8,128)S(1)}) custom-call(s32[5]{0:T(128)S(1)} %stack.23.bits, f32[120,512]{1,0:T(8,128)S(1)} %add_after.3.refs_0_.mine, f32[120,512]{1,0:T(8,128)S(1)} %collective-permute-done.4.refs_1_, f32[120,512]{1,0:T(8,128)S(1)} %collective-permute-done.5.refs_2_, ...), custom_call_target="tpu_custom_call" | custom-call | tf_op jit(solution)/shard_map/part_gram/pallas_call | solution.py:447
  42.5 2.6 %collective-permute-start.8 = (f32[160,128]{1,0:T(8,128)S(1)}, f32[160,128]{1,0:T(8,128)S(1)}, u32[]{:S(2)}, u32[]{:S(2)}) collective-permute-start(f32[160,128]{1,0:T(8,128)S(1)} %add.23.token.refs_0_), channel_id=1, source_target_pairs={{0,16},{4,20},{8,24},{12,28},{16,0},{20,4},{24,8},{28,12},{1,17},{... | collective-permute-start | bytes 245768 | tf_op jit(solution)/shard_map/ppermute | solution.py:225
  45.2 3.4 %part_raw.1 = (f32[192,512]{1,0:T(8,128)S(1)}, f32[192,512]{1,0:T(8,128)S(1)}) custom-call(s32[5]{0:T(128)S(1)} %stack.23.bits, f32[160,128]{1,0:T(8,128)S(1)} %add.23.token.refs_0_, f32[120,512]{1,0:T(8,128)S(1)} %add_after.3.refs_0_.mine, f32[120,512]{1,0:T(8,128)S(1)} %collective-permute-done.4.refs_1_, f32[120,512]{1,0:T(8,128)S(1)} %collective-permute-done.5.refs_2_, ...), custom_call_target="tpu_custom_call" | custom-call | tf_op jit(solution)/shard_map/part_raw/pallas_call | solution.py:456
  49.7 5.3 %all_gather.7.a = f32[320,128]{1,0:T(8,128)S(1)} all-gather(f32[160,128]{1,0:T(8,128)S(1)} %add_after.4), channel_id=1, replica_groups={{0,4},{8,12},{16,20},{24,28},{1,5},{9,13},{17,21},{25,29},{2,6},{10,14}..., dimensions={0}, use_global_device_ids=true | all-gather | bytes 245760 | tf_op jit(solution)/shard_map/all_gather | solution.py:470
  56.5 3.8 %collective-permute-done.14.c = f32[320,128]{1,0:T(8,128)S(1)} collective-permute-done((f32[320,128]{1,0:T(8,128)S(1)}, f32[320,128]{1,0:T(8,128)S(1)}, u32[]{:S(2)}, u32[]{:S(2)}) %collective-permute-start.14) | collective-permute-done | bytes 163872 | tf_op jit(solution)/shard_map/ppermute | solution.py:225
  61.7 5.1 %factor_first.1 = (f32[128,512]{1,0:T(8,128)S(1)}, f32[512,512]{1,0:T(8,128)S(1)}) custom-call(s32[5]{0:T(128)S(1)} %stack.23.bits, f32[320,128]{1,0:T(8,128)S(1)} %all_gather.7.a, f32[320,128]{1,0:T(8,128)S(1)} %collective-permute-done.13.b, f32[320,128]{1,0:T(8,128)S(1)} %collective-permute-done.14.c, f32[320,128]{1,0:T(8,128)S(1)} %collective-permute-done.15.d), custom_call_target="tpu_custom_call" | custom-call | tf_op jit(solution)/shard_map/factor_first/pallas_call | solution.py:169
  66.8 2.1 %collective-permute-done.16.refs_1_ = f32[192,512]{1,0:T(8,128)S(1)} collective-permute-done((f32[192,512]{1,0:T(8,128)S(1)}, f32[192,512]{1,0:T(8,128)S(1)}, u32[]{:S(2)}, u32[]{:S(2)}) %collective-permute-start.16) | collective-permute-done | bytes 393248 | tf_op jit(solution)/shard_map/ppermute | solution.py:225
  69.0 2.0 %collective-permute-start.18 = (f32[192,512]{1,0:T(8,128)S(1)}, f32[192,512]{1,0:T(8,128)S(1)}, u32[]{:S(2)}, u32[]{:S(2)}) collective-permute-start(f32[192,512]{1,0:T(8,128)S(1)} %add_after.5.own), channel_id=1, source_target_pairs={{0,8},{4,12},{8,0},{12,4},{16,24},{20,28},{24,16},{28,20},{1,9},{5... | collective-permute-start | bytes 1179656 | tf_op jit(solution)/shard_map/ppermute | solution.py:225
  72.2 13.5 %factor_later.1 = (f32[512,512]{1,0:T(8,128)S(1)}, f32[192,512]{1,0:T(8,128)S(1)}, f32[1,512]{1,0:T(1,128)S(1)}) custom-call(f32[512,512]{1,0:T(8,128)S(1)} %get-tuple-element.45.before, f32[128,512]{1,0:T(8,128)S(1)} %get-tuple-element.46.refs_2_.first, f32[192,512]{1,0:T(8,128)S(1)} %add_after.5.own), custom_call_target="tpu_custom_call" | custom-call | tf_op jit(solution)/shard_map/factor_later/pallas_call | solution.py:189
  85.7 2.7 %collective-permute-done.19.received = f32[192,512]{1,0:T(8,128)S(1)} collective-permute-done((f32[192,512]{1,0:T(8,128)S(1)}, f32[192,512]{1,0:T(8,128)S(1)}, u32[]{:S(2)}, u32[]{:S(2)}) %collective-permute-start.19) | collective-permute-done | bytes 393248 | tf_op jit(solution)/shard_map/ppermute | solution.py:225
  93.8 2.1 %collective-permute-done.21 = f32[1,512]{1,0:T(1,128)S(1)} collective-permute-done((f32[1,512]{1,0:T(1,128)S(1)}, f32[1,512]{1,0:T(1,128)S(1)}, u32[]{:S(2)}, u32[]{:S(2)}) %collective-permute-start.21) | collective-permute-done | bytes 2080 | tf_op jit(solution)/shard_map/ppermute | solution.py:225
  97.8 2.2 %beside.1 = (f32[384,512]{1,0:T(8,128)S(1)}, f32[104,512]{1,0:T(8,128)S(1)}, f32[104,512]{1,0:T(8,128)S(1)}) custom-call(f32[512,512]{1,0:T(8,128)S(1)} %get-tuple-element.48.inverse, f32[192,512]{1,0:T(8,128)S(1)} %collective-permute-done.17.one, f32[192,512]{1,0:T(8,128)S(1)} %collective-permute-done.18.two, f32[1,512]{1,0:T(1,128)S(1)} %add.25.token), custom_call_target="tpu_custom_call" | custom-call | tf_op jit(solution)/shard_map/beside/pallas_call | solution.py:495
  102.3 2.1 %collective-permute-start.26 = (f32[96,512]{1,0:T(8,128)S(1)}, f32[96,512]{1,0:T(8,128)S(1)}, u32[]{:S(2)}, u32[]{:S(2)}) collective-permute-start(f32[96,512]{1,0:T(8,128)S(1)} %get-tuple-element.57), channel_id=1, source_target_pairs={{0,8},{4,12},{8,0},{12,4},{16,24},{20,28},{24,16},{28,20},{1,9},{5... | collective-permute-start | bytes 589832 | tf_op jit(solution)/shard_map/ppermute | solution.py:225
  106.1 2.2 %collective-permute-done.27.one = f32[104,512]{1,0:T(8,128)S(1)} collective-permute-done((f32[104,512]{1,0:T(8,128)S(1)}, f32[104,512]{1,0:T(8,128)S(1)}, u32[]{:S(2)}, u32[]{:S(2)}) %collective-permute-start.27) | collective-permute-done | bytes 213024 | tf_op jit(solution)/shard_map/ppermute | solution.py:225
  109.3 2.9 %new_momentum.1 = (f32[240,1536]{1,0:T(8,128)}, f32[240,512]{1,0:T(8,128)}, bf16[576,1536]{1,0:T(8,128)(2,1)S(1)}, bf16[576,1536]{1,0:T(8,128)(2,1)S(1)}) custom-call(s32[5]{0:T(128)S(1)} %stack.23.bits, f32[240,512]{1,0:T(8,128)S(1)} %left.1, f32[192,512]{1,0:T(8,128)S(1)} %get-tuple-element.51.own_right, f32[384,512]{1,0:T(8,128)S(1)} %get-tuple-element.52.rights, ...), custom_call_target="tpu_custom_call" | custom-call | bytes 16777216 | tf_op jit(solution)/shard_map/new_momentum/pallas_call | solution.py:518
  112.3 3.7 %last.1 = (f32[240,1536]{1,0:T(8,128)}, bf16[240,1536]{1,0:T(8,128)(2,1)}, f32[192,512]{1,0:T(8,128)}) custom-call(s32[5]{0:T(128)S(1)} %stack.23.bits, f32[1,512]{1,0:T(1,128)S(1)} %add.26.squares, f32[240,512]{1,0:T(8,128)S(1)} %left.1, f32[192,512]{1,0:T(8,128)S(1)} %get-tuple-element.51.own_right, ...), custom_call_target="tpu_custom_call", output_to_operand_aliasing={{0}: (16, {})} | custom-call | tf_op jit(solution)/shard_map/last/pallas_call | solution.py:542
  (64 shorter events, 27.7 us)
Async XLA Ops:
  3.9 20.8 %collective-permute-start.1 = (f32[240,384]{1,0:T(8,128)S(1)}, f32[240,384]{1,0:T(8,128)S(1)}, u32[]{:S(2)}, u32[]{:S(2)}) collective-permute-start(f32[240,384]{1,0:T(8,128)S(1)} %get-tuple-element.39.refs_1_), channel_id=1, source_target_pairs={{0,4},{4,0},{8,12},{12,8},{16,20},{20,16},{24,28},{28,24},{1,5},{5... | collective-permute-start | bytes 1105928 | tf_op jit(solution)/shard_map/ppermute | solution.py:225
  6.9 17.8 %collective-permute-start.2 = (f32[240,384]{1,0:T(8,128)S(1)}, f32[240,384]{1,0:T(8,128)S(1)}, u32[]{:S(2)}, u32[]{:S(2)}) collective-permute-start(f32[240,384]{1,0:T(8,128)S(1)} %get-tuple-element.40.refs_2_), channel_id=1, source_target_pairs={{0,8},{4,12},{8,0},{12,4},{16,24},{20,28},{24,16},{28,20},{1,9},{5... | collective-permute-start | bytes 1105928 | tf_op jit(solution)/shard_map/ppermute | solution.py:225
  8.5 16.3 %collective-permute-start.3 = (f32[240,384]{1,0:T(8,128)S(1)}, f32[240,384]{1,0:T(8,128)S(1)}, u32[]{:S(2)}, u32[]{:S(2)}) collective-permute-start(f32[240,384]{1,0:T(8,128)S(1)} %get-tuple-element.41.refs_8_), channel_id=1, source_target_pairs={{0,12},{4,8},{8,4},{12,0},{16,28},{20,24},{24,20},{28,16},{1,13},{... | collective-permute-start | bytes 1105928 | tf_op jit(solution)/shard_map/ppermute | solution.py:225
  16.5 8.3 %collective-permute-start = (f32[120,512]{1,0:T(8,128)S(1)}, f32[120,512]{1,0:T(8,128)S(1)}, u32[]{:S(2)}, u32[]{:S(2)}) collective-permute-start(f32[120,512]{1,0:T(8,128)S(1)} %core_add.1.refs_0_), channel_id=1, source_target_pairs={{0,2},{1,3},{2,0},{3,1},{4,6},{5,7},{6,4},{7,5},{8,10},{9,11},{10,... | collective-permute-start | bytes 737288 | tf_op jit(solution)/shard_map/ppermute | solution.py:225
  24.8 9.9 %collective-permute-start.6 = (f32[120,512]{1,0:T(8,128)S(1)}, f32[120,512]{1,0:T(8,128)S(1)}, u32[]{:S(2)}, u32[]{:S(2)}) collective-permute-start(f32[120,512]{1,0:T(8,128)S(1)} %add_after.3.refs_0_.mine), channel_id=1, source_target_pairs={{0,12},{4,8},{8,4},{12,0},{16,28},{20,24},{24,20},{28,16},{1,13},{... | collective-permute-start | bytes 737288 | tf_op jit(solution)/shard_map/ppermute | solution.py:225
  27.6 10.9 %collective-permute-start.5 = (f32[120,512]{1,0:T(8,128)S(1)}, f32[120,512]{1,0:T(8,128)S(1)}, u32[]{:S(2)}, u32[]{:S(2)}) collective-permute-start(f32[120,512]{1,0:T(8,128)S(1)} %add_after.3.refs_0_.mine), channel_id=1, source_target_pairs={{0,8},{4,12},{8,0},{12,4},{16,24},{20,28},{24,16},{28,20},{1,9},{5... | collective-permute-start | bytes 737288 | tf_op jit(solution)/shard_map/ppermute | solution.py:225
  28.1 10.5 %collective-permute-start.4 = (f32[120,512]{1,0:T(8,128)S(1)}, f32[120,512]{1,0:T(8,128)S(1)}, u32[]{:S(2)}, u32[]{:S(2)}) collective-permute-start(f32[120,512]{1,0:T(8,128)S(1)} %add_after.3.refs_0_.mine), channel_id=1, source_target_pairs={{0,4},{4,0},{8,12},{12,8},{16,20},{20,16},{24,28},{28,24},{1,5},{5... | collective-permute-start | bytes 737288 | tf_op jit(solution)/shard_map/ppermute | solution.py:225
  28.4 16.7 %collective-permute-start.9 = (f32[120,512]{1,0:T(8,128)S(1)}, f32[120,512]{1,0:T(8,128)S(1)}, u32[]{:S(2)}, u32[]{:S(2)}) collective-permute-start(f32[120,512]{1,0:T(8,128)S(1)} %add_after.3.refs_0_.mine), channel_id=1, source_target_pairs={{0,1},{1,0},{2,3},{3,2},{4,5},{5,4},{6,7},{7,6},{8,9},{9,8},{10,11... | collective-permute-start | bytes 737288 | tf_op jit(solution)/shard_map/ppermute | solution.py:225
  34.7 10.4 %collective-permute-start.12 = (f32[120,512]{1,0:T(8,128)S(1)}, f32[120,512]{1,0:T(8,128)S(1)}, u32[]{:S(2)}, u32[]{:S(2)}) collective-permute-start(f32[120,512]{1,0:T(8,128)S(1)} %collective-permute-done.6.refs_3_), channel_id=1, source_target_pairs={{0,1},{1,0},{2,3},{3,2},{4,5},{5,4},{6,7},{7,6},{8,9},{9,8},{10,11... | collective-permute-start | bytes 737288 | tf_op jit(solution)/shard_map/ppermute | solution.py:225
  38.5 6.6 %collective-permute-start.11 = (f32[120,512]{1,0:T(8,128)S(1)}, f32[120,512]{1,0:T(8,128)S(1)}, u32[]{:S(2)}, u32[]{:S(2)}) collective-permute-start(f32[120,512]{1,0:T(8,128)S(1)} %collective-permute-done.5.refs_2_), channel_id=1, source_target_pairs={{0,1},{1,0},{2,3},{3,2},{4,5},{5,4},{6,7},{7,6},{8,9},{9,8},{10,11... | collective-permute-start | bytes 737288 | tf_op jit(solution)/shard_map/ppermute | solution.py:225
  38.5 6.6 %collective-permute-start.10 = (f32[120,512]{1,0:T(8,128)S(1)}, f32[120,512]{1,0:T(8,128)S(1)}, u32[]{:S(2)}, u32[]{:S(2)}) collective-permute-start(f32[120,512]{1,0:T(8,128)S(1)} %collective-permute-done.4.refs_1_), channel_id=1, source_target_pairs={{0,1},{1,0},{2,3},{3,2},{4,5},{5,4},{6,7},{7,6},{8,9},{9,8},{10,11... | collective-permute-start | bytes 737288 | tf_op jit(solution)/shard_map/ppermute | solution.py:225
  42.5 7.2 %collective-permute-start.8 = (f32[160,128]{1,0:T(8,128)S(1)}, f32[160,128]{1,0:T(8,128)S(1)}, u32[]{:S(2)}, u32[]{:S(2)}) collective-permute-start(f32[160,128]{1,0:T(8,128)S(1)} %add.23.token.refs_0_), channel_id=1, source_target_pairs={{0,16},{4,20},{8,24},{12,28},{16,0},{20,4},{24,8},{28,12},{1,17},{... | collective-permute-start | bytes 245768 | tf_op jit(solution)/shard_map/ppermute | solution.py:225
  48.6 20.3 %collective-permute-start.16 = (f32[192,512]{1,0:T(8,128)S(1)}, f32[192,512]{1,0:T(8,128)S(1)}, u32[]{:S(2)}, u32[]{:S(2)}) collective-permute-start(f32[192,512]{1,0:T(8,128)S(1)} %get-tuple-element.47), channel_id=1, source_target_pairs={{0,16},{4,20},{8,24},{12,28},{16,0},{20,4},{24,8},{28,12},{1,17},{... | collective-permute-start | bytes 1179656 | tf_op jit(solution)/shard_map/ppermute | solution.py:225
  55.0 5.3 %collective-permute-start.14 = (f32[320,128]{1,0:T(8,128)S(1)}, f32[320,128]{1,0:T(8,128)S(1)}, u32[]{:S(2)}, u32[]{:S(2)}) collective-permute-start(f32[320,128]{1,0:T(8,128)S(1)} %all_gather.7.a), channel_id=1, source_target_pairs={{0,2},{1,3},{2,0},{3,1},{4,6},{5,7},{6,4},{7,5},{8,10},{9,11},{10,... | collective-permute-start | bytes 491528 | tf_op jit(solution)/shard_map/ppermute | solution.py:225
  68.9 19.5 %collective-permute-start.19 = (f32[192,512]{1,0:T(8,128)S(1)}, f32[192,512]{1,0:T(8,128)S(1)}, u32[]{:S(2)}, u32[]{:S(2)}) collective-permute-start(f32[192,512]{1,0:T(8,128)S(1)} %add_after.5.own), channel_id=1, source_target_pairs={{0,16},{4,20},{8,24},{12,28},{16,0},{20,4},{24,8},{28,12},{1,17},{... | collective-permute-start | bytes 1179656 | tf_op jit(solution)/shard_map/ppermute | solution.py:225
  69.0 19.5 %collective-permute-start.18 = (f32[192,512]{1,0:T(8,128)S(1)}, f32[192,512]{1,0:T(8,128)S(1)}, u32[]{:S(2)}, u32[]{:S(2)}) collective-permute-start(f32[192,512]{1,0:T(8,128)S(1)} %add_after.5.own), channel_id=1, source_target_pairs={{0,8},{4,12},{8,0},{12,4},{16,24},{20,28},{24,16},{28,20},{1,9},{5... | collective-permute-start | bytes 1179656 | tf_op jit(solution)/shard_map/ppermute | solution.py:225
  71.0 17.6 %collective-permute-start.17 = (f32[192,512]{1,0:T(8,128)S(1)}, f32[192,512]{1,0:T(8,128)S(1)}, u32[]{:S(2)}, u32[]{:S(2)}) collective-permute-start(f32[192,512]{1,0:T(8,128)S(1)} %add_after.5.own), channel_id=1, source_target_pairs={{0,4},{4,0},{8,12},{12,8},{16,20},{20,16},{24,28},{28,24},{1,5},{5... | collective-permute-start | bytes 1179656 | tf_op jit(solution)/shard_map/ppermute | solution.py:225
  89.7 11.2 %collective-permute-start.24 = (f32[192,512]{1,0:T(8,128)S(1)}, f32[192,512]{1,0:T(8,128)S(1)}, u32[]{:S(2)}, u32[]{:S(2)}) collective-permute-start(f32[192,512]{1,0:T(8,128)S(1)} %get-tuple-element.53.refs_3_.refs_0_), channel_id=1, source_target_pairs={{0,8},{4,12},{8,0},{12,4},{16,24},{20,28},{24,16},{28,20},{1,9},{5... | collective-permute-start | bytes 1179656 | tf_op jit(solution)/shard_map/ppermute | solution.py:225
  89.8 11.2 %collective-permute-start.23 = (f32[192,512]{1,0:T(8,128)S(1)}, f32[192,512]{1,0:T(8,128)S(1)}, u32[]{:S(2)}, u32[]{:S(2)}) collective-permute-start(f32[192,512]{1,0:T(8,128)S(1)} %get-tuple-element.53.refs_3_.refs_0_), channel_id=1, source_target_pairs={{0,4},{4,0},{8,12},{12,8},{16,20},{20,16},{24,28},{28,24},{1,5},{5... | collective-permute-start | bytes 1179656 | tf_op jit(solution)/shard_map/ppermute | solution.py:225
  95.9 5.0 %collective-permute-start.22 = (f32[1,512]{1,0:T(1,128)S(1)}, f32[1,512]{1,0:T(1,128)S(1)}, u32[]{:S(2)}, u32[]{:S(2)}) collective-permute-start(f32[1,512]{1,0:T(1,128)S(1)} %add.25.token), channel_id=1, source_target_pairs={{0,8},{4,12},{8,0},{12,4},{16,24},{20,28},{24,16},{28,20},{1,9},{5... | collective-permute-start | bytes 6152 | tf_op jit(solution)/shard_map/ppermute | solution.py:225
  100.1 8.3 %collective-permute-start.27 = (f32[104,512]{1,0:T(8,128)S(1)}, f32[104,512]{1,0:T(8,128)S(1)}, u32[]{:S(2)}, u32[]{:S(2)}) collective-permute-start(f32[104,512]{1,0:T(8,128)S(1)} %get-tuple-element.58), channel_id=1, source_target_pairs={{0,4},{4,0},{8,12},{12,8},{16,20},{20,16},{24,28},{28,24},{1,5},{5... | collective-permute-start | bytes 638984 | tf_op jit(solution)/shard_map/ppermute | solution.py:225
  100.9 8.0 %collective-permute-start.28 = (f32[104,512]{1,0:T(8,128)S(1)}, f32[104,512]{1,0:T(8,128)S(1)}, u32[]{:S(2)}, u32[]{:S(2)}) collective-permute-start(f32[104,512]{1,0:T(8,128)S(1)} %get-tuple-element.59), channel_id=1, source_target_pairs={{0,8},{4,12},{8,0},{12,4},{16,24},{20,28},{24,16},{28,20},{1,9},{5... | collective-permute-start | bytes 638984 | tf_op jit(solution)/shard_map/ppermute | solution.py:225
  101.0 11.2 %collective-permute-start.25 = (f32[104,512]{1,0:T(8,128)S(1)}, f32[104,512]{1,0:T(8,128)S(1)}, u32[]{:S(2)}, u32[]{:S(2)}) collective-permute-start(f32[104,512]{1,0:T(8,128)S(1)} %get-tuple-element.56), channel_id=1, source_target_pairs={{0,4},{4,0},{8,12},{12,8},{16,20},{20,16},{24,28},{28,24},{1,5},{5... | collective-permute-start | bytes 638984 | tf_op jit(solution)/shard_map/ppermute | solution.py:225
  102.3 9.9 %collective-permute-start.26 = (f32[96,512]{1,0:T(8,128)S(1)}, f32[96,512]{1,0:T(8,128)S(1)}, u32[]{:S(2)}, u32[]{:S(2)}) collective-permute-start(f32[96,512]{1,0:T(8,128)S(1)} %get-tuple-element.57), channel_id=1, source_target_pairs={{0,8},{4,12},{8,0},{12,4},{16,24},{20,28},{24,16},{28,20},{1,9},{5... | collective-permute-start | bytes 589832 | tf_op jit(solution)/shard_map/ppermute | solution.py:225
  (8 other events, 15.7 us)
